TPU v7x, 32 devices: a whole 2x2x4 slice. The times are simulated.
32 devices in a mesh: parts: 2 (over x), region: 2 (over core), shard: 8 (over z, y).
Axes of the slice: x: 2, y: 2, z: 4, core: 2. Of those that a mesh axis runs over, the one named last changes fastest.
Arguments:
- vectors: bfloat16 [131072, 768], P(('parts', 'region', 'shard')), parts along dimension 0, may hold values from -6 to 6
- tile_region: int32 [1024], P(('parts', 'region', 'shard')), parts along dimension 0, may hold values from 0 to 1, as said below
- tile_block: int32 [1024], P(('parts', 'region', 'shard')), parts along dimension 0, may hold values from 0 to 63
- primary_pick: int32 [131072], P(('parts', 'region', 'shard')), parts along dimension 0, may hold values from 0 to 511
- spill_pick: int32 [131072], P(('parts', 'region', 'shard')), parts along dimension 0, may hold values from 0 to 511
- centers: bfloat16 [2, 32768, 768], P('region', 'shard'), may hold values from -6 to 6
Outputs:
- spill_scores: bfloat16 [131072, 512], P(('parts', 'region', 'shard')), parts along dimension 0
- primary_score: bfloat16 [131072], P(('parts', 'region', 'shard')), parts along dimension 0
- spill_chosen: bfloat16 [131072], P(('parts', 'region', 'shard')), parts along dimension 0
There are 2 independent parts, one for each index of `parts`. A program takes and returns all parts, laid end to end along the dimension named above; an argument that names none is the same for every part. Nothing has to cross between parts.
Inputs may be any that keep to these rules, and one draw needn't show every extreme that they name: For the 64 tiles of one device (aligned blocks of tile_region and tile_block), the pair (tile_region, tile_block // 8) takes any one value at most 4 times, and some value exactly 4 times.
All inputs are finite; a program needn't handle non-finite values.
Results may differ from a plain program's by a relative error of at most 0.0034.
Values may be sent and summed in bfloat16 or wider, within the bound.
No kernel may reach another device: no remote copies, remote signals or barrier semaphores. Data moves between devices by JAX's collectives and lax.ppermute only.
A program may use at most 128 MiB of HBM per device.

v0:
```python
import jax
import jax.numpy as jnp
from jax import lax
from jax.sharding import PartitionSpec as P

D = 768
TILE = 128
BLOCK = 512


soar_weight = 1.0
small_term = 1e-05


def as_sent(array):

    def short(part):
        return part.astype(jnp.bfloat16) if part.dtype == jnp.float32 else part

    return jax.tree.map(short, array)


def score_tile(points, block_rows, center_sq, primary_idx):
    point_f = points.astype(jnp.float32)
    point_sq = jnp.sum(point_f * point_f, axis=1)
    chosen = jnp.take(block_rows, primary_idx, axis=0).astype(jnp.float32)
    residue = point_f - chosen
    residue_sq = jnp.sum(residue * residue, axis=1)
    along = jnp.sum(residue * point_f, axis=1)
    residue_b = residue.astype(jnp.bfloat16)
    cross = jnp.einsum("td,cd->tc", points, block_rows, preferred_element_type=jnp.float32)
    against = jnp.einsum("td,cd->tc", residue_b, block_rows, preferred_element_type=jnp.float32)
    distance = point_sq[:, None] - 2.0 * cross + center_sq[None, :]
    scale_term = residue_sq / D + small_term
    penalty = jnp.square((along[:, None] - against) / D) / scale_term[:, None]
    spill = (distance / D + soar_weight * penalty).astype(jnp.bfloat16)
    primary = (residue_sq / D).astype(jnp.bfloat16)
    return (spill, primary)


def local(vectors, tile_region, tile_block, primary_pick, spill_pick, centers):
    n_region = lax.axis_size("region")
    n_shard = lax.axis_size("shard")
    targets = n_region * n_shard
    tile_dev = tile_region.shape[0]
    capacity = 2 * tile_dev // targets
    local_centers = centers[0]
    blk_dev = local_centers.shape[0] // BLOCK
    blocks = local_centers.reshape(blk_dev, BLOCK, D)
    center_norms = jnp.sum(jnp.square(blocks.astype(jnp.float32)), axis=2)
    target = tile_region * n_shard + tile_block // blk_dev
    inner_id = tile_block % blk_dev
    onehot = (target[:, None] == jnp.arange(targets, dtype=jnp.int32)[None, :]).astype(jnp.int32)
    earlier = jnp.cumsum(onehot, axis=0) - onehot
    rank_in = jnp.sum(earlier * onehot, axis=1)
    slot_of = target * capacity + rank_in
    slot_total = targets * capacity
    slot_hits = (slot_of[None, :] == jnp.arange(slot_total, dtype=jnp.int32)[:, None]).astype(
        jnp.int32
    )
    source = jnp.sum(slot_hits * jnp.arange(tile_dev, dtype=jnp.int32)[None, :], axis=1)
    filled = jnp.sum(slot_hits, axis=1) > 0
    tile_rows = vectors.reshape(tile_dev, TILE, D)
    primary_rows = primary_pick.reshape(tile_dev, TILE)
    tile_meta = jnp.stack(
        [jnp.broadcast_to(inner_id[:, None], (tile_dev, TILE)), primary_rows], axis=1
    )
    send_vectors = jnp.where(
        filled[:, None, None], jnp.take(tile_rows, source, axis=0), jnp.zeros((), jnp.bfloat16)
    )
    send_meta = jnp.where(filled[:, None, None], jnp.take(tile_meta, source, axis=0), 0)
    shaped_vectors = send_vectors.reshape(targets, capacity, TILE, D)
    shaped_meta = send_meta.reshape(targets, capacity, 2, TILE)
    recv_vectors = lax.all_to_all(
        shaped_vectors, ("region", "shard"), split_axis=0, concat_axis=0, tiled=True
    )
    recv_meta = lax.all_to_all(
        shaped_meta, ("region", "shard"), split_axis=0, concat_axis=0, tiled=True
    )
    senders = recv_vectors.shape[0]
    per_sender = recv_vectors.shape[1]
    flat_count = senders * per_sender

    def per_packet(packet):
        points, meta_one = packet
        inner_block = meta_one[0, 0]
        block_rows = lax.dynamic_index_in_dim(blocks, inner_block, 0, keepdims=False)
        center_sq = lax.dynamic_index_in_dim(center_norms, inner_block, 0, keepdims=False)
        return score_tile(points, block_rows, center_sq, meta_one[1])

    block_scores, primary_part = lax.map(
        per_packet,
        (recv_vectors.reshape(flat_count, TILE, D), recv_meta.reshape(flat_count, 2, TILE)),
        batch_size=8,
    )
    block_scores = block_scores.reshape(senders, per_sender, TILE, BLOCK)
    primary_part = primary_part.reshape(senders, per_sender, TILE)
    returned = lax.all_to_all(
        as_sent(block_scores), ("region", "shard"), split_axis=0, concat_axis=0, tiled=True
    ).astype(block_scores.dtype)
    primary_back = lax.all_to_all(
        as_sent(primary_part), ("region", "shard"), split_axis=0, concat_axis=0, tiled=True
    ).astype(primary_part.dtype)
    returned = returned.reshape(slot_total, TILE, BLOCK)
    primary_back = primary_back.reshape(slot_total, TILE)
    spill_scores = jnp.take(returned, slot_of, axis=0).reshape(tile_dev * TILE, BLOCK)
    primary_score = jnp.take(primary_back, slot_of, axis=0).reshape(tile_dev * TILE)
    spill_chosen = jnp.take_along_axis(spill_scores, spill_pick[:, None], axis=1)[:, 0]
    return (spill_scores, primary_score, spill_chosen)


def solution(mesh):
    in_specs = (
        P(("parts", "region", "shard"), None),
        P(("parts", "region", "shard")),
        P(("parts", "region", "shard")),
        P(("parts", "region", "shard")),
        P(("parts", "region", "shard")),
        P("region", "shard", None),
    )
    out_specs = (
        P(("parts", "region", "shard"), None),
        P(("parts", "region", "shard")),
        P(("parts", "region", "shard")),
    )
    return jax.shard_map(local, mesh=mesh, in_specs=in_specs, out_specs=out_specs, check_vma=False)
```

profile of v0, /device:TPU:9, one launch (start us, length us, event | category | flops | bytes accessed | tf_op | source)
XLA Modules:
  0.0 1116.1 jit_solution(12171758920007989790)
XLA Ops:
  4.2 6.6 all-to-all-start.1
  10.8 10.0 gather_fusion.3
  20.8 11.0 select_select_fusion
  31.9 6.0 all-to-all-start
  37.9 4.1 multiply_reduce_fusion.1
  42.0 268.8 %all-to-all-done = bf16[16,4,128,768]{3,2,1,0:T(8,128)(2,1)} async-done(((bf16[16,4,128,768]{3,2,1,0:T(8,128)(2,1)}), bf16[16,4,128,768]{3,2,1,0:T(8,128)(2,1)}, u32[]{:S(2)}, u32[]{:S(2)}) %all-to-all-start) | async-done | bytes 12582944 | tf_op jit(solution)/shard_map/all_to_all | solution.py:74
  310.8 304.0 %while.12 = (s32[]{:T(128)}, bf16[8,8,128,512]{3,2,1,0:T(8,128)(2,1)}, bf16[8,8,128]{2,1,0:T(8,128)(2,1)S(1)}, bf16[8,8,128,768]{3,2,1,0:T(8,128)(2,1)}, s32[8,8...) while((s32[]{:T(128)}, ...), condition=%wide.region_9.10_spmd, body=%wide.region_5.9_spmd.sunk | while | flops 1627667456 | bytes 41548672 | solution.py:91
  310.9 6.3 gather_fusion
  317.3 14.2 %gather_fusion.1 = bf16[1024,768]{1,0:T(8,128)(2,1)S(1)} fusion(bf16[8,512,768]{2,1,0:T(8,128)(2,1)} %gather_fusion, s32[1024]{0:T(1024)S(1)} %fusion.52), kind=kCustom, calls=%fused_computation.2.clone.1 | custom fusion | bytes 3153920 | tf_op jit(solution)/shard_map/while/body/eval_jaxpr/vmap(jit(_take))/gather | solution.py:26
  331.5 2.7 fusion.53
  334.2 6.7 fusion.51
  341.5 7.3 fusion.54
  348.9 6.3 gather_fusion
  355.3 14.2 %gather_fusion.1 = bf16[1024,768]{1,0:T(8,128)(2,1)S(1)} fusion(bf16[8,512,768]{2,1,0:T(8,128)(2,1)} %gather_fusion, s32[1024]{0:T(1024)S(1)} %fusion.52), kind=kCustom, calls=%fused_computation.2.clone.1 | custom fusion | bytes 3153920 | tf_op jit(solution)/shard_map/while/body/eval_jaxpr/vmap(jit(_take))/gather | solution.py:26
  372.3 6.7 fusion.51
  379.6 7.1 fusion.54
  386.8 6.3 gather_fusion
  393.2 14.2 %gather_fusion.1 = bf16[1024,768]{1,0:T(8,128)(2,1)S(1)} fusion(bf16[8,512,768]{2,1,0:T(8,128)(2,1)} %gather_fusion, s32[1024]{0:T(1024)S(1)} %fusion.52), kind=kCustom, calls=%fused_computation.2.clone.1 | custom fusion | bytes 3153920 | tf_op jit(solution)/shard_map/while/body/eval_jaxpr/vmap(jit(_take))/gather | solution.py:26
  410.2 6.7 fusion.51
  417.5 7.1 fusion.54
  424.8 6.3 gather_fusion
  431.2 14.3 %gather_fusion.1 = bf16[1024,768]{1,0:T(8,128)(2,1)S(1)} fusion(bf16[8,512,768]{2,1,0:T(8,128)(2,1)} %gather_fusion, s32[1024]{0:T(1024)S(1)} %fusion.52), kind=kCustom, calls=%fused_computation.2.clone.1 | custom fusion | bytes 3153920 | tf_op jit(solution)/shard_map/while/body/eval_jaxpr/vmap(jit(_take))/gather | solution.py:26
  445.5 2.7 fusion.53
  448.3 6.7 fusion.51
  455.6 7.1 fusion.54
  462.9 6.3 gather_fusion
  469.2 14.2 %gather_fusion.1 = bf16[1024,768]{1,0:T(8,128)(2,1)S(1)} fusion(bf16[8,512,768]{2,1,0:T(8,128)(2,1)} %gather_fusion, s32[1024]{0:T(1024)S(1)} %fusion.52), kind=kCustom, calls=%fused_computation.2.clone.1 | custom fusion | bytes 3153920 | tf_op jit(solution)/shard_map/while/body/eval_jaxpr/vmap(jit(_take))/gather | solution.py:26
  486.3 6.7 fusion.51
  493.5 7.2 fusion.54
  500.9 6.3 gather_fusion
  507.3 14.3 %gather_fusion.1 = bf16[1024,768]{1,0:T(8,128)(2,1)S(1)} fusion(bf16[8,512,768]{2,1,0:T(8,128)(2,1)} %gather_fusion, s32[1024]{0:T(1024)S(1)} %fusion.52), kind=kCustom, calls=%fused_computation.2.clone.1 | custom fusion | bytes 3153920 | tf_op jit(solution)/shard_map/while/body/eval_jaxpr/vmap(jit(_take))/gather | solution.py:26
  524.3 6.7 fusion.51
  531.6 7.1 fusion.54
  538.9 6.3 gather_fusion
  545.2 14.2 %gather_fusion.1 = bf16[1024,768]{1,0:T(8,128)(2,1)S(1)} fusion(bf16[8,512,768]{2,1,0:T(8,128)(2,1)} %gather_fusion, s32[1024]{0:T(1024)S(1)} %fusion.52), kind=kCustom, calls=%fused_computation.2.clone.1 | custom fusion | bytes 3153920 | tf_op jit(solution)/shard_map/while/body/eval_jaxpr/vmap(jit(_take))/gather | solution.py:26
  559.5 2.7 fusion.53
  562.2 6.7 fusion.51
  569.6 7.2 fusion.54
  576.8 6.3 gather_fusion
  583.2 14.3 %gather_fusion.1 = bf16[1024,768]{1,0:T(8,128)(2,1)S(1)} fusion(bf16[8,512,768]{2,1,0:T(8,128)(2,1)} %gather_fusion, s32[1024]{0:T(1024)S(1)} %fusion.52), kind=kCustom, calls=%fused_computation.2.clone.1 | custom fusion | bytes 3153920 | tf_op jit(solution)/shard_map/while/body/eval_jaxpr/vmap(jit(_take))/gather | solution.py:26
  600.3 6.7 fusion.51
  607.6 7.2 fusion.54
  614.8 246.5 %all_to_all.20 = bf16[16,4,128]{2,1,0:T(4,128)(2,1)S(1)} all-to-all(bf16[16,4,128]{2,1,0:T(4,128)(2,1)S(1)} %bitcast.106), channel_id=1, replica_groups=mesh['parts'=2,'region'=2,'shard'=8] {'region','shard'}, dimensions={0} | all-to-all | bytes 32768 | tf_op jit(solution)/shard_map/all_to_all | solution.py:101
  861.3 6.4 all-to-all-start.2
  869.2 181.6 %all-to-all-done.2 = bf16[16,4,128,512]{3,2,1,0:T(8,128)(2,1)} async-done(((bf16[16,4,128,512]{3,2,1,0:T(8,128)(2,1)}), bf16[16,4,128,512]{3,2,1,0:T(8,128)(2,1)}, u32[]{:S(2)}, u32[]{:S(2)}) %all-to-all-start.2) | async-done | bytes 8388640 | tf_op jit(solution)/shard_map/all_to_all | solution.py:98
  1050.8 6.2 gather_fusion.5
  1057.0 3.9 bitcast_select_fusion
  1060.9 54.6 %gather_fusion.7 = bf16[4096]{0:T(1024)(128)(2,1)S(1)} fusion(bf16[4096,512]{1,0:T(8,128)(2,1)} %bitcast_select_fusion, s32[4096]{0:T(1024)S(1)} %bitcast.95), kind=kCustom, calls=%fused_computation.7 | custom fusion | bytes 49152 | tf_op jit(solution)/shard_map/jit(take_along_axis)/gather | solution.py:108
  (102 shorter events, 25.2 us)
Async XLA Ops:
  4.2 27.7 %all-to-all-start.1 = ((s32[16,4,2,128]{3,1,2,0:T(4,128)}), s32[16,4,2,128]{3,1,2,0:T(4,128)S(1)}, u32[]{:S(2)}, u32[]{:S(2)}) async-start(s32[16,4,2,128]{3,1,2,0:T(4,128)} %fusion.28), calls=%async_computation.1 | async-start | bytes 131072 | tf_op jit(solution)/shard_map/all_to_all | solution.py:77
  31.9 278.9 %all-to-all-start = ((bf16[16,4,128,768]{3,2,1,0:T(8,128)(2,1)}), bf16[16,4,128,768]{3,2,1,0:T(8,128)(2,1)}, u32[]{:S(2)}, u32[]{:S(2)}) async-start(bf16[16,4,128,768]{3,2,1,0:T(8,128)(2,1)} %select_select_fusion), calls=%async_computation | async-start | bytes 25165824 | tf_op jit(solution)/shard_map/all_to_all | solution.py:74
  861.3 6.5 copy-start
  861.3 189.5 %all-to-all-start.2 = ((bf16[16,4,128,512]{3,2,1,0:T(8,128)(2,1)}), bf16[16,4,128,512]{3,2,1,0:T(8,128)(2,1)}, u32[]{:S(2)}, u32[]{:S(2)}) async-start(bf16[16,4,128,512]{3,2,1,0:T(8,128)(2,1)} %bitcast.101), calls=%async_computation.2 | async-start | bytes 16777216 | tf_op jit(solution)/shard_map/all_to_all | solution.py:98
where the time goes:
time: 1130 us; the launch traced here: 1120 us
  waiting for transfers between devices  450 us (40%)
  blocking collectives  247 us (22%)
  local copies, waits for them, and re-layouts  243 us (22%)
  matrix products  111 us (10%)
  other arithmetic  45.3 us (4%)
  starting transfers between devices  19 us (2%)
    all_to_all x1, waiting for transfers between devices, local(): lax.all_to_all(shaped_vectors, ('region', 'shard'), split_axis=0, concat_...  269 us
    all_to_all x1, blocking collectives, local(): lax.all_to_all(as_sent(primary_part), ('region', 'shard'), split_axis=0,...  247 us
    all_to_all x1, waiting for transfers between devices, local(): lax.all_to_all(as_sent(block_scores), ('region', 'shard'), split_axis=0,...  182 us
    gather x8, local copies, waits for them, and re-layouts, score_tile(): chosen = jnp.take(block_rows, primary_idx, axis=0).astype(jnp.float32)  114 us
    dot_general x8, matrix products, score_tile(): jnp.einsum('td,cd->tc', residue_b, block_rows, preferred_element_type=jnp...  57.4 us
    gather x1, local copies, waits for them, and re-layouts, local(): jnp.take_along_axis(spill_scores, spill_pick[:, None], axis=1)[:, 0]  54.6 us
    dot_general x8, matrix products, score_tile(): jnp.einsum('td,cd->tc', points, block_rows, preferred_element_type=jnp.fl...  53.7 us
    gather x8, local copies, waits for them, and re-layouts, per_packet(): lax.dynamic_index_in_dim(blocks, inner_block, 0, keepdims=False)  50.8 us
  transfers between devices with their start and end apart: 3, of which 2 were waited for; matrix products, arithmetic and copies ran while one was open for 2% of the time, Pallas kernels for 0%

commit v1 on v0

v1 whole, which is shorter than its diff:
```python
import functools

import jax
import jax.numpy as jnp
from jax import lax
from jax.experimental import pallas as pl
from jax.experimental.pallas import tpu as pltpu
from jax.sharding import PartitionSpec as P

D = 768
TILE = 128
BLOCK = 512
SMALL_TERM = 1e-05
AXES = ("parts", "region", "shard")
F32 = jnp.float32
BF16 = jnp.bfloat16
I32 = jnp.int32
ANY = pl.BlockSpec(memory_space=pl.ANY)
SMEM = pl.BlockSpec(memory_space=pltpu.SMEM)
VMEM = pl.BlockSpec(memory_space=pltpu.VMEM)


def dispatch_kernel(nz, cap, blk_dev, me, region, block, primary, spill, vec, *refs):
    tiles, metas, inv, count, sems = refs[:4], refs[4:8], refs[8], refs[9], refs[10]
    slots = nz * cap
    z, y, core = me[0], me[1], me[2]
    tile_dev = vec.shape[0]
    for d in range(4):
        metas[d][...] = jnp.full(metas[d].shape, -1, I32)

    def clear(i, carry):
        inv[i] = -1
        return carry

    def clear_count(i, carry):
        count[i] = 0
        return carry

    lax.fori_loop(0, 4 * slots, clear, 0)
    lax.fori_loop(0, 4 * nz, clear_count, 0)

    def place(t, carry):
        b = block[t]
        shard = b // blk_dev
        inner = b - shard * blk_dev
        partner = 2 * ((shard & 1) ^ y) + (region[t] ^ core)
        cls = (shard >> 1) ^ z
        at = partner * nz + cls
        rank = count[at]
        count[at] = rank + 1
        slot = cls * cap + rank
        inv[partner * slots + slot] = t
        rows = jnp.concatenate(
            [
                jnp.full((1, TILE), inner, I32),
                primary[pl.ds(t, 1), :],
                spill[pl.ds(t, 1), :],
                jnp.zeros((5, TILE), I32),
            ],
            axis=0,
        )
        for d in range(4):

            @pl.when(partner == d)
            def _():
                metas[d][slot] = rows
                pltpu.make_async_copy(vec.at[t], tiles[d].at[slot], sems.at[t]).start()

        return carry

    lax.fori_loop(0, tile_dev, place, 0)

    def finish(t, carry):
        pltpu.make_async_copy(vec.at[t], tiles[0].at[0], sems.at[t]).wait()
        return carry

    lax.fori_loop(0, tile_dev, finish, 0)


def dispatch(me, region, block, primary, spill, vec, nz, cap, blk_dev):
    slots = nz * cap
    tile_dev = vec.shape[0]
    out = pl.pallas_call(
        functools.partial(dispatch_kernel, nz, cap, blk_dev),
        out_shape=[jax.ShapeDtypeStruct((slots, TILE, D), BF16)] * 4
        + [jax.ShapeDtypeStruct((slots, 8, TILE), I32)] * 4
        + [jax.ShapeDtypeStruct((4 * slots,), I32)],
        in_specs=[SMEM, SMEM, SMEM, VMEM, VMEM, ANY],
        out_specs=[ANY] * 4 + [VMEM] * 4 + [SMEM],
        scratch_shapes=[pltpu.SMEM((4 * nz,), I32), pltpu.SemaphoreType.DMA((tile_dev,))],
        name="dispatch",
    )(me, region, block, primary, spill, vec)
    return out[:4], out[4:8], out[8]


def score_math(points, block_rows, meta):
    picks = meta.astype(F32).T.astype(I32)
    lane = lax.broadcasted_iota(I32, (TILE, BLOCK), 1)
    onehot = (lane == picks[:, 1:2]).astype(F32).astype(BF16)
    chosen = jnp.dot(onehot, block_rows, preferred_element_type=F32)
    point_f = points.astype(F32)
    residue = point_f - chosen
    point_sq = jnp.sum(point_f * point_f, axis=1, keepdims=True)
    residue_sq = jnp.sum(residue * residue, axis=1, keepdims=True)
    along = jnp.sum(residue * point_f, axis=1, keepdims=True)
    both = jnp.concatenate([points, residue.astype(BF16)], axis=0)
    products = lax.dot_general(
        both, block_rows, (((1,), (1,)), ((), ())), preferred_element_type=F32
    )
    cross, against = products[:TILE], products[TILE:]
    block_f = block_rows.astype(F32)
    squares = block_f * block_f
    partial = squares[:, :128]
    for k in range(1, D // 128):
        partial = partial + squares[:, k * 128 : (k + 1) * 128]
    center_sq = jnp.sum(partial.T, axis=0, keepdims=True)
    distance = point_sq - 2.0 * cross + center_sq
    mean_sq = residue_sq / D
    off = (along - against) / D
    scores = (distance / D + off * off * (1.0 / (mean_sq + SMALL_TERM))).astype(BF16)
    picked = jnp.sum(
        jnp.where(lane == picks[:, 2:3], scores.astype(F32), 0.0), axis=1, keepdims=True
    )
    column = lax.broadcasted_iota(I32, (TILE, 128), 1)
    small = jnp.where(column == 0, mean_sq, jnp.where(column == 1, picked, 0.0))
    return scores, small.T[:8]


def score_kernel(nz, cap, blk_dev, sub_blocks, group, order, fetched, me, ids, meta, *refs):
    slots = nz * cap
    wide = len(group) * cap
    n = len(order)
    tiles, refs = refs[:n], refs[n:]
    local, refs = refs[0], refs[1:]
    parts, refs = refs[: len(fetched)], refs[len(fetched) :]
    scores = refs[:n]
    small, work, xbuf, cbuf, obuf, xsem, csem, osem = refs[n:]
    z, half = me[0], me[3]
    half_blocks = blk_dev // 2
    base = group[0] * cap

    total = jnp.int32(0)
    for place, partner in enumerate(order):
        for k in range(wide):
            g = partner * slots + base + k
            work[total] = place * wide + k
            total = total + (ids[g] >= 0).astype(I32)

    def start(i, buf):
        code = work[i]
        place = code // wide
        slot = base + code - place * wide
        partner = jnp.int32(order[0])
        for other in range(1, n):
            partner = jnp.where(place == other, order[other], partner)
        b = ids[partner * slots + slot]
        for other in range(n):

            @pl.when(place == other)
            def _():
                pltpu.make_async_copy(tiles[other].at[slot], xbuf.at[buf], xsem.at[buf]).start()

        step = (z ^ (slot // cap)) - z
        own = b // half_blocks == half
        inside = b % half_blocks
        part = inside // sub_blocks
        row = inside % sub_blocks

        if group[0] == 0:

            @pl.when(step == 0)
            def _():
                pltpu.make_async_copy(local.at[b], cbuf.at[buf], csem.at[buf]).start()

        for ref, (hops, direct, index) in zip(parts, fetched):
            right = own if direct else jnp.logical_not(own)

            @pl.when((step == hops) & right & (part == index))
            def _():
                pltpu.make_async_copy(ref.at[row], cbuf.at[buf], csem.at[buf]).start()

    @pl.when(total > 0)
    def _():
        start(jnp.int32(0), jnp.int32(0))

    def body(i, carry):
        buf = i & 1

        @pl.when(i + 1 < total)
        def _():
            start(i + 1, 1 - buf)

        code = work[i]
        place = code // wide
        k = code - place * wide
        partner = jnp.int32(order[0])
        for other in range(1, n):
            partner = jnp.where(place == other, order[other], partner)
        pltpu.make_async_copy(tiles[0].at[0], xbuf.at[buf], xsem.at[buf]).wait()
        pltpu.make_async_copy(local.at[0], cbuf.at[buf], csem.at[buf]).wait()
        value, rows = score_math(xbuf[buf], cbuf[buf], meta[partner * slots + base + k])
        small[code] = rows

        @pl.when(i >= 2)
        def _():
            pltpu.make_async_copy(obuf.at[buf], scores[0].at[0], osem.at[buf]).wait()

        obuf[buf] = value
        for other in range(n):

            @pl.when(place == other)
            def _():
                pltpu.make_async_copy(obuf.at[buf], scores[other].at[k], osem.at[buf]).start()

        return carry

    lax.fori_loop(0, total, body, 0)

    for back in (2, 1):

        @pl.when(total >= back)
        def _():
            buf = (total - back) & 1
            pltpu.make_async_copy(obuf.at[buf], scores[0].at[0], osem.at[buf]).wait()


def score_call(nz, cap, blk_dev, sub_blocks, group, order, fetched, me, ids, meta, tiles, local, parts):
    wide = len(group) * cap
    n = len(order)
    items = n * wide
    out = pl.pallas_call(
        functools.partial(score_kernel, nz, cap, blk_dev, sub_blocks, group, order, fetched),
        out_shape=[jax.ShapeDtypeStruct((wide, TILE, BLOCK), BF16)] * n
        + [jax.ShapeDtypeStruct((items, 8, TILE), F32)],
        in_specs=[SMEM, SMEM, VMEM] + [ANY] * (n + 1 + len(parts)),
        out_specs=[ANY] * n + [VMEM],
        scratch_shapes=[
            pltpu.SMEM((items + 1,), I32),
            pltpu.VMEM((2, TILE, D), BF16),
            pltpu.VMEM((2, BLOCK, D), BF16),
            pltpu.VMEM((2, TILE, BLOCK), BF16),
            pltpu.SemaphoreType.DMA((2,)),
            pltpu.SemaphoreType.DMA((2,)),
            pltpu.SemaphoreType.DMA((2,)),
        ],
        compiler_params=pltpu.CompilerParams(vmem_limit_bytes=32 * 1024 * 1024),
        cost_estimate=pl.CostEstimate(
            flops=items * 3 * TILE * BLOCK * D, bytes_accessed=items * BLOCK * D, transcendentals=0
        ),
        name="score",
    )(me, ids, meta, *[tiles[p] for p in order], local, *parts)
    return {p: out[i] for i, p in enumerate(order)}, {
        p: out[n][i * wide : (i + 1) * wide] for i, p in enumerate(order)
    }


def assemble_kernel(slots, spans, inv, small, *refs):
    sources, (out, primary, picked, sems) = refs[: len(spans)], refs[len(spans) :]
    for ref, (first, count) in zip(sources, spans):
        for k in range(count):
            g = first + k
            t = inv[g]

            @pl.when(t >= 0)
            def _():
                pltpu.make_async_copy(ref.at[k], out.at[t], sems.at[g]).start()
                rows = small[g]
                primary[pl.ds(t, 1), :] = rows[0:1]
                picked[pl.ds(t, 1), :] = rows[1:2]

    for ref, (first, count) in zip(sources, spans):
        for k in range(count):
            g = first + k
            t = inv[g]

            @pl.when(t >= 0)
            def _():
                pltpu.make_async_copy(ref.at[k], out.at[t], sems.at[g]).wait()


def assemble(tile_dev, slots, spans, inv, small, sources):
    return pl.pallas_call(
        functools.partial(assemble_kernel, slots, spans),
        out_shape=[
            jax.ShapeDtypeStruct((tile_dev, TILE, BLOCK), BF16),
            jax.ShapeDtypeStruct((tile_dev, TILE), F32),
            jax.ShapeDtypeStruct((tile_dev, TILE), F32),
        ],
        in_specs=[SMEM, VMEM] + [ANY] * len(sources),
        out_specs=[ANY, VMEM, VMEM],
        scratch_shapes=[pltpu.SemaphoreType.DMA((4 * slots,))],
        name="assemble",
    )(inv, small, *sources)


def local_part(pieces, vectors, tile_region, tile_block, primary_pick, spill_pick, centers):
    n_parts, n_region, n_shard = (lax.axis_size(a) for a in AXES)
    nz = n_shard // 2
    tile_dev = tile_region.shape[0]
    cap = 2 * tile_dev // (n_region * n_shard)
    slots = nz * cap
    blk_dev = centers.shape[1] // BLOCK
    half_blocks = blk_dev // 2
    pieces = min(pieces, half_blocks)
    sub_blocks = half_blocks // pieces
    shard = lax.axis_index("shard")
    half = lax.axis_index("parts") & 1
    me = jnp.stack([shard >> 1, shard & 1, lax.axis_index("region"), half]).astype(I32)

    def device(p, r, s):
        return (p * n_region + r) * n_shard + s

    every = [(p, r, s) for p in range(n_parts) for r in range(n_region) for s in range(n_shard)]

    def permute(value, target, keep=lambda z: True):
        perm = []
        for p, r, s in every:
            to = target(p, r, s)
            if 0 <= to[2] < n_shard and keep(to[2] >> 1):
                perm.append((device(p, r, s), device(*to)))
        return lax.ppermute(value, AXES, perm)

    local = centers[0].reshape(blk_dev, BLOCK, D)

    own = [
        lax.dynamic_slice_in_dim(local, half * half_blocks + i * sub_blocks, sub_blocks, 0)
        for i in range(pieces)
    ]
    fetched = {}
    moving = {1: own, -1: own}
    for j in range(1, nz):
        for sign in (1, -1):
            keep = (lambda z, j=j: z + j < nz) if sign == 1 else (lambda z, j=j: z >= j)
            moving[sign] = [
                permute(piece, lambda p, r, s: (p, r, s - 2 * sign), keep) for piece in moving[sign]
            ]
            for i, piece in enumerate(moving[sign]):
                fetched[sign * j, True, i] = piece
                fetched[sign * j, False, i] = permute(piece, lambda p, r, s: (p ^ 1, r, s), keep)

    sent, meta_sent, inv = dispatch(
        me,
        tile_region,
        tile_block,
        primary_pick.reshape(tile_dev, TILE),
        spill_pick.reshape(tile_dev, TILE),
        vectors.reshape(tile_dev, TILE, D),
        nz,
        cap,
        blk_dev,
    )

    def exchange(value, partner):
        if partner == 0:
            return value
        return permute(value, lambda p, r, s: (p, r ^ (partner & 1), s ^ (partner >> 1)))

    metas = [exchange(meta_sent[d], d) for d in range(4)]
    tiles = [exchange(sent[d], d) for d in range(4)]
    meta = jnp.concatenate(metas, axis=0)
    ids = meta[:, 0, 0]

    cuts = sorted({0, nz // 2, 3 * nz // 4, nz})
    groups = [tuple(range(a, b)) for a, b in zip(cuts, cuts[1:])]
    spans, sources, smalls = [], [], {d: [] for d in range(4)}
    for group in groups:
        keys = []
        for q in group:
            for z in range(nz):
                hops = (z ^ q) - z
                if hops:
                    for direct in (True, False):
                        keys += [(hops, direct, i) for i in range(pieces)]
        keys = tuple(dict.fromkeys(keys))
        scores, small = score_call(
            nz, cap, blk_dev, sub_blocks, group, (2, 3, 1, 0), keys, me, ids, meta, tiles, local,
            [fetched[k] for k in keys],
        )
        for d in range(4):
            sources.append(exchange(scores[d], d))
            spans.append((d * slots + group[0] * cap, len(group) * cap))
            smalls[d].append(small[d])
    small = jnp.concatenate(
        [exchange(jnp.concatenate(smalls[d], axis=0), d) for d in range(4)], axis=0
    )
    spill_scores, primary, picked = assemble(tile_dev, slots, spans, inv, small, sources)
    return (
        spill_scores.reshape(tile_dev * TILE, BLOCK),
        primary.astype(BF16).reshape(tile_dev * TILE),
        picked.astype(BF16).reshape(tile_dev * TILE),
    )


def solution(mesh):
    rows = P(AXES, None)
    flat = P(AXES)
    return jax.shard_map(
        functools.partial(local_part, 1),
        mesh=mesh,
        in_specs=(rows, flat, flat, flat, flat, P("region", "shard", None)),
        out_specs=(rows, flat, flat),
        check_vma=False,
    )
```

time: 1130 us -> 792 us (0.70)
  Pallas kernels: 0 us -> 386 us
  blocking collectives: 247 us -> 0 us
  local copies, waits for them, and re-layouts: 243 us -> 13 us
  waiting for transfers between devices: 450 us -> 331 us
  matrix products: 111 us -> 0 us
  other arithmetic: 45.3 us -> 1.96 us
  starting transfers between devices: 19 us -> 50.1 us
    all_to_all x3 -> x0, waiting for transfers between devices: 450 us -> none  [the longest x1 269 us: local(): lax.all_to_all(shaped_vectors, ('region', 'shard'), split_axis=0, concat_...]
    pallas_call x0 -> x5, Pallas kernels: none -> 386 us  [the longest x1 194 us: dispatch(): pl.pallas_call(functools.partial(dispatch_kernel, nz, cap, blk_dev), out_...]
    ppermute x0 -> x30, waiting for transfers between devices: none -> 331 us  [permute(): return lax.ppermute(value, AXES, perm)]
    all_to_all x1 -> x0, blocking collectives: 247 us -> none  [local(): lax.all_to_all(as_sent(primary_part), ('region', 'shard'), split_axis=0,...]
    gather x29 -> x0, local copies, waits for them, and re-layouts: 241 us -> none  [the longest x8 114 us: score_tile(): chosen = jnp.take(block_rows, primary_idx, axis=0).astype(jnp.float32)]
    dot_general x16 -> x0, matrix products: 111 us -> none  [the longest x8 57.4 us: score_tile(): jnp.einsum('td,cd->tc', residue_b, block_rows, preferred_element_type=jnp...]
    ppermute x0 -> x30, starting transfers between devices: none -> 50.1 us  [permute(): return lax.ppermute(value, AXES, perm)]
    reduce_sum x11 -> x0, other arithmetic: 26.3 us -> none  [the longest x8 21.9 us: score_tile(): along = jnp.sum(residue * point_f, axis=1)]
  transfers between devices with their start and end apart: 3 -> 30, of which waited for: 2 -> 11; matrix products, arithmetic and copies ran while one was open for 2% -> 0% of each run, Pallas kernels for 0% -> 33%
where the time goes in v1:
time: 792 us; the launch traced here: 783 us
  Pallas kernels  386 us (49%)
  waiting for transfers between devices  331 us (42%)
  starting transfers between devices  50.1 us (6%)
  local copies, waits for them, and re-layouts  13 us (2%)
    ppermute x30, waiting for transfers between devices, permute(): return lax.ppermute(value, AXES, perm)  331 us
    pallas_call x1, Pallas kernels, dispatch(): pl.pallas_call(functools.partial(dispatch_kernel, nz, cap, blk_dev), out_...  194 us
    pallas_call x1, Pallas kernels, assemble(): pl.pallas_call(functools.partial(assemble_kernel, slots, spans), out_shap...  130 us
    pallas_call x3, Pallas kernels, score_call(): pl.pallas_call(functools.partial(score_kernel, nz, cap, blk_dev, sub_bloc...  61.2 us
    ppermute x30, starting transfers between devices, permute(): return lax.ppermute(value, AXES, perm)  50.1 us
  transfers between devices with their start and end apart: 30, of which 11 were waited for; matrix products, arithmetic and copies ran while one was open for 0% of the time, Pallas kernels for 33%

profile of v1, /device:TPU:9, one launch (start us, length us, event | category | flops | bytes accessed | tf_op | source)
XLA Modules:
  0.0 783.0 jit_solution(16281885324080905407)
XLA Ops:
  0.6 3.8 constant_dynamic-slice_fusion
  4.4 1.9 collective-permute-start.6
  6.4 3.4 collective-permute-start.8
  10.3 194.0 %dispatch.1 = (bf16[16,128,768]{2,1,0:T(8,128)(2,1)}, bf16[16,128,768]{2,1,0:T(8,128)(2,1)}, bf16[16,128,768]{2,1,0:T(8,128)(2,1)}, bf16[16,128,768]{2,1,0:T(8,1...) custom-call(s32[4]{0:T(128)} %pad_add_fusion.me, ...), custom_call_target="tpu_custom_call" | custom-call | tf_op jit(solution)/shard_map/dispatch/pallas_call | solution.py:83
  204.3 1.3 collective-permute-start.3
  205.6 3.7 collective-permute-start.10
  209.3 3.5 collective-permute-start.12
  212.8 2.2 collective-permute-start.4
  215.0 1.5 collective-permute-done
  216.5 1.2 collective-permute-start.1
  217.7 123.7 %collective-permute-done.1 = s32[16,8,128]{2,1,0:T(8,128)S(1)} collective-permute-done((s32[16,8,128]{2,1,0:T(8,128)}, s32[16,8,128]{2,1,0:T(8,128)S(1)}, u32[]{:S(2)}, u32[]{:S(2)}) %collective-permute-start.1) | collective-permute-done | bytes 65568 | tf_op jit(solution)/shard_map/ppermute | solution.py:321
  341.5 3.6 collective-permute-start.2
  345.0 3.0 collective-permute-done.2
  348.4 3.1 collective-permute-start.7
  351.6 3.9 collective-permute-start.14
  355.5 2.4 collective-permute-start.16
  357.9 1.9 collective-permute-start.9
  359.8 3.4 collective-permute-start.11
  363.2 56.7 %collective-permute-done.7.refs_6_.refs_8_ = bf16[4,512,768]{2,1,0:T(8,128)(2,1)S(1)} collective-permute-done((bf16[4,512,768]{2,1,0:T(8,128)(2,1)S(1)}, bf16[4,512,768]{2,1,0:T(8,128)(2,1)S(1)}, u32[]{:S(2)}, u32[]{:S(2)}) %collective-permute-start.7) | collective-permute-done | bytes 3145760 | tf_op jit(solution)/shard_map/ppermute | solution.py:321
  419.9 2.6 collective-permute-start.13
  422.5 0.9 collective-permute-start.15
  423.3 2.3 collective-permute-start.17
  425.7 0.8 constant_dynamic-update-slice_fusion.3
  426.6 1.3 slice_reduce_fusion.ids
  427.8 59.5 %collective-permute-done.9.refs_8_.refs_10_ = bf16[4,512,768]{2,1,0:T(8,128)(2,1)S(1)} collective-permute-done((bf16[4,512,768]{2,1,0:T(8,128)(2,1)}, bf16[4,512,768]{2,1,0:T(8,128)(2,1)S(1)}, u32[]{:S(2)}, u32[]{:S(2)}) %collective-permute-start.9) | collective-permute-done | bytes 3145760 | tf_op jit(solution)/shard_map/ppermute | solution.py:321
  487.3 1.7 copy-done.7
  489.0 1.9 copy-done
  490.9 29.0 %score.3 = (bf16[8,128,512]{2,1,0:T(8,128)(2,1)}, bf16[8,128,512]{2,1,0:T(8,128)(2,1)S(1)}, bf16[8,128,512]{2,1,0:T(8,128)(2,1)}, bf16[8,128,512]{2,1,0:T(8,128)(2,1)S(1)}, f32[32,8,128]{2,1,0:T(8,128)S(1)}) custom-call(s32[4]{0:T(128)S(1)} %copy-done.5, s32[64]{0:T(128)S(1)} %slice_reduce_fusion.ids, ...), custom_call_target="tpu_custom_call" | custom-call | flops 4831838208 | bytes 12582912 | tf_op jit(solution)/shard_map/score/pallas_call | solution.py:231
  519.9 1.0 copy-done.2
  521.0 33.8 %collective-permute-done.11.refs_6_ = bf16[4,512,768]{2,1,0:T(8,128)(2,1)} collective-permute-done((bf16[4,512,768]{2,1,0:T(8,128)(2,1)S(1)}, bf16[4,512,768]{2,1,0:T(8,128)(2,1)}, u32[]{:S(2)}, u32[]{:S(2)}) %collective-permute-start.11) | collective-permute-done | bytes 3145760 | tf_op jit(solution)/shard_map/ppermute | solution.py:321
  554.8 0.8 collective-permute-start.22
  555.6 1.8 collective-permute-start.23
  557.4 24.9 %score.4 = (bf16[4,128,512]{2,1,0:T(8,128)(2,1)S(1)}, bf16[4,128,512]{2,1,0:T(8,128)(2,1)S(1)}, bf16[4,128,512]{2,1,0:T(8,128)(2,1)S(1)}, bf16[4,128,512]{2,1,0:T(8,128)(2,1)S(1)}, f32[16,8,128]{2,1,0:T(8,128)S(1)}) custom-call(s32[4]{0:T(128)S(1)} %copy-done.5, s32[64]{0:T(128)S(1)} %slice_reduce_fusion.ids, ...), custom_call_target="tpu_custom_call" | custom-call | flops 2415919104 | bytes 6291456 | tf_op jit(solution)/shard_map/score/pallas_call | solution.py:231
  582.3 0.8 copy-done.3
  583.3 7.3 score.5
  590.6 0.8 copy-done.4
  591.6 2.2 collective-permute-start.20
  593.8 10.3 %collective-permute-done.23.refs_3_ = bf16[8,128,512]{2,1,0:T(8,128)(2,1)S(1)} collective-permute-done((bf16[8,128,512]{2,1,0:T(8,128)(2,1)S(1)}, bf16[8,128,512]{2,1,0:T(8,128)(2,1)S(1)}, u32[]{:S(2)}, u32[]{:S(2)}) %collective-permute-start.23) | collective-permute-done | bytes 1048608 | tf_op jit(solution)/shard_map/ppermute | solution.py:321
  604.8 1.1 collective-permute-start.27
  605.9 0.7 collective-permute-start.28
  606.6 1.0 collective-permute-start.29
  607.7 10.0 %collective-permute-done.25.refs_6_ = bf16[4,128,512]{2,1,0:T(8,128)(2,1)S(1)} collective-permute-done((bf16[4,128,512]{2,1,0:T(8,128)(2,1)S(1)}, bf16[4,128,512]{2,1,0:T(8,128)(2,1)S(1)}, u32[]{:S(2)}, u32[]{:S(2)}) %collective-permute-start.25) | collective-permute-done | bytes 524320 | tf_op jit(solution)/shard_map/ppermute | solution.py:321
  617.6 10.3 %collective-permute-done.26.refs_7_ = bf16[4,128,512]{2,1,0:T(8,128)(2,1)S(1)} collective-permute-done((bf16[4,128,512]{2,1,0:T(8,128)(2,1)S(1)}, bf16[4,128,512]{2,1,0:T(8,128)(2,1)S(1)}, u32[]{:S(2)}, u32[]{:S(2)}) %collective-permute-start.26) | collective-permute-done | bytes 524320 | tf_op jit(solution)/shard_map/ppermute | solution.py:321
  628.0 12.1 %collective-permute-done.28.refs_10_ = bf16[4,128,512]{2,1,0:T(8,128)(2,1)S(1)} collective-permute-done((bf16[4,128,512]{2,1,0:T(8,128)(2,1)S(1)}, bf16[4,128,512]{2,1,0:T(8,128)(2,1)S(1)}, u32[]{:S(2)}, u32[]{:S(2)}) %collective-permute-start.28) | collective-permute-done | bytes 524320 | tf_op jit(solution)/shard_map/ppermute | solution.py:321
  640.1 10.3 %collective-permute-done.29.refs_11_ = bf16[4,128,512]{2,1,0:T(8,128)(2,1)S(1)} collective-permute-done((bf16[4,128,512]{2,1,0:T(8,128)(2,1)S(1)}, bf16[4,128,512]{2,1,0:T(8,128)(2,1)S(1)}, u32[]{:S(2)}, u32[]{:S(2)}) %collective-permute-start.29) | collective-permute-done | bytes 524320 | tf_op jit(solution)/shard_map/ppermute | solution.py:321
  650.5 0.8 copy-done.16
  651.3 130.3 %assemble.1 = (bf16[32,128,512]{2,1,0:T(8,128)(2,1)}, f32[32,128]{1,0:T(8,128)}, f32[32,128]{1,0:T(8,128)}) custom-call(s32[64]{0:T(128)} %get-tuple-element.30.inv, f32[64,8,128]{2,1,0:T(8,128)} %copy-done.17, bf16[8,128,512]{2,1,0:T(8,128)(2,1)} %copy-done.2, bf16[8,128,512]{2,1,0:T(8,128)(2,1)} %copy-done.8, bf16[8,128,512]{2,1,0:T(8,128)(2,1)} %copy-done.9, ...), custom_call_target="tpu_custom_call" | custom-call | tf_op jit(solution)/shard_map/assemble/pallas_call | solution.py:282
  781.6 1.3 convert_bitcast_fusion
  (70 shorter events, 2.1 us)
Async XLA Ops:
  4.4 201.2 %collective-permute-start.6 = (bf16[4,512,768]{2,1,0:T(8,128)(2,1)}, bf16[4,512,768]{2,1,0:T(8,128)(2,1)S(1)}, u32[]{:S(2)}, u32[]{:S(2)}) collective-permute-start(bf16[4,512,768]{2,1,0:T(8,128)(2,1)} %constant_dynamic-slice_fusion), channel_id=1, source_target_pairs={{2,0},{3,1},{4,2},{5,3},{6,4},{7,5},{10,8},{11,9},{12,10},{13,11},... | collective-permute-start | bytes 9437192 | tf_op jit(solution)/shard_map/ppermute | solution.py:321
  6.4 203.0 %collective-permute-start.8 = (bf16[4,512,768]{2,1,0:T(8,128)(2,1)}, bf16[4,512,768]{2,1,0:T(8,128)(2,1)}, u32[]{:S(2)}, u32[]{:S(2)}) collective-permute-start(bf16[4,512,768]{2,1,0:T(8,128)(2,1)} %constant_dynamic-slice_fusion), channel_id=1, source_target_pairs={{0,2},{1,3},{2,4},{3,5},{4,6},{5,7},{8,10},{9,11},{10,12},{11,13},... | collective-permute-start | bytes 9437192 | tf_op jit(solution)/shard_map/ppermute | solution.py:321
  10.3 478.7 %copy-start.5 = (s32[4]{0:T(128)S(1)}, s32[4]{0:T(128)}, u32[]{:S(2)}) copy-start(s32[4]{0:T(128)} %pad_add_fusion.me) | copy-start | bytes 52
  204.3 144.1 %collective-permute-start.3 = (bf16[16,128,768]{2,1,0:T(8,128)(2,1)}, bf16[16,128,768]{2,1,0:T(8,128)(2,1)S(1)}, u32[]{:S(2)}, u32[]{:S(2)}) collective-permute-start(bf16[16,128,768]{2,1,0:T(8,128)(2,1)} %get-tuple-element.35), channel_id=1, source_target_pairs={{0,1},{1,0},{2,3},{3,2},{4,5},{5,4},{6,7},{7,6},{8,9},{9,8},{10,11... | collective-permute-start | bytes 9437192 | tf_op jit(solution)/shard_map/ppermute | solution.py:321
  205.6 314.3 %copy-start.1 = (bf16[4,512,768]{2,1,0:T(8,128)(2,1)}, bf16[4,512,768]{2,1,0:T(8,128)(2,1)S(1)}, u32[]{:S(2)}) copy-start(bf16[4,512,768]{2,1,0:T(8,128)(2,1)S(1)} %collective-permute-done.6.refs_5_.refs_7_) | copy-start | bytes 9437188
  205.6 145.9 %collective-permute-start.10 = (bf16[4,512,768]{2,1,0:T(8,128)(2,1)S(1)}, bf16[4,512,768]{2,1,0:T(8,128)(2,1)S(1)}, u32[]{:S(2)}, u32[]{:S(2)}) collective-permute-start(bf16[4,512,768]{2,1,0:T(8,128)(2,1)S(1)} %collective-permute-done.6.refs_5_.refs_7_), channel_id=1, source_target_pairs={{2,0},{3,1},{4,2},{5,3},{10,8},{11,9},{12,10},{13,11},{18,16},{19,... | collective-permute-start | bytes 9437192 | tf_op jit(solution)/shard_map/ppermute | solution.py:321
  209.3 146.1 %collective-permute-start.12 = (bf16[4,512,768]{2,1,0:T(8,128)(2,1)}, bf16[4,512,768]{2,1,0:T(8,128)(2,1)}, u32[]{:S(2)}, u32[]{:S(2)}) collective-permute-start(bf16[4,512,768]{2,1,0:T(8,128)(2,1)} %collective-permute-done.8.refs_7_.refs_9_), channel_id=1, source_target_pairs={{2,4},{3,5},{4,6},{5,7},{10,12},{11,13},{12,14},{13,15},{18,20},{1... | collective-permute-start | bytes 9437192 | tf_op jit(solution)/shard_map/ppermute | solution.py:321
  212.8 145.0 %collective-permute-start.4 = (bf16[16,128,768]{2,1,0:T(8,128)(2,1)}, bf16[16,128,768]{2,1,0:T(8,128)(2,1)S(1)}, u32[]{:S(2)}, u32[]{:S(2)}) collective-permute-start(bf16[16,128,768]{2,1,0:T(8,128)(2,1)} %get-tuple-element.36), channel_id=1, source_target_pairs={{0,9},{1,8},{2,11},{3,10},{4,13},{5,12},{6,15},{7,14},{8,1},{9,0},... | collective-permute-start | bytes 9437192 | tf_op jit(solution)/shard_map/ppermute | solution.py:321
  215.0 1.5 collective-permute-start
  216.5 124.9 %collective-permute-start.1 = (s32[16,8,128]{2,1,0:T(8,128)}, s32[16,8,128]{2,1,0:T(8,128)S(1)}, u32[]{:S(2)}, u32[]{:S(2)}) collective-permute-start(s32[16,8,128]{2,1,0:T(8,128)} %get-tuple-element.33), channel_id=1, source_target_pairs={{0,1},{1,0},{2,3},{3,2},{4,5},{5,4},{6,7},{7,6},{8,9},{9,8},{10,11... | collective-permute-start | bytes 196616 | tf_op jit(solution)/shard_map/ppermute | solution.py:321
  341.5 6.6 collective-permute-start.2
  348.1 11.7 %collective-permute-start.5 = (bf16[16,128,768]{2,1,0:T(8,128)(2,1)}, bf16[16,128,768]{2,1,0:T(8,128)(2,1)S(1)}, u32[]{:S(2)}, u32[]{:S(2)}) collective-permute-start(bf16[16,128,768]{2,1,0:T(8,128)(2,1)} %get-tuple-element.37), channel_id=1, source_target_pairs={{0,8},{1,9},{2,10},{3,11},{4,12},{5,13},{6,14},{7,15},{8,0},{9,1},... | collective-permute-start | bytes 9437192 | tf_op jit(solution)/shard_map/ppermute | solution.py:321
  348.4 71.4 %collective-permute-start.7 = (bf16[4,512,768]{2,1,0:T(8,128)(2,1)S(1)}, bf16[4,512,768]{2,1,0:T(8,128)(2,1)S(1)}, u32[]{:S(2)}, u32[]{:S(2)}) collective-permute-start(bf16[4,512,768]{2,1,0:T(8,128)(2,1)S(1)} %collective-permute-done.6.refs_5_.refs_7_), channel_id=1, source_target_pairs={{0,16},{1,17},{2,18},{3,19},{4,20},{5,21},{8,24},{9,25},{10,26},{1... | collective-permute-start | bytes 9437192 | tf_op jit(solution)/shard_map/ppermute | solution.py:321
  351.6 70.9 %collective-permute-start.14 = (bf16[4,512,768]{2,1,0:T(8,128)(2,1)S(1)}, bf16[4,512,768]{2,1,0:T(8,128)(2,1)S(1)}, u32[]{:S(2)}, u32[]{:S(2)}) collective-permute-start(bf16[4,512,768]{2,1,0:T(8,128)(2,1)S(1)} %collective-permute-done.10.refs_5_), channel_id=1, source_target_pairs={{2,0},{3,1},{10,8},{11,9},{18,16},{19,17},{26,24},{27,25}} | collective-permute-start | bytes 9437192 | tf_op jit(solution)/shard_map/ppermute | solution.py:321
  355.5 67.8 %collective-permute-start.16 = (bf16[4,512,768]{2,1,0:T(8,128)(2,1)}, bf16[4,512,768]{2,1,0:T(8,128)(2,1)}, u32[]{:S(2)}, u32[]{:S(2)}) collective-permute-start(bf16[4,512,768]{2,1,0:T(8,128)(2,1)} %collective-permute-done.12.refs_7_), channel_id=1, source_target_pairs={{4,6},{5,7},{12,14},{13,15},{20,22},{21,23},{28,30},{29,31}} | collective-permute-start | bytes 9437192 | tf_op jit(solution)/shard_map/ppermute | solution.py:321
  357.9 129.4 %collective-permute-start.9 = (bf16[4,512,768]{2,1,0:T(8,128)(2,1)}, bf16[4,512,768]{2,1,0:T(8,128)(2,1)S(1)}, u32[]{:S(2)}, u32[]{:S(2)}) collective-permute-start(bf16[4,512,768]{2,1,0:T(8,128)(2,1)} %collective-permute-done.8.refs_7_.refs_9_), channel_id=1, source_target_pairs={{2,18},{3,19},{4,20},{5,21},{6,22},{7,23},{10,26},{11,27},{12,28},... | collective-permute-start | bytes 9437192 | tf_op jit(solution)/shard_map/ppermute | solution.py:321
  359.8 195.0 %collective-permute-start.11 = (bf16[4,512,768]{2,1,0:T(8,128)(2,1)S(1)}, bf16[4,512,768]{2,1,0:T(8,128)(2,1)}, u32[]{:S(2)}, u32[]{:S(2)}) collective-permute-start(bf16[4,512,768]{2,1,0:T(8,128)(2,1)S(1)} %collective-permute-done.10.refs_5_), channel_id=1, source_target_pairs={{0,16},{1,17},{2,18},{3,19},{8,24},{9,25},{10,26},{11,27},{16,0},{... | collective-permute-start | bytes 9437192 | tf_op jit(solution)/shard_map/ppermute | solution.py:321
  419.9 2.6 copy-start.6
  419.9 135.7 %collective-permute-start.13 = (bf16[4,512,768]{2,1,0:T(8,128)(2,1)}, bf16[4,512,768]{2,1,0:T(8,128)(2,1)}, u32[]{:S(2)}, u32[]{:S(2)}) collective-permute-start(bf16[4,512,768]{2,1,0:T(8,128)(2,1)} %collective-permute-done.12.refs_7_), channel_id=1, source_target_pairs={{4,20},{5,21},{6,22},{7,23},{12,28},{13,29},{14,30},{15,31},{20,4}... | collective-permute-start | bytes 9437192 | tf_op jit(solution)/shard_map/ppermute | solution.py:321
  422.5 160.7 %collective-permute-start.15 = (bf16[4,512,768]{2,1,0:T(8,128)(2,1)S(1)}, bf16[4,512,768]{2,1,0:T(8,128)(2,1)S(1)}, u32[]{:S(2)}, u32[]{:S(2)}) collective-permute-start(bf16[4,512,768]{2,1,0:T(8,128)(2,1)S(1)} %collective-permute-done.14.refs_5_), channel_id=1, source_target_pairs={{0,16},{1,17},{8,24},{9,25},{16,0},{17,1},{24,8},{25,9}} | collective-permute-start | bytes 9437192 | tf_op jit(solution)/shard_map/ppermute | solution.py:321
  423.3 159.9 %collective-permute-start.17 = (bf16[4,512,768]{2,1,0:T(8,128)(2,1)}, bf16[4,512,768]{2,1,0:T(8,128)(2,1)}, u32[]{:S(2)}, u32[]{:S(2)}) collective-permute-start(bf16[4,512,768]{2,1,0:T(8,128)(2,1)} %collective-permute-done.16.refs_11_), channel_id=1, source_target_pairs={{6,22},{7,23},{14,30},{15,31},{22,6},{23,7},{30,14},{31,15}} | collective-permute-start | bytes 9437192 | tf_op jit(solution)/shard_map/ppermute | solution.py:321
  487.3 1.7 copy-start.7
  489.0 1.9 copy-start
  519.9 1.0 copy-start.2
  521.0 70.5 %collective-permute-start.21 = (bf16[8,128,512]{2,1,0:T(8,128)(2,1)}, bf16[8,128,512]{2,1,0:T(8,128)(2,1)S(1)}, u32[]{:S(2)}, u32[]{:S(2)}) collective-permute-start(bf16[8,128,512]{2,1,0:T(8,128)(2,1)} %get-tuple-element.43), channel_id=1, source_target_pairs={{0,8},{1,9},{2,10},{3,11},{4,12},{5,13},{6,14},{7,15},{8,0},{9,1},... | collective-permute-start | bytes 3145736 | tf_op jit(solution)/shard_map/ppermute | solution.py:321
  554.8 36.8 %collective-permute-start.22 = (bf16[8,128,512]{2,1,0:T(8,128)(2,1)}, bf16[8,128,512]{2,1,0:T(8,128)(2,1)S(1)}, u32[]{:S(2)}, u32[]{:S(2)}) collective-permute-start(bf16[8,128,512]{2,1,0:T(8,128)(2,1)} %get-tuple-element.44), channel_id=1, source_target_pairs={{0,1},{1,0},{2,3},{3,2},{4,5},{5,4},{6,7},{7,6},{8,9},{9,8},{10,11... | collective-permute-start | bytes 3145736 | tf_op jit(solution)/shard_map/ppermute | solution.py:321
  555.6 48.4 %collective-permute-start.23 = (bf16[8,128,512]{2,1,0:T(8,128)(2,1)S(1)}, bf16[8,128,512]{2,1,0:T(8,128)(2,1)S(1)}, u32[]{:S(2)}, u32[]{:S(2)}) collective-permute-start(bf16[8,128,512]{2,1,0:T(8,128)(2,1)S(1)} %get-tuple-element.45), channel_id=1, source_target_pairs={{0,9},{1,8},{2,11},{3,10},{4,13},{5,12},{6,15},{7,14},{8,1},{9,0},... | collective-permute-start | bytes 3145736 | tf_op jit(solution)/shard_map/ppermute | solution.py:321
  582.3 0.8 copy-start.3
  583.2 21.6 %collective-permute-start.24 = (bf16[4,128,512]{2,1,0:T(8,128)(2,1)S(1)}, bf16[4,128,512]{2,1,0:T(8,128)(2,1)S(1)}, u32[]{:S(2)}, u32[]{:S(2)}) collective-permute-start(bf16[4,128,512]{2,1,0:T(8,128)(2,1)S(1)} %get-tuple-element.47), channel_id=1, source_target_pairs={{0,8},{1,9},{2,10},{3,11},{4,12},{5,13},{6,14},{7,15},{8,0},{9,1},... | collective-permute-start | bytes 1572872 | tf_op jit(solution)/shard_map/ppermute | solution.py:321
  590.6 0.8 copy-start.4
  591.4 13.4 %collective-permute-start.18 = (f32[16,8,128]{2,1,0:T(8,128)S(1)}, f32[16,8,128]{2,1,0:T(8,128)S(1)}, u32[]{:S(2)}, u32[]{:S(2)}) collective-permute-start(f32[16,8,128]{2,1,0:T(8,128)S(1)} %pad_maximum_fusion), channel_id=1, source_target_pairs={{0,8},{1,9},{2,10},{3,11},{4,12},{5,13},{6,14},{7,15},{8,0},{9,1},... | collective-permute-start | bytes 196616 | tf_op jit(solution)/shard_map/ppermute | solution.py:321
  591.5 59.7 %copy-start.8 = (bf16[8,128,512]{2,1,0:T(8,128)(2,1)}, bf16[8,128,512]{2,1,0:T(8,128)(2,1)S(1)}, u32[]{:S(2)}) copy-start(bf16[8,128,512]{2,1,0:T(8,128)(2,1)S(1)} %collective-permute-done.21.refs_1_) | copy-start | bytes 3145732
  591.5 14.4 %collective-permute-start.19 = (f32[16,8,128]{2,1,0:T(8,128)S(1)}, f32[16,8,128]{2,1,0:T(8,128)S(1)}, u32[]{:S(2)}, u32[]{:S(2)}) collective-permute-start(f32[16,8,128]{2,1,0:T(8,128)S(1)} %pad_maximum_fusion.1), channel_id=1, source_target_pairs={{0,1},{1,0},{2,3},{3,2},{4,5},{5,4},{6,7},{7,6},{8,9},{9,8},{10,11... | collective-permute-start | bytes 196616 | tf_op jit(solution)/shard_map/ppermute | solution.py:321
  591.6 59.6 %copy-start.9 = (bf16[8,128,512]{2,1,0:T(8,128)(2,1)}, bf16[8,128,512]{2,1,0:T(8,128)(2,1)S(1)}, u32[]{:S(2)}) copy-start(bf16[8,128,512]{2,1,0:T(8,128)(2,1)S(1)} %collective-permute-done.22.refs_2_) | copy-start | bytes 3145732
  591.6 15.0 %collective-permute-start.20 = (f32[16,8,128]{2,1,0:T(8,128)S(1)}, f32[16,8,128]{2,1,0:T(8,128)S(1)}, u32[]{:S(2)}, u32[]{:S(2)}) collective-permute-start(f32[16,8,128]{2,1,0:T(8,128)S(1)} %pad_maximum_fusion.2), channel_id=1, source_target_pairs={{0,9},{1,8},{2,11},{3,10},{4,13},{5,12},{6,15},{7,14},{8,1},{9,0},... | collective-permute-start | bytes 196616 | tf_op jit(solution)/shard_map/ppermute | solution.py:321
  604.0 47.2 %copy-start.10 = (bf16[8,128,512]{2,1,0:T(8,128)(2,1)}, bf16[8,128,512]{2,1,0:T(8,128)(2,1)S(1)}, u32[]{:S(2)}) copy-start(bf16[8,128,512]{2,1,0:T(8,128)(2,1)S(1)} %collective-permute-done.23.refs_3_) | copy-start | bytes 3145732
  604.0 13.6 %collective-permute-start.25 = (bf16[4,128,512]{2,1,0:T(8,128)(2,1)S(1)}, bf16[4,128,512]{2,1,0:T(8,128)(2,1)S(1)}, u32[]{:S(2)}, u32[]{:S(2)}) collective-permute-start(bf16[4,128,512]{2,1,0:T(8,128)(2,1)S(1)} %get-tuple-element.48), channel_id=1, source_target_pairs={{0,1},{1,0},{2,3},{3,2},{4,5},{5,4},{6,7},{7,6},{8,9},{9,8},{10,11... | collective-permute-start | bytes 1572872 | tf_op jit(solution)/shard_map/ppermute | solution.py:321
  604.7 45.7 %copy-start.11 = (bf16[4,128,512]{2,1,0:T(8,128)(2,1)}, bf16[4,128,512]{2,1,0:T(8,128)(2,1)S(1)}, u32[]{:S(2)}) copy-start(bf16[4,128,512]{2,1,0:T(8,128)(2,1)S(1)} %collective-permute-done.24.refs_5_) | copy-start | bytes 1572868
  604.7 23.2 %collective-permute-start.26 = (bf16[4,128,512]{2,1,0:T(8,128)(2,1)S(1)}, bf16[4,128,512]{2,1,0:T(8,128)(2,1)S(1)}, u32[]{:S(2)}, u32[]{:S(2)}) collective-permute-start(bf16[4,128,512]{2,1,0:T(8,128)(2,1)S(1)} %get-tuple-element.49), channel_id=1, source_target_pairs={{0,9},{1,8},{2,11},{3,10},{4,13},{5,12},{6,15},{7,14},{8,1},{9,0},... | collective-permute-start | bytes 1572872 | tf_op jit(solution)/shard_map/ppermute | solution.py:321
  604.8 23.2 %collective-permute-start.27 = (bf16[4,128,512]{2,1,0:T(8,128)(2,1)S(1)}, bf16[4,128,512]{2,1,0:T(8,128)(2,1)S(1)}, u32[]{:S(2)}, u32[]{:S(2)}) collective-permute-start(bf16[4,128,512]{2,1,0:T(8,128)(2,1)S(1)} %get-tuple-element.51), channel_id=1, source_target_pairs={{0,8},{1,9},{2,10},{3,11},{4,12},{5,13},{6,14},{7,15},{8,0},{9,1},... | collective-permute-start | bytes 1572872 | tf_op jit(solution)/shard_map/ppermute | solution.py:321
  605.9 34.2 %collective-permute-start.28 = (bf16[4,128,512]{2,1,0:T(8,128)(2,1)S(1)}, bf16[4,128,512]{2,1,0:T(8,128)(2,1)S(1)}, u32[]{:S(2)}, u32[]{:S(2)}) collective-permute-start(bf16[4,128,512]{2,1,0:T(8,128)(2,1)S(1)} %get-tuple-element.52), channel_id=1, source_target_pairs={{0,1},{1,0},{2,3},{3,2},{4,5},{5,4},{6,7},{7,6},{8,9},{9,8},{10,11... | collective-permute-start | bytes 1572872 | tf_op jit(solution)/shard_map/ppermute | solution.py:321
  606.6 43.8 %collective-permute-start.29 = (bf16[4,128,512]{2,1,0:T(8,128)(2,1)S(1)}, bf16[4,128,512]{2,1,0:T(8,128)(2,1)S(1)}, u32[]{:S(2)}, u32[]{:S(2)}) collective-permute-start(bf16[4,128,512]{2,1,0:T(8,128)(2,1)S(1)} %get-tuple-element.53), channel_id=1, source_target_pairs={{0,9},{1,8},{2,11},{3,10},{4,13},{5,12},{6,15},{7,14},{8,1},{9,0},... | collective-permute-start | bytes 1572872 | tf_op jit(solution)/shard_map/ppermute | solution.py:321
  607.6 43.6 %copy-start.17 = (f32[64,8,128]{2,1,0:T(8,128)}, f32[64,8,128]{2,1,0:T(8,128)S(1)}, u32[]{:S(2)}) copy-start(f32[64,8,128]{2,1,0:T(8,128)S(1)} %constant_dynamic-update-slice_fusion.4.small) | copy-start | bytes 786436
  617.6 32.8 %copy-start.12 = (bf16[4,128,512]{2,1,0:T(8,128)(2,1)}, bf16[4,128,512]{2,1,0:T(8,128)(2,1)S(1)}, u32[]{:S(2)}) copy-start(bf16[4,128,512]{2,1,0:T(8,128)(2,1)S(1)} %collective-permute-done.25.refs_6_) | copy-start | bytes 1572868
  628.0 22.5 %copy-start.13 = (bf16[4,128,512]{2,1,0:T(8,128)(2,1)}, bf16[4,128,512]{2,1,0:T(8,128)(2,1)S(1)}, u32[]{:S(2)}) copy-start(bf16[4,128,512]{2,1,0:T(8,128)(2,1)S(1)} %collective-permute-done.26.refs_7_) | copy-start | bytes 1572868
  628.0 22.5 %copy-start.14 = (bf16[4,128,512]{2,1,0:T(8,128)(2,1)}, bf16[4,128,512]{2,1,0:T(8,128)(2,1)S(1)}, u32[]{:S(2)}) copy-start(bf16[4,128,512]{2,1,0:T(8,128)(2,1)S(1)} %collective-permute-done.27.refs_9_) | copy-start | bytes 1572868
  640.1 10.4 %copy-start.15 = (bf16[4,128,512]{2,1,0:T(8,128)(2,1)}, bf16[4,128,512]{2,1,0:T(8,128)(2,1)S(1)}, u32[]{:S(2)}) copy-start(bf16[4,128,512]{2,1,0:T(8,128)(2,1)S(1)} %collective-permute-done.28.refs_10_) | copy-start | bytes 1572868
  650.4 0.8 copy-start.16

commit v2 on v1

v2 whole, which is shorter than its diff:
```python
import functools

import jax
import jax.numpy as jnp
from jax import lax
from jax.experimental import pallas as pl
from jax.experimental.pallas import tpu as pltpu
from jax.sharding import PartitionSpec as P

D = 768
TILE = 128
BLOCK = 512
SMALL_TERM = 1e-05
AXES = ("parts", "region", "shard")
F32 = jnp.float32
BF16 = jnp.bfloat16
I32 = jnp.int32
ANY = pl.BlockSpec(memory_space=pl.ANY)
SMEM = pl.BlockSpec(memory_space=pltpu.SMEM)
VMEM_BYTES = 56 * 1024 * 1024
VMEM = pl.BlockSpec(memory_space=pltpu.VMEM)


def ring_place(nz):
    ring = list(range(0, nz, 2))[:1] + list(range(1, nz, 2)) + list(range(2, nz, 2))[::-1]
    return ring, [ring.index(z) for z in range(nz)]


def place_of(z, nz):
    return jnp.where(z == 0, 0, jnp.where(z & 1 == 1, (z + 1) // 2, nz - z // 2))


def plan_kernel(nz, cap, blk_dev, me, region, block, primary, spill, *refs):
    metas, at_slot, inv, count = refs[:4], refs[4], refs[5], refs[6]
    slots = nz * cap
    at_ring, y, core = me[0], me[1], me[2]
    for d in range(4):
        metas[d][...] = jnp.full(metas[d].shape, -1, I32)

    def clear(i, carry):
        inv[i] = -1
        return carry

    def clear_count(i, carry):
        count[i] = 0
        return carry

    lax.fori_loop(0, 4 * slots, clear, 0)
    lax.fori_loop(0, 4 * nz, clear_count, 0)

    def place(t, carry):
        b = block[t]
        shard = b // blk_dev
        inner = b - shard * blk_dev
        partner = 2 * ((shard & 1) ^ y) + (region[t] ^ core)
        cls = lax.rem(at_ring - place_of(shard >> 1, nz) + nz, nz)
        at = partner * nz + cls
        rank = count[at]
        count[at] = rank + 1
        slot = cls * cap + rank
        inv[partner * slots + slot] = t
        at_slot[t] = partner * slots + slot
        rows = jnp.concatenate(
            [
                jnp.full((1, TILE), inner, I32),
                primary[pl.ds(t, 1), :],
                spill[pl.ds(t, 1), :],
                jnp.zeros((5, TILE), I32),
            ],
            axis=0,
        )
        for d in range(4):

            @pl.when(partner == d)
            def _():
                metas[d][slot] = rows

        return carry

    lax.fori_loop(0, region.shape[0], place, 0)


def plan(me, region, block, primary, spill, nz, cap, blk_dev):
    slots = nz * cap
    out = pl.pallas_call(
        functools.partial(plan_kernel, nz, cap, blk_dev),
        out_shape=[jax.ShapeDtypeStruct((slots, 8, TILE), I32)] * 4
        + [
            jax.ShapeDtypeStruct(region.shape, I32),
            jax.ShapeDtypeStruct((4 * slots,), I32),
        ],
        in_specs=[SMEM, SMEM, SMEM, VMEM, VMEM],
        out_specs=[VMEM] * 4 + [SMEM, SMEM],
        scratch_shapes=[pltpu.SMEM((4 * nz,), I32)],
        name="plan",
    )(me, region, block, primary, spill)
    return out[:4], out[4], out[5]


def dispatch_kernel(slots, at_slot, vec, *refs):
    refs = refs[4:]
    tiles, (held, in_sems, out_sems) = refs[:5], refs[5:]
    tile_dev = vec.shape[0]
    part = slots // 2

    def each(act):
        def body(t, carry):
            partner = at_slot[t] // slots

            @pl.when(partner > 0)
            def _():
                act(t, at_slot[t])

            return carry

        lax.fori_loop(0, tile_dev, body, 0)

    def bring(t, g):
        pltpu.make_async_copy(vec.at[t], held.at[t], in_sems.at[t]).start()

    def send(t, g):
        pltpu.make_async_copy(vec.at[t], held.at[t], in_sems.at[t]).wait()
        for i, first in enumerate((slots, 2 * slots, 2 * slots + part, 3 * slots, 3 * slots + part)):
            count = slots if i == 0 else part

            @pl.when((g >= first) & (g < first + count))
            def _():
                pltpu.make_async_copy(held.at[t], tiles[i].at[g - first], out_sems.at[t]).start()

    def finish(t, g):
        pltpu.make_async_copy(held.at[t], tiles[0].at[0], out_sems.at[t]).wait()

    each(bring)
    each(send)
    each(finish)


def dispatch(at_slot, vec, metas, slots):
    tile_dev = vec.shape[0]
    return pl.pallas_call(
        functools.partial(dispatch_kernel, slots),
        out_shape=[
            jax.ShapeDtypeStruct((n, TILE, D), BF16) for n in (slots,) + (slots // 2,) * 4
        ],
        in_specs=[SMEM, ANY] + [ANY] * 4,
        out_specs=[ANY] * 5,
        scratch_shapes=[
            pltpu.VMEM((tile_dev, TILE, D), BF16),
            pltpu.SemaphoreType.DMA((tile_dev,)),
            pltpu.SemaphoreType.DMA((tile_dev,)),
        ],
        compiler_params=pltpu.CompilerParams(vmem_limit_bytes=VMEM_BYTES),
        name="dispatch",
    )(at_slot, vec, *metas)


def gate_kernel(*refs):
    pass


def gate(passed, others):
    n = len(passed)
    return pl.pallas_call(
        gate_kernel,
        out_shape=[jax.ShapeDtypeStruct(v.shape, v.dtype) for v in passed],
        in_specs=[ANY] * (n + len(others)),
        out_specs=[ANY] * n,
        input_output_aliases={i: i for i in range(n)},
        compiler_params=pltpu.CompilerParams(vmem_limit_bytes=VMEM_BYTES),
        name="gate",
    )(*passed, *others)


def score_math(points, block_rows, meta):
    picks = meta.astype(F32).T.astype(I32)
    lane = lax.broadcasted_iota(I32, (TILE, BLOCK), 1)
    onehot = (lane == picks[:, 1:2]).astype(F32).astype(BF16)
    chosen = jnp.dot(onehot, block_rows, preferred_element_type=F32)
    point_f = points.astype(F32)
    residue = point_f - chosen
    point_sq = jnp.sum(point_f * point_f, axis=1, keepdims=True)
    residue_sq = jnp.sum(residue * residue, axis=1, keepdims=True)
    along = jnp.sum(residue * point_f, axis=1, keepdims=True)
    both = jnp.concatenate([points, residue.astype(BF16)], axis=0)
    products = lax.dot_general(
        both, block_rows, (((1,), (1,)), ((), ())), preferred_element_type=F32
    )
    cross, against = products[:TILE], products[TILE:]
    block_f = block_rows.astype(F32)
    squares = block_f * block_f
    partial = squares[:, :128]
    for k in range(1, D // 128):
        partial = partial + squares[:, k * 128 : (k + 1) * 128]
    center_sq = jnp.sum(partial.T, axis=0, keepdims=True)
    distance = point_sq - 2.0 * cross + center_sq
    mean_sq = residue_sq / D
    off = (along - against) / D
    scores = (distance / D + off * off * (1.0 / (mean_sq + SMALL_TERM))).astype(BF16)
    picked = jnp.sum(
        jnp.where(lane == picks[:, 2:3], scores.astype(F32), 0.0), axis=1, keepdims=True
    )
    column = lax.broadcasted_iota(I32, (TILE, 128), 1)
    small = jnp.where(column == 0, mean_sq, jnp.where(column == 1, picked, 0.0))
    return scores, small.T[:8]


def score_kernel(nz, cap, blk_dev, sub_blocks, group, order, fetched, bases, me, ids, inv, meta, *refs):
    slots = nz * cap
    wide = len(group) * cap
    n = len(order)
    tiles, refs = refs[:n], refs[n:]
    local, refs = refs[0], refs[1:]
    before, refs = (refs[:n], refs[n:]) if group[0] else ((), refs)
    parts, refs = refs[: len(fetched)], refs[len(fetched) :]
    scores, smalls = refs[:n], refs[n : 2 * n]
    work, xbuf, cbuf, obuf, xsem, csem, osem = refs[2 * n :]
    half = me[3]
    half_blocks = blk_dev // 2
    base = group[0] * cap
    for old, new in zip(before, smalls):
        new[...] = old[...]

    total = jnp.int32(0)
    for place, partner in enumerate(order):
        for k in range(wide):
            g = partner * slots + base + k
            work[total] = place * wide + k
            total = total + (ids[g] >= 0).astype(I32)

    def start(i, buf):
        code = work[i]
        place = code // wide
        slot = base + code - place * wide
        partner = jnp.int32(order[0])
        for other in range(1, n):
            partner = jnp.where(place == other, order[other], partner)
        b = ids[partner * slots + slot]
        for other in range(n):
            row = slot - bases[other] if order[other] else jnp.maximum(inv[slot], 0)

            @pl.when(place == other)
            def _():
                pltpu.make_async_copy(tiles[other].at[row], xbuf.at[buf], xsem.at[buf]).start()

        cls = slot // cap
        own = b // half_blocks == half
        inside = b % half_blocks
        part = inside // sub_blocks
        row = inside % sub_blocks

        if group[0] == 0:

            @pl.when(cls == 0)
            def _():
                pltpu.make_async_copy(local.at[b], cbuf.at[buf], csem.at[buf]).start()

        for ref, (hops, direct, index) in zip(parts, fetched):
            right = own if direct else jnp.logical_not(own)

            @pl.when((cls == hops) & right & (part == index))
            def _():
                pltpu.make_async_copy(ref.at[row], cbuf.at[buf], csem.at[buf]).start()

    @pl.when(total > 0)
    def _():
        start(jnp.int32(0), jnp.int32(0))

    def body(i, carry):
        buf = i & 1

        @pl.when(i + 1 < total)
        def _():
            start(i + 1, 1 - buf)

        code = work[i]
        place = code // wide
        k = code - place * wide
        partner = jnp.int32(order[0])
        for other in range(1, n):
            partner = jnp.where(place == other, order[other], partner)
        pltpu.make_async_copy(tiles[0].at[0], xbuf.at[buf], xsem.at[buf]).wait()
        pltpu.make_async_copy(local.at[0], cbuf.at[buf], csem.at[buf]).wait()
        value, rows = score_math(xbuf[buf], cbuf[buf], meta[partner * slots + base + k])
        @pl.when(i >= 2)
        def _():
            pltpu.make_async_copy(obuf.at[buf], scores[0].at[0], osem.at[buf]).wait()

        obuf[buf] = value
        for other in range(n):

            @pl.when(place == other)
            def _():
                smalls[other][base + k] = rows
                pltpu.make_async_copy(obuf.at[buf], scores[other].at[k], osem.at[buf]).start()

        return carry

    lax.fori_loop(0, total, body, 0)

    for back in (2, 1):

        @pl.when(total >= back)
        def _():
            buf = (total - back) & 1
            pltpu.make_async_copy(obuf.at[buf], scores[0].at[0], osem.at[buf]).wait()


def score_call(
    nz, cap, blk_dev, sub_blocks, group, order, fetched, bases, me, ids, inv, meta, tiles, local, before, parts
):
    wide = len(group) * cap
    n = len(order)
    items = n * wide
    out = pl.pallas_call(
        functools.partial(score_kernel, nz, cap, blk_dev, sub_blocks, group, order, fetched, bases),
        out_shape=[jax.ShapeDtypeStruct((wide, TILE, BLOCK), BF16)] * n
        + [jax.ShapeDtypeStruct((nz * cap, 8, TILE), F32)] * n,
        in_specs=[SMEM, SMEM, SMEM, VMEM]
        + [ANY] * (n + 1)
        + [VMEM] * len(before)
        + [ANY] * len(parts),
        out_specs=[ANY] * n + [VMEM] * n,
        scratch_shapes=[
            pltpu.SMEM((items + 1,), I32),
            pltpu.VMEM((2, TILE, D), BF16),
            pltpu.VMEM((2, BLOCK, D), BF16),
            pltpu.VMEM((2, TILE, BLOCK), BF16),
            pltpu.SemaphoreType.DMA((2,)),
            pltpu.SemaphoreType.DMA((2,)),
            pltpu.SemaphoreType.DMA((2,)),
        ],
        compiler_params=pltpu.CompilerParams(vmem_limit_bytes=VMEM_BYTES),
        cost_estimate=pl.CostEstimate(
            flops=items * 3 * TILE * BLOCK * D, bytes_accessed=items * BLOCK * D, transcendentals=0
        ),
        name="score",
    )(me, ids, inv, meta, *tiles, local, *before, *parts)
    return out[:n], out[n:]


def assemble_kernel(first, wide, n_before, slots, inv, *refs):
    n = len(first)
    sources, refs = refs[:n], refs[n + n_before :]
    smalls, refs = (refs[:4], refs[4:]) if slots else ((), refs)
    out, refs = refs[0], refs[1:]
    (primary, picked), refs = (refs[:2], refs[2:]) if slots else ((None, None), refs)
    held, in_sems, out_sems = refs

    def each(act):
        for d in range(n):
            for k in range(wide):
                t = inv[first[d] + k]

                @pl.when(t >= 0)
                def _():
                    act(d, k, t, d * wide + k)

    def bring(d, k, t, n):
        pltpu.make_async_copy(sources[d].at[k], held.at[n], in_sems.at[n]).start()

    def send(d, k, t, n):
        pltpu.make_async_copy(sources[d].at[k], held.at[n], in_sems.at[n]).wait()
        pltpu.make_async_copy(held.at[n], out.at[t], out_sems.at[n]).start()

    def finish(d, k, t, n):
        pltpu.make_async_copy(held.at[n], out.at[t], out_sems.at[n]).wait()

    each(bring)
    for d, small in enumerate(smalls):
        for k in range(slots):
            t = inv[d * slots + k]

            @pl.when(t >= 0)
            def _():
                primary[pl.ds(t, 1), :] = small[k, 0:1, :]
                picked[pl.ds(t, 1), :] = small[k, 1:2, :]

    each(send)
    each(finish)


def assemble(tile_dev, first, wide, inv, sources, before, smalls=()):
    count = len(first) * wide
    n = len(sources)
    slots = smalls[0].shape[0] if smalls else 0
    rows = [jax.ShapeDtypeStruct((tile_dev, TILE), F32)] * 2 if smalls else []
    return pl.pallas_call(
        functools.partial(assemble_kernel, first, wide, len(before), slots),
        out_shape=[jax.ShapeDtypeStruct((tile_dev, TILE, BLOCK), BF16)] + rows,
        in_specs=[SMEM] + [ANY] * (n + len(before)) + [VMEM] * len(smalls),
        out_specs=[ANY] + [VMEM] * len(rows),
        scratch_shapes=[
            pltpu.VMEM((count, TILE, BLOCK), BF16),
            pltpu.SemaphoreType.DMA((count,)),
            pltpu.SemaphoreType.DMA((count,)),
        ],
        input_output_aliases={1 + n: 0} if before else {},
        compiler_params=pltpu.CompilerParams(vmem_limit_bytes=VMEM_BYTES),
        name="assemble",
    )(inv, *sources, *before, *smalls)


def local_part(pieces, vectors, tile_region, tile_block, primary_pick, spill_pick, centers):
    n_parts, n_region, n_shard = (lax.axis_size(a) for a in AXES)
    nz = n_shard // 2
    tile_dev = tile_region.shape[0]
    cap = 2 * tile_dev // (n_region * n_shard)
    slots = nz * cap
    blk_dev = centers.shape[1] // BLOCK
    half_blocks = blk_dev // 2
    pieces = min(pieces, half_blocks)
    sub_blocks = half_blocks // pieces
    shard = lax.axis_index("shard")
    half = lax.axis_index("parts") & 1
    ring, at_ring = ring_place(nz)
    me = jnp.stack(
        [place_of(shard >> 1, nz), shard & 1, lax.axis_index("region"), half]
    ).astype(I32)

    def device(p, r, s):
        return (p * n_region + r) * n_shard + s

    every = [(p, r, s) for p in range(n_parts) for r in range(n_region) for s in range(n_shard)]

    def permute(value, target):
        return lax.ppermute(value, AXES, [(device(*a), device(*target(*a))) for a in every])

    def next_z(p, r, s):
        return (p, r, 2 * ring[(at_ring[s >> 1] + 1) % nz] + (s & 1))

    def other_part(p, r, s):
        return (p ^ 1, r, s)

    local = centers[0].reshape(blk_dev, BLOCK, D)

    tile_rows = vectors.reshape(tile_dev, TILE, D)
    meta_sent, at_slot, inv = plan(
        me,
        tile_region,
        tile_block,
        primary_pick.reshape(tile_dev, TILE),
        spill_pick.reshape(tile_dev, TILE),
        nz,
        cap,
        blk_dev,
    )

    def exchange(value, partner):
        if partner == 0:
            return value
        return permute(value, lambda p, r, s: (p, r ^ (partner & 1), s ^ (partner >> 1)))

    metas = [exchange(meta_sent[d], d) for d in range(4)]
    meta = jnp.concatenate(metas, axis=0)
    ids = meta[:, 0, 0]
    sent = dispatch(at_slot, tile_rows, metas, slots)

    env, waits, opens = {}, {}, {}

    def send(name, payload, target, done):
        env[name] = permute(env[payload], target)
        waits.setdefault(done, []).append(name)

    def hold(name, value, until):
        env[name] = value
        opens.setdefault(until, []).append(name)

    def across(d):
        return lambda p, r, s: (p, r ^ (d & 1), s ^ (d >> 1))

    steps = (nz - 1) * pieces
    last = steps + 1
    tile_gates = [min(steps, (j * pieces + 1) // 2 + 1) for j in range(1, 5)]
    tile_names = [("t", 2, 0), ("t", 3, 0), ("t", 2, 1), ("t", 3, 1)]
    for j, name in enumerate(tile_names):
        value = sent[1 + 2 * (name[1] - 2) + name[2]]
        hold(("sent",) + name[1:], value, 0 if j < 2 else tile_gates[j - 2])
    for i in range(pieces):
        hold(
            ("own", i),
            lax.dynamic_slice_in_dim(local, half * half_blocks + i * sub_blocks, sub_blocks, 0),
            0,
        )
    env["core"] = sent[0]
    send(("t", 1, 0), "core", across(1), tile_gates[0])
    cuts = sorted({0, nz // 2, 3 * nz // 4, nz})
    groups = [tuple(range(a, b)) for a, b in zip(cuts, cuts[1:])]
    ready = [max(tile_gates[1], (groups[0][-1]) * pieces + 1)]
    ready += [max(tile_gates[3], group[-1] * pieces + 1) for group in groups[1:]]
    smalls = {}
    output = ()

    def score(n, order):
        group = groups[n]
        part = 1 if 2 * group[0] >= nz else 0
        keys = tuple(
            (hops, direct, i)
            for hops in group
            if hops > 0
            for direct in (True, False)
            for i in range(pieces)
        )
        tiles = [tile_rows if d == 0 else env["t", d, part if d > 1 else 0] for d in order]
        bases = [part * slots // 2 if d > 1 else 0 for d in order]
        scores, small = score_call(
            nz, cap, blk_dev, sub_blocks, group, order, keys, bases, me, ids, inv, meta, tiles, local,
            [smalls[d] for d in order] if n else [],
            [env[("z" if direct else "x"), (hops - 1) * pieces + i + 1] for hops, direct, i in keys],
        )
        for d, values, rows in zip(order, scores, small):
            env["s", n, d] = values
            smalls[d] = rows

    def place(n, before, with_smalls=()):
        wide = len(groups[n]) * cap
        return assemble(
            tile_dev,
            [d * slots + groups[n][0] * cap for d in range(4)],
            wide,
            inv,
            [env["s", n, 0]] + [env["r", n, d] for d in (1, 2, 3)],
            before,
            with_smalls,
        )

    stride = max(1, pieces // 2)
    back = {
        (0, 2): (tile_gates[2], tile_gates[3] + stride),
        (0, 3): (tile_gates[3], last),
        (0, 1): (tile_gates[3], tile_gates[3] + stride),
        (1, 2): (tile_gates[3] + stride, last),
        (1, 3): (tile_gates[3] + stride, last),
        (1, 1): (tile_gates[3] + stride, last),
    }
    for key, (begin, end) in back.items():
        begin = max(begin, ready[key[0]] + 1)
        back[key] = begin, max(end, begin + 1)
    scored = 0
    for k in range(last + 1):
        if k:
            passed = waits.get(k, []) + opens.get(k, [])
            passed = [name for name in passed if name in env]
            for name, value in zip(passed, gate([env[n] for n in passed], [])):
                env[name] = value
        if k == 0:
            for i in range(min(pieces, steps)):
                send(("z", i + 1), ("own", i), next_z, i + 1)
            for name in tile_names[:2]:
                send(name, ("sent",) + name[1:], across(name[1]), tile_gates[tile_names.index(name)])
        elif k <= steps:
            if k + pieces <= steps:
                send(("z", k + pieces), ("z", k), next_z, k + pieces)
            send(("x", k), ("z", k), other_part, k + 1)
        for j in (2, 3):
            if k and k == tile_gates[j - 2]:
                send(tile_names[j], ("sent",) + tile_names[j][1:], across(tile_names[j][1]), tile_gates[j])
        for (n, d), (begin, end) in back.items():
            if k and begin == k and n < scored:
                send(("r", n, d), ("s", n, d), across(d), end)
        while scored < len(groups) and k == ready[scored]:
            score(scored, (2, 3))
            if scored < len(groups) - 1:
                score(scored, (1, 0))
                for d in (1, 2, 3):
                    opens.setdefault(back[scored, d][0], []).append(("s", scored, d))
            scored += 1
    n = len(groups) - 1
    for d in (2, 3):
        env["r", n, d] = exchange(env["s", n, d], d)
        smalls[d] = exchange(smalls[d], d)
    score(n, (1, 0))
    env["r", n, 1] = exchange(env["s", n, 1], 1)
    smalls[1] = exchange(smalls[1], 1)
    before = []
    for i in range(n):
        before = [place(i, before)[0]]
    spill_scores, primary, picked = place(n, before, [smalls[d] for d in range(4)])
    return (
        spill_scores.reshape(tile_dev * TILE, BLOCK),
        primary.astype(BF16).reshape(tile_dev * TILE),
        picked.astype(BF16).reshape(tile_dev * TILE),
    )


def solution(mesh):
    rows = P(AXES, None)
    flat = P(AXES)
    return jax.shard_map(
        functools.partial(local_part, 2),
        mesh=mesh,
        in_specs=(rows, flat, flat, flat, flat, P("region", "shard", None)),
        out_specs=(rows, flat, flat),
        check_vma=False,
    )
```

time: 792 us -> 334 us (0.42)
  the two profiles are of different devices: /device:TPU:9 before, /device:TPU:15 now
where the time goes in v2:
time: 334 us; the launch traced here: 331 us
  waiting for transfers between devices  170 us (51%)
  Pallas kernels  88.1 us (26%)
  starting transfers between devices  50.5 us (15%)
  local copies, waits for them, and re-layouts  19.4 us (6%)
    ppermute x32, waiting for transfers between devices, permute(): lax.ppermute(value, AXES, [(device(*a), device(*target(*a))) for a in eve...  170 us
    pallas_call x6, Pallas kernels, score_call(): pl.pallas_call(functools.partial(score_kernel, nz, cap, blk_dev, sub_bloc...  69.3 us
    ppermute x32, starting transfers between devices, permute(): lax.ppermute(value, AXES, [(device(*a), device(*target(*a))) for a in eve...  50.5 us
    unnamed x79, local copies, waits for them, and re-layouts  13.5 us
    pallas_call x3, Pallas kernels, assemble(): pl.pallas_call(functools.partial(assemble_kernel, first, wide, len(before...  10.2 us
  transfers between devices with their start and end apart: 32, of which 15 were waited for; matrix products, arithmetic and copies ran while one was open for 2% of the time, Pallas kernels for 21%

profile of v2, /device:TPU:15, one launch (start us, length us, event | category | flops | bytes accessed | tf_op | source)
XLA Modules:
  0.0 331.0 jit_solution(7718938708022165704)
XLA Ops:
  1.2 3.6 %plan.1 = (s32[16,8,128]{2,1,0:T(8,128)}, s32[16,8,128]{2,1,0:T(8,128)}, s32[16,8,128]{2,1,0:T(8,128)}, s32[16,8,128]{2,1,0:T(8,128)}, s32[32]{0:T(128)}, /*index=5*/s32[64]{0:T(128)}) custom-call(s32[4]{0:T(128)} %pad_add_fusion.me, s32[32]{0:T(128)} %region.1, s32[32]{0:T(128)} %block.1, s32[32,128]{1,0:T(8,128)} %bitcast.25, s32[32,128]{1,0:T(8,128)} %bitcast.26), custom_call_target="tpu_custom_call" | custom-call | tf_op jit(solution)/shard_map/plan/pallas_call | solution.py:85
  5.8 1.5 collective-permute-start.2
  7.3 3.3 constant_dynamic-slice_fusion
  10.5 2.3 collective-permute-start.6
  13.6 5.0 %dispatch.1 = (bf16[16,128,768]{2,1,0:T(8,128)(2,1)}, bf16[8,128,768]{2,1,0:T(8,128)(2,1)}, bf16[8,128,768]{2,1,0:T(8,128)(2,1)}, bf16[8,128,768]{2,1,0:T(8,128)(2,1)}, bf16[8,128,768]{2,1,0:T(8,128)(2,1)}) custom-call(s32[32]{0:T(128)} %get-tuple-element.76.at_slot, bf16[32,128,768]{2,1,0:T(8,128)(2,1)} %bitcast.20, ...), custom_call_target="tpu_custom_call" | custom-call | tf_op jit(solution)/shard_map/dispatch/pallas_call | solution.py:140
  18.6 1.2 collective-permute-start.3
  20.8 25.7 %collective-permute-done.6.refs_0_ = bf16[2,512,768]{2,1,0:T(8,128)(2,1)S(1)} collective-permute-done((bf16[2,512,768]{2,1,0:T(8,128)(2,1)S(1)}, bf16[2,512,768]{2,1,0:T(8,128)(2,1)S(1)}, u32[]{:S(2)}, u32[]{:S(2)}) %collective-permute-start.6) | collective-permute-done | bytes 1572896 | tf_op jit(solution)/shard_map/ppermute | solution.py:426
  46.5 1.2 copy-done.3
  47.9 1.9 collective-permute-start.8
  49.9 30.5 %collective-permute-done.4.refs_1_ = bf16[2,512,768]{2,1,0:T(8,128)(2,1)S(1)} collective-permute-done((bf16[2,512,768]{2,1,0:T(8,128)(2,1)}, bf16[2,512,768]{2,1,0:T(8,128)(2,1)S(1)}, u32[]{:S(2)}, u32[]{:S(2)}) %collective-permute-start.4) | collective-permute-done | bytes 1572896 | tf_op jit(solution)/shard_map/ppermute | solution.py:426
  80.3 3.0 collective-permute-start.9
  85.7 2.1 collective-permute-start.11
  88.1 2.0 collective-permute-done.8.refs_0_
  90.1 26.3 %collective-permute-done.9.refs_1_ = bf16[2,512,768]{2,1,0:T(8,128)(2,1)S(1)} collective-permute-done((bf16[2,512,768]{2,1,0:T(8,128)(2,1)}, bf16[2,512,768]{2,1,0:T(8,128)(2,1)S(1)}, u32[]{:S(2)}, u32[]{:S(2)}) %collective-permute-start.9) | collective-permute-done | bytes 1572896 | tf_op jit(solution)/shard_map/ppermute | solution.py:426
  116.4 3.9 %collective-permute-done.10.refs_2_ = bf16[2,512,768]{2,1,0:T(8,128)(2,1)S(1)} collective-permute-done((bf16[2,512,768]{2,1,0:T(8,128)(2,1)}, bf16[2,512,768]{2,1,0:T(8,128)(2,1)S(1)}, u32[]{:S(2)}, u32[]{:S(2)}) %collective-permute-start.10) | collective-permute-done | bytes 1572896 | tf_op jit(solution)/shard_map/ppermute | solution.py:426
  123.1 1.8 slice_reduce_fusion.ids
  126.1 3.6 %collective-permute-start.15 = (bf16[8,128,768]{2,1,0:T(8,128)(2,1)}, bf16[8,128,768]{2,1,0:T(8,128)(2,1)S(1)}, u32[]{:S(2)}, u32[]{:S(2)}) collective-permute-start(bf16[8,128,768]{2,1,0:T(8,128)(2,1)} %get-tuple-element.95), channel_id=1, source_target_pairs={{0,9},{1,8},{2,11},{3,10},{4,13},{5,12},{6,15},{7,14},{8,1},{9,0},... | collective-permute-start | bytes 4718600 | tf_op jit(solution)/shard_map/ppermute | solution.py:426
  129.7 12.3 %score.7 = (bf16[8,128,512]{2,1,0:T(8,128)(2,1)}, bf16[8,128,512]{2,1,0:T(8,128)(2,1)}, f32[16,8,128]{2,1,0:T(8,128)}, f32[16,8,128]{2,1,0:T(8,128)}) custom-call(s32[4]{0:T(128)} %pad_add_fusion.me, s32[64]{0:T(128)} %slice_reduce_fusion.ids, s32[64]{0:T(128)} %get-tuple-element.71.inv, s32[64,8,128]{2,1,0:T(8,128)} %copy-done.16, ...), custom_call_target="tpu_custom_call" | custom-call | flops 2415919104 | bytes 6291456 | tf_op jit(solution)/shard_map/score/pallas_call | solution.py:314
  142.0 8.0 %collective-permute-done.11.refs_0_ = bf16[2,512,768]{2,1,0:T(8,128)(2,1)S(1)} collective-permute-done((bf16[2,512,768]{2,1,0:T(8,128)(2,1)}, bf16[2,512,768]{2,1,0:T(8,128)(2,1)S(1)}, u32[]{:S(2)}, u32[]{:S(2)}) %collective-permute-start.11) | collective-permute-done | bytes 1572896 | tf_op jit(solution)/shard_map/ppermute | solution.py:426
  150.1 5.1 %collective-permute-done.13.refs_2_ = bf16[2,512,768]{2,1,0:T(8,128)(2,1)S(1)} collective-permute-done((bf16[2,512,768]{2,1,0:T(8,128)(2,1)}, bf16[2,512,768]{2,1,0:T(8,128)(2,1)S(1)}, u32[]{:S(2)}, u32[]{:S(2)}) %collective-permute-start.13) | collective-permute-done | bytes 1572896 | tf_op jit(solution)/shard_map/ppermute | solution.py:426
  155.2 1.2 copy-done.8
  156.6 12.4 %score.6 = (bf16[8,128,512]{2,1,0:T(8,128)(2,1)}, bf16[8,128,512]{2,1,0:T(8,128)(2,1)}, f32[16,8,128]{2,1,0:T(8,128)}, f32[16,8,128]{2,1,0:T(8,128)}) custom-call(s32[4]{0:T(128)} %pad_add_fusion.me, s32[64]{0:T(128)} %slice_reduce_fusion.ids, s32[64]{0:T(128)} %get-tuple-element.71.inv, s32[64,8,128]{2,1,0:T(8,128)} %copy-done.16, ...), custom_call_target="tpu_custom_call" | custom-call | flops 2415919104 | bytes 6291456 | tf_op jit(solution)/shard_map/score/pallas_call | solution.py:314
  169.0 9.0 %collective-permute-start.17 = (bf16[2,512,768]{2,1,0:T(8,128)(2,1)S(1)}, bf16[2,512,768]{2,1,0:T(8,128)(2,1)S(1)}, u32[]{:S(2)}, u32[]{:S(2)}) collective-permute-start(bf16[2,512,768]{2,1,0:T(8,128)(2,1)S(1)} %copy-done.5), channel_id=1, source_target_pairs={{0,2},{1,3},{2,6},{3,7},{4,0},{5,1},{6,4},{7,5},{8,10},{9,11},{10,... | collective-permute-start | bytes 4718600 | tf_op jit(solution)/shard_map/ppermute | solution.py:426
  177.9 5.8 %collective-permute-done.14.refs_0_ = bf16[2,512,768]{2,1,0:T(8,128)(2,1)S(1)} collective-permute-done((bf16[2,512,768]{2,1,0:T(8,128)(2,1)}, bf16[2,512,768]{2,1,0:T(8,128)(2,1)S(1)}, u32[]{:S(2)}, u32[]{:S(2)}) %collective-permute-start.14) | collective-permute-done | bytes 1572896 | tf_op jit(solution)/shard_map/ppermute | solution.py:426
  183.8 5.4 %collective-permute-done.16.refs_2_ = bf16[2,512,768]{2,1,0:T(8,128)(2,1)S(1)} collective-permute-done((bf16[2,512,768]{2,1,0:T(8,128)(2,1)}, bf16[2,512,768]{2,1,0:T(8,128)(2,1)S(1)}, u32[]{:S(2)}, u32[]{:S(2)}) %collective-permute-start.16) | collective-permute-done | bytes 1572896 | tf_op jit(solution)/shard_map/ppermute | solution.py:426
  189.2 1.2 copy-done.15
  190.9 4.7 %collective-permute-start.20 = (bf16[8,128,512]{2,1,0:T(8,128)(2,1)}, bf16[8,128,512]{2,1,0:T(8,128)(2,1)S(1)}, u32[]{:S(2)}, u32[]{:S(2)}) collective-permute-start(bf16[8,128,512]{2,1,0:T(8,128)(2,1)} %get-tuple-element.103), channel_id=1, source_target_pairs={{0,8},{1,9},{2,10},{3,11},{4,12},{5,13},{6,14},{7,15},{8,0},{9,1},... | collective-permute-start | bytes 3145736 | tf_op jit(solution)/shard_map/ppermute | solution.py:426
  195.6 12.3 %score.8 = (bf16[4,128,512]{2,1,0:T(8,128)(2,1)}, bf16[4,128,512]{2,1,0:T(8,128)(2,1)}, f32[16,8,128]{2,1,0:T(8,128)}, f32[16,8,128]{2,1,0:T(8,128)}) custom-call(s32[4]{0:T(128)} %pad_add_fusion.me, s32[64]{0:T(128)} %slice_reduce_fusion.ids, s32[64]{0:T(128)} %get-tuple-element.71.inv, s32[64,8,128]{2,1,0:T(8,128)} %copy-done.16, ...), custom_call_target="tpu_custom_call" | custom-call | flops 1207959552 | bytes 3145728 | tf_op jit(solution)/shard_map/score/pallas_call | solution.py:314
  207.8 7.8 %score.9 = (bf16[4,128,512]{2,1,0:T(8,128)(2,1)}, bf16[4,128,512]{2,1,0:T(8,128)(2,1)}, f32[16,8,128]{2,1,0:T(8,128)}, f32[16,8,128]{2,1,0:T(8,128)}) custom-call(s32[4]{0:T(128)} %pad_add_fusion.me, s32[64]{0:T(128)} %slice_reduce_fusion.ids, s32[64]{0:T(128)} %get-tuple-element.71.inv, s32[64,8,128]{2,1,0:T(8,128)} %copy-done.16, ...), custom_call_target="tpu_custom_call" | custom-call | flops 1207959552 | bytes 3145728 | tf_op jit(solution)/shard_map/score/pallas_call | solution.py:314
  215.7 1.7 collective-permute-done.17.refs_0_
  217.4 5.0 %collective-permute-done.19.refs_2_ = bf16[2,512,768]{2,1,0:T(8,128)(2,1)S(1)} collective-permute-done((bf16[2,512,768]{2,1,0:T(8,128)(2,1)}, bf16[2,512,768]{2,1,0:T(8,128)(2,1)S(1)}, u32[]{:S(2)}, u32[]{:S(2)}) %collective-permute-start.19) | collective-permute-done | bytes 1572896 | tf_op jit(solution)/shard_map/ppermute | solution.py:426
  222.4 1.2 copy-done.14
  224.8 5.6 %collective-permute-start.21 = (bf16[8,128,512]{2,1,0:T(8,128)(2,1)S(1)}, bf16[8,128,512]{2,1,0:T(8,128)(2,1)S(1)}, u32[]{:S(2)}, u32[]{:S(2)}) collective-permute-start(bf16[8,128,512]{2,1,0:T(8,128)(2,1)S(1)} %copy-done.23), channel_id=1, source_target_pairs={{0,9},{1,8},{2,11},{3,10},{4,13},{5,12},{6,15},{7,14},{8,1},{9,0},... | collective-permute-start | bytes 3145736 | tf_op jit(solution)/shard_map/ppermute | solution.py:426
  230.4 1.3 collective-permute-start.23
  232.2 21.2 %collective-permute-done.21.refs_0_ = bf16[8,128,512]{2,1,0:T(8,128)(2,1)S(1)} collective-permute-done((bf16[8,128,512]{2,1,0:T(8,128)(2,1)S(1)}, bf16[8,128,512]{2,1,0:T(8,128)(2,1)S(1)}, u32[]{:S(2)}, u32[]{:S(2)}) %collective-permute-start.21) | collective-permute-done | bytes 1048608 | tf_op jit(solution)/shard_map/ppermute | solution.py:426
  253.4 12.9 %collective-permute-done.23.refs_2_ = bf16[4,128,512]{2,1,0:T(8,128)(2,1)S(1)} collective-permute-done((bf16[4,128,512]{2,1,0:T(8,128)(2,1)}, bf16[4,128,512]{2,1,0:T(8,128)(2,1)S(1)}, u32[]{:S(2)}, u32[]{:S(2)}) %collective-permute-start.23) | collective-permute-done | bytes 524320 | tf_op jit(solution)/shard_map/ppermute | solution.py:426
  266.3 9.5 %collective-permute-done.24.refs_3_ = bf16[4,128,512]{2,1,0:T(8,128)(2,1)S(1)} collective-permute-done((bf16[4,128,512]{2,1,0:T(8,128)(2,1)}, bf16[4,128,512]{2,1,0:T(8,128)(2,1)S(1)}, u32[]{:S(2)}, u32[]{:S(2)}) %collective-permute-start.24) | collective-permute-done | bytes 524320 | tf_op jit(solution)/shard_map/ppermute | solution.py:426
  276.9 1.2 copy-done.9
  278.0 12.3 %score.11 = (bf16[4,128,512]{2,1,0:T(8,128)(2,1)}, bf16[4,128,512]{2,1,0:T(8,128)(2,1)}, f32[16,8,128]{2,1,0:T(8,128)}, f32[16,8,128]{2,1,0:T(8,128)}) custom-call(s32[4]{0:T(128)} %pad_add_fusion.me, s32[64]{0:T(128)} %slice_reduce_fusion.ids, s32[64]{0:T(128)} %get-tuple-element.71.inv, s32[64,8,128]{2,1,0:T(8,128)} %copy-done.16, ...), custom_call_target="tpu_custom_call" | custom-call | flops 1207959552 | bytes 3145728 | tf_op jit(solution)/shard_map/score/pallas_call | solution.py:314
  290.4 3.0 collective-permute-start.28
  293.4 12.3 %score.10 = (bf16[4,128,512]{2,1,0:T(8,128)(2,1)}, bf16[4,128,512]{2,1,0:T(8,128)(2,1)}, f32[16,8,128]{2,1,0:T(8,128)}, f32[16,8,128]{2,1,0:T(8,128)}) custom-call(s32[4]{0:T(128)} %pad_add_fusion.me, s32[64]{0:T(128)} %slice_reduce_fusion.ids, s32[64]{0:T(128)} %get-tuple-element.71.inv, s32[64,8,128]{2,1,0:T(8,128)} %copy-done.16, ...), custom_call_target="tpu_custom_call" | custom-call | flops 1207959552 | bytes 3145728 | tf_op jit(solution)/shard_map/score/pallas_call | solution.py:314
  305.9 2.0 collective-permute-start.31
  307.9 7.0 %collective-permute-done.30.refs_7_ = f32[16,8,128]{2,1,0:T(8,128)S(1)} collective-permute-done((f32[16,8,128]{2,1,0:T(8,128)S(1)}, f32[16,8,128]{2,1,0:T(8,128)S(1)}, u32[]{:S(2)}, u32[]{:S(2)}) %collective-permute-start.30) | collective-permute-done | bytes 65568 | tf_op jit(solution)/shard_map/ppermute | solution.py:426
  314.9 3.3 %collective-permute-start.29 = (f32[16,8,128]{2,1,0:T(8,128)}, f32[16,8,128]{2,1,0:T(8,128)S(1)}, u32[]{:S(2)}, u32[]{:S(2)}) collective-permute-start(f32[16,8,128]{2,1,0:T(8,128)} %get-tuple-element.133), channel_id=1, source_target_pairs={{0,8},{1,9},{2,10},{3,11},{4,12},{5,13},{6,14},{7,15},{8,0},{9,1},... | collective-permute-start | bytes 196616 | tf_op jit(solution)/shard_map/ppermute | solution.py:426
  318.2 3.2 assemble.3.refs_4_
  321.5 3.1 assemble.4.refs_4_
  325.7 3.9 %assemble.5 = (bf16[32,128,512]{2,1,0:T(8,128)(2,1)}, f32[32,128]{1,0:T(8,128)}, f32[32,128]{1,0:T(8,128)}) custom-call(s32[64]{0:T(128)} %get-tuple-element.71.inv, bf16[4,128,512]{2,1,0:T(8,128)(2,1)} %get-tuple-element.118.refs_0_, bf16[4,128,512]{2,1,0:T(8,128)(2,1)} %copy-done.26, ...), custom_call_target="tpu_custom_call", output_to_operand_aliasing={{0}: (5, {})} | custom-call | tf_op jit(solution)/shard_map/assemble/pallas_call | solution.py:387
  329.7 1.3 convert_bitcast_fusion
  (118 shorter events, 15.0 us)
Async XLA Ops:
  4.8 8.0 %collective-permute-start = (s32[16,8,128]{2,1,0:T(8,128)}, s32[16,8,128]{2,1,0:T(8,128)S(1)}, u32[]{:S(2)}, u32[]{:S(2)}) collective-permute-start(s32[16,8,128]{2,1,0:T(8,128)} %get-tuple-element.73), channel_id=1, source_target_pairs={{0,8},{1,9},{2,10},{3,11},{4,12},{5,13},{6,14},{7,15},{8,0},{9,1},... | collective-permute-start | bytes 196616 | tf_op jit(solution)/shard_map/ppermute | solution.py:426
  5.6 7.3 %collective-permute-start.1 = (s32[16,8,128]{2,1,0:T(8,128)}, s32[16,8,128]{2,1,0:T(8,128)S(1)}, u32[]{:S(2)}, u32[]{:S(2)}) collective-permute-start(s32[16,8,128]{2,1,0:T(8,128)} %get-tuple-element.74), channel_id=1, source_target_pairs={{0,1},{1,0},{2,3},{3,2},{4,5},{5,4},{6,7},{7,6},{8,9},{9,8},{10,11... | collective-permute-start | bytes 196616 | tf_op jit(solution)/shard_map/ppermute | solution.py:426
  5.8 7.1 %collective-permute-start.2 = (s32[16,8,128]{2,1,0:T(8,128)}, s32[16,8,128]{2,1,0:T(8,128)S(1)}, u32[]{:S(2)}, u32[]{:S(2)}) collective-permute-start(s32[16,8,128]{2,1,0:T(8,128)} %get-tuple-element.75), channel_id=1, source_target_pairs={{0,9},{1,8},{2,11},{3,10},{4,13},{5,12},{6,15},{7,14},{8,1},{9,0},... | collective-permute-start | bytes 196616 | tf_op jit(solution)/shard_map/ppermute | solution.py:426
  10.5 36.0 %collective-permute-start.6 = (bf16[2,512,768]{2,1,0:T(8,128)(2,1)S(1)}, bf16[2,512,768]{2,1,0:T(8,128)(2,1)S(1)}, u32[]{:S(2)}, u32[]{:S(2)}) collective-permute-start(bf16[2,512,768]{2,1,0:T(8,128)(2,1)S(1)} %get-tuple-element.139), channel_id=1, source_target_pairs={{0,2},{1,3},{2,6},{3,7},{4,0},{5,1},{6,4},{7,5},{8,10},{9,11},{10,... | collective-permute-start | bytes 4718600 | tf_op jit(solution)/shard_map/ppermute | solution.py:426
  18.6 64.8 %collective-permute-start.3 = (bf16[16,128,768]{2,1,0:T(8,128)(2,1)}, bf16[16,128,768]{2,1,0:T(8,128)(2,1)S(1)}, u32[]{:S(2)}, u32[]{:S(2)}) collective-permute-start(bf16[16,128,768]{2,1,0:T(8,128)(2,1)} %get-tuple-element.77), channel_id=1, source_target_pairs={{0,8},{1,9},{2,10},{3,11},{4,12},{5,13},{6,14},{7,15},{8,0},{9,1},... | collective-permute-start | bytes 9437192 | tf_op jit(solution)/shard_map/ppermute | solution.py:426
  19.8 60.6 %collective-permute-start.4 = (bf16[2,512,768]{2,1,0:T(8,128)(2,1)}, bf16[2,512,768]{2,1,0:T(8,128)(2,1)S(1)}, u32[]{:S(2)}, u32[]{:S(2)}) collective-permute-start(bf16[2,512,768]{2,1,0:T(8,128)(2,1)} %get-tuple-element.140), channel_id=1, source_target_pairs={{0,2},{1,3},{2,6},{3,7},{4,0},{5,1},{6,4},{7,5},{8,10},{9,11},{10,... | collective-permute-start | bytes 4718600 | tf_op jit(solution)/shard_map/ppermute | solution.py:426
  19.8 63.5 %collective-permute-start.5 = (bf16[8,128,768]{2,1,0:T(8,128)(2,1)}, bf16[8,128,768]{2,1,0:T(8,128)(2,1)}, u32[]{:S(2)}, u32[]{:S(2)}) collective-permute-start(bf16[8,128,768]{2,1,0:T(8,128)(2,1)} %get-tuple-element.78), channel_id=1, source_target_pairs={{0,1},{1,0},{2,3},{3,2},{4,5},{5,4},{6,7},{7,6},{8,9},{9,8},{10,11... | collective-permute-start | bytes 4718600 | tf_op jit(solution)/shard_map/ppermute | solution.py:426
  47.7 35.6 %collective-permute-start.7 = (bf16[2,512,768]{2,1,0:T(8,128)(2,1)}, bf16[2,512,768]{2,1,0:T(8,128)(2,1)S(1)}, u32[]{:S(2)}, u32[]{:S(2)}) collective-permute-start(bf16[2,512,768]{2,1,0:T(8,128)(2,1)} %gate.7.refs_3_), channel_id=1, source_target_pairs={{0,16},{1,17},{2,18},{3,19},{4,20},{5,21},{6,22},{7,23},{8,24},{9,... | collective-permute-start | bytes 4718600 | tf_op jit(solution)/shard_map/ppermute | solution.py:426
  47.9 42.2 %collective-permute-start.8 = (bf16[8,128,768]{2,1,0:T(8,128)(2,1)}, bf16[8,128,768]{2,1,0:T(8,128)(2,1)}, u32[]{:S(2)}, u32[]{:S(2)}) collective-permute-start(bf16[8,128,768]{2,1,0:T(8,128)(2,1)} %get-tuple-element.83), channel_id=1, source_target_pairs={{0,9},{1,8},{2,11},{3,10},{4,13},{5,12},{6,15},{7,14},{8,1},{9,0},... | collective-permute-start | bytes 4718600 | tf_op jit(solution)/shard_map/ppermute | solution.py:426
  80.3 3.0 copy-start.1
  80.3 36.0 %collective-permute-start.9 = (bf16[2,512,768]{2,1,0:T(8,128)(2,1)}, bf16[2,512,768]{2,1,0:T(8,128)(2,1)S(1)}, u32[]{:S(2)}, u32[]{:S(2)}) collective-permute-start(bf16[2,512,768]{2,1,0:T(8,128)(2,1)} %gate.7.refs_3_), channel_id=1, source_target_pairs={{0,2},{1,3},{2,6},{3,7},{4,0},{5,1},{6,4},{7,5},{8,10},{9,11},{10,... | collective-permute-start | bytes 4718600 | tf_op jit(solution)/shard_map/ppermute | solution.py:426
  85.5 34.7 %collective-permute-start.10 = (bf16[2,512,768]{2,1,0:T(8,128)(2,1)}, bf16[2,512,768]{2,1,0:T(8,128)(2,1)S(1)}, u32[]{:S(2)}, u32[]{:S(2)}) collective-permute-start(bf16[2,512,768]{2,1,0:T(8,128)(2,1)} %get-tuple-element.81.refs_4_), channel_id=1, source_target_pairs={{0,16},{1,17},{2,18},{3,19},{4,20},{5,21},{6,22},{7,23},{8,24},{9,... | collective-permute-start | bytes 4718600 | tf_op jit(solution)/shard_map/ppermute | solution.py:426
  85.7 64.3 %collective-permute-start.11 = (bf16[2,512,768]{2,1,0:T(8,128)(2,1)}, bf16[2,512,768]{2,1,0:T(8,128)(2,1)S(1)}, u32[]{:S(2)}, u32[]{:S(2)}) collective-permute-start(bf16[2,512,768]{2,1,0:T(8,128)(2,1)} %get-tuple-element.81.refs_4_), channel_id=1, source_target_pairs={{0,2},{1,3},{2,6},{3,7},{4,0},{5,1},{6,4},{7,5},{8,10},{9,11},{10,... | collective-permute-start | bytes 4718600 | tf_op jit(solution)/shard_map/ppermute | solution.py:426
  87.9 62.2 %collective-permute-start.12 = (bf16[8,128,768]{2,1,0:T(8,128)(2,1)}, bf16[8,128,768]{2,1,0:T(8,128)(2,1)S(1)}, u32[]{:S(2)}, u32[]{:S(2)}) collective-permute-start(bf16[8,128,768]{2,1,0:T(8,128)(2,1)} %get-tuple-element.89), channel_id=1, source_target_pairs={{0,1},{1,0},{2,3},{3,2},{4,5},{5,4},{6,7},{7,6},{8,9},{9,8},{10,11... | collective-permute-start | bytes 4718600 | tf_op jit(solution)/shard_map/ppermute | solution.py:426
  116.3 3.9 %copy-start.7 = (bf16[2,512,768]{2,1,0:T(8,128)(2,1)}, bf16[2,512,768]{2,1,0:T(8,128)(2,1)S(1)}, u32[]{:S(2)}) copy-start(bf16[2,512,768]{2,1,0:T(8,128)(2,1)S(1)} %collective-permute-done.9.refs_1_) | copy-start | bytes 4718596
  121.4 33.8 %collective-permute-start.13 = (bf16[2,512,768]{2,1,0:T(8,128)(2,1)}, bf16[2,512,768]{2,1,0:T(8,128)(2,1)S(1)}, u32[]{:S(2)}, u32[]{:S(2)}) collective-permute-start(bf16[2,512,768]{2,1,0:T(8,128)(2,1)} %get-tuple-element.88.refs_5_), channel_id=1, source_target_pairs={{0,16},{1,17},{2,18},{3,19},{4,20},{5,21},{6,22},{7,23},{8,24},{9,... | collective-permute-start | bytes 4718600 | tf_op jit(solution)/shard_map/ppermute | solution.py:426
  123.1 6.6 %copy-start.16 = (s32[64,8,128]{2,1,0:T(8,128)}, s32[64,8,128]{2,1,0:T(8,128)S(1)}, u32[]{:S(2)}) copy-start(s32[64,8,128]{2,1,0:T(8,128)S(1)} %constant_dynamic-update-slice_fusion.meta) | copy-start | bytes 786436
  124.9 58.9 %collective-permute-start.14 = (bf16[2,512,768]{2,1,0:T(8,128)(2,1)}, bf16[2,512,768]{2,1,0:T(8,128)(2,1)S(1)}, u32[]{:S(2)}, u32[]{:S(2)}) collective-permute-start(bf16[2,512,768]{2,1,0:T(8,128)(2,1)} %get-tuple-element.88.refs_5_), channel_id=1, source_target_pairs={{0,2},{1,3},{2,6},{3,7},{4,0},{5,1},{6,4},{7,5},{8,10},{9,11},{10,... | collective-permute-start | bytes 4718600 | tf_op jit(solution)/shard_map/ppermute | solution.py:426
  126.1 57.7 %collective-permute-start.15 = (bf16[8,128,768]{2,1,0:T(8,128)(2,1)}, bf16[8,128,768]{2,1,0:T(8,128)(2,1)S(1)}, u32[]{:S(2)}, u32[]{:S(2)}) collective-permute-start(bf16[8,128,768]{2,1,0:T(8,128)(2,1)} %get-tuple-element.95), channel_id=1, source_target_pairs={{0,9},{1,8},{2,11},{3,10},{4,13},{5,12},{6,15},{7,14},{8,1},{9,0},... | collective-permute-start | bytes 4718600 | tf_op jit(solution)/shard_map/ppermute | solution.py:426
  150.1 5.1 %copy-start.4 = (bf16[2,512,768]{2,1,0:T(8,128)(2,1)}, bf16[2,512,768]{2,1,0:T(8,128)(2,1)S(1)}, u32[]{:S(2)}) copy-start(bf16[2,512,768]{2,1,0:T(8,128)(2,1)S(1)} %collective-permute-done.11.refs_0_) | copy-start | bytes 4718596
  150.1 5.1 %copy-start.6 = (bf16[8,128,768]{2,1,0:T(8,128)(2,1)}, bf16[8,128,768]{2,1,0:T(8,128)(2,1)S(1)}, u32[]{:S(2)}) copy-start(bf16[8,128,768]{2,1,0:T(8,128)(2,1)S(1)} %collective-permute-done.12.refs_1_) | copy-start | bytes 4718596
  156.3 32.9 %collective-permute-start.16 = (bf16[2,512,768]{2,1,0:T(8,128)(2,1)}, bf16[2,512,768]{2,1,0:T(8,128)(2,1)S(1)}, u32[]{:S(2)}, u32[]{:S(2)}) collective-permute-start(bf16[2,512,768]{2,1,0:T(8,128)(2,1)} %get-tuple-element.93.refs_6_), channel_id=1, source_target_pairs={{0,16},{1,17},{2,18},{3,19},{4,20},{5,21},{6,22},{7,23},{8,24},{9,... | collective-permute-start | bytes 4718600 | tf_op jit(solution)/shard_map/ppermute | solution.py:426
  156.6 12.4 %copy-start.5 = (bf16[2,512,768]{2,1,0:T(8,128)(2,1)S(1)}, bf16[2,512,768]{2,1,0:T(8,128)(2,1)}, u32[]{:S(2)}) copy-start(bf16[2,512,768]{2,1,0:T(8,128)(2,1)} %get-tuple-element.93.refs_6_) | copy-start | bytes 4718596
  169.0 48.4 %collective-permute-start.17 = (bf16[2,512,768]{2,1,0:T(8,128)(2,1)S(1)}, bf16[2,512,768]{2,1,0:T(8,128)(2,1)S(1)}, u32[]{:S(2)}, u32[]{:S(2)}) collective-permute-start(bf16[2,512,768]{2,1,0:T(8,128)(2,1)S(1)} %copy-done.5), channel_id=1, source_target_pairs={{0,2},{1,3},{2,6},{3,7},{4,0},{5,1},{6,4},{7,5},{8,10},{9,11},{10,... | collective-permute-start | bytes 4718600 | tf_op jit(solution)/shard_map/ppermute | solution.py:426
  183.8 5.5 %copy-start.12 = (bf16[2,512,768]{2,1,0:T(8,128)(2,1)}, bf16[2,512,768]{2,1,0:T(8,128)(2,1)S(1)}, u32[]{:S(2)}) copy-start(bf16[2,512,768]{2,1,0:T(8,128)(2,1)S(1)} %collective-permute-done.14.refs_0_) | copy-start | bytes 4718596
  183.8 5.5 %copy-start.13 = (bf16[8,128,768]{2,1,0:T(8,128)(2,1)}, bf16[8,128,768]{2,1,0:T(8,128)(2,1)S(1)}, u32[]{:S(2)}) copy-start(bf16[8,128,768]{2,1,0:T(8,128)(2,1)S(1)} %collective-permute-done.15.refs_1_) | copy-start | bytes 4718596
  190.4 32.0 %collective-permute-start.19 = (bf16[2,512,768]{2,1,0:T(8,128)(2,1)}, bf16[2,512,768]{2,1,0:T(8,128)(2,1)S(1)}, u32[]{:S(2)}, u32[]{:S(2)}) collective-permute-start(bf16[2,512,768]{2,1,0:T(8,128)(2,1)} %get-tuple-element.101.refs_5_), channel_id=1, source_target_pairs={{0,16},{1,17},{2,18},{3,19},{4,20},{5,21},{6,22},{7,23},{8,24},{9,... | collective-permute-start | bytes 4718600 | tf_op jit(solution)/shard_map/ppermute | solution.py:426
  190.6 25.0 %collective-permute-start.18 = (bf16[8,128,512]{2,1,0:T(8,128)(2,1)}, bf16[8,128,512]{2,1,0:T(8,128)(2,1)S(1)}, u32[]{:S(2)}, u32[]{:S(2)}) collective-permute-start(bf16[8,128,512]{2,1,0:T(8,128)(2,1)} %get-tuple-element.102), channel_id=1, source_target_pairs={{0,1},{1,0},{2,3},{3,2},{4,5},{5,4},{6,7},{7,6},{8,9},{9,8},{10,11... | collective-permute-start | bytes 3145736 | tf_op jit(solution)/shard_map/ppermute | solution.py:426
  190.9 26.5 %collective-permute-start.20 = (bf16[8,128,512]{2,1,0:T(8,128)(2,1)}, bf16[8,128,512]{2,1,0:T(8,128)(2,1)S(1)}, u32[]{:S(2)}, u32[]{:S(2)}) collective-permute-start(bf16[8,128,512]{2,1,0:T(8,128)(2,1)} %get-tuple-element.103), channel_id=1, source_target_pairs={{0,8},{1,9},{2,10},{3,11},{4,12},{5,13},{6,14},{7,15},{8,0},{9,1},... | collective-permute-start | bytes 3145736 | tf_op jit(solution)/shard_map/ppermute | solution.py:426
  215.7 6.7 %copy-start.17 = (bf16[8,128,512]{2,1,0:T(8,128)(2,1)}, bf16[8,128,512]{2,1,0:T(8,128)(2,1)S(1)}, u32[]{:S(2)}) copy-start(bf16[8,128,512]{2,1,0:T(8,128)(2,1)S(1)} %collective-permute-done.18.refs_1_) | copy-start | bytes 3145732
  217.4 5.0 %copy-start.11 = (bf16[2,512,768]{2,1,0:T(8,128)(2,1)}, bf16[2,512,768]{2,1,0:T(8,128)(2,1)S(1)}, u32[]{:S(2)}) copy-start(bf16[2,512,768]{2,1,0:T(8,128)(2,1)S(1)} %collective-permute-done.17.refs_0_) | copy-start | bytes 4718596
  217.4 5.0 %copy-start.18 = (bf16[8,128,512]{2,1,0:T(8,128)(2,1)}, bf16[8,128,512]{2,1,0:T(8,128)(2,1)S(1)}, u32[]{:S(2)}) copy-start(bf16[8,128,512]{2,1,0:T(8,128)(2,1)S(1)} %collective-permute-done.20.refs_3_) | copy-start | bytes 3145732
  223.5 52.4 %collective-permute-start.22 = (bf16[2,512,768]{2,1,0:T(8,128)(2,1)}, bf16[2,512,768]{2,1,0:T(8,128)(2,1)S(1)}, u32[]{:S(2)}, u32[]{:S(2)}) collective-permute-start(bf16[2,512,768]{2,1,0:T(8,128)(2,1)} %get-tuple-element.111.refs_6_), channel_id=1, source_target_pairs={{0,16},{1,17},{2,18},{3,19},{4,20},{5,21},{6,22},{7,23},{8,24},{9,... | collective-permute-start | bytes 4718600 | tf_op jit(solution)/shard_map/ppermute | solution.py:426
  224.8 28.7 %collective-permute-start.21 = (bf16[8,128,512]{2,1,0:T(8,128)(2,1)S(1)}, bf16[8,128,512]{2,1,0:T(8,128)(2,1)S(1)}, u32[]{:S(2)}, u32[]{:S(2)}) collective-permute-start(bf16[8,128,512]{2,1,0:T(8,128)(2,1)S(1)} %copy-done.23), channel_id=1, source_target_pairs={{0,9},{1,8},{2,11},{3,10},{4,13},{5,12},{6,15},{7,14},{8,1},{9,0},... | collective-permute-start | bytes 3145736 | tf_op jit(solution)/shard_map/ppermute | solution.py:426
  230.4 35.9 %collective-permute-start.23 = (bf16[4,128,512]{2,1,0:T(8,128)(2,1)}, bf16[4,128,512]{2,1,0:T(8,128)(2,1)S(1)}, u32[]{:S(2)}, u32[]{:S(2)}) collective-permute-start(bf16[4,128,512]{2,1,0:T(8,128)(2,1)} %get-tuple-element.114), channel_id=1, source_target_pairs={{0,1},{1,0},{2,3},{3,2},{4,5},{5,4},{6,7},{7,6},{8,9},{9,8},{10,11... | collective-permute-start | bytes 1572872 | tf_op jit(solution)/shard_map/ppermute | solution.py:426
  231.7 44.2 %collective-permute-start.24 = (bf16[4,128,512]{2,1,0:T(8,128)(2,1)}, bf16[4,128,512]{2,1,0:T(8,128)(2,1)S(1)}, u32[]{:S(2)}, u32[]{:S(2)}) collective-permute-start(bf16[4,128,512]{2,1,0:T(8,128)(2,1)} %get-tuple-element.115), channel_id=1, source_target_pairs={{0,9},{1,8},{2,11},{3,10},{4,13},{5,12},{6,15},{7,14},{8,1},{9,0},... | collective-permute-start | bytes 1572872 | tf_op jit(solution)/shard_map/ppermute | solution.py:426
  232.0 43.9 %collective-permute-start.25 = (bf16[4,128,512]{2,1,0:T(8,128)(2,1)}, bf16[4,128,512]{2,1,0:T(8,128)(2,1)S(1)}, u32[]{:S(2)}, u32[]{:S(2)}) collective-permute-start(bf16[4,128,512]{2,1,0:T(8,128)(2,1)} %get-tuple-element.116), channel_id=1, source_target_pairs={{0,8},{1,9},{2,10},{3,11},{4,12},{5,13},{6,14},{7,15},{8,0},{9,1},... | collective-permute-start | bytes 1572872 | tf_op jit(solution)/shard_map/ppermute | solution.py:426
  253.4 22.5 %copy-start.19 = (bf16[8,128,512]{2,1,0:T(8,128)(2,1)}, bf16[8,128,512]{2,1,0:T(8,128)(2,1)S(1)}, u32[]{:S(2)}) copy-start(bf16[8,128,512]{2,1,0:T(8,128)(2,1)S(1)} %collective-permute-done.21.refs_0_) | copy-start | bytes 3145732
  266.3 9.6 %copy-start.20 = (bf16[4,128,512]{2,1,0:T(8,128)(2,1)}, bf16[4,128,512]{2,1,0:T(8,128)(2,1)S(1)}, u32[]{:S(2)}) copy-start(bf16[4,128,512]{2,1,0:T(8,128)(2,1)S(1)} %collective-permute-done.23.refs_2_) | copy-start | bytes 1572868
  290.3 34.3 %collective-permute-start.27 = (bf16[4,128,512]{2,1,0:T(8,128)(2,1)}, bf16[4,128,512]{2,1,0:T(8,128)(2,1)S(1)}, u32[]{:S(2)}, u32[]{:S(2)}) collective-permute-start(bf16[4,128,512]{2,1,0:T(8,128)(2,1)} %get-tuple-element.122), channel_id=1, source_target_pairs={{0,1},{1,0},{2,3},{3,2},{4,5},{5,4},{6,7},{7,6},{8,9},{9,8},{10,11... | collective-permute-start | bytes 1572872 | tf_op jit(solution)/shard_map/ppermute | solution.py:426
  290.4 34.2 %collective-permute-start.28 = (bf16[4,128,512]{2,1,0:T(8,128)(2,1)}, bf16[4,128,512]{2,1,0:T(8,128)(2,1)S(1)}, u32[]{:S(2)}, u32[]{:S(2)}) collective-permute-start(bf16[4,128,512]{2,1,0:T(8,128)(2,1)} %get-tuple-element.123), channel_id=1, source_target_pairs={{0,9},{1,8},{2,11},{3,10},{4,13},{5,12},{6,15},{7,14},{8,1},{9,0},... | collective-permute-start | bytes 1572872 | tf_op jit(solution)/shard_map/ppermute | solution.py:426
  293.4 12.4 %copy-start.37 = (f32[16,8,128]{2,1,0:T(8,128)S(1)}, f32[16,8,128]{2,1,0:T(8,128)}, u32[]{:S(2)}) copy-start(f32[16,8,128]{2,1,0:T(8,128)} %get-tuple-element.134) | copy-start | bytes 196612
  293.4 12.5 %copy-start.36 = (f32[16,8,128]{2,1,0:T(8,128)S(1)}, f32[16,8,128]{2,1,0:T(8,128)}, u32[]{:S(2)}) copy-start(f32[16,8,128]{2,1,0:T(8,128)} %get-tuple-element.135) | copy-start | bytes 196612
  305.7 18.9 %collective-permute-start.26 = (bf16[4,128,512]{2,1,0:T(8,128)(2,1)}, bf16[4,128,512]{2,1,0:T(8,128)(2,1)S(1)}, u32[]{:S(2)}, u32[]{:S(2)}) collective-permute-start(bf16[4,128,512]{2,1,0:T(8,128)(2,1)} %get-tuple-element.119), channel_id=1, source_target_pairs={{0,8},{1,9},{2,10},{3,11},{4,12},{5,13},{6,14},{7,15},{8,0},{9,1},... | collective-permute-start | bytes 1572872 | tf_op jit(solution)/shard_map/ppermute | solution.py:426
  305.8 9.1 %collective-permute-start.30 = (f32[16,8,128]{2,1,0:T(8,128)S(1)}, f32[16,8,128]{2,1,0:T(8,128)S(1)}, u32[]{:S(2)}, u32[]{:S(2)}) collective-permute-start(f32[16,8,128]{2,1,0:T(8,128)S(1)} %copy-done.37), channel_id=1, source_target_pairs={{0,1},{1,0},{2,3},{3,2},{4,5},{5,4},{6,7},{7,6},{8,9},{9,8},{10,11... | collective-permute-start | bytes 196616 | tf_op jit(solution)/shard_map/ppermute | solution.py:426
  305.9 18.6 %collective-permute-start.31 = (f32[16,8,128]{2,1,0:T(8,128)S(1)}, f32[16,8,128]{2,1,0:T(8,128)S(1)}, u32[]{:S(2)}, u32[]{:S(2)}) collective-permute-start(f32[16,8,128]{2,1,0:T(8,128)S(1)} %copy-done.36), channel_id=1, source_target_pairs={{0,9},{1,8},{2,11},{3,10},{4,13},{5,12},{6,15},{7,14},{8,1},{9,0},... | collective-permute-start | bytes 196616 | tf_op jit(solution)/shard_map/ppermute | solution.py:426
  314.9 6.5 %copy-start.33 = (f32[16,8,128]{2,1,0:T(8,128)}, f32[16,8,128]{2,1,0:T(8,128)S(1)}, u32[]{:S(2)}) copy-start(f32[16,8,128]{2,1,0:T(8,128)S(1)} %collective-permute-done.30.refs_7_) | copy-start | bytes 196612
  314.9 9.6 %collective-permute-start.29 = (f32[16,8,128]{2,1,0:T(8,128)}, f32[16,8,128]{2,1,0:T(8,128)S(1)}, u32[]{:S(2)}, u32[]{:S(2)}) collective-permute-start(f32[16,8,128]{2,1,0:T(8,128)} %get-tuple-element.133), channel_id=1, source_target_pairs={{0,8},{1,9},{2,10},{3,11},{4,12},{5,13},{6,14},{7,15},{8,0},{9,1},... | collective-permute-start | bytes 196616 | tf_op jit(solution)/shard_map/ppermute | solution.py:426
  (22 other events, 22.0 us)

commit v3 on v2

v3 whole, which is shorter than its diff:
```python
import functools

import jax
import jax.numpy as jnp
from jax import lax
from jax.experimental import pallas as pl
from jax.experimental.pallas import tpu as pltpu
from jax.sharding import PartitionSpec as P

D = 768
TILE = 128
BLOCK = 512
SMALL_TERM = 1e-05
AXES = ("parts", "region", "shard")
F32 = jnp.float32
BF16 = jnp.bfloat16
I32 = jnp.int32
ANY = pl.BlockSpec(memory_space=pl.ANY)
SMEM = pl.BlockSpec(memory_space=pltpu.SMEM)
SHORT = pl.CostEstimate(flops=1, bytes_accessed=1, transcendentals=0)
VMEM_BYTES = 62 * 1024 * 1024
VMEM = pl.BlockSpec(memory_space=pltpu.VMEM)


def ring_place(nz):
    ring = list(range(0, nz, 2))[:1] + list(range(1, nz, 2)) + list(range(2, nz, 2))[::-1]
    return ring, [ring.index(z) for z in range(nz)]


def place_of(z, nz):
    return jnp.where(z == 0, 0, jnp.where(z & 1 == 1, (z + 1) // 2, nz - z // 2))


def slot_of(nz, cap, blk_dev, at_ring, y, core, region, block):
    shard = block // blk_dev
    partner = 2 * ((shard & 1) ^ y) + (region ^ core)
    cls = lax.rem(at_ring - place_of(shard >> 1, nz) + nz, nz)
    at = partner * nz + cls
    return partner, cls * cap, at


def zero(ref, n):
    def body(i, carry):
        ref[i] = 0
        return carry

    lax.fori_loop(0, n, body, 0)


def plan_kernel(nz, cap, blk_dev, n_before, me, region, block, *refs):
    at_slot, inv, count = refs[n_before:]
    slots = nz * cap

    def clear(i, carry):
        inv[i] = -1
        return carry

    lax.fori_loop(0, 4 * slots, clear, 0)
    zero(count, 4 * nz)

    def place(t, carry):
        partner, first, at = slot_of(nz, cap, blk_dev, me[0], me[1], me[2], region[t], block[t])
        rank = count[at]
        count[at] = rank + 1
        g = partner * slots + first + rank
        inv[g] = t
        at_slot[t] = g
        return carry

    lax.fori_loop(0, region.shape[0], place, 0)


def plan(me, region, block, before, nz, cap, blk_dev):
    return pl.pallas_call(
        functools.partial(plan_kernel, nz, cap, blk_dev, len(before)),
        out_shape=[
            jax.ShapeDtypeStruct(region.shape, I32),
            jax.ShapeDtypeStruct((4 * nz * cap,), I32),
        ],
        in_specs=[SMEM, SMEM, SMEM] + [ANY] * len(before),
        out_specs=[SMEM, SMEM],
        scratch_shapes=[pltpu.SMEM((4 * nz,), I32)],
        compiler_params=pltpu.CompilerParams(vmem_limit_bytes=VMEM_BYTES),
        cost_estimate=SHORT,
        name="plan",
    )(me, region, block, *before)


def receive_kernel(nz, cap, blk_dev, tile_dev, me, *refs):
    packs, (meta, ids, held, scalars, count, held_sems, scalar_sems) = refs[:4], refs[4:]
    slots = nz * cap
    at_ring, y, core = me[0], me[1], me[2]

    def copies(d):
        return (
            pltpu.make_async_copy(packs[d], held.at[d], held_sems.at[d]),
            pltpu.make_async_copy(packs[d].at[pl.ds(2 * tile_dev, 8)], scalars.at[d], scalar_sems.at[d]),
        )

    for d in range(4):
        for copy in copies(d):
            copy.start()

    def clear(i, carry):
        ids[i] = -1
        return carry

    lax.fori_loop(0, 4 * slots, clear, 0)
    for d in range(4):
        for copy in copies(d):
            copy.wait()
        zero(count, 4 * nz)

        def place(t, carry):
            block = scalars[d, 1, t]
            partner, first, at = slot_of(
                nz, cap, blk_dev, at_ring, y ^ (d >> 1), core ^ (d & 1), scalars[d, 0, t], block
            )

            @pl.when(partner == d)
            def _():
                rank = count[at]
                count[at] = rank + 1
                g = d * slots + first + rank
                ids[g] = lax.rem(block, blk_dev)
                meta[g, 1:2, :] = held[d, pl.ds(t, 1), :]
                meta[g, 2:3, :] = held[d, pl.ds(tile_dev + t, 1), :]

            return carry

        lax.fori_loop(0, tile_dev, place, 0)


def receive(me, packs, nz, cap, blk_dev, tile_dev):
    slots = nz * cap
    return pl.pallas_call(
        functools.partial(receive_kernel, nz, cap, blk_dev, tile_dev),
        out_shape=[
            jax.ShapeDtypeStruct((4 * slots, 8, TILE), I32),
            jax.ShapeDtypeStruct((4 * slots,), I32),
        ],
        in_specs=[SMEM] + [ANY] * 4,
        out_specs=[VMEM, SMEM],
        scratch_shapes=[
            pltpu.VMEM((4,) + packs[0].shape, I32),
            pltpu.SMEM((4, 8, TILE), I32),
            pltpu.SMEM((4 * nz,), I32),
            pltpu.SemaphoreType.DMA((4,)),
            pltpu.SemaphoreType.DMA((4,)),
        ],
        compiler_params=pltpu.CompilerParams(vmem_limit_bytes=VMEM_BYTES),
        cost_estimate=SHORT,
        name="receive",
    )(me, *packs)


def dispatch_kernel(slots, runs, n_before, at_slot, vec, *refs):
    refs = refs[n_before:]
    tiles, (held, in_sems, out_sems) = refs[: len(runs)], refs[len(runs) :]
    tile_dev = vec.shape[0]

    def each(act):
        def body(t, carry):
            g = at_slot[t]

            @pl.when(g >= slots)
            def _():
                act(t, g)

            return carry

        lax.fori_loop(0, tile_dev, body, 0)

    def bring(t, g):
        pltpu.make_async_copy(vec.at[t], held.at[t], in_sems.at[t]).start()

    def send(t, g):
        pltpu.make_async_copy(vec.at[t], held.at[t], in_sems.at[t]).wait()
        for ref, (d, first, count) in zip(tiles, runs):
            begin = d * slots + first

            @pl.when((g >= begin) & (g < begin + count))
            def _():
                pltpu.make_async_copy(held.at[t], ref.at[g - begin], out_sems.at[t]).start()

    def finish(t, g):
        pltpu.make_async_copy(held.at[t], tiles[0].at[0], out_sems.at[t]).wait()

    each(bring)
    each(send)
    each(finish)


def dispatch(at_slot, vec, before, slots, runs):
    tile_dev = vec.shape[0]
    return pl.pallas_call(
        functools.partial(dispatch_kernel, slots, runs, len(before)),
        out_shape=[jax.ShapeDtypeStruct((count, TILE, D), BF16) for _, _, count in runs],
        in_specs=[SMEM, ANY] + [ANY] * len(before),
        out_specs=[ANY] * len(runs),
        scratch_shapes=[
            pltpu.VMEM((tile_dev, TILE, D), BF16),
            pltpu.SemaphoreType.DMA((tile_dev,)),
            pltpu.SemaphoreType.DMA((tile_dev,)),
        ],
        compiler_params=pltpu.CompilerParams(vmem_limit_bytes=VMEM_BYTES),
        cost_estimate=SHORT,
        name="dispatch",
    )(at_slot, vec, *before)


def gate_kernel(*refs):
    pass


def gate(passed):
    n = len(passed)
    return pl.pallas_call(
        gate_kernel,
        out_shape=[jax.ShapeDtypeStruct(v.shape, v.dtype) for v in passed],
        in_specs=[ANY] * n,
        out_specs=[ANY] * n,
        input_output_aliases={i: i for i in range(n)},
        compiler_params=pltpu.CompilerParams(vmem_limit_bytes=VMEM_BYTES),
        cost_estimate=SHORT,
        name="gate",
    )(*passed)


def score_math(points, block_rows, meta):
    picks = meta.astype(F32).T.astype(I32)
    lane = lax.broadcasted_iota(I32, (TILE, BLOCK), 1)
    onehot = (lane == picks[:, 1:2]).astype(F32).astype(BF16)
    chosen = jnp.dot(onehot, block_rows, preferred_element_type=F32)
    point_f = points.astype(F32)
    residue = point_f - chosen
    point_sq = jnp.sum(point_f * point_f, axis=1, keepdims=True)
    residue_sq = jnp.sum(residue * residue, axis=1, keepdims=True)
    along = jnp.sum(residue * point_f, axis=1, keepdims=True)
    both = jnp.concatenate([points, residue.astype(BF16)], axis=0)
    products = lax.dot_general(
        both, block_rows, (((1,), (1,)), ((), ())), preferred_element_type=F32
    )
    cross, against = products[:TILE], products[TILE:]
    block_f = block_rows.astype(F32)
    squares = block_f * block_f
    partial = squares[:, :128]
    for k in range(1, D // 128):
        partial = partial + squares[:, k * 128 : (k + 1) * 128]
    center_sq = jnp.sum(partial.T, axis=0, keepdims=True)
    distance = point_sq - 2.0 * cross + center_sq
    mean_sq = residue_sq / D
    off = (along - against) / D
    scores = (distance / D + off * off * (1.0 / (mean_sq + SMALL_TERM))).astype(BF16)
    picked = jnp.sum(
        jnp.where(lane == picks[:, 2:3], scores.astype(F32), 0.0), axis=1, keepdims=True
    )
    column = lax.broadcasted_iota(I32, (TILE, 128), 1)
    small = jnp.where(column == 0, mean_sq, jnp.where(column == 1, picked, 0.0))
    return scores, small.T[:8]


def score_kernel(nz, cap, blk_dev, group, order, runs, fetched, late, resident, aliased, n_extra, me, ids, inv, meta, *refs):
    slots = nz * cap
    wide = len(group) * cap
    n = len(order)
    tiles, refs = refs[: len(runs)], refs[len(runs) :]
    local, parts = refs[0], refs[1 : 1 + len(fetched)]
    refs = refs[1 + len(fetched) + aliased + n_extra :]
    scores = refs[:n]
    work, xbuf, cbuf, obuf, tail, tail_b, xsem, csem, osem, tsem = refs[n:]
    half = me[3]
    half_blocks = blk_dev // 2
    base = group[0] * cap

    total = jnp.int32(0)
    for place, partner in enumerate(order):
        for k in range(wide):
            b = ids[partner * slots + base + k]
            valid = b >= 0
            if late is not None:
                first, wanted = late
                is_late = (b // half_blocks != half) & (b % half_blocks >= first)
                is_late = is_late & (group[k // cap] == nz - 1)
                valid = valid & (is_late == wanted)
            work[total] = place * wide + k
            total = total + valid.astype(I32)

    def start(i):
        code = work[i]
        place = code // wide
        slot = base + code - place * wide
        partner = jnp.int32(order[0])
        for other in range(1, n):
            partner = jnp.where(place == other, order[other], partner)
        b = ids[partner * slots + slot]
        for ref, (d, first, count) in zip(tiles, runs):
            row = slot - first if d else jnp.maximum(inv[slot], 0)

            @pl.when((partner == d) & (slot >= first) & (slot < first + count))
            def _():
                pltpu.make_async_copy(ref.at[row], xbuf.at[i], xsem.at[i]).start()

        cls = slot // cap
        own = b // half_blocks == half
        inside = b % half_blocks

        if resident:
            return

        if group[0] == 0:

            @pl.when(cls == 0)
            def _():
                pltpu.make_async_copy(local.at[b], cbuf.at[i], csem.at[i]).start()

        for ref, (hops, direct, first, count) in zip(parts, fetched):
            right = own if direct else jnp.logical_not(own)

            @pl.when((cls == hops) & right & (inside >= first) & (inside < first + count))
            def _():
                pltpu.make_async_copy(ref.at[inside - first], cbuf.at[i], csem.at[i]).start()

    def begin(i, carry):
        start(i)
        return carry

    lax.fori_loop(0, total, begin, 0)
    tail_rows = pl.ds(wide * TILE + 16 * (aliased > 0), 16)
    tail[...] = jnp.zeros(tail.shape, F32)

    def centers_of(i, slot, partner):
        if not resident:
            return cbuf[i]
        inside = ids[partner * slots + slot] % half_blocks
        rows = parts[0][jnp.clip(inside - fetched[0][2], 0, fetched[0][3] - 1)]
        for ref, (hops, direct, first, count) in zip(parts[1:], fetched[1:]):
            rows = jnp.where(inside >= first, ref[jnp.clip(inside - first, 0, count - 1)], rows)
        return rows

    def where(i):
        code = work[i]
        place = code // wide
        partner = jnp.int32(order[0])
        for other in range(1, n):
            partner = jnp.where(place == other, order[other], partner)
        return place, code - place * wide, partner

    def body(pair, carry):
        both = (2 * pair, jnp.minimum(2 * pair + 1, total - 1))
        spots = [where(i) for i in both]
        values = []
        for j, i in enumerate(both):

            @pl.when(2 * pair + j < total)
            def _():
                pltpu.make_async_copy(tiles[0].at[0], xbuf.at[i], xsem.at[i]).wait()
                if not resident:
                    pltpu.make_async_copy(local.at[0], cbuf.at[i], csem.at[i]).wait()

        for i, (place, k, partner) in zip(both, spots):
            rows = centers_of(i, base + k, partner)
            values.append(score_math(xbuf[i], rows, meta[partner * slots + base + k]))
        for i, (place, k, partner), (value, rows) in zip(both, spots, values):
            obuf[i] = value
            tail[place, pl.ds(k, 1), 0 : 2 * TILE] = jnp.concatenate([rows[0:1], rows[1:2]], axis=1)
        for j, (i, (place, k, partner)) in enumerate(zip(both, spots)):
            for other in range(n):

                @pl.when((place == other) & (2 * pair + j < total))
                def _():
                    pltpu.make_async_copy(
                        obuf.at[i], scores[other].at[pl.ds(k * TILE, TILE)], osem.at[i]
                    ).start()

        return carry

    lax.fori_loop(0, (total + 1) // 2, body, 0)

    tail_b[...] = tail[...].astype(BF16)
    for place in range(n):
        pltpu.make_async_copy(tail_b.at[place], scores[place].at[tail_rows], tsem.at[place]).start()

    def finish(i, carry):
        pltpu.make_async_copy(obuf.at[i], scores[0].at[pl.ds(0, TILE)], osem.at[i]).wait()
        return carry

    lax.fori_loop(0, total, finish, 0)
    for place in range(n):
        pltpu.make_async_copy(tail_b.at[place], scores[place].at[tail_rows], tsem.at[place]).wait()


def score_call(
    nz, cap, blk_dev, group, order, runs, fetched, late, resident, me, ids, inv, meta, tiles, local, parts, before, extra
):
    wide = len(group) * cap
    n = len(order)
    items = n * wide
    first_before = 5 + len(runs) + len(parts)
    return pl.pallas_call(
        functools.partial(
            score_kernel, nz, cap, blk_dev, group, order, runs, fetched, late, resident, len(before), len(extra)
        ),
        out_shape=[jax.ShapeDtypeStruct((wide * TILE + (32 if late else 16), BLOCK), BF16)] * n,
        in_specs=[SMEM, SMEM, SMEM, VMEM]
        + [ANY] * (len(runs) + 1)
        + [VMEM if resident else ANY] * len(parts)
        + [ANY] * (len(before) + len(extra)),
        out_specs=[ANY] * n,
        scratch_shapes=[
            pltpu.SMEM((items + 1,), I32),
            pltpu.VMEM((items, TILE, D), BF16),
            pltpu.VMEM((1 if resident else items, BLOCK, D), BF16),
            pltpu.VMEM((items, TILE, BLOCK), BF16),
            pltpu.VMEM((n, 16, BLOCK), F32),
            pltpu.VMEM((n, 16, BLOCK), BF16),
            pltpu.SemaphoreType.DMA((items,)),
            pltpu.SemaphoreType.DMA((items,)),
            pltpu.SemaphoreType.DMA((items,)),
            pltpu.SemaphoreType.DMA((n,)),
        ],
        input_output_aliases={first_before + i: i for i in range(len(before))},
        compiler_params=pltpu.CompilerParams(vmem_limit_bytes=VMEM_BYTES),
        cost_estimate=SHORT,
        name="score",
    )(me, ids, inv, meta, *tiles, local, *parts, *before, *extra)


def assemble_kernel(spans, n_before, n_earlier, inv, *refs):
    n = len(spans)
    sources, before, refs = refs[:n], refs[n : n + n_before], refs[n + n_before + n_earlier :]
    out, primary, picked, held, tail, in_sems, out_sems, tail_sems = refs
    if n_before:
        primary[...] = before[1][...]
        picked[...] = before[2][...]

    def each(act):
        at = 0
        for d, (first, wide) in enumerate(spans):
            for k in range(wide):
                t = inv[first + k]

                @pl.when(t >= 0)
                def _():
                    act(d, k, t, at)

                at += 1

    def tail_copy(d):
        return pltpu.make_async_copy(
            sources[d].at[pl.ds(spans[d][1] * TILE, tail.shape[1])], tail.at[d], tail_sems.at[d]
        )

    def bring(d, k, t, n):
        pltpu.make_async_copy(sources[d].at[pl.ds(k * TILE, TILE)], held.at[n], in_sems.at[n]).start()

    def send(d, k, t, n):
        pltpu.make_async_copy(sources[d].at[pl.ds(k * TILE, TILE)], held.at[n], in_sems.at[n]).wait()
        pltpu.make_async_copy(held.at[n], out.at[t], out_sems.at[n]).start()

    def finish(d, k, t, n):
        pltpu.make_async_copy(held.at[n], out.at[t], out_sems.at[n]).wait()

    for d in range(n):
        tail_copy(d).start()
    each(bring)
    for d in range(n):
        tail_copy(d).wait()
    each(send)
    rows = []
    for d in range(n):
        both = tail[d].astype(F32)
        rows.append(both if both.shape[0] == 16 else both[:16] + both[16:])

    def write(d, k, t, n):
        primary[pl.ds(t, 1), :] = rows[d][k : k + 1, :TILE]
        picked[pl.ds(t, 1), :] = rows[d][k : k + 1, TILE : 2 * TILE]

    each(write)
    each(finish)


def assemble(tile_dev, spans, inv, sources, before, earlier):
    n = len(sources)
    count = sum(wide for _, wide in spans)
    return pl.pallas_call(
        functools.partial(assemble_kernel, spans, len(before), len(earlier)),
        out_shape=[jax.ShapeDtypeStruct((tile_dev, TILE, BLOCK), BF16)]
        + [jax.ShapeDtypeStruct((tile_dev, TILE), F32)] * 2,
        in_specs=[SMEM] + [ANY] * n + [ANY, VMEM, VMEM][: len(before)] + [ANY] * len(earlier),
        out_specs=[ANY, VMEM, VMEM],
        scratch_shapes=[
            pltpu.VMEM((count, TILE, BLOCK), BF16),
            pltpu.VMEM((n, sources[0].shape[0] - spans[0][1] * TILE, BLOCK), BF16),
            pltpu.SemaphoreType.DMA((count,)),
            pltpu.SemaphoreType.DMA((count,)),
            pltpu.SemaphoreType.DMA((n,)),
        ],
        input_output_aliases={1 + n: 0} if before else {},
        compiler_params=pltpu.CompilerParams(vmem_limit_bytes=VMEM_BYTES),
        cost_estimate=SHORT,
        name="assemble",
    )(inv, *sources, *before, *earlier)


def local_part(pieces, vectors, tile_region, tile_block, primary_pick, spill_pick, centers):
    n_parts, n_region, n_shard = (lax.axis_size(a) for a in AXES)
    nz = n_shard // 2
    tile_dev = tile_region.shape[0]
    cap = 2 * tile_dev // (n_region * n_shard)
    slots = nz * cap
    blk_dev = centers.shape[1] // BLOCK
    half_blocks = blk_dev // 2
    pieces = min(pieces, half_blocks)
    sub_blocks = half_blocks // pieces
    shard = lax.axis_index("shard")
    half = lax.axis_index("parts") & 1
    ring, at_ring = ring_place(nz)
    me = jnp.stack(
        [place_of(shard >> 1, nz), shard & 1, lax.axis_index("region"), half]
    ).astype(I32)

    def device(p, r, s):
        return (p * n_region + r) * n_shard + s

    every = [(p, r, s) for p in range(n_parts) for r in range(n_region) for s in range(n_shard)]

    def permute(value, target):
        return lax.ppermute(value, AXES, [(device(*a), device(*target(*a))) for a in every])

    def next_z(p, r, s):
        return (p, r, 2 * ring[(at_ring[s >> 1] + 1) % nz] + (s & 1))

    def other_part(p, r, s):
        return (p ^ 1, r, s)

    local = centers[0].reshape(blk_dev, BLOCK, D)

    def own_piece(i, half):
        return lax.dynamic_slice_in_dim(local, half * half_blocks + i * sub_blocks, sub_blocks, 0)

    own = [own_piece(i, half) for i in range(pieces)]
    tile_rows = vectors.reshape(tile_dev, TILE, D)
    scalars = jnp.pad(jnp.stack([tile_region, tile_block]), ((0, 6), (0, TILE - tile_dev)))
    pack = jnp.concatenate(
        [primary_pick.reshape(tile_dev, TILE), spill_pick.reshape(tile_dev, TILE), scalars]
    )
    at_slot, inv = plan(me, tile_region, tile_block, own, nz, cap, blk_dev)

    def exchange(value, partner):
        if partner == 0:
            return value
        return permute(value, lambda p, r, s: (p, r ^ (partner & 1), s ^ (partner >> 1)))

    packs = [exchange(pack, d) for d in range(4)]
    part = slots // 2
    runs = tuple((d, first, part) for first in (0, part) for d in (2, 3, 1))
    sent = dispatch(at_slot, tile_rows, packs[1:], slots, runs)
    meta, ids = receive(me, packs, nz, cap, blk_dev, tile_dev)

    env, waits, opens = {}, {}, {}

    def across(d):
        return lambda p, r, s: (p, r ^ (d & 1), s ^ (d >> 1))

    steps = (nz - 1) * pieces
    split = sub_blocks // 2 if nz > 2 else 0
    last = steps + 1
    fetched = {}
    starts = {}
    env.update({("z", i + 1 - pieces): own[i] for i in range(pieces)})

    def start(at, name, payload, target, done):
        starts.setdefault(at, []).append((name, payload, target, done))

    for k in range(1, steps + 1):
        hops, first = (k - 1) // pieces + 1, (k - 1) % pieces * sub_blocks
        if split and k == steps:
            start(k - 2, ("z", k), ("z", k - pieces), next_z, None)
            start(k - 1, ("z", last), ("cut", 0), next_z, None)
            start(k - 1, ("x", k), ("cut", 1), other_part, None)
            fetched[hops, True, first, sub_blocks] = ("z", k)
            fetched[hops, False, first, split] = ("x", k)
            fetched[hops, False, first + split, sub_blocks - split] = ("z", last)
        else:
            start(max(0, k - 2), ("z", k), ("z", k - pieces), next_z, k)
            start(k, ("x", k), ("z", k), other_part, k + 1 if k < steps else None)
            fetched[hops, True, first, sub_blocks] = ("z", k)
            fetched[hops, False, first, sub_blocks] = ("x", k)

    times = {0: (0, 2), 1: (0, 3), 2: (5, 6), 3: (2, 4), 4: (3, 5), 5: (5, 6)}
    for i, run in enumerate(runs):
        if run[0] == 1:
            continue
        at, done = (min(g, last - 2 + j) for j, g in enumerate(times[i]))
        env["sent", i] = sent[i]
        if at:
            opens.setdefault(at, []).append(("sent", i))
        start(at, ("t", i), ("sent", i), across(run[0]), done)
    for i, run in enumerate(runs):
        if run[0] == 1:
            env["sent", i] = sent[i]
            opens.setdefault(min(5, last - 1), []).append(("sent", i))
            start(min(5, last - 1), ("t", i), ("sent", i), across(1), None)
    env["t", len(runs)] = tile_rows
    runs += ((0, 0, slots),)

    def score(group, order, late=None, into=False, extra=()):
        resident = into
        keys = tuple(
            key
            for key in fetched
            if key[0] in group and (fetched[key] in (("x", steps), ("z", last))) == resident and fetched[key] in env
        )
        low, high = group[0] * cap, (group[-1] + 1) * cap
        used = [
            i for i, (d, first, count) in enumerate(runs) if d in order and first < high and first + count > low
        ]
        scores = score_call(
            nz, cap, blk_dev, group, order, tuple(runs[i] for i in used), keys, late, resident, me, ids, inv, meta,
            [env["t", i] for i in used], local,
            [env[fetched[key]] for key in keys],
            [env["s", d, group] for d in order] if into else [],
            extra,
        )
        for d, values in zip(order, scores):
            env["s", d, group] = values

    def place(sources, before, earlier=()):
        return assemble(
            tile_dev,
            [(d * slots + group[0] * cap, len(group) * cap) for d, group in sources],
            inv,
            [env["r" if d else "s", d, group] for d, group in sources],
            before,
            earlier,
        )

    one, two, three = (tuple(range(a, b)) for a, b in ((0, nz // 2), (nz // 2, 3 * nz // 4), (3 * nz // 4, nz)))
    plans, at_once = {}, {}
    for ready, order, group, back in (
        (3, (2, 3, 0), one, {2: (4, 5), 3: (5, 6)}),
        (5, (2, 3, 0), two, {2: (0, 6), 3: (6, 7)}),
        (5, (1,), one, {}),
        (5, (1,), two, {}),
    ):
        ready = max(ready, group[-1] * pieces + 1)
        plans.setdefault(ready, []).append((group, order))
        for d, (at, done) in back.items():
            if at:
                at = min(last - 1, max(at, ready + 1))
                opens.setdefault(at, []).append(("s", d, group))
                start(at, ("r", d, group), ("s", d, group), across(d), min(last, max(done, at + 1)))
            else:
                at_once.setdefault(ready, []).append((d, group, min(last, max(done, ready + 1))))
    opens.setdefault(last - 1, []).extend([("s", 1, one), ("s", 1, two)])
    first_late = (pieces - 1) * sub_blocks
    env["token"] = jnp.zeros((8, TILE), F32)
    for k in range(last + 1):
        if k:
            passed = waits.get(k, []) + opens.get(k, [])
            source = ("z", k + 2 - pieces)
            if k + 2 <= steps and k + 2 - pieces < k:
                passed.append(source)
            passed.append("token")
            for name, value in zip(passed, gate([env[n] for n in passed])):
                env[name] = value
        if split and k == steps - 1:
            env["cut", 0] = env["x", steps - pieces][split:]
            env["cut", 1] = env["z", steps][:split]
        for name, payload, target, done in starts.get(k, []):
            env[name] = permute(env[payload], target)
            if done is not None:
                waits.setdefault(done, []).append(name)
        for group, order in plans.get(k, []):
            score(group, order, extra=[env["token"]])
        for d, group, done in at_once.get(k, []):
            env["r", d, group] = exchange(env["s", d, group], d)
            waits.setdefault(done, []).append(("r", d, group))
        if k == last - 1:
            score(three, (2, 3, 1, 0), (first_late, False), extra=[env["token"]])
    score(three, (2, 3, 1, 0), (first_late, True), True, [env["token"]])
    for d in (2, 3, 1):
        env["r", d, three] = exchange(env["s", d, three], d)
    for group in (one, two):
        env["r", 1, group] = exchange(env["s", 1, group], 1)
    outputs = place([(2, one), (3, one), (0, one)], [], [env["s", 0, three]])
    outputs = place([(2, two), (3, two), (0, two), (1, one), (1, two)], outputs, [env["s", 0, three]])
    spill_scores, primary, picked = place([(d, three) for d in (0, 1, 2, 3)], outputs)
    return (
        spill_scores.reshape(tile_dev * TILE, BLOCK),
        primary.astype(BF16).reshape(tile_dev * TILE),
        picked.astype(BF16).reshape(tile_dev * TILE),
    )


def solution(mesh):
    rows = P(AXES, None)
    flat = P(AXES)
    return jax.shard_map(
        functools.partial(local_part, 2),
        mesh=mesh,
        in_specs=(rows, flat, flat, flat, flat, P("region", "shard", None)),
        out_specs=(rows, flat, flat),
        check_vma=False,
    )
```

time: 334 us -> 288 us (0.86)
  the two profiles are of different devices: /device:TPU:15 before, /device:TPU:9 now
where the time goes in v3:
time: 288 us; the launch traced here: 283 us
  waiting for transfers between devices  140 us (49%)
  Pallas kernels  83.1 us (29%)
  starting transfers between devices  43.6 us (15%)
  local copies, waits for them, and re-layouts  13.8 us (5%)
    ppermute x31, waiting for transfers between devices, permute(): lax.ppermute(value, AXES, [(device(*a), device(*target(*a))) for a in eve...  140 us
    pallas_call x6, Pallas kernels, score_call(): pl.pallas_call(functools.partial(score_kernel, nz, cap, blk_dev, group, o...  56.5 us
    ppermute x31, starting transfers between devices, permute(): lax.ppermute(value, AXES, [(device(*a), device(*target(*a))) for a in eve...  43.6 us
    pallas_call x3, Pallas kernels, assemble(): pl.pallas_call(functools.partial(assemble_kernel, spans, len(before), len...  12.2 us
    pallas_call x1, Pallas kernels, receive(): pl.pallas_call(functools.partial(receive_kernel, nz, cap, blk_dev, tile_d...  7.38 us
  transfers between devices with their start and end apart: 31, of which 11 were waited for; matrix products, arithmetic and copies ran while one was open for 2% of the time, Pallas kernels for 28%

profile of v3, /device:TPU:9, one launch (start us, length us, event | category | flops | bytes accessed | tf_op | source)
XLA Modules:
  0.0 283.3 jit_solution(12226723155465767989)
XLA Ops:
  0.7 3.8 %constant_dynamic-slice_fusion = (bf16[2,512,768]{2,1,0:T(8,128)(2,1)}, bf16[2,512,768]{2,1,0:T(8,128)(2,1)}) fusion(bf16[8,512,768]{2,1,0:T(8,128)(2,1)} %bitcast.15, s32[]{:T(128)S(6)} %select_n.26, s32[]{:T(128)S(6)} %select_n.25), kind=kLoop, calls=%fused_computation.5 | loop fusion | bytes 6291464 | tf_op jit(solution)/shard_map/dynamic_slice | solution.py:540
  4.5 2.3 collective-permute-start.5
  6.9 1.0 collective-permute-start
  7.9 1.3 collective-permute-start.1
  10.4 2.8 plan.1
  13.9 4.1 %dispatch.1 = (bf16[8,128,768]{2,1,0:T(8,128)(2,1)}, bf16[8,128,768]{2,1,0:T(8,128)(2,1)}, bf16[8,128,768]{2,1,0:T(8,128)(2,1)}, bf16[8,128,768]{2,1,0:T(8,128)(...) custom-call(s32[32]{0:T(128)} %get-tuple-element.73.at_slot, bf16[32,128,768]{2,1,0:T(8,128)(2,1)} %bitcast.22, ...), custom_call_target="tpu_custom_call" | custom-call | flops 1 | bytes 1 | tf_op jit(solution)/shard_map/dispatch/pallas_call | solution.py:196
  18.0 3.2 %collective-permute-start.4 = (bf16[8,128,768]{2,1,0:T(8,128)(2,1)}, bf16[8,128,768]{2,1,0:T(8,128)(2,1)}, u32[]{:S(2)}, u32[]{:S(2)}) collective-permute-start(bf16[8,128,768]{2,1,0:T(8,128)(2,1)} %get-tuple-element.74), channel_id=1, source_target_pairs={{0,1},{1,0},{2,3},{3,2},{4,5},{5,4},{6,7},{7,6},{8,9},{9,8},{10,11... | collective-permute-start | bytes 4718600 | tf_op jit(solution)/shard_map/ppermute | solution.py:529
  21.2 19.0 %collective-permute-done.5.refs_0_ = bf16[2,512,768]{2,1,0:T(8,128)(2,1)S(1)} collective-permute-done((bf16[2,512,768]{2,1,0:T(8,128)(2,1)}, bf16[2,512,768]{2,1,0:T(8,128)(2,1)S(1)}, u32[]{:S(2)}, u32[]{:S(2)}) %collective-permute-start.5) | collective-permute-done | bytes 1572896 | tf_op jit(solution)/shard_map/ppermute | solution.py:529
  41.3 1.2 collective-permute-start.6
  42.5 4.1 %collective-permute-start.9 = (bf16[8,128,768]{2,1,0:T(8,128)(2,1)}, bf16[8,128,768]{2,1,0:T(8,128)(2,1)}, u32[]{:S(2)}, u32[]{:S(2)}) collective-permute-start(bf16[8,128,768]{2,1,0:T(8,128)(2,1)} %get-tuple-element.80), channel_id=1, source_target_pairs={{0,9},{1,8},{2,11},{3,10},{4,13},{5,12},{6,15},{7,14},{8,1},{9,0},... | collective-permute-start | bytes 4718600 | tf_op jit(solution)/shard_map/ppermute | solution.py:529
  46.6 3.0 %collective-permute-start.10 = (bf16[2,512,768]{2,1,0:T(8,128)(2,1)}, bf16[2,512,768]{2,1,0:T(8,128)(2,1)}, u32[]{:S(2)}, u32[]{:S(2)}) collective-permute-start(bf16[2,512,768]{2,1,0:T(8,128)(2,1)} %get-tuple-element.75.refs_4_.refs_2_), channel_id=1, source_target_pairs={{0,2},{1,3},{2,6},{3,7},{4,0},{5,1},{6,4},{7,5},{8,10},{9,11},{10,... | collective-permute-start | bytes 4718600 | tf_op jit(solution)/shard_map/ppermute | solution.py:529
  49.6 24.3 %collective-permute-done.3.refs_0_ = bf16[2,512,768]{2,1,0:T(8,128)(2,1)} collective-permute-done((bf16[2,512,768]{2,1,0:T(8,128)(2,1)}, bf16[2,512,768]{2,1,0:T(8,128)(2,1)}, u32[]{:S(2)}, u32[]{:S(2)}) %collective-permute-start.3) | collective-permute-done | bytes 1572896 | tf_op jit(solution)/shard_map/ppermute | solution.py:529
  73.9 0.9 collective-permute-done.6.refs_2_
  74.8 1.1 copy-done.2
  76.0 1.2 collective-permute-start.11
  77.2 3.0 %collective-permute-start.7 = (bf16[2,512,768]{2,1,0:T(8,128)(2,1)}, bf16[2,512,768]{2,1,0:T(8,128)(2,1)}, u32[]{:S(2)}, u32[]{:S(2)}) collective-permute-start(bf16[2,512,768]{2,1,0:T(8,128)(2,1)} %get-tuple-element.78.refs_6_.refs_4_), channel_id=1, source_target_pairs={{0,2},{1,3},{2,6},{3,7},{4,0},{5,1},{6,4},{7,5},{8,10},{9,11},{10,... | collective-permute-start | bytes 4718600 | tf_op jit(solution)/shard_map/ppermute | solution.py:529
  80.2 1.2 collective-permute-start.8
  81.4 9.5 %collective-permute-done.9.refs_0_ = bf16[8,128,768]{2,1,0:T(8,128)(2,1)} collective-permute-done((bf16[8,128,768]{2,1,0:T(8,128)(2,1)}, bf16[8,128,768]{2,1,0:T(8,128)(2,1)}, u32[]{:S(2)}, u32[]{:S(2)}) %collective-permute-start.9) | collective-permute-done | bytes 1572896 | tf_op jit(solution)/shard_map/ppermute | solution.py:529
  90.9 16.7 %collective-permute-done.10.refs_1_ = bf16[2,512,768]{2,1,0:T(8,128)(2,1)} collective-permute-done((bf16[2,512,768]{2,1,0:T(8,128)(2,1)}, bf16[2,512,768]{2,1,0:T(8,128)(2,1)}, u32[]{:S(2)}, u32[]{:S(2)}) %collective-permute-start.10) | collective-permute-done | bytes 1572896 | tf_op jit(solution)/shard_map/ppermute | solution.py:529
  107.6 1.1 collective-permute-done.11.refs_2_
  108.7 1.1 copy-done.3
  109.8 1.2 collective-permute-start.12
  111.0 7.4 %receive.1 = (s32[64,8,128]{2,1,0:T(8,128)}, s32[64]{0:T(128)}) custom-call(s32[4]{0:T(128)} %pad_add_fusion.2.me, s32[72,128]{1,0:T(8,128)} %copy-done.8, s32[72,128]{1,0:T(8,128)} %copy-done.9, s32[72,128]{1,0:T(8,128)} %copy-done.10, s32[72,128]{1,0:T(8,128)} %copy-done.11), custom_call_target="tpu_custom_call" | custom-call | flops 1 | bytes 1 | tf_op jit(solution)/shard_map/receive/pallas_call | solution.py:136
  118.4 3.0 %collective-permute-start.13 = (bf16[2,512,768]{2,1,0:T(8,128)(2,1)}, bf16[2,512,768]{2,1,0:T(8,128)(2,1)}, u32[]{:S(2)}, u32[]{:S(2)}) collective-permute-start(bf16[2,512,768]{2,1,0:T(8,128)(2,1)} %get-tuple-element.83.refs_4_.refs_2_), channel_id=1, source_target_pairs={{0,2},{1,3},{2,6},{3,7},{4,0},{5,1},{6,4},{7,5},{8,10},{9,11},{10,... | collective-permute-start | bytes 4718600 | tf_op jit(solution)/shard_map/ppermute | solution.py:529
  121.4 5.9 %collective-permute-start.14 = (bf16[8,128,768]{2,1,0:T(8,128)(2,1)}, bf16[8,128,768]{2,1,0:T(8,128)(2,1)S(1)}, u32[]{:S(2)}, u32[]{:S(2)}) collective-permute-start(bf16[8,128,768]{2,1,0:T(8,128)(2,1)} %get-tuple-element.91), channel_id=1, source_target_pairs={{0,9},{1,8},{2,11},{3,10},{4,13},{5,12},{6,15},{7,14},{8,1},{9,0},... | collective-permute-start | bytes 4718600 | tf_op jit(solution)/shard_map/ppermute | solution.py:529
  127.3 20.7 %score.6 = (bf16[1040,512]{1,0:T(8,128)(2,1)}, bf16[1040,512]{1,0:T(8,128)(2,1)}, bf16[1040,512]{1,0:T(8,128)(2,1)}) custom-call(s32[4]{0:T(128)} %pad_add_fusion.2.me, s32[64]{0:T(128)} %get-tuple-element.71.ids, s32[64]{0:T(128)} %get-tuple-element.70.inv, s32[64,8,128]{2,1,0:T(8,128)} %get-tuple-element.72.meta, ...), custom_call_target="tpu_custom_call" | custom-call | flops 1 | bytes 1 | tf_op jit(solution)/shard_map/score/pallas_call | solution.py:400
  148.3 26.7 %collective-permute-done.13.refs_0_ = bf16[2,512,768]{2,1,0:T(8,128)(2,1)} collective-permute-done((bf16[2,512,768]{2,1,0:T(8,128)(2,1)}, bf16[2,512,768]{2,1,0:T(8,128)(2,1)}, u32[]{:S(2)}, u32[]{:S(2)}) %collective-permute-start.13) | collective-permute-done | bytes 1572896 | tf_op jit(solution)/shard_map/ppermute | solution.py:529
  175.0 10.6 %collective-permute-done.16.refs_3_ = bf16[1040,512]{1,0:T(8,128)(2,1)} collective-permute-done((bf16[1040,512]{1,0:T(8,128)(2,1)}, bf16[1040,512]{1,0:T(8,128)(2,1)}, u32[]{:S(2)}, u32[]{:S(2)}) %collective-permute-start.16) | collective-permute-done | bytes 1064992 | tf_op jit(solution)/shard_map/ppermute | solution.py:529
  187.0 6.3 %score.7 = (bf16[528,512]{1,0:T(8,128)(2,1)}, bf16[528,512]{1,0:T(8,128)(2,1)}, bf16[528,512]{1,0:T(8,128)(2,1)}) custom-call(s32[4]{0:T(128)} %pad_add_fusion.2.me, s32[64]{0:T(128)} %get-tuple-element.71.ids, s32[64]{0:T(128)} %get-tuple-element.70.inv, s32[64,8,128]{2,1,0:T(8,128)} %get-tuple-element.72.meta, ...), custom_call_target="tpu_custom_call" | custom-call | flops 1 | bytes 1 | tf_op jit(solution)/shard_map/score/pallas_call | solution.py:400
  193.3 15.4 %collective-permute-done.18.refs_7_ = bf16[2,512,768]{2,1,0:T(8,128)(2,1)} collective-permute-done((bf16[2,512,768]{2,1,0:T(8,128)(2,1)}, bf16[2,512,768]{2,1,0:T(8,128)(2,1)}, u32[]{:S(2)}, u32[]{:S(2)}) %collective-permute-start.18) | collective-permute-done | bytes 1572896 | tf_op jit(solution)/shard_map/ppermute | solution.py:529
  208.7 1.2 collective-permute-start.23
  209.9 2.1 slice.7
  212.0 2.1 slice.8
  214.1 3.1 %collective-permute-start.20 = (bf16[1,512,768]{2,1,0:T(8,128)(2,1)}, bf16[1,512,768]{2,1,0:T(8,128)(2,1)}, u32[]{:S(2)}, u32[]{:S(2)}) collective-permute-start(bf16[1,512,768]{2,1,0:T(8,128)(2,1)} %slice.7), channel_id=1, source_target_pairs={{0,2},{1,3},{2,6},{3,7},{4,0},{5,1},{6,4},{7,5},{8,10},{9,11},{10,... | collective-permute-start | bytes 2359304 | tf_op jit(solution)/shard_map/ppermute | solution.py:529
  217.2 1.2 collective-permute-start.19
  218.4 1.7 score.9.refs_5_
  220.1 8.9 %score.8.refs_4_ = bf16[1040,512]{1,0:T(8,128)(2,1)} custom-call(s32[4]{0:T(128)} %pad_add_fusion.2.me, s32[64]{0:T(128)} %get-tuple-element.71.ids, s32[64]{0:T(128)} %get-tuple-element.70.inv, s32[64,8,128]{2,1,0:T(8,128)} %get-tuple-element.72.meta, bf16[8,128,768]{2,1,0:T(8,128)(2,1)} %collective-permute-done.24.refs_0_, bf16[8,512,768]{2,1,0:T(8,128)(2,1)} %bitcast.19, ...), custom_call_target="tpu_custom_call" | custom-call | flops 1 | bytes 1 | tf_op jit(solution)/shard_map/score/pallas_call | solution.py:400
  229.3 13.7 %score.10 = (bf16[544,512]{1,0:T(8,128)(2,1)}, bf16[544,512]{1,0:T(8,128)(2,1)}, bf16[544,512]{1,0:T(8,128)(2,1)}, bf16[544,512]{1,0:T(8,128)(2,1)}) custom-call(s32[4]{0:T(128)} %pad_add_fusion.2.me, s32[64]{0:T(128)} %get-tuple-element.71.ids, s32[64]{0:T(128)} %get-tuple-element.70.inv, s32[64,8,128]{2,1,0:T(8,128)} %get-tuple-element.72.meta, ...), custom_call_target="tpu_custom_call" | custom-call | flops 1 | bytes 1 | tf_op jit(solution)/shard_map/score/pallas_call | solution.py:400
  243.8 5.3 %score.11 = (bf16[544,512]{1,0:T(8,128)(2,1)}, bf16[544,512]{1,0:T(8,128)(2,1)}, bf16[544,512]{1,0:T(8,128)(2,1)}, bf16[544,512]{1,0:T(8,128)(2,1)}) custom-call(s32[4]{0:T(128)} %pad_add_fusion.2.me, s32[64]{0:T(128)} %get-tuple-element.71.ids, ...), custom_call_target="tpu_custom_call", output_to_operand_aliasing={{0}: (11, {}), {1}: (12, {}), {2}: (13, {}), {3}: (14, {})} | custom-call | flops 1 | bytes 1 | tf_op jit(solution)/shard_map/score/pallas_call | solution.py:400
  249.1 2.1 collective-permute-start.26
  251.6 1.4 collective-permute-start.28
  253.1 3.8 %assemble.3 = (bf16[32,128,512]{2,1,0:T(8,128)(2,1)}, f32[32,128]{1,0:T(8,128)}, f32[32,128]{1,0:T(8,128)}) custom-call(s32[64]{0:T(128)} %get-tuple-element.70.inv, bf16[1040,512]{1,0:T(8,128)(2,1)} %get-tuple-element.125.refs_0_, bf16[1040,512]{1,0:T(8,128)(2,1)} %get-tuple-element.126.refs_1_, bf16[1040,512]{1,0:T(8,128)(2,1)} %get-tuple-element.127.refs_2_, ...), custom_call_target="tpu_custom_call" | custom-call | flops 1 | bytes 1 | tf_op jit(solution)/shard_map/assemble/pallas_call | solution.py:486
  257.0 1.0 copy-done.7
  258.0 4.2 %assemble.4 = (bf16[32,128,512]{2,1,0:T(8,128)(2,1)}, f32[32,128]{1,0:T(8,128)}, f32[32,128]{1,0:T(8,128)}) custom-call(s32[64]{0:T(128)} %get-tuple-element.70.inv, bf16[528,512]{1,0:T(8,128)(2,1)} %get-tuple-element.120.refs_0_, bf16[528,512]{1,0:T(8,128)(2,1)} %get-tuple-element.121.refs_1_, ...), custom_call_target="tpu_custom_call", output_to_operand_aliasing={{0}: (6, {})} | custom-call | flops 1 | bytes 1 | tf_op jit(solution)/shard_map/assemble/pallas_call | solution.py:486
  262.2 3.5 %collective-permute-done.27.refs_2_ = bf16[544,512]{1,0:T(8,128)(2,1)} collective-permute-done((bf16[544,512]{1,0:T(8,128)(2,1)}, bf16[544,512]{1,0:T(8,128)(2,1)}, u32[]{:S(2)}, u32[]{:S(2)}) %collective-permute-start.27) | collective-permute-done | bytes 557088 | tf_op jit(solution)/shard_map/ppermute | solution.py:529
  265.7 12.1 %collective-permute-done.28.refs_3_ = bf16[544,512]{1,0:T(8,128)(2,1)} collective-permute-done((bf16[544,512]{1,0:T(8,128)(2,1)}, bf16[544,512]{1,0:T(8,128)(2,1)}, u32[]{:S(2)}, u32[]{:S(2)}) %collective-permute-start.28) | collective-permute-done | bytes 557088 | tf_op jit(solution)/shard_map/ppermute | solution.py:529
  277.8 4.1 %assemble.5 = (bf16[32,128,512]{2,1,0:T(8,128)(2,1)}, f32[32,128]{1,0:T(8,128)}, f32[32,128]{1,0:T(8,128)}) custom-call(s32[64]{0:T(128)} %get-tuple-element.70.inv, bf16[544,512]{1,0:T(8,128)(2,1)} %get-tuple-element.116.refs_3_.refs_8_.refs_0_, bf16[544,512]{1,0:T(8,128)(2,1)} %collective-permute-done.26.refs_1_, ...), custom_call_target="tpu_custom_call", output_to_operand_aliasing={{0}: (5, {})} | custom-call | flops 1 | bytes 1 | tf_op jit(solution)/shard_map/assemble/pallas_call | solution.py:486
  282.0 1.3 convert_bitcast_fusion
  (73 shorter events, 6.2 us)
Async XLA Ops:
  0.6 6.2 %copy-start.14 = (s32[32]{0:T(128)S(1)}, s32[32]{0:T(128)}, u32[]{:S(2)}) copy-start(s32[32]{0:T(128)} %region.1) | copy-start | bytes 388
  0.6 6.1 %copy-start.15 = (s32[32]{0:T(128)S(1)}, s32[32]{0:T(128)}, u32[]{:S(2)}) copy-start(s32[32]{0:T(128)} %block.1) | copy-start | bytes 388
  0.7 6.1 %copy-start.12 = (s32[4096]{0:T(1024)S(1)}, s32[4096]{0:T(1024)}, u32[]{:S(2)}) copy-start(s32[4096]{0:T(1024)} %param.10) | copy-start | bytes 49156
  0.7 6.1 %copy-start.13 = (s32[4096]{0:T(1024)S(1)}, s32[4096]{0:T(1024)}, u32[]{:S(2)}) copy-start(s32[4096]{0:T(1024)} %param.9) | copy-start | bytes 49156
  4.5 35.7 %collective-permute-start.5 = (bf16[2,512,768]{2,1,0:T(8,128)(2,1)}, bf16[2,512,768]{2,1,0:T(8,128)(2,1)S(1)}, u32[]{:S(2)}, u32[]{:S(2)}) collective-permute-start(bf16[2,512,768]{2,1,0:T(8,128)(2,1)} %get-tuple-element.138.refs_0_), channel_id=1, source_target_pairs={{0,2},{1,3},{2,6},{3,7},{4,0},{5,1},{6,4},{7,5},{8,10},{9,11},{10,... | collective-permute-start | bytes 4718600 | tf_op jit(solution)/shard_map/ppermute | solution.py:529
  6.8 6.4 %copy-start.8 = (s32[72,128]{1,0:T(8,128)}, s32[72,128]{1,0:T(8,128)S(1)}, u32[]{:S(2)}) copy-start(s32[72,128]{1,0:T(8,128)S(1)} %pad_add_fusion.refs_0_) | copy-start | bytes 110596
  6.9 6.4 %collective-permute-start = (s32[72,128]{1,0:T(8,128)S(1)}, s32[72,128]{1,0:T(8,128)S(1)}, u32[]{:S(2)}, u32[]{:S(2)}) collective-permute-start(s32[72,128]{1,0:T(8,128)S(1)} %pad_add_fusion.refs_0_), channel_id=1, source_target_pairs={{0,8},{1,9},{2,10},{3,11},{4,12},{5,13},{6,14},{7,15},{8,0},{9,1},... | collective-permute-start | bytes 110600 | tf_op jit(solution)/shard_map/ppermute | solution.py:529
  7.9 5.4 %collective-permute-start.1 = (s32[72,128]{1,0:T(8,128)S(1)}, s32[72,128]{1,0:T(8,128)S(1)}, u32[]{:S(2)}, u32[]{:S(2)}) collective-permute-start(s32[72,128]{1,0:T(8,128)S(1)} %pad_add_fusion.refs_0_), channel_id=1, source_target_pairs={{0,1},{1,0},{2,3},{3,2},{4,5},{5,4},{6,7},{7,6},{8,9},{9,8},{10,11... | collective-permute-start | bytes 110600 | tf_op jit(solution)/shard_map/ppermute | solution.py:529
  9.1 4.1 %collective-permute-start.2 = (s32[72,128]{1,0:T(8,128)S(1)}, s32[72,128]{1,0:T(8,128)S(1)}, u32[]{:S(2)}, u32[]{:S(2)}) collective-permute-start(s32[72,128]{1,0:T(8,128)S(1)} %pad_add_fusion.refs_0_), channel_id=1, source_target_pairs={{0,9},{1,8},{2,11},{3,10},{4,13},{5,12},{6,15},{7,14},{8,1},{9,0},... | collective-permute-start | bytes 110600 | tf_op jit(solution)/shard_map/ppermute | solution.py:529
  10.2 63.7 %collective-permute-start.3 = (bf16[2,512,768]{2,1,0:T(8,128)(2,1)}, bf16[2,512,768]{2,1,0:T(8,128)(2,1)}, u32[]{:S(2)}, u32[]{:S(2)}) collective-permute-start(bf16[2,512,768]{2,1,0:T(8,128)(2,1)} %get-tuple-element.137.refs_1_), channel_id=1, source_target_pairs={{0,2},{1,3},{2,6},{3,7},{4,0},{5,1},{6,4},{7,5},{8,10},{9,11},{10,... | collective-permute-start | bytes 4718600 | tf_op jit(solution)/shard_map/ppermute | solution.py:529
  13.2 0.6 copy-start.9
  13.2 0.6 copy-start.10
  13.3 0.6 copy-start.11
  18.0 55.9 %collective-permute-start.4 = (bf16[8,128,768]{2,1,0:T(8,128)(2,1)}, bf16[8,128,768]{2,1,0:T(8,128)(2,1)}, u32[]{:S(2)}, u32[]{:S(2)}) collective-permute-start(bf16[8,128,768]{2,1,0:T(8,128)(2,1)} %get-tuple-element.74), channel_id=1, source_target_pairs={{0,1},{1,0},{2,3},{3,2},{4,5},{5,4},{6,7},{7,6},{8,9},{9,8},{10,11... | collective-permute-start | bytes 4718600 | tf_op jit(solution)/shard_map/ppermute | solution.py:529
  40.2 1.1 copy-start.1
  41.3 33.5 %collective-permute-start.6 = (bf16[2,512,768]{2,1,0:T(8,128)(2,1)}, bf16[2,512,768]{2,1,0:T(8,128)(2,1)S(1)}, u32[]{:S(2)}, u32[]{:S(2)}) collective-permute-start(bf16[2,512,768]{2,1,0:T(8,128)(2,1)} %get-tuple-element.75.refs_4_.refs_2_), channel_id=1, source_target_pairs={{0,16},{1,17},{2,18},{3,19},{4,20},{5,21},{6,22},{7,23},{8,24},{9,... | collective-permute-start | bytes 4718600 | tf_op jit(solution)/shard_map/ppermute | solution.py:529
  42.5 48.4 %collective-permute-start.9 = (bf16[8,128,768]{2,1,0:T(8,128)(2,1)}, bf16[8,128,768]{2,1,0:T(8,128)(2,1)}, u32[]{:S(2)}, u32[]{:S(2)}) collective-permute-start(bf16[8,128,768]{2,1,0:T(8,128)(2,1)} %get-tuple-element.80), channel_id=1, source_target_pairs={{0,9},{1,8},{2,11},{3,10},{4,13},{5,12},{6,15},{7,14},{8,1},{9,0},... | collective-permute-start | bytes 4718600 | tf_op jit(solution)/shard_map/ppermute | solution.py:529
  46.6 61.0 %collective-permute-start.10 = (bf16[2,512,768]{2,1,0:T(8,128)(2,1)}, bf16[2,512,768]{2,1,0:T(8,128)(2,1)}, u32[]{:S(2)}, u32[]{:S(2)}) collective-permute-start(bf16[2,512,768]{2,1,0:T(8,128)(2,1)} %get-tuple-element.75.refs_4_.refs_2_), channel_id=1, source_target_pairs={{0,2},{1,3},{2,6},{3,7},{4,0},{5,1},{6,4},{7,5},{8,10},{9,11},{10,... | collective-permute-start | bytes 4718600 | tf_op jit(solution)/shard_map/ppermute | solution.py:529
  74.8 1.1 copy-start.2
  76.0 32.7 %collective-permute-start.11 = (bf16[2,512,768]{2,1,0:T(8,128)(2,1)}, bf16[2,512,768]{2,1,0:T(8,128)(2,1)S(1)}, u32[]{:S(2)}, u32[]{:S(2)}) collective-permute-start(bf16[2,512,768]{2,1,0:T(8,128)(2,1)} %get-tuple-element.78.refs_6_.refs_4_), channel_id=1, source_target_pairs={{0,16},{1,17},{2,18},{3,19},{4,20},{5,21},{6,22},{7,23},{8,24},{9,... | collective-permute-start | bytes 4718600 | tf_op jit(solution)/shard_map/ppermute | solution.py:529
  77.2 70.9 %collective-permute-start.7 = (bf16[2,512,768]{2,1,0:T(8,128)(2,1)}, bf16[2,512,768]{2,1,0:T(8,128)(2,1)}, u32[]{:S(2)}, u32[]{:S(2)}) collective-permute-start(bf16[2,512,768]{2,1,0:T(8,128)(2,1)} %get-tuple-element.78.refs_6_.refs_4_), channel_id=1, source_target_pairs={{0,2},{1,3},{2,6},{3,7},{4,0},{5,1},{6,4},{7,5},{8,10},{9,11},{10,... | collective-permute-start | bytes 4718600 | tf_op jit(solution)/shard_map/ppermute | solution.py:529
  80.2 67.9 %collective-permute-start.8 = (bf16[8,128,768]{2,1,0:T(8,128)(2,1)}, bf16[8,128,768]{2,1,0:T(8,128)(2,1)}, u32[]{:S(2)}, u32[]{:S(2)}) collective-permute-start(bf16[8,128,768]{2,1,0:T(8,128)(2,1)} %get-tuple-element.79), channel_id=1, source_target_pairs={{0,1},{1,0},{2,3},{3,2},{4,5},{5,4},{6,7},{7,6},{8,9},{9,8},{10,11... | collective-permute-start | bytes 4718600 | tf_op jit(solution)/shard_map/ppermute | solution.py:529
  108.7 1.1 copy-start.3
  109.8 38.2 %collective-permute-start.12 = (bf16[2,512,768]{2,1,0:T(8,128)(2,1)}, bf16[2,512,768]{2,1,0:T(8,128)(2,1)}, u32[]{:S(2)}, u32[]{:S(2)}) collective-permute-start(bf16[2,512,768]{2,1,0:T(8,128)(2,1)} %get-tuple-element.83.refs_4_.refs_2_), channel_id=1, source_target_pairs={{0,16},{1,17},{2,18},{3,19},{4,20},{5,21},{6,22},{7,23},{8,24},{9,... | collective-permute-start | bytes 4718600 | tf_op jit(solution)/shard_map/ppermute | solution.py:529
  118.4 56.6 %collective-permute-start.13 = (bf16[2,512,768]{2,1,0:T(8,128)(2,1)}, bf16[2,512,768]{2,1,0:T(8,128)(2,1)}, u32[]{:S(2)}, u32[]{:S(2)}) collective-permute-start(bf16[2,512,768]{2,1,0:T(8,128)(2,1)} %get-tuple-element.83.refs_4_.refs_2_), channel_id=1, source_target_pairs={{0,2},{1,3},{2,6},{3,7},{4,0},{5,1},{6,4},{7,5},{8,10},{9,11},{10,... | collective-permute-start | bytes 4718600 | tf_op jit(solution)/shard_map/ppermute | solution.py:529
  121.4 53.6 %collective-permute-start.14 = (bf16[8,128,768]{2,1,0:T(8,128)(2,1)}, bf16[8,128,768]{2,1,0:T(8,128)(2,1)S(1)}, u32[]{:S(2)}, u32[]{:S(2)}) collective-permute-start(bf16[8,128,768]{2,1,0:T(8,128)(2,1)} %get-tuple-element.91), channel_id=1, source_target_pairs={{0,9},{1,8},{2,11},{3,10},{4,13},{5,12},{6,15},{7,14},{8,1},{9,0},... | collective-permute-start | bytes 4718600 | tf_op jit(solution)/shard_map/ppermute | solution.py:529
  148.1 37.5 %collective-permute-start.15 = (bf16[2,512,768]{2,1,0:T(8,128)(2,1)}, bf16[2,512,768]{2,1,0:T(8,128)(2,1)}, u32[]{:S(2)}, u32[]{:S(2)}) collective-permute-start(bf16[2,512,768]{2,1,0:T(8,128)(2,1)} %get-tuple-element.92.refs_6_.refs_4_), channel_id=1, source_target_pairs={{0,16},{1,17},{2,18},{3,19},{4,20},{5,21},{6,22},{7,23},{8,24},{9,... | collective-permute-start | bytes 4718600 | tf_op jit(solution)/shard_map/ppermute | solution.py:529
  148.2 37.4 %collective-permute-start.16 = (bf16[1040,512]{1,0:T(8,128)(2,1)}, bf16[1040,512]{1,0:T(8,128)(2,1)}, u32[]{:S(2)}, u32[]{:S(2)}) collective-permute-start(bf16[1040,512]{1,0:T(8,128)(2,1)} %get-tuple-element.93), channel_id=1, source_target_pairs={{0,1},{1,0},{2,3},{3,2},{4,5},{5,4},{6,7},{7,6},{8,9},{9,8},{10,11... | collective-permute-start | bytes 3194888 | tf_op jit(solution)/shard_map/ppermute | solution.py:529
  148.2 60.5 %collective-permute-start.18 = (bf16[2,512,768]{2,1,0:T(8,128)(2,1)}, bf16[2,512,768]{2,1,0:T(8,128)(2,1)}, u32[]{:S(2)}, u32[]{:S(2)}) collective-permute-start(bf16[2,512,768]{2,1,0:T(8,128)(2,1)} %get-tuple-element.92.refs_6_.refs_4_), channel_id=1, source_target_pairs={{0,2},{1,3},{2,6},{3,7},{4,0},{5,1},{6,4},{7,5},{8,10},{9,11},{10,... | collective-permute-start | bytes 4718600 | tf_op jit(solution)/shard_map/ppermute | solution.py:529
  175.0 10.6 %copy-start = (bf16[8,128,768]{2,1,0:T(8,128)(2,1)}, bf16[8,128,768]{2,1,0:T(8,128)(2,1)S(1)}, u32[]{:S(2)}) copy-start(bf16[8,128,768]{2,1,0:T(8,128)(2,1)S(1)} %collective-permute-done.14.refs_1_) | copy-start | bytes 4718596
  185.6 28.5 %collective-permute-start.17 = (bf16[8,128,768]{2,1,0:T(8,128)(2,1)}, bf16[8,128,768]{2,1,0:T(8,128)(2,1)S(1)}, u32[]{:S(2)}, u32[]{:S(2)}) collective-permute-start(bf16[8,128,768]{2,1,0:T(8,128)(2,1)} %get-tuple-element.99), channel_id=1, source_target_pairs={{0,8},{1,9},{2,10},{3,11},{4,12},{5,13},{6,14},{7,15},{8,0},{9,1},... | collective-permute-start | bytes 4718600 | tf_op jit(solution)/shard_map/ppermute | solution.py:529
  186.1 31.1 %collective-permute-start.24 = (bf16[8,128,768]{2,1,0:T(8,128)(2,1)}, bf16[8,128,768]{2,1,0:T(8,128)(2,1)}, u32[]{:S(2)}, u32[]{:S(2)}) collective-permute-start(bf16[8,128,768]{2,1,0:T(8,128)(2,1)} %get-tuple-element.107), channel_id=1, source_target_pairs={{0,8},{1,9},{2,10},{3,11},{4,12},{5,13},{6,14},{7,15},{8,0},{9,1},... | collective-permute-start | bytes 4718600 | tf_op jit(solution)/shard_map/ppermute | solution.py:529
  186.1 43.0 %collective-permute-start.21 = (bf16[2,512,768]{2,1,0:T(8,128)(2,1)}, bf16[2,512,768]{2,1,0:T(8,128)(2,1)}, u32[]{:S(2)}, u32[]{:S(2)}) collective-permute-start(bf16[2,512,768]{2,1,0:T(8,128)(2,1)} %get-tuple-element.101.refs_5_), channel_id=1, source_target_pairs={{0,16},{1,17},{2,18},{3,19},{4,20},{5,21},{6,22},{7,23},{8,24},{9,... | collective-permute-start | bytes 4718600 | tf_op jit(solution)/shard_map/ppermute | solution.py:529
  186.4 42.7 %collective-permute-start.22 = (bf16[1040,512]{1,0:T(8,128)(2,1)}, bf16[1040,512]{1,0:T(8,128)(2,1)}, u32[]{:S(2)}, u32[]{:S(2)}) collective-permute-start(bf16[1040,512]{1,0:T(8,128)(2,1)} %get-tuple-element.102), channel_id=1, source_target_pairs={{0,9},{1,8},{2,11},{3,10},{4,13},{5,12},{6,15},{7,14},{8,1},{9,0},... | collective-permute-start | bytes 3194888 | tf_op jit(solution)/shard_map/ppermute | solution.py:529
  208.7 20.4 %collective-permute-start.23 = (bf16[528,512]{1,0:T(8,128)(2,1)}, bf16[528,512]{1,0:T(8,128)(2,1)}, u32[]{:S(2)}, u32[]{:S(2)}) collective-permute-start(bf16[528,512]{1,0:T(8,128)(2,1)} %get-tuple-element.105), channel_id=1, source_target_pairs={{0,1},{1,0},{2,3},{3,2},{4,5},{5,4},{6,7},{7,6},{8,9},{9,8},{10,11... | collective-permute-start | bytes 1622024 | tf_op jit(solution)/shard_map/ppermute | solution.py:529
  214.1 4.3 %copy-start.4 = (bf16[8,128,768]{2,1,0:T(8,128)(2,1)}, bf16[8,128,768]{2,1,0:T(8,128)(2,1)S(1)}, u32[]{:S(2)}) copy-start(bf16[8,128,768]{2,1,0:T(8,128)(2,1)S(1)} %collective-permute-done.17.refs_0_.refs_2_) | copy-start | bytes 4718596
  214.1 29.7 %collective-permute-start.20 = (bf16[1,512,768]{2,1,0:T(8,128)(2,1)}, bf16[1,512,768]{2,1,0:T(8,128)(2,1)}, u32[]{:S(2)}, u32[]{:S(2)}) collective-permute-start(bf16[1,512,768]{2,1,0:T(8,128)(2,1)} %slice.7), channel_id=1, source_target_pairs={{0,2},{1,3},{2,6},{3,7},{4,0},{5,1},{6,4},{7,5},{8,10},{9,11},{10,... | collective-permute-start | bytes 2359304 | tf_op jit(solution)/shard_map/ppermute | solution.py:529
  217.2 26.6 %collective-permute-start.19 = (bf16[1,512,768]{2,1,0:T(8,128)(2,1)}, bf16[1,512,768]{2,1,0:T(8,128)(2,1)}, u32[]{:S(2)}, u32[]{:S(2)}) collective-permute-start(bf16[1,512,768]{2,1,0:T(8,128)(2,1)} %slice.8), channel_id=1, source_target_pairs={{0,16},{1,17},{2,18},{3,19},{4,20},{5,21},{6,22},{7,23},{8,24},{9,... | collective-permute-start | bytes 2359304 | tf_op jit(solution)/shard_map/ppermute | solution.py:529
  229.1 13.9 %collective-permute-start.25 = (bf16[528,512]{1,0:T(8,128)(2,1)}, bf16[528,512]{1,0:T(8,128)(2,1)S(1)}, u32[]{:S(2)}, u32[]{:S(2)}) collective-permute-start(bf16[528,512]{1,0:T(8,128)(2,1)} %get-tuple-element.114), channel_id=1, source_target_pairs={{0,9},{1,8},{2,11},{3,10},{4,13},{5,12},{6,15},{7,14},{8,1},{9,0},... | collective-permute-start | bytes 1622024 | tf_op jit(solution)/shard_map/ppermute | solution.py:529
  229.2 27.8 %collective-permute-start.29 = (bf16[1040,512]{1,0:T(8,128)(2,1)}, bf16[1040,512]{1,0:T(8,128)(2,1)S(1)}, u32[]{:S(2)}, u32[]{:S(2)}) collective-permute-start(bf16[1040,512]{1,0:T(8,128)(2,1)} %get-tuple-element.123), channel_id=1, source_target_pairs={{0,8},{1,9},{2,10},{3,11},{4,12},{5,13},{6,14},{7,15},{8,0},{9,1},... | collective-permute-start | bytes 3194888 | tf_op jit(solution)/shard_map/ppermute | solution.py:529
  243.0 0.8 copy-start.5
  243.8 9.1 %copy-start.6 = (bf16[528,512]{1,0:T(8,128)(2,1)S(1)}, bf16[528,512]{1,0:T(8,128)(2,1)}, u32[]{:S(2)}) copy-start(bf16[528,512]{1,0:T(8,128)(2,1)} %get-tuple-element.124) | copy-start | bytes 1622020
  249.1 13.1 %collective-permute-start.26 = (bf16[544,512]{1,0:T(8,128)(2,1)}, bf16[544,512]{1,0:T(8,128)(2,1)}, u32[]{:S(2)}, u32[]{:S(2)}) collective-permute-start(bf16[544,512]{1,0:T(8,128)(2,1)} %get-tuple-element.117), channel_id=1, source_target_pairs={{0,8},{1,9},{2,10},{3,11},{4,12},{5,13},{6,14},{7,15},{8,0},{9,1},... | collective-permute-start | bytes 1671176 | tf_op jit(solution)/shard_map/ppermute | solution.py:529
  251.2 14.5 %collective-permute-start.27 = (bf16[544,512]{1,0:T(8,128)(2,1)}, bf16[544,512]{1,0:T(8,128)(2,1)}, u32[]{:S(2)}, u32[]{:S(2)}) collective-permute-start(bf16[544,512]{1,0:T(8,128)(2,1)} %get-tuple-element.118), channel_id=1, source_target_pairs={{0,1},{1,0},{2,3},{3,2},{4,5},{5,4},{6,7},{7,6},{8,9},{9,8},{10,11... | collective-permute-start | bytes 1671176 | tf_op jit(solution)/shard_map/ppermute | solution.py:529
  251.6 26.3 %collective-permute-start.28 = (bf16[544,512]{1,0:T(8,128)(2,1)}, bf16[544,512]{1,0:T(8,128)(2,1)}, u32[]{:S(2)}, u32[]{:S(2)}) collective-permute-start(bf16[544,512]{1,0:T(8,128)(2,1)} %get-tuple-element.119), channel_id=1, source_target_pairs={{0,9},{1,8},{2,11},{3,10},{4,13},{5,12},{6,15},{7,14},{8,1},{9,0},... | collective-permute-start | bytes 1671176 | tf_op jit(solution)/shard_map/ppermute | solution.py:529
  252.9 4.0 %collective-permute-start.30 = (bf16[528,512]{1,0:T(8,128)(2,1)S(1)}, bf16[528,512]{1,0:T(8,128)(2,1)}, u32[]{:S(2)}, u32[]{:S(2)}) collective-permute-start(bf16[528,512]{1,0:T(8,128)(2,1)S(1)} %copy-done.6), channel_id=1, source_target_pairs={{0,8},{1,9},{2,10},{3,11},{4,12},{5,13},{6,14},{7,15},{8,0},{9,1},... | collective-permute-start | bytes 1622024 | tf_op jit(solution)/shard_map/ppermute | solution.py:529
  256.9 1.0 copy-start.7

commit v4 on v3

--- a/solution.py
+++ b/solution.py
@@ -213,18 +213,18 @@
     pass
 
 
-def gate(passed):
+def gate(passed, others=()):
     n = len(passed)
     return pl.pallas_call(
         gate_kernel,
         out_shape=[jax.ShapeDtypeStruct(v.shape, v.dtype) for v in passed],
-        in_specs=[ANY] * n,
+        in_specs=[ANY] * n + [VMEM] * len(others),
         out_specs=[ANY] * n,
         input_output_aliases={i: i for i in range(n)},
         compiler_params=pltpu.CompilerParams(vmem_limit_bytes=VMEM_BYTES),
         cost_estimate=SHORT,
         name="gate",
-    )(*passed)
+    )(*passed, *others)
 
 
 def score_math(points, block_rows, meta):
@@ -319,7 +319,8 @@
 
             @pl.when((cls == hops) & right & (inside >= first) & (inside < first + count))
             def _():
-                pltpu.make_async_copy(ref.at[inside - first], cbuf.at[i], csem.at[i]).start()
+                rows = ref.at[inside - first, pl.ds(0, BLOCK)]
+                pltpu.make_async_copy(rows, cbuf.at[i], csem.at[i]).start()
 
     def begin(i, carry):
         start(i)
@@ -401,7 +402,9 @@
         functools.partial(
             score_kernel, nz, cap, blk_dev, group, order, runs, fetched, late, resident, len(before), len(extra)
         ),
-        out_shape=[jax.ShapeDtypeStruct((wide * TILE + (32 if late else 16), BLOCK), BF16)] * n,
+        out_shape=[
+            jax.ShapeDtypeStruct((wide * TILE + ((48 if d > 1 else 32) if late else 16), BLOCK), BF16) for d in order
+        ],
         in_specs=[SMEM, SMEM, SMEM, VMEM]
         + [ANY] * (len(runs) + 1)
         + [VMEM if resident else ANY] * len(parts)
@@ -426,10 +429,10 @@
     )(me, ids, inv, meta, *tiles, local, *parts, *before, *extra)
 
 
-def assemble_kernel(spans, n_before, n_earlier, inv, *refs):
+def assemble_kernel(spans, held_already, n_before, n_earlier, last, inv, *refs):
     n = len(spans)
     sources, before, refs = refs[:n], refs[n : n + n_before], refs[n + n_before + n_earlier :]
-    out, primary, picked, held, tail, in_sems, out_sems, tail_sems = refs
+    out, primary_out, picked_out, primary, picked, held, tail, in_sems, out_sems, tail_sems = refs
     if n_before:
         primary[...] = before[1][...]
         picked[...] = before[2][...]
@@ -442,7 +445,7 @@
 
                 @pl.when(t >= 0)
                 def _():
-                    act(d, k, t, at)
+                    act(d, pl.ds(k * TILE, TILE), t, at, k)
 
                 at += 1
 
@@ -451,47 +454,64 @@
             sources[d].at[pl.ds(spans[d][1] * TILE, tail.shape[1])], tail.at[d], tail_sems.at[d]
         )
 
-    def bring(d, k, t, n):
-        pltpu.make_async_copy(sources[d].at[pl.ds(k * TILE, TILE)], held.at[n], in_sems.at[n]).start()
-
-    def send(d, k, t, n):
-        pltpu.make_async_copy(sources[d].at[pl.ds(k * TILE, TILE)], held.at[n], in_sems.at[n]).wait()
-        pltpu.make_async_copy(held.at[n], out.at[t], out_sems.at[n]).start()
-
-    def finish(d, k, t, n):
-        pltpu.make_async_copy(held.at[n], out.at[t], out_sems.at[n]).wait()
+    def bring(d, rows, t, at, k):
+        if not held_already[d]:
+            pltpu.make_async_copy(sources[d].at[rows], held.at[at], in_sems.at[at]).start()
+
+    def send(d, rows, t, at, k):
+        if held_already[d]:
+            pltpu.make_async_copy(sources[d].at[rows], out.at[t], out_sems.at[at]).start()
+        else:
+            pltpu.make_async_copy(sources[d].at[rows], held.at[at], in_sems.at[at]).wait()
+            pltpu.make_async_copy(held.at[at], out.at[t], out_sems.at[at]).start()
+
+    def finish(d, rows, t, at, k):
+        pltpu.make_async_copy(held.at[at], out.at[t], out_sems.at[at]).wait()
 
     for d in range(n):
-        tail_copy(d).start()
+        if not held_already[d]:
+            tail_copy(d).start()
     each(bring)
+    each(send)
+    values = []
     for d in range(n):
-        tail_copy(d).wait()
-    each(send)
-    rows = []
-    for d in range(n):
-        both = tail[d].astype(F32)
-        rows.append(both if both.shape[0] == 16 else both[:16] + both[16:])
-
-    def write(d, k, t, n):
-        primary[pl.ds(t, 1), :] = rows[d][k : k + 1, :TILE]
-        picked[pl.ds(t, 1), :] = rows[d][k : k + 1, TILE : 2 * TILE]
+        if held_already[d]:
+            first = spans[d][1] * TILE
+            both = sources[d][pl.ds(first, min(32, sources[d].shape[0] - first))].astype(F32)
+        else:
+            tail_copy(d).wait()
+            both = tail[d].astype(F32)
+        values.append(both if both.shape[0] == 16 else both[:16] + both[16:])
+
+    def write(d, rows, t, at, k):
+        primary[pl.ds(t, 1), :] = values[d][k : k + 1, :TILE]
+        picked[pl.ds(t, 1), :] = values[d][k : k + 1, TILE : 2 * TILE]
 
     each(write)
+    primary_out[...] = primary[...].astype(primary_out.dtype)
+    picked_out[...] = picked[...].astype(picked_out.dtype)
     each(finish)
 
 
-def assemble(tile_dev, spans, inv, sources, before, earlier):
+def assemble(tile_dev, spans, inv, sources, before, earlier, last):
     n = len(sources)
     count = sum(wide for _, wide in spans)
+    tail_rows = 32 if last else 16
+    held_already = [last and i > 0 for i in range(n)]
     return pl.pallas_call(
-        functools.partial(assemble_kernel, spans, len(before), len(earlier)),
+        functools.partial(assemble_kernel, spans, held_already, len(before), len(earlier), last),
         out_shape=[jax.ShapeDtypeStruct((tile_dev, TILE, BLOCK), BF16)]
-        + [jax.ShapeDtypeStruct((tile_dev, TILE), F32)] * 2,
-        in_specs=[SMEM] + [ANY] * n + [ANY, VMEM, VMEM][: len(before)] + [ANY] * len(earlier),
+        + [jax.ShapeDtypeStruct((tile_dev, TILE), BF16 if last else F32)] * 2,
+        in_specs=[SMEM]
+        + [VMEM if held else ANY for held in held_already]
+        + [ANY, VMEM, VMEM][: len(before)]
+        + [ANY] * len(earlier),
         out_specs=[ANY, VMEM, VMEM],
         scratch_shapes=[
+            pltpu.VMEM((tile_dev, TILE), F32),
+            pltpu.VMEM((tile_dev, TILE), F32),
             pltpu.VMEM((count, TILE, BLOCK), BF16),
-            pltpu.VMEM((n, sources[0].shape[0] - spans[0][1] * TILE, BLOCK), BF16),
+            pltpu.VMEM((n, tail_rows, BLOCK), BF16),
             pltpu.SemaphoreType.DMA((count,)),
             pltpu.SemaphoreType.DMA((count,)),
             pltpu.SemaphoreType.DMA((n,)),
@@ -501,6 +521,29 @@
         cost_estimate=SHORT,
         name="assemble",
     )(inv, *sources, *before, *earlier)
+
+
+def cut_kernel(first, source, target, held, sem):
+    rows = pl.ds(0, BLOCK)
+    copy = pltpu.make_async_copy(source.at[pl.ds(first, target.shape[0]), rows], held, sem)
+    copy.start()
+    copy.wait()
+    copy = pltpu.make_async_copy(held, target.at[pl.ds(0, target.shape[0]), rows], sem)
+    copy.start()
+    copy.wait()
+
+
+def cut(source, first, count, rows=BLOCK):
+    return pl.pallas_call(
+        functools.partial(cut_kernel, first),
+        out_shape=jax.ShapeDtypeStruct((count, rows, D), BF16),
+        in_specs=[ANY],
+        out_specs=ANY,
+        scratch_shapes=[pltpu.VMEM((count, BLOCK, D), BF16), pltpu.SemaphoreType.DMA],
+        compiler_params=pltpu.CompilerParams(vmem_limit_bytes=VMEM_BYTES),
+        cost_estimate=SHORT,
+        name="cut",
+    )(source)
 
 
 def local_part(pieces, vectors, tile_region, tile_block, primary_pick, spill_pick, centers):
@@ -576,9 +619,8 @@
     for k in range(1, steps + 1):
         hops, first = (k - 1) // pieces + 1, (k - 1) % pieces * sub_blocks
         if split and k == steps:
-            start(k - 2, ("z", k), ("z", k - pieces), next_z, None)
+            start(k - 2, ("z", k), "wide", next_z, None)
             start(k - 1, ("z", last), ("cut", 0), next_z, None)
-            start(k - 1, ("x", k), ("cut", 1), other_part, None)
             fetched[hops, True, first, sub_blocks] = ("z", k)
             fetched[hops, False, first, split] = ("x", k)
             fetched[hops, False, first + split, sub_blocks - split] = ("z", last)
@@ -600,8 +642,9 @@
     for i, run in enumerate(runs):
         if run[0] == 1:
             env["sent", i] = sent[i]
-            opens.setdefault(min(5, last - 1), []).append(("sent", i))
-            start(min(5, last - 1), ("t", i), ("sent", i), across(1), None)
+            at = last if run[1] else min(5, last - 1)
+            opens.setdefault(at, []).append(("sent", i))
+            start(at, ("t", i), ("sent", i), across(1), None)
     env["t", len(runs)] = tile_rows
     runs += ((0, 0, slots),)
 
@@ -610,7 +653,7 @@
         keys = tuple(
             key
             for key in fetched
-            if key[0] in group and (fetched[key] in (("x", steps), ("z", last))) == resident and fetched[key] in env
+            if key[0] in group and (late is None or (fetched[key] in (("x", steps), ("z", last))) == resident)
         )
         low, high = group[0] * cap, (group[-1] + 1) * cap
         used = [
@@ -626,7 +669,7 @@
         for d, values in zip(order, scores):
             env["s", d, group] = values
 
-    def place(sources, before, earlier=()):
+    def place(sources, before, earlier=(), last_call=False):
         return assemble(
             tile_dev,
             [(d * slots + group[0] * cap, len(group) * cap) for d, group in sources],
@@ -634,6 +677,7 @@
             [env["r" if d else "s", d, group] for d, group in sources],
             before,
             earlier,
+            last_call,
         )
 
     one, two, three = (tuple(range(a, b)) for a, b in ((0, nz // 2), (nz // 2, 3 * nz // 4), (3 * nz // 4, nz)))
@@ -642,7 +686,6 @@
         (3, (2, 3, 0), one, {2: (4, 5), 3: (5, 6)}),
         (5, (2, 3, 0), two, {2: (0, 6), 3: (6, 7)}),
         (5, (1,), one, {}),
-        (5, (1,), two, {}),
     ):
         ready = max(ready, group[-1] * pieces + 1)
         plans.setdefault(ready, []).append((group, order))
@@ -653,7 +696,7 @@
                 start(at, ("r", d, group), ("s", d, group), across(d), min(last, max(done, at + 1)))
             else:
                 at_once.setdefault(ready, []).append((d, group, min(last, max(done, ready + 1))))
-    opens.setdefault(last - 1, []).extend([("s", 1, one), ("s", 1, two)])
+    opens.setdefault(last - 1, []).append(("s", 1, one))
     first_late = (pieces - 1) * sub_blocks
     env["token"] = jnp.zeros((8, TILE), F32)
     for k in range(last + 1):
@@ -663,34 +706,41 @@
             if k + 2 <= steps and k + 2 - pieces < k:
                 passed.append(source)
             passed.append("token")
-            for name, value in zip(passed, gate([env[n] for n in passed])):
+            others = [env["x", steps], env["z", last]] if split and k == last else []
+            for name, value in zip(passed, gate([env[n] for n in passed], others)):
                 env[name] = value
+        if split and k == steps - 2:
+            env["wide"] = cut(env["z", k], 0, sub_blocks, rows=BLOCK + 16)
         if split and k == steps - 1:
-            env["cut", 0] = env["x", steps - pieces][split:]
-            env["cut", 1] = env["z", steps][:split]
+            env["cut", 0] = cut(env["x", steps - pieces], split, sub_blocks - split)
         for name, payload, target, done in starts.get(k, []):
             env[name] = permute(env[payload], target)
             if done is not None:
                 waits.setdefault(done, []).append(name)
         for group, order in plans.get(k, []):
             score(group, order, extra=[env["token"]])
+        if split and k == steps - 1:
+            env["x", steps] = permute(cut(env["z", steps], 0, split), other_part)
         for d, group, done in at_once.get(k, []):
             env["r", d, group] = exchange(env["s", d, group], d)
             waits.setdefault(done, []).append(("r", d, group))
         if k == last - 1:
-            score(three, (2, 3, 1, 0), (first_late, False), extra=[env["token"]])
-    score(three, (2, 3, 1, 0), (first_late, True), True, [env["token"]])
-    for d in (2, 3, 1):
+            score(three, (2, 3, 0), (first_late, False), extra=[env["token"]])
+    score(three, (2, 3), (first_late, True), True, [env["token"]])
+    for d in (2, 3):
         env["r", d, three] = exchange(env["s", d, three], d)
-    for group in (one, two):
+    score(three, (0,), (first_late, True), True, [env["s", 2, three]])
+    for group in (two, three):
+        score(group, (1,), extra=[env["s", 2, three]])
+    for group in (one, two, three):
         env["r", 1, group] = exchange(env["s", 1, group], 1)
-    outputs = place([(2, one), (3, one), (0, one)], [], [env["s", 0, three]])
-    outputs = place([(2, two), (3, two), (0, two), (1, one), (1, two)], outputs, [env["s", 0, three]])
-    spill_scores, primary, picked = place([(d, three) for d in (0, 1, 2, 3)], outputs)
+    outputs = place([(0, one), (2, one), (3, one)], [], [env["s", 0, three]])
+    outputs = place([(0, two), (2, two), (3, two), (1, one), (1, two)], outputs, [env["s", 0, three]])
+    spill_scores, primary, picked = place([(d, three) for d in (0, 1, 2, 3)], outputs, last_call=True)
     return (
         spill_scores.reshape(tile_dev * TILE, BLOCK),
-        primary.astype(BF16).reshape(tile_dev * TILE),
-        picked.astype(BF16).reshape(tile_dev * TILE),
+        primary.reshape(tile_dev * TILE),
+        picked.reshape(tile_dev * TILE),
     )
 
 

time: 288 us -> 285 us (0.990); the launches traced: 283 us -> 284 us
  waiting for transfers between devices: 140 us -> 129 us
  Pallas kernels: 83.1 us -> 93.4 us
  starting transfers between devices: 43.6 us -> 47.8 us
    ppermute x31, waiting for transfers between devices: 140 us -> 129 us  [permute(): lax.ppermute(value, AXES, [(device(*a), device(*target(*a))) for a in eve...]
    pallas_call x3 -> x6, Pallas kernels: 12.2 us -> 18.7 us  [the longest x3 12.1 us: assemble(): pl.pallas_call(functools.partial(assemble_kernel, spans, held_already, le...]
    ppermute x31, starting transfers between devices: 43.6 us -> 47.8 us  [permute(): lax.ppermute(value, AXES, [(device(*a), device(*target(*a))) for a in eve...]
    slice x2 -> x0, local copies, waits for them, and re-layouts: 4.16 us -> none  [the longest x1 2.09 us: local_part(): env['cut', 0] = env['x', steps - pieces][split:]]
    unnamed x32 -> x34, local copies, waits for them, and re-layouts: 5.27 us -> 8.21 us
    pallas_call x6 -> x8, Pallas kernels: 56.5 us -> 57.5 us  [score_call(): pl.pallas_call(functools.partial(score_kernel, nz, cap, blk_dev, group, o...]
  transfers between devices with their start and end apart: 31 -> 31, of which waited for: 11 -> 15; matrix products, arithmetic and copies ran while one was open for 2% -> 0% of each run, Pallas kernels for 28% -> 31%
where the time goes in v4:
time: 285 us; the launch traced here: 284 us
  waiting for transfers between devices  129 us (45%)
  Pallas kernels  93.4 us (33%)
  starting transfers between devices  47.8 us (17%)
  local copies, waits for them, and re-layouts  12.6 us (4%)
    ppermute x31, waiting for transfers between devices, permute(): lax.ppermute(value, AXES, [(device(*a), device(*target(*a))) for a in eve...  129 us
    pallas_call x8, Pallas kernels, score_call(): pl.pallas_call(functools.partial(score_kernel, nz, cap, blk_dev, group, o...  57.5 us
    ppermute x31, starting transfers between devices, permute(): lax.ppermute(value, AXES, [(device(*a), device(*target(*a))) for a in eve...  47.8 us
    pallas_call x3, Pallas kernels, assemble(): pl.pallas_call(functools.partial(assemble_kernel, spans, held_already, le...  12.1 us
    unnamed x34, local copies, waits for them, and re-layouts  8.21 us
    pallas_call x1, Pallas kernels, receive(): pl.pallas_call(functools.partial(receive_kernel, nz, cap, blk_dev, tile_d...  7.33 us
    pallas_call x3, Pallas kernels, cut(): pl.pallas_call(functools.partial(cut_kernel, first), out_shape=jax.ShapeD...  6.59 us
  transfers between devices with their start and end apart: 31, of which 15 were waited for; matrix products, arithmetic and copies ran while one was open for 0% of the time, Pallas kernels for 31%

profile of v4, /device:TPU:9, one launch (start us, length us, event | category | flops | bytes accessed | tf_op | source)
XLA Modules:
  0.0 284.4 jit_solution(17455705506444008262)
XLA Ops:
  0.7 3.8 %constant_dynamic-slice_fusion = (bf16[2,512,768]{2,1,0:T(8,128)(2,1)}, bf16[2,512,768]{2,1,0:T(8,128)(2,1)}) fusion(bf16[8,512,768]{2,1,0:T(8,128)(2,1)} %bitcast.13, s32[]{:T(128)S(6)} %select_n.26, s32[]{:T(128)S(6)} %select_n.25), kind=kLoop, calls=%fused_computation.3 | loop fusion | bytes 6291464 | tf_op jit(solution)/shard_map/dynamic_slice | solution.py:583
  4.5 2.3 collective-permute-start.5
  6.8 2.1 collective-permute-start.2
  10.3 2.8 plan.1
  13.8 5.6 %dispatch.1 = (bf16[8,128,768]{2,1,0:T(8,128)(2,1)}, bf16[8,128,768]{2,1,0:T(8,128)(2,1)}, bf16[8,128,768]{2,1,0:T(8,128)(2,1)}, bf16[8,128,768]{2,1,0:T(8,128)(...) custom-call(s32[32]{0:T(128)} %get-tuple-element.69.at_slot, bf16[32,128,768]{2,1,0:T(8,128)(2,1)} %bitcast.22, ...), custom_call_target="tpu_custom_call" | custom-call | flops 1 | bytes 1 | tf_op jit(solution)/shard_map/dispatch/pallas_call | solution.py:196
  20.5 19.6 %collective-permute-done.5.refs_0_ = bf16[2,512,768]{2,1,0:T(8,128)(2,1)S(1)} collective-permute-done((bf16[2,512,768]{2,1,0:T(8,128)(2,1)}, bf16[2,512,768]{2,1,0:T(8,128)(2,1)S(1)}, u32[]{:S(2)}, u32[]{:S(2)}) %collective-permute-start.5) | collective-permute-done | bytes 1572896 | tf_op jit(solution)/shard_map/ppermute | solution.py:572
  41.3 1.2 collective-permute-start.6
  42.5 4.1 %collective-permute-start.9 = (bf16[8,128,768]{2,1,0:T(8,128)(2,1)}, bf16[8,128,768]{2,1,0:T(8,128)(2,1)}, u32[]{:S(2)}, u32[]{:S(2)}) collective-permute-start(bf16[8,128,768]{2,1,0:T(8,128)(2,1)} %get-tuple-element.76), channel_id=1, source_target_pairs={{0,9},{1,8},{2,11},{3,10},{4,13},{5,12},{6,15},{7,14},{8,1},{9,0},... | collective-permute-start | bytes 4718600 | tf_op jit(solution)/shard_map/ppermute | solution.py:572
  46.6 3.0 %collective-permute-start.10 = (bf16[2,512,768]{2,1,0:T(8,128)(2,1)}, bf16[2,512,768]{2,1,0:T(8,128)(2,1)}, u32[]{:S(2)}, u32[]{:S(2)}) collective-permute-start(bf16[2,512,768]{2,1,0:T(8,128)(2,1)} %get-tuple-element.71.refs_4_.refs_2_), channel_id=1, source_target_pairs={{0,2},{1,3},{2,6},{3,7},{4,0},{5,1},{6,4},{7,5},{8,10},{9,11},{10,... | collective-permute-start | bytes 4718600 | tf_op jit(solution)/shard_map/ppermute | solution.py:572
  49.6 24.2 %collective-permute-done.3.refs_0_ = bf16[2,512,768]{2,1,0:T(8,128)(2,1)} collective-permute-done((bf16[2,512,768]{2,1,0:T(8,128)(2,1)}, bf16[2,512,768]{2,1,0:T(8,128)(2,1)}, u32[]{:S(2)}, u32[]{:S(2)}) %collective-permute-start.3) | collective-permute-done | bytes 1572896 | tf_op jit(solution)/shard_map/ppermute | solution.py:572
  74.8 1.2 copy-done.4
  76.0 1.2 collective-permute-start.11
  77.2 3.0 %collective-permute-start.7 = (bf16[2,512,768]{2,1,0:T(8,128)(2,1)}, bf16[2,512,768]{2,1,0:T(8,128)(2,1)}, u32[]{:S(2)}, u32[]{:S(2)}) collective-permute-start(bf16[2,512,768]{2,1,0:T(8,128)(2,1)} %get-tuple-element.74.refs_6_.refs_4_), channel_id=1, source_target_pairs={{0,2},{1,3},{2,6},{3,7},{4,0},{5,1},{6,4},{7,5},{8,10},{9,11},{10,... | collective-permute-start | bytes 4718600 | tf_op jit(solution)/shard_map/ppermute | solution.py:572
  80.2 1.2 collective-permute-start.8
  81.4 9.5 %collective-permute-done.9.refs_0_ = bf16[8,128,768]{2,1,0:T(8,128)(2,1)} collective-permute-done((bf16[8,128,768]{2,1,0:T(8,128)(2,1)}, bf16[8,128,768]{2,1,0:T(8,128)(2,1)}, u32[]{:S(2)}, u32[]{:S(2)}) %collective-permute-start.9) | collective-permute-done | bytes 1572896 | tf_op jit(solution)/shard_map/ppermute | solution.py:572
  90.9 16.6 %collective-permute-done.10.refs_1_ = bf16[2,512,768]{2,1,0:T(8,128)(2,1)} collective-permute-done((bf16[2,512,768]{2,1,0:T(8,128)(2,1)}, bf16[2,512,768]{2,1,0:T(8,128)(2,1)}, u32[]{:S(2)}, u32[]{:S(2)}) %collective-permute-start.10) | collective-permute-done | bytes 1572896 | tf_op jit(solution)/shard_map/ppermute | solution.py:572
  108.7 1.2 collective-permute-start.12
  109.9 7.3 %receive.1 = (s32[64,8,128]{2,1,0:T(8,128)}, s32[64]{0:T(128)}) custom-call(s32[4]{0:T(128)} %pad_add_fusion.2.me, s32[72,128]{1,0:T(8,128)} %copy-done.9, s32[72,128]{1,0:T(8,128)} %copy-done.12, s32[72,128]{1,0:T(8,128)} %copy-done.11, s32[72,128]{1,0:T(8,128)} %copy-done.10), custom_call_target="tpu_custom_call" | custom-call | flops 1 | bytes 1 | tf_op jit(solution)/shard_map/receive/pallas_call | solution.py:136
  117.2 3.1 %collective-permute-start.15 = (bf16[2,512,768]{2,1,0:T(8,128)(2,1)}, bf16[2,512,768]{2,1,0:T(8,128)(2,1)}, u32[]{:S(2)}, u32[]{:S(2)}) collective-permute-start(bf16[2,512,768]{2,1,0:T(8,128)(2,1)} %get-tuple-element.79.refs_4_.refs_2_), channel_id=1, source_target_pairs={{0,2},{1,3},{2,6},{3,7},{4,0},{5,1},{6,4},{7,5},{8,10},{9,11},{10,... | collective-permute-start | bytes 4718600 | tf_op jit(solution)/shard_map/ppermute | solution.py:572
  120.3 7.0 %collective-permute-start.16 = (bf16[8,128,768]{2,1,0:T(8,128)(2,1)}, bf16[8,128,768]{2,1,0:T(8,128)(2,1)}, u32[]{:S(2)}, u32[]{:S(2)}) collective-permute-start(bf16[8,128,768]{2,1,0:T(8,128)(2,1)} %get-tuple-element.87), channel_id=1, source_target_pairs={{0,9},{1,8},{2,11},{3,10},{4,13},{5,12},{6,15},{7,14},{8,1},{9,0},... | collective-permute-start | bytes 4718600 | tf_op jit(solution)/shard_map/ppermute | solution.py:572
  127.3 6.7 %score.8 = (bf16[1040,512]{1,0:T(8,128)(2,1)}, bf16[1040,512]{1,0:T(8,128)(2,1)}, bf16[1040,512]{1,0:T(8,128)(2,1)}) custom-call(s32[4]{0:T(128)} %pad_add_fusion.2.me, s32[64]{0:T(128)} %get-tuple-element.67.ids, s32[64]{0:T(128)} %get-tuple-element.66.inv, s32[64,8,128]{2,1,0:T(8,128)} %get-tuple-element.68.meta, ...), custom_call_target="tpu_custom_call" | custom-call | flops 1 | bytes 1 | tf_op jit(solution)/shard_map/score/pallas_call | solution.py:401
  134.0 7.2 %collective-permute-done.7.refs_0_ = bf16[2,512,768]{2,1,0:T(8,128)(2,1)} collective-permute-done((bf16[2,512,768]{2,1,0:T(8,128)(2,1)}, bf16[2,512,768]{2,1,0:T(8,128)(2,1)}, u32[]{:S(2)}, u32[]{:S(2)}) %collective-permute-start.7) | collective-permute-done | bytes 1572896 | tf_op jit(solution)/shard_map/ppermute | solution.py:572
  141.5 2.6 collective-permute-start.17
  144.2 2.9 %collective-permute-start.18 = (bf16[1040,512]{1,0:T(8,128)(2,1)}, bf16[1040,512]{1,0:T(8,128)(2,1)}, u32[]{:S(2)}, u32[]{:S(2)}) collective-permute-start(bf16[1040,512]{1,0:T(8,128)(2,1)} %get-tuple-element.88), channel_id=1, source_target_pairs={{0,1},{1,0},{2,3},{3,2},{4,5},{5,4},{6,7},{7,6},{8,9},{9,8},{10,11... | collective-permute-start | bytes 3194888 | tf_op jit(solution)/shard_map/ppermute | solution.py:572
  147.1 2.6 cut.3
  149.7 13.1 %collective-permute-done.16.refs_1_ = bf16[8,128,768]{2,1,0:T(8,128)(2,1)} collective-permute-done((bf16[8,128,768]{2,1,0:T(8,128)(2,1)}, bf16[8,128,768]{2,1,0:T(8,128)(2,1)}, u32[]{:S(2)}, u32[]{:S(2)}) %collective-permute-start.16) | collective-permute-done | bytes 1572896 | tf_op jit(solution)/shard_map/ppermute | solution.py:572
  162.8 12.1 %collective-permute-done.15.refs_0_ = bf16[2,512,768]{2,1,0:T(8,128)(2,1)} collective-permute-done((bf16[2,512,768]{2,1,0:T(8,128)(2,1)}, bf16[2,512,768]{2,1,0:T(8,128)(2,1)}, u32[]{:S(2)}, u32[]{:S(2)}) %collective-permute-start.15) | collective-permute-done | bytes 1572896 | tf_op jit(solution)/shard_map/ppermute | solution.py:572
  175.0 10.5 %collective-permute-done.18.refs_3_ = bf16[1040,512]{1,0:T(8,128)(2,1)} collective-permute-done((bf16[1040,512]{1,0:T(8,128)(2,1)}, bf16[1040,512]{1,0:T(8,128)(2,1)}, u32[]{:S(2)}, u32[]{:S(2)}) %collective-permute-start.18) | collective-permute-done | bytes 1064992 | tf_op jit(solution)/shard_map/ppermute | solution.py:572
  188.0 12.4 %score.9 = (bf16[528,512]{1,0:T(8,128)(2,1)}, bf16[528,512]{1,0:T(8,128)(2,1)}, bf16[528,512]{1,0:T(8,128)(2,1)}) custom-call(s32[4]{0:T(128)} %pad_add_fusion.2.me, s32[64]{0:T(128)} %get-tuple-element.67.ids, s32[64]{0:T(128)} %get-tuple-element.66.inv, s32[64,8,128]{2,1,0:T(8,128)} %get-tuple-element.68.meta, ...), custom_call_target="tpu_custom_call" | custom-call | flops 1 | bytes 1 | tf_op jit(solution)/shard_map/score/pallas_call | solution.py:401
  200.5 2.0 cut.5
  202.5 7.2 %collective-permute-done.13.source.refs_6_.refs_4_ = bf16[2,528,768]{2,1,0:T(8,128)(2,1)} collective-permute-done((bf16[2,528,768]{2,1,0:T(8,128)(2,1)}, bf16[2,528,768]{2,1,0:T(8,128)(2,1)}, u32[]{:S(2)}, u32[]{:S(2)}) %collective-permute-start.13) | collective-permute-done | bytes 1622048 | tf_op jit(solution)/shard_map/ppermute | solution.py:572
  209.7 3.1 %collective-permute-start.19 = (bf16[1,512,768]{2,1,0:T(8,128)(2,1)}, bf16[1,512,768]{2,1,0:T(8,128)(2,1)}, u32[]{:S(2)}, u32[]{:S(2)}) collective-permute-start(bf16[1,512,768]{2,1,0:T(8,128)(2,1)} %cut.5), channel_id=1, source_target_pairs={{0,2},{1,3},{2,6},{3,7},{4,0},{5,1},{6,4},{7,5},{8,10},{9,11},{10,... | collective-permute-start | bytes 2359304 | tf_op jit(solution)/shard_map/ppermute | solution.py:572
  212.8 2.0 cut.4
  214.9 1.3 collective-permute-start.14
  216.2 6.2 %score.10.refs_4_ = bf16[1040,512]{1,0:T(8,128)(2,1)} custom-call(s32[4]{0:T(128)} %pad_add_fusion.2.me, s32[64]{0:T(128)} %get-tuple-element.67.ids, s32[64]{0:T(128)} %get-tuple-element.66.inv, s32[64,8,128]{2,1,0:T(8,128)} %get-tuple-element.68.meta, bf16[8,128,768]{2,1,0:T(8,128)(2,1)} %collective-permute-done.23.refs_0_, bf16[8,512,768]{2,1,0:T(8,128)(2,1)} %bitcast.16, ...), custom_call_target="tpu_custom_call" | custom-call | flops 1 | bytes 1 | tf_op jit(solution)/shard_map/score/pallas_call | solution.py:401
  222.3 2.5 collective-permute-done.22.refs_2_
  226.8 10.7 %score.11 = (bf16[560,512]{1,0:T(8,128)(2,1)}, bf16[560,512]{1,0:T(8,128)(2,1)}, bf16[544,512]{1,0:T(8,128)(2,1)}) custom-call(s32[4]{0:T(128)} %pad_add_fusion.2.me, s32[64]{0:T(128)} %get-tuple-element.67.ids, s32[64]{0:T(128)} %get-tuple-element.66.inv, s32[64,8,128]{2,1,0:T(8,128)} %get-tuple-element.68.meta, ...), custom_call_target="tpu_custom_call" | custom-call | flops 1 | bytes 1 | tf_op jit(solution)/shard_map/score/pallas_call | solution.py:401
  237.5 2.8 collective-permute-done.14.refs_3_.refs_2_.refs_5_
  241.8 1.4 gate.13
  243.7 4.9 %score.12 = (bf16[560,512]{1,0:T(8,128)(2,1)}, bf16[560,512]{1,0:T(8,128)(2,1)}) custom-call(s32[4]{0:T(128)} %pad_add_fusion.2.me, s32[64]{0:T(128)} %get-tuple-element.67.ids, s32[64]{0:T(128)} %get-tuple-element.66.inv, s32[64,8,128]{2,1,0:T(8,128)} %get-tuple-element.68.meta, ...), custom_call_target="tpu_custom_call", output_to_operand_aliasing={{0}: (9, {}), {1}: (10, {})} | custom-call | flops 1 | bytes 1 | tf_op jit(solution)/shard_map/score/pallas_call | solution.py:401
  248.6 1.7 collective-permute-start.28
  250.3 1.5 collective-permute-start.27
  253.0 6.1 %score.15 = bf16[528,512]{1,0:T(8,128)(2,1)} custom-call(s32[4]{0:T(128)} %pad_add_fusion.2.me, s32[64]{0:T(128)} %get-tuple-element.67.ids, s32[64]{0:T(128)} %get-tuple-element.66.inv, s32[64,8,128]{2,1,0:T(8,128)} %get-tuple-element.68.meta, bf16[8,128,768]{2,1,0:T(8,128)(2,1)} %copy-done.5, bf16[8,512,768]{2,1,0:T(8,128)(2,1)} %bitcast.19, ...), custom_call_target="tpu_custom_call" | custom-call | flops 1 | bytes 1 | tf_op jit(solution)/shard_map/score/pallas_call | solution.py:401
  259.1 6.1 %score.14 = bf16[528,512]{1,0:T(8,128)(2,1)} custom-call(s32[4]{0:T(128)} %pad_add_fusion.2.me, s32[64]{0:T(128)} %get-tuple-element.67.ids, s32[64]{0:T(128)} %get-tuple-element.66.inv, s32[64,8,128]{2,1,0:T(8,128)} %get-tuple-element.68.meta, bf16[8,128,768]{2,1,0:T(8,128)(2,1)} %copy-done.5, bf16[8,512,768]{2,1,0:T(8,128)(2,1)} %bitcast.20, ...), custom_call_target="tpu_custom_call" | custom-call | flops 1 | bytes 1 | tf_op jit(solution)/shard_map/score/pallas_call | solution.py:401
  265.8 4.6 %score.13.refs_3_.refs_8_.refs_0_ = bf16[544,512]{1,0:T(8,128)(2,1)} custom-call(s32[4]{0:T(128)} %pad_add_fusion.2.me, s32[64]{0:T(128)} %get-tuple-element.67.ids, s32[64]{0:T(128)} %get-tuple-element.66.inv, s32[64,8,128]{2,1,0:T(8,128)} %get-tuple-element.68.meta, bf16[32,128,768]{2,1,0:T(8,128)(2,1)} %bitcast.26, ...), custom_call_target="tpu_custom_call", output_to_operand_aliasing={{}: (8, {})} | custom-call | flops 1 | bytes 1 | tf_op jit(solution)/shard_map/score/pallas_call | solution.py:401
  270.4 3.7 %assemble.3 = (bf16[32,128,512]{2,1,0:T(8,128)(2,1)}, f32[32,128]{1,0:T(8,128)}, f32[32,128]{1,0:T(8,128)}) custom-call(s32[64]{0:T(128)} %get-tuple-element.66.inv, bf16[1040,512]{1,0:T(8,128)(2,1)} %get-tuple-element.117.refs_0_, bf16[1040,512]{1,0:T(8,128)(2,1)} %get-tuple-element.118.refs_1_, bf16[1040,512]{1,0:T(8,128)(2,1)} %get-tuple-element.119.refs_2_, ...), custom_call_target="tpu_custom_call" | custom-call | flops 1 | bytes 1 | tf_op jit(solution)/shard_map/assemble/pallas_call | solution.py:501
  274.9 3.9 %assemble.4 = (bf16[32,128,512]{2,1,0:T(8,128)(2,1)}, f32[32,128]{1,0:T(8,128)}, f32[32,128]{1,0:T(8,128)}) custom-call(s32[64]{0:T(128)} %get-tuple-element.66.inv, bf16[528,512]{1,0:T(8,128)(2,1)} %get-tuple-element.113.refs_0_, bf16[528,512]{1,0:T(8,128)(2,1)} %get-tuple-element.114.refs_1_, ...), custom_call_target="tpu_custom_call", output_to_operand_aliasing={{0}: (6, {})} | custom-call | flops 1 | bytes 1 | tf_op jit(solution)/shard_map/assemble/pallas_call | solution.py:501
  279.7 4.5 %assemble.5 = (bf16[32,128,512]{2,1,0:T(8,128)(2,1)}, bf16[32,128]{1,0:T(8,128)(2,1)}, bf16[32,128]{1,0:T(8,128)(2,1)}) custom-call(s32[64]{0:T(128)} %get-tuple-element.66.inv, bf16[544,512]{1,0:T(8,128)(2,1)} %score.13.refs_3_.refs_8_.refs_0_, bf16[528,512]{1,0:T(8,128)(2,1)} %copy-done.7, ...), custom_call_target="tpu_custom_call", output_to_operand_aliasing={{0}: (5, {})} | custom-call | flops 1 | bytes 1 | tf_op jit(solution)/shard_map/assemble/pallas_call | solution.py:501
  (77 shorter events, 16.5 us)
Async XLA Ops:
  0.6 6.1 %copy-start.15 = (s32[32]{0:T(128)S(1)}, s32[32]{0:T(128)}, u32[]{:S(2)}) copy-start(s32[32]{0:T(128)} %region.1) | copy-start | bytes 388
  0.6 6.1 %copy-start.16 = (s32[32]{0:T(128)S(1)}, s32[32]{0:T(128)}, u32[]{:S(2)}) copy-start(s32[32]{0:T(128)} %block.1) | copy-start | bytes 388
  0.7 6.1 %copy-start.13 = (s32[4096]{0:T(1024)S(1)}, s32[4096]{0:T(1024)}, u32[]{:S(2)}) copy-start(s32[4096]{0:T(1024)} %param.10) | copy-start | bytes 49156
  0.7 6.1 %copy-start.14 = (s32[4096]{0:T(1024)S(1)}, s32[4096]{0:T(1024)}, u32[]{:S(2)}) copy-start(s32[4096]{0:T(1024)} %param.9) | copy-start | bytes 49156
  4.5 35.7 %collective-permute-start.5 = (bf16[2,512,768]{2,1,0:T(8,128)(2,1)}, bf16[2,512,768]{2,1,0:T(8,128)(2,1)S(1)}, u32[]{:S(2)}, u32[]{:S(2)}) collective-permute-start(bf16[2,512,768]{2,1,0:T(8,128)(2,1)} %get-tuple-element.130.refs_0_), channel_id=1, source_target_pairs={{0,2},{1,3},{2,6},{3,7},{4,0},{5,1},{6,4},{7,5},{8,10},{9,11},{10,... | collective-permute-start | bytes 4718600 | tf_op jit(solution)/shard_map/ppermute | solution.py:572
  6.8 6.3 %copy-start.9 = (s32[72,128]{1,0:T(8,128)}, s32[72,128]{1,0:T(8,128)S(1)}, u32[]{:S(2)}) copy-start(s32[72,128]{1,0:T(8,128)S(1)} %pad_add_fusion.refs_0_) | copy-start | bytes 110596
  6.8 6.3 %collective-permute-start.2 = (s32[72,128]{1,0:T(8,128)S(1)}, s32[72,128]{1,0:T(8,128)S(1)}, u32[]{:S(2)}, u32[]{:S(2)}) collective-permute-start(s32[72,128]{1,0:T(8,128)S(1)} %pad_add_fusion.refs_0_), channel_id=1, source_target_pairs={{0,9},{1,8},{2,11},{3,10},{4,13},{5,12},{6,15},{7,14},{8,1},{9,0},... | collective-permute-start | bytes 110600 | tf_op jit(solution)/shard_map/ppermute | solution.py:572
  9.0 4.2 %collective-permute-start.1 = (s32[72,128]{1,0:T(8,128)S(1)}, s32[72,128]{1,0:T(8,128)S(1)}, u32[]{:S(2)}, u32[]{:S(2)}) collective-permute-start(s32[72,128]{1,0:T(8,128)S(1)} %pad_add_fusion.refs_0_), channel_id=1, source_target_pairs={{0,1},{1,0},{2,3},{3,2},{4,5},{5,4},{6,7},{7,6},{8,9},{9,8},{10,11... | collective-permute-start | bytes 110600 | tf_op jit(solution)/shard_map/ppermute | solution.py:572
  9.2 4.0 %collective-permute-start = (s32[72,128]{1,0:T(8,128)S(1)}, s32[72,128]{1,0:T(8,128)S(1)}, u32[]{:S(2)}, u32[]{:S(2)}) collective-permute-start(s32[72,128]{1,0:T(8,128)S(1)} %pad_add_fusion.refs_0_), channel_id=1, source_target_pairs={{0,8},{1,9},{2,10},{3,11},{4,12},{5,13},{6,14},{7,15},{8,0},{9,1},... | collective-permute-start | bytes 110600 | tf_op jit(solution)/shard_map/ppermute | solution.py:572
  10.1 63.8 %collective-permute-start.3 = (bf16[2,512,768]{2,1,0:T(8,128)(2,1)}, bf16[2,512,768]{2,1,0:T(8,128)(2,1)}, u32[]{:S(2)}, u32[]{:S(2)}) collective-permute-start(bf16[2,512,768]{2,1,0:T(8,128)(2,1)} %get-tuple-element.129.refs_1_), channel_id=1, source_target_pairs={{0,2},{1,3},{2,6},{3,7},{4,0},{5,1},{6,4},{7,5},{8,10},{9,11},{10,... | collective-permute-start | bytes 4718600 | tf_op jit(solution)/shard_map/ppermute | solution.py:572
  13.1 0.6 copy-start.10
  13.1 0.6 copy-start.11
  13.2 0.6 copy-start.12
  19.4 54.4 %collective-permute-start.4 = (bf16[8,128,768]{2,1,0:T(8,128)(2,1)}, bf16[8,128,768]{2,1,0:T(8,128)(2,1)}, u32[]{:S(2)}, u32[]{:S(2)}) collective-permute-start(bf16[8,128,768]{2,1,0:T(8,128)(2,1)} %get-tuple-element.70), channel_id=1, source_target_pairs={{0,1},{1,0},{2,3},{3,2},{4,5},{5,4},{6,7},{7,6},{8,9},{9,8},{10,11... | collective-permute-start | bytes 4718600 | tf_op jit(solution)/shard_map/ppermute | solution.py:572
  40.1 1.2 copy-start.3
  41.3 33.5 %collective-permute-start.6 = (bf16[2,512,768]{2,1,0:T(8,128)(2,1)}, bf16[2,512,768]{2,1,0:T(8,128)(2,1)S(1)}, u32[]{:S(2)}, u32[]{:S(2)}) collective-permute-start(bf16[2,512,768]{2,1,0:T(8,128)(2,1)} %get-tuple-element.71.refs_4_.refs_2_), channel_id=1, source_target_pairs={{0,16},{1,17},{2,18},{3,19},{4,20},{5,21},{6,22},{7,23},{8,24},{9,... | collective-permute-start | bytes 4718600 | tf_op jit(solution)/shard_map/ppermute | solution.py:572
  42.5 48.4 %collective-permute-start.9 = (bf16[8,128,768]{2,1,0:T(8,128)(2,1)}, bf16[8,128,768]{2,1,0:T(8,128)(2,1)}, u32[]{:S(2)}, u32[]{:S(2)}) collective-permute-start(bf16[8,128,768]{2,1,0:T(8,128)(2,1)} %get-tuple-element.76), channel_id=1, source_target_pairs={{0,9},{1,8},{2,11},{3,10},{4,13},{5,12},{6,15},{7,14},{8,1},{9,0},... | collective-permute-start | bytes 4718600 | tf_op jit(solution)/shard_map/ppermute | solution.py:572
  46.6 60.9 %collective-permute-start.10 = (bf16[2,512,768]{2,1,0:T(8,128)(2,1)}, bf16[2,512,768]{2,1,0:T(8,128)(2,1)}, u32[]{:S(2)}, u32[]{:S(2)}) collective-permute-start(bf16[2,512,768]{2,1,0:T(8,128)(2,1)} %get-tuple-element.71.refs_4_.refs_2_), channel_id=1, source_target_pairs={{0,2},{1,3},{2,6},{3,7},{4,0},{5,1},{6,4},{7,5},{8,10},{9,11},{10,... | collective-permute-start | bytes 4718600 | tf_op jit(solution)/shard_map/ppermute | solution.py:572
  74.8 1.2 copy-start.4
  76.0 32.7 %collective-permute-start.11 = (bf16[2,512,768]{2,1,0:T(8,128)(2,1)}, bf16[2,512,768]{2,1,0:T(8,128)(2,1)}, u32[]{:S(2)}, u32[]{:S(2)}) collective-permute-start(bf16[2,512,768]{2,1,0:T(8,128)(2,1)} %get-tuple-element.74.refs_6_.refs_4_), channel_id=1, source_target_pairs={{0,16},{1,17},{2,18},{3,19},{4,20},{5,21},{6,22},{7,23},{8,24},{9,... | collective-permute-start | bytes 4718600 | tf_op jit(solution)/shard_map/ppermute | solution.py:572
  77.2 64.1 %collective-permute-start.7 = (bf16[2,512,768]{2,1,0:T(8,128)(2,1)}, bf16[2,512,768]{2,1,0:T(8,128)(2,1)}, u32[]{:S(2)}, u32[]{:S(2)}) collective-permute-start(bf16[2,512,768]{2,1,0:T(8,128)(2,1)} %get-tuple-element.74.refs_6_.refs_4_), channel_id=1, source_target_pairs={{0,2},{1,3},{2,6},{3,7},{4,0},{5,1},{6,4},{7,5},{8,10},{9,11},{10,... | collective-permute-start | bytes 4718600 | tf_op jit(solution)/shard_map/ppermute | solution.py:572
  80.2 53.8 %collective-permute-start.8 = (bf16[8,128,768]{2,1,0:T(8,128)(2,1)}, bf16[8,128,768]{2,1,0:T(8,128)(2,1)S(1)}, u32[]{:S(2)}, u32[]{:S(2)}) collective-permute-start(bf16[8,128,768]{2,1,0:T(8,128)(2,1)} %get-tuple-element.75), channel_id=1, source_target_pairs={{0,1},{1,0},{2,3},{3,2},{4,5},{5,4},{6,7},{7,6},{8,9},{9,8},{10,11... | collective-permute-start | bytes 4718600 | tf_op jit(solution)/shard_map/ppermute | solution.py:572
  108.7 32.8 %collective-permute-start.12 = (bf16[2,512,768]{2,1,0:T(8,128)(2,1)}, bf16[2,512,768]{2,1,0:T(8,128)(2,1)}, u32[]{:S(2)}, u32[]{:S(2)}) collective-permute-start(bf16[2,512,768]{2,1,0:T(8,128)(2,1)} %get-tuple-element.79.refs_4_.refs_2_), channel_id=1, source_target_pairs={{0,16},{1,17},{2,18},{3,19},{4,20},{5,21},{6,22},{7,23},{8,24},{9,... | collective-permute-start | bytes 4718600 | tf_op jit(solution)/shard_map/ppermute | solution.py:572
  117.2 57.7 %collective-permute-start.15 = (bf16[2,512,768]{2,1,0:T(8,128)(2,1)}, bf16[2,512,768]{2,1,0:T(8,128)(2,1)}, u32[]{:S(2)}, u32[]{:S(2)}) collective-permute-start(bf16[2,512,768]{2,1,0:T(8,128)(2,1)} %get-tuple-element.79.refs_4_.refs_2_), channel_id=1, source_target_pairs={{0,2},{1,3},{2,6},{3,7},{4,0},{5,1},{6,4},{7,5},{8,10},{9,11},{10,... | collective-permute-start | bytes 4718600 | tf_op jit(solution)/shard_map/ppermute | solution.py:572
  120.3 42.5 %collective-permute-start.16 = (bf16[8,128,768]{2,1,0:T(8,128)(2,1)}, bf16[8,128,768]{2,1,0:T(8,128)(2,1)}, u32[]{:S(2)}, u32[]{:S(2)}) collective-permute-start(bf16[8,128,768]{2,1,0:T(8,128)(2,1)} %get-tuple-element.87), channel_id=1, source_target_pairs={{0,9},{1,8},{2,11},{3,10},{4,13},{5,12},{6,15},{7,14},{8,1},{9,0},... | collective-permute-start | bytes 4718600 | tf_op jit(solution)/shard_map/ppermute | solution.py:572
  134.0 7.5 %copy-start = (bf16[8,128,768]{2,1,0:T(8,128)(2,1)}, bf16[8,128,768]{2,1,0:T(8,128)(2,1)S(1)}, u32[]{:S(2)}) copy-start(bf16[8,128,768]{2,1,0:T(8,128)(2,1)S(1)} %collective-permute-done.8.refs_1_) | copy-start | bytes 4718596
  141.5 44.0 %collective-permute-start.17 = (bf16[2,512,768]{2,1,0:T(8,128)(2,1)}, bf16[2,512,768]{2,1,0:T(8,128)(2,1)S(1)}, u32[]{:S(2)}, u32[]{:S(2)}) collective-permute-start(bf16[2,512,768]{2,1,0:T(8,128)(2,1)} %get-tuple-element.86.source.refs_6_.refs_4_), channel_id=1, source_target_pairs={{0,16},{1,17},{2,18},{3,19},{4,20},{5,21},{6,22},{7,23},{8,24},{9,... | collective-permute-start | bytes 4718600 | tf_op jit(solution)/shard_map/ppermute | solution.py:572
  144.2 41.3 %collective-permute-start.18 = (bf16[1040,512]{1,0:T(8,128)(2,1)}, bf16[1040,512]{1,0:T(8,128)(2,1)}, u32[]{:S(2)}, u32[]{:S(2)}) collective-permute-start(bf16[1040,512]{1,0:T(8,128)(2,1)} %get-tuple-element.88), channel_id=1, source_target_pairs={{0,1},{1,0},{2,3},{3,2},{4,5},{5,4},{6,7},{7,6},{8,9},{9,8},{10,11... | collective-permute-start | bytes 3194888 | tf_op jit(solution)/shard_map/ppermute | solution.py:572
  149.7 60.1 %collective-permute-start.13 = (bf16[2,528,768]{2,1,0:T(8,128)(2,1)}, bf16[2,528,768]{2,1,0:T(8,128)(2,1)}, u32[]{:S(2)}, u32[]{:S(2)}) collective-permute-start(bf16[2,528,768]{2,1,0:T(8,128)(2,1)} %cut.3), channel_id=1, source_target_pairs={{0,2},{1,3},{2,6},{3,7},{4,0},{5,1},{6,4},{7,5},{8,10},{9,11},{10,... | collective-permute-start | bytes 4866056 | tf_op jit(solution)/shard_map/ppermute | solution.py:572
  185.5 1.2 copy-start.1
  186.7 28.2 %collective-permute-start.23 = (bf16[8,128,768]{2,1,0:T(8,128)(2,1)}, bf16[8,128,768]{2,1,0:T(8,128)(2,1)}, u32[]{:S(2)}, u32[]{:S(2)}) collective-permute-start(bf16[8,128,768]{2,1,0:T(8,128)(2,1)} %get-tuple-element.101), channel_id=1, source_target_pairs={{0,8},{1,9},{2,10},{3,11},{4,12},{5,13},{6,14},{7,15},{8,0},{9,1},... | collective-permute-start | bytes 4718600 | tf_op jit(solution)/shard_map/ppermute | solution.py:572
  187.1 37.7 %collective-permute-start.20 = (bf16[2,512,768]{2,1,0:T(8,128)(2,1)}, bf16[2,512,768]{2,1,0:T(8,128)(2,1)S(1)}, u32[]{:S(2)}, u32[]{:S(2)}) collective-permute-start(bf16[2,512,768]{2,1,0:T(8,128)(2,1)} %get-tuple-element.95.refs_4_.refs_2_), channel_id=1, source_target_pairs={{0,16},{1,17},{2,18},{3,19},{4,20},{5,21},{6,22},{7,23},{8,24},{9,... | collective-permute-start | bytes 4718600 | tf_op jit(solution)/shard_map/ppermute | solution.py:572
  187.4 37.4 %collective-permute-start.21 = (bf16[1040,512]{1,0:T(8,128)(2,1)}, bf16[1040,512]{1,0:T(8,128)(2,1)}, u32[]{:S(2)}, u32[]{:S(2)}) collective-permute-start(bf16[1040,512]{1,0:T(8,128)(2,1)} %get-tuple-element.96), channel_id=1, source_target_pairs={{0,9},{1,8},{2,11},{3,10},{4,13},{5,12},{6,15},{7,14},{8,1},{9,0},... | collective-permute-start | bytes 3194888 | tf_op jit(solution)/shard_map/ppermute | solution.py:572
  200.4 24.4 %collective-permute-start.22 = (bf16[528,512]{1,0:T(8,128)(2,1)}, bf16[528,512]{1,0:T(8,128)(2,1)}, u32[]{:S(2)}, u32[]{:S(2)}) collective-permute-start(bf16[528,512]{1,0:T(8,128)(2,1)} %get-tuple-element.99), channel_id=1, source_target_pairs={{0,1},{1,0},{2,3},{3,2},{4,5},{5,4},{6,7},{7,6},{8,9},{9,8},{10,11... | collective-permute-start | bytes 1622024 | tf_op jit(solution)/shard_map/ppermute | solution.py:572
  209.7 27.7 %collective-permute-start.19 = (bf16[1,512,768]{2,1,0:T(8,128)(2,1)}, bf16[1,512,768]{2,1,0:T(8,128)(2,1)}, u32[]{:S(2)}, u32[]{:S(2)}) collective-permute-start(bf16[1,512,768]{2,1,0:T(8,128)(2,1)} %cut.5), channel_id=1, source_target_pairs={{0,2},{1,3},{2,6},{3,7},{4,0},{5,1},{6,4},{7,5},{8,10},{9,11},{10,... | collective-permute-start | bytes 2359304 | tf_op jit(solution)/shard_map/ppermute | solution.py:572
  214.9 25.4 %collective-permute-start.14 = (bf16[1,512,768]{2,1,0:T(8,128)(2,1)}, bf16[1,512,768]{2,1,0:T(8,128)(2,1)}, u32[]{:S(2)}, u32[]{:S(2)}) collective-permute-start(bf16[1,512,768]{2,1,0:T(8,128)(2,1)} %cut.4), channel_id=1, source_target_pairs={{0,16},{1,17},{2,18},{3,19},{4,20},{5,21},{6,22},{7,23},{8,24},{9,... | collective-permute-start | bytes 2359304 | tf_op jit(solution)/shard_map/ppermute | solution.py:572
  224.8 1.1 copy-start.2
  226.0 15.0 %collective-permute-start.24 = (bf16[528,512]{1,0:T(8,128)(2,1)}, bf16[528,512]{1,0:T(8,128)(2,1)S(1)}, u32[]{:S(2)}, u32[]{:S(2)}) collective-permute-start(bf16[528,512]{1,0:T(8,128)(2,1)} %get-tuple-element.107), channel_id=1, source_target_pairs={{0,9},{1,8},{2,11},{3,10},{4,13},{5,12},{6,15},{7,14},{8,1},{9,0},... | collective-permute-start | bytes 1622024 | tf_op jit(solution)/shard_map/ppermute | solution.py:572
  241.0 0.8 copy-start.6
  243.2 8.6 %collective-permute-start.25 = (bf16[8,128,768]{2,1,0:T(8,128)(2,1)}, bf16[8,128,768]{2,1,0:T(8,128)(2,1)S(1)}, u32[]{:S(2)}, u32[]{:S(2)}) collective-permute-start(bf16[8,128,768]{2,1,0:T(8,128)(2,1)} %get-tuple-element.111), channel_id=1, source_target_pairs={{0,8},{1,9},{2,10},{3,11},{4,12},{5,13},{6,14},{7,15},{8,0},{9,1},... | collective-permute-start | bytes 4718600 | tf_op jit(solution)/shard_map/ppermute | solution.py:572
  243.6 30.5 %collective-permute-start.29 = (bf16[1040,512]{1,0:T(8,128)(2,1)}, bf16[1040,512]{1,0:T(8,128)(2,1)}, u32[]{:S(2)}, u32[]{:S(2)}) collective-permute-start(bf16[1040,512]{1,0:T(8,128)(2,1)} %get-tuple-element.116), channel_id=1, source_target_pairs={{0,8},{1,9},{2,10},{3,11},{4,12},{5,13},{6,14},{7,15},{8,0},{9,1},... | collective-permute-start | bytes 3194888 | tf_op jit(solution)/shard_map/ppermute | solution.py:572
  248.6 30.3 %collective-permute-start.28 = (bf16[560,512]{1,0:T(8,128)(2,1)}, bf16[560,512]{1,0:T(8,128)(2,1)}, u32[]{:S(2)}, u32[]{:S(2)}) collective-permute-start(bf16[560,512]{1,0:T(8,128)(2,1)} %get-tuple-element.112), channel_id=1, source_target_pairs={{0,9},{1,8},{2,11},{3,10},{4,13},{5,12},{6,15},{7,14},{8,1},{9,0},... | collective-permute-start | bytes 1720328 | tf_op jit(solution)/shard_map/ppermute | solution.py:572
  250.3 28.6 %collective-permute-start.27 = (bf16[560,512]{1,0:T(8,128)(2,1)}, bf16[560,512]{1,0:T(8,128)(2,1)}, u32[]{:S(2)}, u32[]{:S(2)}) collective-permute-start(bf16[560,512]{1,0:T(8,128)(2,1)} %get-tuple-element.110.refs_5_.refs_7_.refs_6_), channel_id=1, source_target_pairs={{0,1},{1,0},{2,3},{3,2},{4,5},{5,4},{6,7},{7,6},{8,9},{9,8},{10,11... | collective-permute-start | bytes 1720328 | tf_op jit(solution)/shard_map/ppermute | solution.py:572
  251.8 1.1 copy-start.5
  259.0 15.1 %collective-permute-start.30 = (bf16[528,512]{1,0:T(8,128)(2,1)}, bf16[528,512]{1,0:T(8,128)(2,1)S(1)}, u32[]{:S(2)}, u32[]{:S(2)}) collective-permute-start(bf16[528,512]{1,0:T(8,128)(2,1)} %score.15), channel_id=1, source_target_pairs={{0,8},{1,9},{2,10},{3,11},{4,12},{5,13},{6,14},{7,15},{8,0},{9,1},... | collective-permute-start | bytes 1622024 | tf_op jit(solution)/shard_map/ppermute | solution.py:572
  265.2 13.8 %collective-permute-start.26 = (bf16[528,512]{1,0:T(8,128)(2,1)}, bf16[528,512]{1,0:T(8,128)(2,1)S(1)}, u32[]{:S(2)}, u32[]{:S(2)}) collective-permute-start(bf16[528,512]{1,0:T(8,128)(2,1)} %score.14), channel_id=1, source_target_pairs={{0,8},{1,9},{2,10},{3,11},{4,12},{5,13},{6,14},{7,15},{8,0},{9,1},... | collective-permute-start | bytes 1622024 | tf_op jit(solution)/shard_map/ppermute | solution.py:572
  274.1 0.8 copy-start.8
  278.9 0.8 copy-start.7

commit v5 on v4

--- a/solution.py
+++ b/solution.py
@@ -18,7 +18,8 @@
 ANY = pl.BlockSpec(memory_space=pl.ANY)
 SMEM = pl.BlockSpec(memory_space=pltpu.SMEM)
 SHORT = pl.CostEstimate(flops=1, bytes_accessed=1, transcendentals=0)
-VMEM_BYTES = 62 * 1024 * 1024
+VMEM_BYTES = 63 * 1024 * 1024 + 512 * 1024
+VMEM_LESS = 60 * 1024 * 1024
 VMEM = pl.BlockSpec(memory_space=pltpu.VMEM)
 
 
@@ -218,7 +219,7 @@
     return pl.pallas_call(
         gate_kernel,
         out_shape=[jax.ShapeDtypeStruct(v.shape, v.dtype) for v in passed],
-        in_specs=[ANY] * n + [VMEM] * len(others),
+        in_specs=[ANY] * (n + len(others)),
         out_specs=[ANY] * n,
         input_output_aliases={i: i for i in range(n)},
         compiler_params=pltpu.CompilerParams(vmem_limit_bytes=VMEM_BYTES),
@@ -260,10 +261,9 @@
     return scores, small.T[:8]
 
 
-def score_kernel(nz, cap, blk_dev, group, order, runs, fetched, late, resident, aliased, n_extra, me, ids, inv, meta, *refs):
+def score_kernel(nz, cap, blk_dev, places, wide, runs, fetched, late, resident, aliased, n_extra, me, ids, inv, meta, *refs):
     slots = nz * cap
-    wide = len(group) * cap
-    n = len(order)
+    n = len(places)
     tiles, refs = refs[: len(runs)], refs[len(runs) :]
     local, parts = refs[0], refs[1 : 1 + len(fetched)]
     refs = refs[1 + len(fetched) + aliased + n_extra :]
@@ -271,28 +271,32 @@
     work, xbuf, cbuf, obuf, tail, tail_b, xsem, csem, osem, tsem = refs[n:]
     half = me[3]
     half_blocks = blk_dev // 2
-    base = group[0] * cap
 
     total = jnp.int32(0)
-    for place, partner in enumerate(order):
+    for place, (partner, base) in enumerate(places):
         for k in range(wide):
             b = ids[partner * slots + base + k]
             valid = b >= 0
             if late is not None:
                 first, wanted = late
                 is_late = (b // half_blocks != half) & (b % half_blocks >= first)
-                is_late = is_late & (group[k // cap] == nz - 1)
+                is_late = is_late & ((base + k) // cap == nz - 1)
                 valid = valid & (is_late == wanted)
             work[total] = place * wide + k
             total = total + valid.astype(I32)
 
-    def start(i):
+    def where(i):
         code = work[i]
         place = code // wide
-        slot = base + code - place * wide
-        partner = jnp.int32(order[0])
+        partner, base = jnp.int32(places[0][0]), jnp.int32(places[0][1])
         for other in range(1, n):
-            partner = jnp.where(place == other, order[other], partner)
+            partner = jnp.where(place == other, places[other][0], partner)
+            base = jnp.where(place == other, places[other][1], base)
+        k = code - place * wide
+        return place, k, partner, base + k
+
+    def start(i):
+        place, k, partner, slot = where(i)
         b = ids[partner * slots + slot]
         for ref, (d, first, count) in zip(tiles, runs):
             row = slot - first if d else jnp.maximum(inv[slot], 0)
@@ -308,7 +312,7 @@
         if resident:
             return
 
-        if group[0] == 0:
+        if any(base == 0 for _, base in places):
 
             @pl.when(cls == 0)
             def _():
@@ -326,6 +330,15 @@
         start(i)
         return carry
 
+    def whole_parts():
+        at = 0
+        for p, (ref, (hops, direct, first, count)) in enumerate(zip(parts, fetched)):
+            yield pltpu.make_async_copy(ref, cbuf.at[pl.ds(at, count)], csem.at[p])
+            at += count
+
+    if resident:
+        for copy in whole_parts():
+            copy.start()
     lax.fori_loop(0, total, begin, 0)
     tail_rows = pl.ds(wide * TILE + 16 * (aliased > 0), 16)
     tail[...] = jnp.zeros(tail.shape, F32)
@@ -334,18 +347,11 @@
         if not resident:
             return cbuf[i]
         inside = ids[partner * slots + slot] % half_blocks
-        rows = parts[0][jnp.clip(inside - fetched[0][2], 0, fetched[0][3] - 1)]
-        for ref, (hops, direct, first, count) in zip(parts[1:], fetched[1:]):
-            rows = jnp.where(inside >= first, ref[jnp.clip(inside - first, 0, count - 1)], rows)
-        return rows
-
-    def where(i):
-        code = work[i]
-        place = code // wide
-        partner = jnp.int32(order[0])
-        for other in range(1, n):
-            partner = jnp.where(place == other, order[other], partner)
-        return place, code - place * wide, partner
+        row, at = jnp.int32(0), 0
+        for hops, direct, first, count in fetched:
+            row = jnp.where((inside >= first) & (inside < first + count), at + inside - first, row)
+            at += count
+        return cbuf[row]
 
     def body(pair, carry):
         both = (2 * pair, jnp.minimum(2 * pair + 1, total - 1))
@@ -359,13 +365,13 @@
                 if not resident:
                     pltpu.make_async_copy(local.at[0], cbuf.at[i], csem.at[i]).wait()
 
-        for i, (place, k, partner) in zip(both, spots):
-            rows = centers_of(i, base + k, partner)
-            values.append(score_math(xbuf[i], rows, meta[partner * slots + base + k]))
-        for i, (place, k, partner), (value, rows) in zip(both, spots, values):
+        for i, (place, k, partner, slot) in zip(both, spots):
+            rows = centers_of(i, slot, partner)
+            values.append(score_math(xbuf[i], rows, meta[partner * slots + slot]))
+        for i, (place, k, _, _), (value, rows) in zip(both, spots, values):
             obuf[i] = value
             tail[place, pl.ds(k, 1), 0 : 2 * TILE] = jnp.concatenate([rows[0:1], rows[1:2]], axis=1)
-        for j, (i, (place, k, partner)) in enumerate(zip(both, spots)):
+        for j, (i, (place, k, _, _)) in enumerate(zip(both, spots)):
             for other in range(n):
 
                 @pl.when((place == other) & (2 * pair + j < total))
@@ -376,6 +382,9 @@
 
         return carry
 
+    if resident:
+        for copy in whole_parts():
+            copy.wait()
     lax.fori_loop(0, (total + 1) // 2, body, 0)
 
     tail_b[...] = tail[...].astype(BF16)
@@ -392,28 +401,26 @@
 
 
 def score_call(
-    nz, cap, blk_dev, group, order, runs, fetched, late, resident, me, ids, inv, meta, tiles, local, parts, before, extra
+    nz, cap, blk_dev, places, wide, runs, fetched, late, resident, me, ids, inv, meta, tiles, local, parts, before, extra
 ):
-    wide = len(group) * cap
-    n = len(order)
+    n = len(places)
     items = n * wide
     first_before = 5 + len(runs) + len(parts)
     return pl.pallas_call(
         functools.partial(
-            score_kernel, nz, cap, blk_dev, group, order, runs, fetched, late, resident, len(before), len(extra)
+            score_kernel, nz, cap, blk_dev, places, wide, runs, fetched, late, resident, len(before), len(extra)
         ),
         out_shape=[
-            jax.ShapeDtypeStruct((wide * TILE + ((48 if d > 1 else 32) if late else 16), BLOCK), BF16) for d in order
+            jax.ShapeDtypeStruct((wide * TILE + (32 if late else 16), BLOCK), BF16) for d, _ in places
         ],
         in_specs=[SMEM, SMEM, SMEM, VMEM]
         + [ANY] * (len(runs) + 1)
-        + [VMEM if resident else ANY] * len(parts)
-        + [ANY] * (len(before) + len(extra)),
+        + [ANY] * (len(parts) + len(before) + len(extra)),
         out_specs=[ANY] * n,
         scratch_shapes=[
             pltpu.SMEM((items + 1,), I32),
             pltpu.VMEM((items, TILE, D), BF16),
-            pltpu.VMEM((1 if resident else items, BLOCK, D), BF16),
+            pltpu.VMEM((sum(key[3] for key in fetched) if resident else items, BLOCK, D), BF16),
             pltpu.VMEM((items, TILE, BLOCK), BF16),
             pltpu.VMEM((n, 16, BLOCK), F32),
             pltpu.VMEM((n, 16, BLOCK), BF16),
@@ -517,7 +524,7 @@
             pltpu.SemaphoreType.DMA((n,)),
         ],
         input_output_aliases={1 + n: 0} if before else {},
-        compiler_params=pltpu.CompilerParams(vmem_limit_bytes=VMEM_BYTES),
+        compiler_params=pltpu.CompilerParams(vmem_limit_bytes=VMEM_LESS if last else VMEM_BYTES),
         cost_estimate=SHORT,
         name="assemble",
     )(inv, *sources, *before, *earlier)
@@ -648,25 +655,29 @@
     env["t", len(runs)] = tile_rows
     runs += ((0, 0, slots),)
 
-    def score(group, order, late=None, into=False, extra=()):
+    def score(where, late=None, into=False, extra=()):
         resident = into
         keys = tuple(
             key
             for key in fetched
-            if key[0] in group and (late is None or (fetched[key] in (("x", steps), ("z", last))) == resident)
+            if any(key[0] in group for _, group in where)
+            and (late is None or (fetched[key] in (("x", steps), ("z", last))) == resident)
         )
-        low, high = group[0] * cap, (group[-1] + 1) * cap
+        wide = len(where[0][1]) * cap
+        places = tuple((d, group[0] * cap) for d, group in where)
         used = [
-            i for i, (d, first, count) in enumerate(runs) if d in order and first < high and first + count > low
+            i
+            for i, (d, first, count) in enumerate(runs)
+            if any(d == partner and first < base + wide and first + count > base for partner, base in places)
         ]
         scores = score_call(
-            nz, cap, blk_dev, group, order, tuple(runs[i] for i in used), keys, late, resident, me, ids, inv, meta,
+            nz, cap, blk_dev, places, wide, tuple(runs[i] for i in used), keys, late, resident, me, ids, inv, meta,
             [env["t", i] for i in used], local,
             [env[fetched[key]] for key in keys],
-            [env["s", d, group] for d in order] if into else [],
+            [env["s", d, group] for d, group in where] if into else [],
             extra,
         )
-        for d, values in zip(order, scores):
+        for (d, group), values in zip(where, scores):
             env["s", d, group] = values
 
     def place(sources, before, earlier=(), last_call=False):
@@ -718,23 +729,22 @@
             if done is not None:
                 waits.setdefault(done, []).append(name)
         for group, order in plans.get(k, []):
-            score(group, order, extra=[env["token"]])
+            score([(d, group) for d in order], extra=[env["token"]])
         if split and k == steps - 1:
             env["x", steps] = permute(cut(env["z", steps], 0, split), other_part)
         for d, group, done in at_once.get(k, []):
             env["r", d, group] = exchange(env["s", d, group], d)
             waits.setdefault(done, []).append(("r", d, group))
         if k == last - 1:
-            score(three, (2, 3, 0), (first_late, False), extra=[env["token"]])
-    score(three, (2, 3), (first_late, True), True, [env["token"]])
+            score([(d, three) for d in (2, 3, 0)], (first_late, False), extra=[env["token"]])
+    score([(2, three), (3, three)], (first_late, True), True, [env["token"]])
     for d in (2, 3):
         env["r", d, three] = exchange(env["s", d, three], d)
-    score(three, (0,), (first_late, True), True, [env["s", 2, three]])
-    for group in (two, three):
-        score(group, (1,), extra=[env["s", 2, three]])
+    score([(0, three)], (first_late, True), True, [env["s", 2, three]])
+    score([(1, two), (1, three)], extra=[env["s", 2, three]])
     for group in (one, two, three):
         env["r", 1, group] = exchange(env["s", 1, group], 1)
-    outputs = place([(0, one), (2, one), (3, one)], [], [env["s", 0, three]])
+    outputs = place([(0, one), (2, one), (3, one)], [], [env["s", 2, three]])
     outputs = place([(0, two), (2, two), (3, two), (1, one), (1, two)], outputs, [env["s", 0, three]])
     spill_scores, primary, picked = place([(d, three) for d in (0, 1, 2, 3)], outputs, last_call=True)
     return (

time: 285 us -> 275 us (0.965)
  Pallas kernels: 93.4 us -> 76.5 us
  local copies, waits for them, and re-layouts: 12.6 us -> 5.01 us
  waiting for transfers between devices: 129 us -> 136 us
  starting transfers between devices: 47.8 us -> 52.7 us
    pallas_call x8 -> x7, Pallas kernels: 57.5 us -> 43.6 us  [score_call(): pl.pallas_call(functools.partial(score_kernel, nz, cap, blk_dev, places,...]
    unnamed x34 -> x16, local copies, waits for them, and re-layouts: 8.21 us -> 0.64 us
    ppermute x31, waiting for transfers between devices: 129 us -> 136 us  [permute(): lax.ppermute(value, AXES, [(device(*a), device(*target(*a))) for a in eve...]
    ppermute x31, starting transfers between devices: 47.8 us -> 52.7 us  [permute(): lax.ppermute(value, AXES, [(device(*a), device(*target(*a))) for a in eve...]
  transfers between devices with their start and end apart: 31 -> 31, of which waited for: 15 -> 11; matrix products, arithmetic and copies ran while one was open for 0% -> 0% of each run, Pallas kernels for 31% -> 27%
where the time goes in v5:
time: 275 us; the launch traced here: 272 us
  waiting for transfers between devices  136 us (49%)
  Pallas kernels  76.5 us (28%)
  starting transfers between devices  52.7 us (19%)
  local copies, waits for them, and re-layouts  5.01 us (2%)
    ppermute x31, waiting for transfers between devices, permute(): lax.ppermute(value, AXES, [(device(*a), device(*target(*a))) for a in eve...  136 us
    ppermute x31, starting transfers between devices, permute(): lax.ppermute(value, AXES, [(device(*a), device(*target(*a))) for a in eve...  52.7 us
    pallas_call x7, Pallas kernels, score_call(): pl.pallas_call(functools.partial(score_kernel, nz, cap, blk_dev, places,...  43.6 us
    pallas_call x3, Pallas kernels, assemble(): pl.pallas_call(functools.partial(assemble_kernel, spans, held_already, le...  11.2 us
    pallas_call x1, Pallas kernels, receive(): pl.pallas_call(functools.partial(receive_kernel, nz, cap, blk_dev, tile_d...  7.28 us
    pallas_call x3, Pallas kernels, cut(): pl.pallas_call(functools.partial(cut_kernel, first), out_shape=jax.ShapeD...  6.6 us
  transfers between devices with their start and end apart: 31, of which 11 were waited for; matrix products, arithmetic and copies ran while one was open for 0% of the time, Pallas kernels for 27%

profile of v5, /device:TPU:9, one launch (start us, length us, event | category | flops | bytes accessed | tf_op | source)
XLA Modules:
  0.0 271.9 jit_solution(15765797346197270225)
XLA Ops:
  0.7 3.8 %constant_dynamic-slice_fusion = (bf16[2,512,768]{2,1,0:T(8,128)(2,1)}, bf16[2,512,768]{2,1,0:T(8,128)(2,1)}) fusion(bf16[8,512,768]{2,1,0:T(8,128)(2,1)} %bitcast.13, s32[]{:T(128)S(6)} %select_n.26, s32[]{:T(128)S(6)} %select_n.25), kind=kLoop, calls=%fused_computation.3 | loop fusion | bytes 6291464 | tf_op jit(solution)/shard_map/dynamic_slice | solution.py:590
  4.5 2.3 collective-permute-start.5
  6.8 2.1 collective-permute-start.2
  9.4 0.6 pad_add_fusion.2.me
  10.2 2.8 %plan.1 = (s32[32]{0:T(128)}, s32[64]{0:T(128)}) custom-call(s32[4]{0:T(128)} %pad_add_fusion.2.me, s32[32]{0:T(128)} %region.1, s32[32]{0:T(128)} %block.1, bf16[2,512,768]{2,1,0:T(8,128)(2,1)} %get-tuple-element.134.refs_0_, bf16[2,512,768]{2,1,0:T(8,128)(2,1)} %get-tuple-element.133.refs_1_), custom_call_target="tpu_custom_call" | custom-call | flops 1 | bytes 1 | tf_op jit(solution)/shard_map/plan/pallas_call | solution.py:75
  13.8 5.0 %dispatch.1 = (bf16[8,128,768]{2,1,0:T(8,128)(2,1)}, bf16[8,128,768]{2,1,0:T(8,128)(2,1)}, bf16[8,128,768]{2,1,0:T(8,128)(2,1)}, bf16[8,128,768]{2,1,0:T(8,128)(...) custom-call(s32[32]{0:T(128)} %get-tuple-element.71.at_slot, bf16[32,128,768]{2,1,0:T(8,128)(2,1)} %bitcast.21, ...), custom_call_target="tpu_custom_call" | custom-call | flops 1 | bytes 1 | tf_op jit(solution)/shard_map/dispatch/pallas_call | solution.py:197
  18.8 1.7 collective-permute-start.4
  20.5 19.7 %collective-permute-done.5.refs_0_ = bf16[2,512,768]{2,1,0:T(8,128)(2,1)} collective-permute-done((bf16[2,512,768]{2,1,0:T(8,128)(2,1)}, bf16[2,512,768]{2,1,0:T(8,128)(2,1)}, u32[]{:S(2)}, u32[]{:S(2)}) %collective-permute-start.5) | collective-permute-done | bytes 1572896 | tf_op jit(solution)/shard_map/ppermute | solution.py:579
  40.7 1.2 collective-permute-start.6
  42.0 4.1 %collective-permute-start.9 = (bf16[8,128,768]{2,1,0:T(8,128)(2,1)}, bf16[8,128,768]{2,1,0:T(8,128)(2,1)}, u32[]{:S(2)}, u32[]{:S(2)}) collective-permute-start(bf16[8,128,768]{2,1,0:T(8,128)(2,1)} %get-tuple-element.78), channel_id=1, source_target_pairs={{0,9},{1,8},{2,11},{3,10},{4,13},{5,12},{6,15},{7,14},{8,1},{9,0},... | collective-permute-start | bytes 4718600 | tf_op jit(solution)/shard_map/ppermute | solution.py:579
  46.1 3.1 %collective-permute-start.10 = (bf16[2,512,768]{2,1,0:T(8,128)(2,1)}, bf16[2,512,768]{2,1,0:T(8,128)(2,1)}, u32[]{:S(2)}, u32[]{:S(2)}) collective-permute-start(bf16[2,512,768]{2,1,0:T(8,128)(2,1)} %get-tuple-element.73.refs_4_.refs_2_), channel_id=1, source_target_pairs={{0,2},{1,3},{2,6},{3,7},{4,0},{5,1},{6,4},{7,5},{8,10},{9,11},{10,... | collective-permute-start | bytes 4718600 | tf_op jit(solution)/shard_map/ppermute | solution.py:579
  49.2 24.7 %collective-permute-done.3.refs_0_ = bf16[2,512,768]{2,1,0:T(8,128)(2,1)} collective-permute-done((bf16[2,512,768]{2,1,0:T(8,128)(2,1)}, bf16[2,512,768]{2,1,0:T(8,128)(2,1)}, u32[]{:S(2)}, u32[]{:S(2)}) %collective-permute-start.3) | collective-permute-done | bytes 1572896 | tf_op jit(solution)/shard_map/ppermute | solution.py:579
  74.3 1.2 collective-permute-start.11
  75.5 3.1 %collective-permute-start.7 = (bf16[2,512,768]{2,1,0:T(8,128)(2,1)}, bf16[2,512,768]{2,1,0:T(8,128)(2,1)}, u32[]{:S(2)}, u32[]{:S(2)}) collective-permute-start(bf16[2,512,768]{2,1,0:T(8,128)(2,1)} %get-tuple-element.76.refs_6_.refs_4_), channel_id=1, source_target_pairs={{0,2},{1,3},{2,6},{3,7},{4,0},{5,1},{6,4},{7,5},{8,10},{9,11},{10,... | collective-permute-start | bytes 4718600 | tf_op jit(solution)/shard_map/ppermute | solution.py:579
  78.6 1.2 collective-permute-start.8
  79.8 11.5 %collective-permute-done.9.refs_0_ = bf16[8,128,768]{2,1,0:T(8,128)(2,1)} collective-permute-done((bf16[8,128,768]{2,1,0:T(8,128)(2,1)}, bf16[8,128,768]{2,1,0:T(8,128)(2,1)}, u32[]{:S(2)}, u32[]{:S(2)}) %collective-permute-start.9) | collective-permute-done | bytes 1572896 | tf_op jit(solution)/shard_map/ppermute | solution.py:579
  91.3 16.2 %collective-permute-done.10.refs_1_ = bf16[2,512,768]{2,1,0:T(8,128)(2,1)} collective-permute-done((bf16[2,512,768]{2,1,0:T(8,128)(2,1)}, bf16[2,512,768]{2,1,0:T(8,128)(2,1)}, u32[]{:S(2)}, u32[]{:S(2)}) %collective-permute-start.10) | collective-permute-done | bytes 1572896 | tf_op jit(solution)/shard_map/ppermute | solution.py:579
  107.6 1.2 collective-permute-start.12
  108.8 7.3 %receive.1 = (s32[64,8,128]{2,1,0:T(8,128)}, s32[64]{0:T(128)}) custom-call(s32[4]{0:T(128)} %pad_add_fusion.2.me, s32[72,128]{1,0:T(8,128)} %copy-done, s32[72,128]{1,0:T(8,128)} %copy-done.3, s32[72,128]{1,0:T(8,128)} %copy-done.2, s32[72,128]{1,0:T(8,128)} %copy-done.1), custom_call_target="tpu_custom_call" | custom-call | flops 1 | bytes 1 | tf_op jit(solution)/shard_map/receive/pallas_call | solution.py:137
  116.1 3.2 %collective-permute-start.15 = (bf16[2,512,768]{2,1,0:T(8,128)(2,1)}, bf16[2,512,768]{2,1,0:T(8,128)(2,1)}, u32[]{:S(2)}, u32[]{:S(2)}) collective-permute-start(bf16[2,512,768]{2,1,0:T(8,128)(2,1)} %get-tuple-element.81.refs_4_.refs_2_), channel_id=1, source_target_pairs={{0,2},{1,3},{2,6},{3,7},{4,0},{5,1},{6,4},{7,5},{8,10},{9,11},{10,... | collective-permute-start | bytes 4718600 | tf_op jit(solution)/shard_map/ppermute | solution.py:579
  119.3 6.2 %collective-permute-start.16 = (bf16[8,128,768]{2,1,0:T(8,128)(2,1)}, bf16[8,128,768]{2,1,0:T(8,128)(2,1)}, u32[]{:S(2)}, u32[]{:S(2)}) collective-permute-start(bf16[8,128,768]{2,1,0:T(8,128)(2,1)} %get-tuple-element.89), channel_id=1, source_target_pairs={{0,9},{1,8},{2,11},{3,10},{4,13},{5,12},{6,15},{7,14},{8,1},{9,0},... | collective-permute-start | bytes 4718600 | tf_op jit(solution)/shard_map/ppermute | solution.py:579
  125.4 18.0 %score.7 = (bf16[1040,512]{1,0:T(8,128)(2,1)}, bf16[1040,512]{1,0:T(8,128)(2,1)}, bf16[1040,512]{1,0:T(8,128)(2,1)}) custom-call(s32[4]{0:T(128)} %pad_add_fusion.2.me, s32[64]{0:T(128)} %get-tuple-element.69.ids, s32[64]{0:T(128)} %get-tuple-element.68.inv, s32[64,8,128]{2,1,0:T(8,128)} %get-tuple-element.70.meta, ...), custom_call_target="tpu_custom_call" | custom-call | flops 1 | bytes 1 | tf_op jit(solution)/shard_map/score/pallas_call | solution.py:409
  143.7 2.6 cut.3
  146.3 3.2 %collective-permute-start.13 = (bf16[2,528,768]{2,1,0:T(8,128)(2,1)}, bf16[2,528,768]{2,1,0:T(8,128)(2,1)}, u32[]{:S(2)}, u32[]{:S(2)}) collective-permute-start(bf16[2,528,768]{2,1,0:T(8,128)(2,1)} %cut.3), channel_id=1, source_target_pairs={{0,2},{1,3},{2,6},{3,7},{4,0},{5,1},{6,4},{7,5},{8,10},{9,11},{10,... | collective-permute-start | bytes 4866056 | tf_op jit(solution)/shard_map/ppermute | solution.py:579
  149.4 11.6 %collective-permute-done.16.refs_1_ = bf16[8,128,768]{2,1,0:T(8,128)(2,1)} collective-permute-done((bf16[8,128,768]{2,1,0:T(8,128)(2,1)}, bf16[8,128,768]{2,1,0:T(8,128)(2,1)}, u32[]{:S(2)}, u32[]{:S(2)}) %collective-permute-start.16) | collective-permute-done | bytes 1572896 | tf_op jit(solution)/shard_map/ppermute | solution.py:579
  161.0 14.0 %collective-permute-done.15.refs_0_ = bf16[2,512,768]{2,1,0:T(8,128)(2,1)} collective-permute-done((bf16[2,512,768]{2,1,0:T(8,128)(2,1)}, bf16[2,512,768]{2,1,0:T(8,128)(2,1)}, u32[]{:S(2)}, u32[]{:S(2)}) %collective-permute-start.15) | collective-permute-done | bytes 1572896 | tf_op jit(solution)/shard_map/ppermute | solution.py:579
  175.0 8.5 %collective-permute-done.18.refs_3_ = bf16[1040,512]{1,0:T(8,128)(2,1)} collective-permute-done((bf16[1040,512]{1,0:T(8,128)(2,1)}, bf16[1040,512]{1,0:T(8,128)(2,1)}, u32[]{:S(2)}, u32[]{:S(2)}) %collective-permute-start.18) | collective-permute-done | bytes 1064992 | tf_op jit(solution)/shard_map/ppermute | solution.py:579
  185.1 6.3 %score.8 = (bf16[528,512]{1,0:T(8,128)(2,1)}, bf16[528,512]{1,0:T(8,128)(2,1)}, bf16[528,512]{1,0:T(8,128)(2,1)}) custom-call(s32[4]{0:T(128)} %pad_add_fusion.2.me, s32[64]{0:T(128)} %get-tuple-element.69.ids, s32[64]{0:T(128)} %get-tuple-element.68.inv, s32[64,8,128]{2,1,0:T(8,128)} %get-tuple-element.70.meta, ...), custom_call_target="tpu_custom_call" | custom-call | flops 1 | bytes 1 | tf_op jit(solution)/shard_map/score/pallas_call | solution.py:409
  191.4 2.0 cut.5
  193.5 16.3 %collective-permute-done.13.source.refs_6_.refs_8_ = bf16[2,528,768]{2,1,0:T(8,128)(2,1)} collective-permute-done((bf16[2,528,768]{2,1,0:T(8,128)(2,1)}, bf16[2,528,768]{2,1,0:T(8,128)(2,1)}, u32[]{:S(2)}, u32[]{:S(2)}) %collective-permute-start.13) | collective-permute-done | bytes 1622048 | tf_op jit(solution)/shard_map/ppermute | solution.py:579
  209.7 3.1 %collective-permute-start.19 = (bf16[1,512,768]{2,1,0:T(8,128)(2,1)}, bf16[1,512,768]{2,1,0:T(8,128)(2,1)}, u32[]{:S(2)}, u32[]{:S(2)}) collective-permute-start(bf16[1,512,768]{2,1,0:T(8,128)(2,1)} %cut.5), channel_id=1, source_target_pairs={{0,2},{1,3},{2,6},{3,7},{4,0},{5,1},{6,4},{7,5},{8,10},{9,11},{10,... | collective-permute-start | bytes 2359304 | tf_op jit(solution)/shard_map/ppermute | solution.py:579
  212.8 2.0 cut.4
  214.9 1.3 collective-permute-start.14
  216.1 9.1 %score.9.refs_4_ = bf16[1040,512]{1,0:T(8,128)(2,1)} custom-call(s32[4]{0:T(128)} %pad_add_fusion.2.me, s32[64]{0:T(128)} %get-tuple-element.69.ids, s32[64]{0:T(128)} %get-tuple-element.68.inv, s32[64,8,128]{2,1,0:T(8,128)} %get-tuple-element.70.meta, bf16[8,128,768]{2,1,0:T(8,128)(2,1)} %collective-permute-done.23.refs_0_, bf16[8,512,768]{2,1,0:T(8,128)(2,1)} %bitcast.16, ...), custom_call_target="tpu_custom_call" | custom-call | flops 1 | bytes 1 | tf_op jit(solution)/shard_map/score/pallas_call | solution.py:409
  225.3 3.7 %collective-permute-start.24 = (bf16[528,512]{1,0:T(8,128)(2,1)}, bf16[528,512]{1,0:T(8,128)(2,1)}, u32[]{:S(2)}, u32[]{:S(2)}) collective-permute-start(bf16[528,512]{1,0:T(8,128)(2,1)} %get-tuple-element.109), channel_id=1, source_target_pairs={{0,9},{1,8},{2,11},{3,10},{4,13},{5,12},{6,15},{7,14},{8,1},{9,0},... | collective-permute-start | bytes 1622024 | tf_op jit(solution)/shard_map/ppermute | solution.py:579
  229.0 2.0 score.10
  231.0 6.1 %collective-permute-done.14.refs_3_.refs_2_.refs_9_ = bf16[1,512,768]{2,1,0:T(8,128)(2,1)} collective-permute-done((bf16[1,512,768]{2,1,0:T(8,128)(2,1)}, bf16[1,512,768]{2,1,0:T(8,128)(2,1)}, u32[]{:S(2)}, u32[]{:S(2)}) %collective-permute-start.14) | collective-permute-done | bytes 786464 | tf_op jit(solution)/shard_map/ppermute | solution.py:579
  237.2 0.9 collective-permute-start.25
  238.1 3.2 %score.11 = (bf16[544,512]{1,0:T(8,128)(2,1)}, bf16[544,512]{1,0:T(8,128)(2,1)}) custom-call(s32[4]{0:T(128)} %pad_add_fusion.2.me, s32[64]{0:T(128)} %get-tuple-element.69.ids, s32[64]{0:T(128)} %get-tuple-element.68.inv, s32[64,8,128]{2,1,0:T(8,128)} %get-tuple-element.70.meta, ...), custom_call_target="tpu_custom_call", output_to_operand_aliasing={{0}: (9, {}), {1}: (10, {})} | custom-call | flops 1 | bytes 1 | tf_op jit(solution)/shard_map/score/pallas_call | solution.py:409
  241.4 1.5 collective-permute-start.28
  242.9 1.8 collective-permute-start.27
  244.7 1.8 score.13
  246.5 4.0 %collective-permute-start.30 = (bf16[528,512]{1,0:T(8,128)(2,1)}, bf16[528,512]{1,0:T(8,128)(2,1)}, u32[]{:S(2)}, u32[]{:S(2)}) collective-permute-start(bf16[528,512]{1,0:T(8,128)(2,1)} %get-tuple-element.120), channel_id=1, source_target_pairs={{0,8},{1,9},{2,10},{3,11},{4,12},{5,13},{6,14},{7,15},{8,0},{9,1},... | collective-permute-start | bytes 1622024 | tf_op jit(solution)/shard_map/ppermute | solution.py:579
  250.7 4.2 %assemble.3 = (bf16[32,128,512]{2,1,0:T(8,128)(2,1)}, f32[32,128]{1,0:T(8,128)}, f32[32,128]{1,0:T(8,128)}) custom-call(s32[64]{0:T(128)} %get-tuple-element.68.inv, bf16[1040,512]{1,0:T(8,128)(2,1)} %get-tuple-element.121.refs_0_, bf16[1040,512]{1,0:T(8,128)(2,1)} %get-tuple-element.122.refs_1_, bf16[1040,512]{1,0:T(8,128)(2,1)} %get-tuple-element.123.refs_2_, ...), custom_call_target="tpu_custom_call" | custom-call | flops 1 | bytes 1 | tf_op jit(solution)/shard_map/assemble/pallas_call | solution.py:508
  254.8 3.1 %score.12.refs_8_.refs_0_ = bf16[544,512]{1,0:T(8,128)(2,1)} custom-call(s32[4]{0:T(128)} %pad_add_fusion.2.me, s32[64]{0:T(128)} %get-tuple-element.69.ids, s32[64]{0:T(128)} %get-tuple-element.68.inv, s32[64,8,128]{2,1,0:T(8,128)} %get-tuple-element.70.meta, bf16[32,128,768]{2,1,0:T(8,128)(2,1)} %bitcast.25, ...), custom_call_target="tpu_custom_call", output_to_operand_aliasing={{}: (8, {})} | custom-call | flops 1 | bytes 1 | tf_op jit(solution)/shard_map/score/pallas_call | solution.py:409
  258.0 3.8 %assemble.4 = (bf16[32,128,512]{2,1,0:T(8,128)(2,1)}, f32[32,128]{1,0:T(8,128)}, f32[32,128]{1,0:T(8,128)}) custom-call(s32[64]{0:T(128)} %get-tuple-element.68.inv, bf16[528,512]{1,0:T(8,128)(2,1)} %get-tuple-element.116.refs_0_, bf16[528,512]{1,0:T(8,128)(2,1)} %get-tuple-element.117.refs_1_, ...), custom_call_target="tpu_custom_call", output_to_operand_aliasing={{0}: (6, {})} | custom-call | flops 1 | bytes 1 | tf_op jit(solution)/shard_map/assemble/pallas_call | solution.py:508
  261.8 6.8 %collective-permute-done.27.refs_2_ = bf16[544,512]{1,0:T(8,128)(2,1)} collective-permute-done((bf16[544,512]{1,0:T(8,128)(2,1)}, bf16[544,512]{1,0:T(8,128)(2,1)}, u32[]{:S(2)}, u32[]{:S(2)}) %collective-permute-start.27) | collective-permute-done | bytes 557088 | tf_op jit(solution)/shard_map/ppermute | solution.py:579
  268.6 3.2 %assemble.5 = (bf16[32,128,512]{2,1,0:T(8,128)(2,1)}, bf16[32,128]{1,0:T(8,128)(2,1)}, bf16[32,128]{1,0:T(8,128)(2,1)}) custom-call(s32[64]{0:T(128)} %get-tuple-element.68.inv, bf16[544,512]{1,0:T(8,128)(2,1)} %score.12.refs_8_.refs_0_, bf16[528,512]{1,0:T(8,128)(2,1)} %collective-permute-done.26.refs_1_, ...), custom_call_target="tpu_custom_call", output_to_operand_aliasing={{0}: (5, {})} | custom-call | flops 1 | bytes 1 | tf_op jit(solution)/shard_map/assemble/pallas_call | solution.py:508
  (58 shorter events, 4.3 us)
Async XLA Ops:
  0.6 6.1 %copy-start.6 = (s32[32]{0:T(128)S(1)}, s32[32]{0:T(128)}, u32[]{:S(2)}) copy-start(s32[32]{0:T(128)} %region.1) | copy-start | bytes 388
  0.6 6.1 %copy-start.7 = (s32[32]{0:T(128)S(1)}, s32[32]{0:T(128)}, u32[]{:S(2)}) copy-start(s32[32]{0:T(128)} %block.1) | copy-start | bytes 388
  0.7 6.1 %copy-start.4 = (s32[4096]{0:T(1024)S(1)}, s32[4096]{0:T(1024)}, u32[]{:S(2)}) copy-start(s32[4096]{0:T(1024)} %param.10) | copy-start | bytes 49156
  0.7 6.1 %copy-start.5 = (s32[4096]{0:T(1024)S(1)}, s32[4096]{0:T(1024)}, u32[]{:S(2)}) copy-start(s32[4096]{0:T(1024)} %param.9) | copy-start | bytes 49156
  4.5 35.7 %collective-permute-start.5 = (bf16[2,512,768]{2,1,0:T(8,128)(2,1)}, bf16[2,512,768]{2,1,0:T(8,128)(2,1)}, u32[]{:S(2)}, u32[]{:S(2)}) collective-permute-start(bf16[2,512,768]{2,1,0:T(8,128)(2,1)} %get-tuple-element.134.refs_0_), channel_id=1, source_target_pairs={{0,2},{1,3},{2,6},{3,7},{4,0},{5,1},{6,4},{7,5},{8,10},{9,11},{10,... | collective-permute-start | bytes 4718600 | tf_op jit(solution)/shard_map/ppermute | solution.py:579
  6.8 6.3 %copy-start = (s32[72,128]{1,0:T(8,128)}, s32[72,128]{1,0:T(8,128)S(1)}, u32[]{:S(2)}) copy-start(s32[72,128]{1,0:T(8,128)S(1)} %pad_add_fusion.refs_0_) | copy-start | bytes 110596
  6.8 6.3 %collective-permute-start.2 = (s32[72,128]{1,0:T(8,128)S(1)}, s32[72,128]{1,0:T(8,128)S(1)}, u32[]{:S(2)}, u32[]{:S(2)}) collective-permute-start(s32[72,128]{1,0:T(8,128)S(1)} %pad_add_fusion.refs_0_), channel_id=1, source_target_pairs={{0,9},{1,8},{2,11},{3,10},{4,13},{5,12},{6,15},{7,14},{8,1},{9,0},... | collective-permute-start | bytes 110600 | tf_op jit(solution)/shard_map/ppermute | solution.py:579
  9.0 4.1 %collective-permute-start.1 = (s32[72,128]{1,0:T(8,128)S(1)}, s32[72,128]{1,0:T(8,128)S(1)}, u32[]{:S(2)}, u32[]{:S(2)}) collective-permute-start(s32[72,128]{1,0:T(8,128)S(1)} %pad_add_fusion.refs_0_), channel_id=1, source_target_pairs={{0,1},{1,0},{2,3},{3,2},{4,5},{5,4},{6,7},{7,6},{8,9},{9,8},{10,11... | collective-permute-start | bytes 110600 | tf_op jit(solution)/shard_map/ppermute | solution.py:579
  9.2 3.9 %collective-permute-start = (s32[72,128]{1,0:T(8,128)S(1)}, s32[72,128]{1,0:T(8,128)S(1)}, u32[]{:S(2)}, u32[]{:S(2)}) collective-permute-start(s32[72,128]{1,0:T(8,128)S(1)} %pad_add_fusion.refs_0_), channel_id=1, source_target_pairs={{0,8},{1,9},{2,10},{3,11},{4,12},{5,13},{6,14},{7,15},{8,0},{9,1},... | collective-permute-start | bytes 110600 | tf_op jit(solution)/shard_map/ppermute | solution.py:579
  10.1 63.8 %collective-permute-start.3 = (bf16[2,512,768]{2,1,0:T(8,128)(2,1)}, bf16[2,512,768]{2,1,0:T(8,128)(2,1)}, u32[]{:S(2)}, u32[]{:S(2)}) collective-permute-start(bf16[2,512,768]{2,1,0:T(8,128)(2,1)} %get-tuple-element.133.refs_1_), channel_id=1, source_target_pairs={{0,2},{1,3},{2,6},{3,7},{4,0},{5,1},{6,4},{7,5},{8,10},{9,11},{10,... | collective-permute-start | bytes 4718600 | tf_op jit(solution)/shard_map/ppermute | solution.py:579
  13.1 0.6 copy-start.1
  13.1 0.6 copy-start.2
  13.1 0.6 copy-start.3
  18.8 55.1 %collective-permute-start.4 = (bf16[8,128,768]{2,1,0:T(8,128)(2,1)}, bf16[8,128,768]{2,1,0:T(8,128)(2,1)}, u32[]{:S(2)}, u32[]{:S(2)}) collective-permute-start(bf16[8,128,768]{2,1,0:T(8,128)(2,1)} %get-tuple-element.72), channel_id=1, source_target_pairs={{0,1},{1,0},{2,3},{3,2},{4,5},{5,4},{6,7},{7,6},{8,9},{9,8},{10,11... | collective-permute-start | bytes 4718600 | tf_op jit(solution)/shard_map/ppermute | solution.py:579
  40.7 33.5 %collective-permute-start.6 = (bf16[2,512,768]{2,1,0:T(8,128)(2,1)}, bf16[2,512,768]{2,1,0:T(8,128)(2,1)}, u32[]{:S(2)}, u32[]{:S(2)}) collective-permute-start(bf16[2,512,768]{2,1,0:T(8,128)(2,1)} %get-tuple-element.73.refs_4_.refs_2_), channel_id=1, source_target_pairs={{0,16},{1,17},{2,18},{3,19},{4,20},{5,21},{6,22},{7,23},{8,24},{9,... | collective-permute-start | bytes 4718600 | tf_op jit(solution)/shard_map/ppermute | solution.py:579
  42.0 49.4 %collective-permute-start.9 = (bf16[8,128,768]{2,1,0:T(8,128)(2,1)}, bf16[8,128,768]{2,1,0:T(8,128)(2,1)}, u32[]{:S(2)}, u32[]{:S(2)}) collective-permute-start(bf16[8,128,768]{2,1,0:T(8,128)(2,1)} %get-tuple-element.78), channel_id=1, source_target_pairs={{0,9},{1,8},{2,11},{3,10},{4,13},{5,12},{6,15},{7,14},{8,1},{9,0},... | collective-permute-start | bytes 4718600 | tf_op jit(solution)/shard_map/ppermute | solution.py:579
  46.1 61.5 %collective-permute-start.10 = (bf16[2,512,768]{2,1,0:T(8,128)(2,1)}, bf16[2,512,768]{2,1,0:T(8,128)(2,1)}, u32[]{:S(2)}, u32[]{:S(2)}) collective-permute-start(bf16[2,512,768]{2,1,0:T(8,128)(2,1)} %get-tuple-element.73.refs_4_.refs_2_), channel_id=1, source_target_pairs={{0,2},{1,3},{2,6},{3,7},{4,0},{5,1},{6,4},{7,5},{8,10},{9,11},{10,... | collective-permute-start | bytes 4718600 | tf_op jit(solution)/shard_map/ppermute | solution.py:579
  74.3 33.3 %collective-permute-start.11 = (bf16[2,512,768]{2,1,0:T(8,128)(2,1)}, bf16[2,512,768]{2,1,0:T(8,128)(2,1)}, u32[]{:S(2)}, u32[]{:S(2)}) collective-permute-start(bf16[2,512,768]{2,1,0:T(8,128)(2,1)} %get-tuple-element.76.refs_6_.refs_4_), channel_id=1, source_target_pairs={{0,16},{1,17},{2,18},{3,19},{4,20},{5,21},{6,22},{7,23},{8,24},{9,... | collective-permute-start | bytes 4718600 | tf_op jit(solution)/shard_map/ppermute | solution.py:579
  75.5 68.0 %collective-permute-start.7 = (bf16[2,512,768]{2,1,0:T(8,128)(2,1)}, bf16[2,512,768]{2,1,0:T(8,128)(2,1)}, u32[]{:S(2)}, u32[]{:S(2)}) collective-permute-start(bf16[2,512,768]{2,1,0:T(8,128)(2,1)} %get-tuple-element.76.refs_6_.refs_4_), channel_id=1, source_target_pairs={{0,2},{1,3},{2,6},{3,7},{4,0},{5,1},{6,4},{7,5},{8,10},{9,11},{10,... | collective-permute-start | bytes 4718600 | tf_op jit(solution)/shard_map/ppermute | solution.py:579
  78.6 64.9 %collective-permute-start.8 = (bf16[8,128,768]{2,1,0:T(8,128)(2,1)}, bf16[8,128,768]{2,1,0:T(8,128)(2,1)}, u32[]{:S(2)}, u32[]{:S(2)}) collective-permute-start(bf16[8,128,768]{2,1,0:T(8,128)(2,1)} %get-tuple-element.77), channel_id=1, source_target_pairs={{0,1},{1,0},{2,3},{3,2},{4,5},{5,4},{6,7},{7,6},{8,9},{9,8},{10,11... | collective-permute-start | bytes 4718600 | tf_op jit(solution)/shard_map/ppermute | solution.py:579
  107.6 35.9 %collective-permute-start.12 = (bf16[2,512,768]{2,1,0:T(8,128)(2,1)}, bf16[2,512,768]{2,1,0:T(8,128)(2,1)}, u32[]{:S(2)}, u32[]{:S(2)}) collective-permute-start(bf16[2,512,768]{2,1,0:T(8,128)(2,1)} %get-tuple-element.81.refs_4_.refs_2_), channel_id=1, source_target_pairs={{0,16},{1,17},{2,18},{3,19},{4,20},{5,21},{6,22},{7,23},{8,24},{9,... | collective-permute-start | bytes 4718600 | tf_op jit(solution)/shard_map/ppermute | solution.py:579
  116.1 58.9 %collective-permute-start.15 = (bf16[2,512,768]{2,1,0:T(8,128)(2,1)}, bf16[2,512,768]{2,1,0:T(8,128)(2,1)}, u32[]{:S(2)}, u32[]{:S(2)}) collective-permute-start(bf16[2,512,768]{2,1,0:T(8,128)(2,1)} %get-tuple-element.81.refs_4_.refs_2_), channel_id=1, source_target_pairs={{0,2},{1,3},{2,6},{3,7},{4,0},{5,1},{6,4},{7,5},{8,10},{9,11},{10,... | collective-permute-start | bytes 4718600 | tf_op jit(solution)/shard_map/ppermute | solution.py:579
  119.3 41.8 %collective-permute-start.16 = (bf16[8,128,768]{2,1,0:T(8,128)(2,1)}, bf16[8,128,768]{2,1,0:T(8,128)(2,1)}, u32[]{:S(2)}, u32[]{:S(2)}) collective-permute-start(bf16[8,128,768]{2,1,0:T(8,128)(2,1)} %get-tuple-element.89), channel_id=1, source_target_pairs={{0,9},{1,8},{2,11},{3,10},{4,13},{5,12},{6,15},{7,14},{8,1},{9,0},... | collective-permute-start | bytes 4718600 | tf_op jit(solution)/shard_map/ppermute | solution.py:579
  143.5 40.0 %collective-permute-start.17 = (bf16[2,512,768]{2,1,0:T(8,128)(2,1)}, bf16[2,512,768]{2,1,0:T(8,128)(2,1)}, u32[]{:S(2)}, u32[]{:S(2)}) collective-permute-start(bf16[2,512,768]{2,1,0:T(8,128)(2,1)} %get-tuple-element.88.source.refs_6_.refs_4_), channel_id=1, source_target_pairs={{0,16},{1,17},{2,18},{3,19},{4,20},{5,21},{6,22},{7,23},{8,24},{9,... | collective-permute-start | bytes 4718600 | tf_op jit(solution)/shard_map/ppermute | solution.py:579
  143.6 39.9 %collective-permute-start.18 = (bf16[1040,512]{1,0:T(8,128)(2,1)}, bf16[1040,512]{1,0:T(8,128)(2,1)}, u32[]{:S(2)}, u32[]{:S(2)}) collective-permute-start(bf16[1040,512]{1,0:T(8,128)(2,1)} %get-tuple-element.90), channel_id=1, source_target_pairs={{0,1},{1,0},{2,3},{3,2},{4,5},{5,4},{6,7},{7,6},{8,9},{9,8},{10,11... | collective-permute-start | bytes 3194888 | tf_op jit(solution)/shard_map/ppermute | solution.py:579
  146.3 63.4 %collective-permute-start.13 = (bf16[2,528,768]{2,1,0:T(8,128)(2,1)}, bf16[2,528,768]{2,1,0:T(8,128)(2,1)}, u32[]{:S(2)}, u32[]{:S(2)}) collective-permute-start(bf16[2,528,768]{2,1,0:T(8,128)(2,1)} %cut.3), channel_id=1, source_target_pairs={{0,2},{1,3},{2,6},{3,7},{4,0},{5,1},{6,4},{7,5},{8,10},{9,11},{10,... | collective-permute-start | bytes 4866056 | tf_op jit(solution)/shard_map/ppermute | solution.py:579
  183.5 31.4 %collective-permute-start.23 = (bf16[8,128,768]{2,1,0:T(8,128)(2,1)}, bf16[8,128,768]{2,1,0:T(8,128)(2,1)}, u32[]{:S(2)}, u32[]{:S(2)}) collective-permute-start(bf16[8,128,768]{2,1,0:T(8,128)(2,1)} %get-tuple-element.103), channel_id=1, source_target_pairs={{0,8},{1,9},{2,10},{3,11},{4,12},{5,13},{6,14},{7,15},{8,0},{9,1},... | collective-permute-start | bytes 4718600 | tf_op jit(solution)/shard_map/ppermute | solution.py:579
  184.1 41.2 %collective-permute-start.20 = (bf16[2,512,768]{2,1,0:T(8,128)(2,1)}, bf16[2,512,768]{2,1,0:T(8,128)(2,1)}, u32[]{:S(2)}, u32[]{:S(2)}) collective-permute-start(bf16[2,512,768]{2,1,0:T(8,128)(2,1)} %get-tuple-element.97.refs_4_.refs_6_), channel_id=1, source_target_pairs={{0,16},{1,17},{2,18},{3,19},{4,20},{5,21},{6,22},{7,23},{8,24},{9,... | collective-permute-start | bytes 4718600 | tf_op jit(solution)/shard_map/ppermute | solution.py:579
  184.5 40.8 %collective-permute-start.21 = (bf16[1040,512]{1,0:T(8,128)(2,1)}, bf16[1040,512]{1,0:T(8,128)(2,1)}, u32[]{:S(2)}, u32[]{:S(2)}) collective-permute-start(bf16[1040,512]{1,0:T(8,128)(2,1)} %get-tuple-element.98), channel_id=1, source_target_pairs={{0,9},{1,8},{2,11},{3,10},{4,13},{5,12},{6,15},{7,14},{8,1},{9,0},... | collective-permute-start | bytes 3194888 | tf_op jit(solution)/shard_map/ppermute | solution.py:579
  191.3 33.9 %collective-permute-start.22 = (bf16[528,512]{1,0:T(8,128)(2,1)}, bf16[528,512]{1,0:T(8,128)(2,1)}, u32[]{:S(2)}, u32[]{:S(2)}) collective-permute-start(bf16[528,512]{1,0:T(8,128)(2,1)} %get-tuple-element.101), channel_id=1, source_target_pairs={{0,1},{1,0},{2,3},{3,2},{4,5},{5,4},{6,7},{7,6},{8,9},{9,8},{10,11... | collective-permute-start | bytes 1622024 | tf_op jit(solution)/shard_map/ppermute | solution.py:579
  209.7 21.3 %collective-permute-start.19 = (bf16[1,512,768]{2,1,0:T(8,128)(2,1)}, bf16[1,512,768]{2,1,0:T(8,128)(2,1)}, u32[]{:S(2)}, u32[]{:S(2)}) collective-permute-start(bf16[1,512,768]{2,1,0:T(8,128)(2,1)} %cut.5), channel_id=1, source_target_pairs={{0,2},{1,3},{2,6},{3,7},{4,0},{5,1},{6,4},{7,5},{8,10},{9,11},{10,... | collective-permute-start | bytes 2359304 | tf_op jit(solution)/shard_map/ppermute | solution.py:579
  214.9 22.3 %collective-permute-start.14 = (bf16[1,512,768]{2,1,0:T(8,128)(2,1)}, bf16[1,512,768]{2,1,0:T(8,128)(2,1)}, u32[]{:S(2)}, u32[]{:S(2)}) collective-permute-start(bf16[1,512,768]{2,1,0:T(8,128)(2,1)} %cut.4), channel_id=1, source_target_pairs={{0,16},{1,17},{2,18},{3,19},{4,20},{5,21},{6,22},{7,23},{8,24},{9,... | collective-permute-start | bytes 2359304 | tf_op jit(solution)/shard_map/ppermute | solution.py:579
  225.3 11.9 %collective-permute-start.24 = (bf16[528,512]{1,0:T(8,128)(2,1)}, bf16[528,512]{1,0:T(8,128)(2,1)}, u32[]{:S(2)}, u32[]{:S(2)}) collective-permute-start(bf16[528,512]{1,0:T(8,128)(2,1)} %get-tuple-element.109), channel_id=1, source_target_pairs={{0,9},{1,8},{2,11},{3,10},{4,13},{5,12},{6,15},{7,14},{8,1},{9,0},... | collective-permute-start | bytes 1622024 | tf_op jit(solution)/shard_map/ppermute | solution.py:579
  237.2 7.5 %collective-permute-start.25 = (bf16[8,128,768]{2,1,0:T(8,128)(2,1)}, bf16[8,128,768]{2,1,0:T(8,128)(2,1)}, u32[]{:S(2)}, u32[]{:S(2)}) collective-permute-start(bf16[8,128,768]{2,1,0:T(8,128)(2,1)} %get-tuple-element.113), channel_id=1, source_target_pairs={{0,8},{1,9},{2,10},{3,11},{4,12},{5,13},{6,14},{7,15},{8,0},{9,1},... | collective-permute-start | bytes 4718600 | tf_op jit(solution)/shard_map/ppermute | solution.py:579
  238.0 19.9 %collective-permute-start.29 = (bf16[1040,512]{1,0:T(8,128)(2,1)}, bf16[1040,512]{1,0:T(8,128)(2,1)}, u32[]{:S(2)}, u32[]{:S(2)}) collective-permute-start(bf16[1040,512]{1,0:T(8,128)(2,1)} %get-tuple-element.119), channel_id=1, source_target_pairs={{0,8},{1,9},{2,10},{3,11},{4,12},{5,13},{6,14},{7,15},{8,0},{9,1},... | collective-permute-start | bytes 3194888 | tf_op jit(solution)/shard_map/ppermute | solution.py:579
  241.4 20.4 %collective-permute-start.28 = (bf16[544,512]{1,0:T(8,128)(2,1)}, bf16[544,512]{1,0:T(8,128)(2,1)}, u32[]{:S(2)}, u32[]{:S(2)}) collective-permute-start(bf16[544,512]{1,0:T(8,128)(2,1)} %get-tuple-element.115), channel_id=1, source_target_pairs={{0,9},{1,8},{2,11},{3,10},{4,13},{5,12},{6,15},{7,14},{8,1},{9,0},... | collective-permute-start | bytes 1671176 | tf_op jit(solution)/shard_map/ppermute | solution.py:579
  242.9 25.7 %collective-permute-start.27 = (bf16[544,512]{1,0:T(8,128)(2,1)}, bf16[544,512]{1,0:T(8,128)(2,1)}, u32[]{:S(2)}, u32[]{:S(2)}) collective-permute-start(bf16[544,512]{1,0:T(8,128)(2,1)} %get-tuple-element.112.refs_5_.refs_11_.refs_3_), channel_id=1, source_target_pairs={{0,1},{1,0},{2,3},{3,2},{4,5},{5,4},{6,7},{7,6},{8,9},{9,8},{10,11... | collective-permute-start | bytes 1671176 | tf_op jit(solution)/shard_map/ppermute | solution.py:579
  246.5 11.4 %collective-permute-start.30 = (bf16[528,512]{1,0:T(8,128)(2,1)}, bf16[528,512]{1,0:T(8,128)(2,1)}, u32[]{:S(2)}, u32[]{:S(2)}) collective-permute-start(bf16[528,512]{1,0:T(8,128)(2,1)} %get-tuple-element.120), channel_id=1, source_target_pairs={{0,8},{1,9},{2,10},{3,11},{4,12},{5,13},{6,14},{7,15},{8,0},{9,1},... | collective-permute-start | bytes 1622024 | tf_op jit(solution)/shard_map/ppermute | solution.py:579
  250.6 18.0 %collective-permute-start.26 = (bf16[528,512]{1,0:T(8,128)(2,1)}, bf16[528,512]{1,0:T(8,128)(2,1)}, u32[]{:S(2)}, u32[]{:S(2)}) collective-permute-start(bf16[528,512]{1,0:T(8,128)(2,1)} %get-tuple-element.114), channel_id=1, source_target_pairs={{0,8},{1,9},{2,10},{3,11},{4,12},{5,13},{6,14},{7,15},{8,0},{9,1},... | collective-permute-start | bytes 1622024 | tf_op jit(solution)/shard_map/ppermute | solution.py:579

commit v6 on v5

--- a/solution.py
+++ b/solution.py
@@ -49,8 +49,9 @@
 
 
 def plan_kernel(nz, cap, blk_dev, n_before, me, region, block, *refs):
-    at_slot, inv, count = refs[n_before:]
+    at_slot, inv, token, count = refs[n_before:]
     slots = nz * cap
+    token[...] = jnp.zeros(token.shape, F32)
 
     def clear(i, carry):
         inv[i] = -1
@@ -77,9 +78,10 @@
         out_shape=[
             jax.ShapeDtypeStruct(region.shape, I32),
             jax.ShapeDtypeStruct((4 * nz * cap,), I32),
+            jax.ShapeDtypeStruct((8, TILE), F32),
         ],
         in_specs=[SMEM, SMEM, SMEM] + [ANY] * len(before),
-        out_specs=[SMEM, SMEM],
+        out_specs=[SMEM, SMEM, VMEM],
         scratch_shapes=[pltpu.SMEM((4 * nz,), I32)],
         compiler_params=pltpu.CompilerParams(vmem_limit_bytes=VMEM_BYTES),
         cost_estimate=SHORT,
@@ -456,9 +458,12 @@
 
                 at += 1
 
+    def tail_rows(d):
+        return sources[d].shape[0] - spans[d][1] * TILE
+
     def tail_copy(d):
         return pltpu.make_async_copy(
-            sources[d].at[pl.ds(spans[d][1] * TILE, tail.shape[1])], tail.at[d], tail_sems.at[d]
+            sources[d].at[pl.ds(spans[d][1] * TILE, tail_rows(d))], tail.at[d, pl.ds(0, tail_rows(d))], tail_sems.at[d]
         )
 
     def bring(d, rows, t, at, k):
@@ -483,11 +488,10 @@
     values = []
     for d in range(n):
         if held_already[d]:
-            first = spans[d][1] * TILE
-            both = sources[d][pl.ds(first, min(32, sources[d].shape[0] - first))].astype(F32)
+            both = sources[d][pl.ds(spans[d][1] * TILE, tail_rows(d))].astype(F32)
         else:
             tail_copy(d).wait()
-            both = tail[d].astype(F32)
+            both = tail[d, pl.ds(0, tail_rows(d))].astype(F32)
         values.append(both if both.shape[0] == 16 else both[:16] + both[16:])
 
     def write(d, rows, t, at, k):
@@ -530,14 +534,61 @@
     )(inv, *sources, *before, *earlier)
 
 
-def cut_kernel(first, source, target, held, sem):
-    rows = pl.ds(0, BLOCK)
-    copy = pltpu.make_async_copy(source.at[pl.ds(first, target.shape[0]), rows], held, sem)
-    copy.start()
-    copy.wait()
-    copy = pltpu.make_async_copy(held, target.at[pl.ds(0, target.shape[0]), rows], sem)
-    copy.start()
-    copy.wait()
+def cut_kernel(first, source, target, held, in_sems, out_sems):
+    step = BLOCK // 4
+    runs = [(i, pl.ds(j * step, step)) for i in range(target.shape[0]) for j in range(4)]
+    brought = [
+        pltpu.make_async_copy(source.at[first + i, rows], held.at[i, rows], in_sems.at[n])
+        for n, (i, rows) in enumerate(runs)
+    ]
+    sent = [
+        pltpu.make_async_copy(held.at[i, rows], target.at[i, rows], out_sems.at[n])
+        for n, (i, rows) in enumerate(runs)
+    ]
+    for copy in brought:
+        copy.start()
+    for arrived, copy in zip(brought, sent):
+        arrived.wait()
+        copy.start()
+    for copy in sent:
+        copy.wait()
+
+
+def own_kernel(blocks, source, *refs):
+    pieces, (held, in_sems, out_sems) = refs[:-3], refs[-3:]
+    total = blocks * len(pieces)
+    first = (lax.axis_index("parts") & 1) * total
+    brought = [
+        pltpu.make_async_copy(source.at[first + i], held.at[i], in_sems.at[i]) for i in range(total)
+    ]
+    sent = [
+        pltpu.make_async_copy(held.at[i], pieces[i // blocks].at[i % blocks], out_sems.at[i]) for i in range(total)
+    ]
+    for copy in brought:
+        copy.start()
+    for arrived, copy in zip(brought, sent):
+        arrived.wait()
+        copy.start()
+    for copy in sent:
+        copy.wait()
+
+
+def own_pieces(source, pieces, blocks):
+    total = pieces * blocks
+    return pl.pallas_call(
+        functools.partial(own_kernel, blocks),
+        out_shape=[jax.ShapeDtypeStruct((blocks, BLOCK, D), BF16)] * pieces,
+        in_specs=[ANY],
+        out_specs=[ANY] * pieces,
+        scratch_shapes=[
+            pltpu.VMEM((total, BLOCK, D), BF16),
+            pltpu.SemaphoreType.DMA((total,)),
+            pltpu.SemaphoreType.DMA((total,)),
+        ],
+        compiler_params=pltpu.CompilerParams(vmem_limit_bytes=VMEM_BYTES),
+        cost_estimate=SHORT,
+        name="own_pieces",
+    )(source)
 
 
 def cut(source, first, count, rows=BLOCK):
@@ -546,7 +597,11 @@
         out_shape=jax.ShapeDtypeStruct((count, rows, D), BF16),
         in_specs=[ANY],
         out_specs=ANY,
-        scratch_shapes=[pltpu.VMEM((count, BLOCK, D), BF16), pltpu.SemaphoreType.DMA],
+        scratch_shapes=[
+            pltpu.VMEM((count, BLOCK, D), BF16),
+            pltpu.SemaphoreType.DMA((4 * count,)),
+            pltpu.SemaphoreType.DMA((4 * count,)),
+        ],
         compiler_params=pltpu.CompilerParams(vmem_limit_bytes=VMEM_BYTES),
         cost_estimate=SHORT,
         name="cut",
@@ -586,16 +641,13 @@
 
     local = centers[0].reshape(blk_dev, BLOCK, D)
 
-    def own_piece(i, half):
-        return lax.dynamic_slice_in_dim(local, half * half_blocks + i * sub_blocks, sub_blocks, 0)
-
-    own = [own_piece(i, half) for i in range(pieces)]
+    own = own_pieces(local, pieces, sub_blocks)
     tile_rows = vectors.reshape(tile_dev, TILE, D)
     scalars = jnp.pad(jnp.stack([tile_region, tile_block]), ((0, 6), (0, TILE - tile_dev)))
     pack = jnp.concatenate(
         [primary_pick.reshape(tile_dev, TILE), spill_pick.reshape(tile_dev, TILE), scalars]
     )
-    at_slot, inv = plan(me, tile_region, tile_block, own, nz, cap, blk_dev)
+    at_slot, inv, token = plan(me, tile_region, tile_block, own, nz, cap, blk_dev)
 
     def exchange(value, partner):
         if partner == 0:
@@ -709,7 +761,7 @@
                 at_once.setdefault(ready, []).append((d, group, min(last, max(done, ready + 1))))
     opens.setdefault(last - 1, []).append(("s", 1, one))
     first_late = (pieces - 1) * sub_blocks
-    env["token"] = jnp.zeros((8, TILE), F32)
+    env["token"] = token
     for k in range(last + 1):
         if k:
             passed = waits.get(k, []) + opens.get(k, [])
@@ -736,12 +788,11 @@
             env["r", d, group] = exchange(env["s", d, group], d)
             waits.setdefault(done, []).append(("r", d, group))
         if k == last - 1:
-            score([(d, three) for d in (2, 3, 0)], (first_late, False), extra=[env["token"]])
+            score([(d, three) for d in (2, 3)], (first_late, False), extra=[env["token"]])
     score([(2, three), (3, three)], (first_late, True), True, [env["token"]])
     for d in (2, 3):
         env["r", d, three] = exchange(env["s", d, three], d)
-    score([(0, three)], (first_late, True), True, [env["s", 2, three]])
-    score([(1, two), (1, three)], extra=[env["s", 2, three]])
+    score([(1, two), (1, three), (0, three)], extra=[env["s", 2, three]])
     for group in (one, two, three):
         env["r", 1, group] = exchange(env["s", 1, group], 1)
     outputs = place([(0, one), (2, one), (3, one)], [], [env["s", 2, three]])

time: 275 us -> 276 us (level)
  Pallas kernels: 76.5 us -> 91.6 us
  waiting for transfers between devices: 136 us -> 131 us
  local copies, waits for them, and re-layouts: 5.01 us -> 0.63 us
  starting transfers between devices: 52.7 us -> 49.4 us
    pallas_call x7 -> x6, Pallas kernels: 43.6 us -> 55.1 us  [score_call(): pl.pallas_call(functools.partial(score_kernel, nz, cap, blk_dev, places,...]
    ppermute x31, waiting for transfers between devices: 136 us -> 131 us  [permute(): lax.ppermute(value, AXES, [(device(*a), device(*target(*a))) for a in eve...]
    dynamic_slice x1 -> x0, local copies, waits for them, and re-layouts: 3.78 us -> none  [own_piece(): lax.dynamic_slice_in_dim(local, half * half_blocks + i * sub_blocks, sub_...]
    ppermute x31, starting transfers between devices: 52.7 us -> 49.4 us  [permute(): lax.ppermute(value, AXES, [(device(*a), device(*target(*a))) for a in eve...]
    pallas_call x0 -> x1, Pallas kernels: none -> 2.9 us  [own_pieces(): pl.pallas_call(functools.partial(own_kernel, blocks), out_shape=[jax.Shap...]
  transfers between devices with their start and end apart: 31 -> 31, of which waited for: 11 -> 11; matrix products, arithmetic and copies ran while one was open for 0% -> 0% of each run, Pallas kernels for 27% -> 31%
where the time goes in v6:
time: 276 us; the launch traced here: 274 us
  waiting for transfers between devices  131 us (47%)
  Pallas kernels  91.6 us (33%)
  starting transfers between devices  49.4 us (18%)
    ppermute x31, waiting for transfers between devices, permute(): lax.ppermute(value, AXES, [(device(*a), device(*target(*a))) for a in eve...  131 us
    pallas_call x6, Pallas kernels, score_call(): pl.pallas_call(functools.partial(score_kernel, nz, cap, blk_dev, places,...  55.1 us
    ppermute x31, starting transfers between devices, permute(): lax.ppermute(value, AXES, [(device(*a), device(*target(*a))) for a in eve...  49.4 us
    pallas_call x3, Pallas kernels, assemble(): pl.pallas_call(functools.partial(assemble_kernel, spans, held_already, le...  12.1 us
    pallas_call x1, Pallas kernels, receive(): pl.pallas_call(functools.partial(receive_kernel, nz, cap, blk_dev, tile_d...  7.38 us
    pallas_call x3, Pallas kernels, cut(): pl.pallas_call(functools.partial(cut_kernel, first), out_shape=jax.ShapeD...  6.2 us
  transfers between devices with their start and end apart: 31, of which 11 were waited for; matrix products, arithmetic and copies ran while one was open for 0% of the time, Pallas kernels for 31%

profile of v6, /device:TPU:9, one launch (start us, length us, event | category | flops | bytes accessed | tf_op | source)
XLA Modules:
  0.0 274.0 jit_solution(12497928284692392715)
XLA Ops:
  0.7 2.9 %own_pieces.1 = (bf16[2,512,768]{2,1,0:T(8,128)(2,1)}, bf16[2,512,768]{2,1,0:T(8,128)(2,1)}) custom-call(bf16[8,512,768]{2,1,0:T(8,128)(2,1)} %bitcast.13), custom_call_target="tpu_custom_call" | custom-call | flops 1 | bytes 1 | tf_op jit(solution)/shard_map/own_pieces/pallas_call | solution.py:578
  3.6 2.4 collective-permute-start.4
  6.0 2.1 collective-permute-start.2
  9.4 2.9 %plan.1 = (s32[32]{0:T(128)}, s32[64]{0:T(128)}, f32[8,128]{1,0:T(8,128)}) custom-call(s32[4]{0:T(128)} %pad_add_fusion.2.me, s32[32]{0:T(128)} %region.1, s32[32]{0:T(128)} %block.1, bf16[2,512,768]{2,1,0:T(8,128)(2,1)} %get-tuple-element.71.refs_0_, bf16[2,512,768]{2,1,0:T(8,128)(2,1)} %get-tuple-element.72.refs_1_), custom_call_target="tpu_custom_call" | custom-call | flops 1 | bytes 1 | tf_op jit(solution)/shard_map/plan/pallas_call | solution.py:76
  13.0 5.0 %dispatch.1 = (bf16[8,128,768]{2,1,0:T(8,128)(2,1)}, bf16[8,128,768]{2,1,0:T(8,128)(2,1)}, bf16[8,128,768]{2,1,0:T(8,128)(2,1)}, bf16[8,128,768]{2,1,0:T(8,128)(...) custom-call(s32[32]{0:T(128)} %get-tuple-element.76.at_slot, bf16[32,128,768]{2,1,0:T(8,128)(2,1)} %bitcast.20, ...), custom_call_target="tpu_custom_call" | custom-call | flops 1 | bytes 1 | tf_op jit(solution)/shard_map/dispatch/pallas_call | solution.py:199
  18.0 1.7 collective-permute-start.7
  19.7 19.6 %collective-permute-done.4.refs_0_ = bf16[2,512,768]{2,1,0:T(8,128)(2,1)} collective-permute-done((bf16[2,512,768]{2,1,0:T(8,128)(2,1)}, bf16[2,512,768]{2,1,0:T(8,128)(2,1)}, u32[]{:S(2)}, u32[]{:S(2)}) %collective-permute-start.4) | collective-permute-done | bytes 1572896 | tf_op jit(solution)/shard_map/ppermute | solution.py:634
  39.3 1.2 collective-permute-start.8
  40.5 4.1 %collective-permute-start.3 = (bf16[8,128,768]{2,1,0:T(8,128)(2,1)}, bf16[8,128,768]{2,1,0:T(8,128)(2,1)}, u32[]{:S(2)}, u32[]{:S(2)}) collective-permute-start(bf16[8,128,768]{2,1,0:T(8,128)(2,1)} %get-tuple-element.77), channel_id=1, source_target_pairs={{0,9},{1,8},{2,11},{3,10},{4,13},{5,12},{6,15},{7,14},{8,1},{9,0},... | collective-permute-start | bytes 4718600 | tf_op jit(solution)/shard_map/ppermute | solution.py:634
  44.6 3.1 %collective-permute-start.5 = (bf16[2,512,768]{2,1,0:T(8,128)(2,1)}, bf16[2,512,768]{2,1,0:T(8,128)(2,1)}, u32[]{:S(2)}, u32[]{:S(2)}) collective-permute-start(bf16[2,512,768]{2,1,0:T(8,128)(2,1)} %get-tuple-element.79.refs_4_.refs_2_), channel_id=1, source_target_pairs={{0,2},{1,3},{2,6},{3,7},{4,0},{5,1},{6,4},{7,5},{8,10},{9,11},{10,... | collective-permute-start | bytes 4718600 | tf_op jit(solution)/shard_map/ppermute | solution.py:634
  47.7 25.3 %collective-permute-done.6.refs_0_ = bf16[2,512,768]{2,1,0:T(8,128)(2,1)} collective-permute-done((bf16[2,512,768]{2,1,0:T(8,128)(2,1)}, bf16[2,512,768]{2,1,0:T(8,128)(2,1)}, u32[]{:S(2)}, u32[]{:S(2)}) %collective-permute-start.6) | collective-permute-done | bytes 1572896 | tf_op jit(solution)/shard_map/ppermute | solution.py:634
  73.0 1.2 collective-permute-start.9
  74.3 3.2 %collective-permute-start.12 = (bf16[2,512,768]{2,1,0:T(8,128)(2,1)}, bf16[2,512,768]{2,1,0:T(8,128)(2,1)}, u32[]{:S(2)}, u32[]{:S(2)}) collective-permute-start(bf16[2,512,768]{2,1,0:T(8,128)(2,1)} %get-tuple-element.83.refs_6_.refs_4_), channel_id=1, source_target_pairs={{0,2},{1,3},{2,6},{3,7},{4,0},{5,1},{6,4},{7,5},{8,10},{9,11},{10,... | collective-permute-start | bytes 4718600 | tf_op jit(solution)/shard_map/ppermute | solution.py:634
  77.4 1.2 collective-permute-start.13
  78.7 11.6 %collective-permute-done.3.refs_0_ = bf16[8,128,768]{2,1,0:T(8,128)(2,1)} collective-permute-done((bf16[8,128,768]{2,1,0:T(8,128)(2,1)}, bf16[8,128,768]{2,1,0:T(8,128)(2,1)}, u32[]{:S(2)}, u32[]{:S(2)}) %collective-permute-start.3) | collective-permute-done | bytes 1572896 | tf_op jit(solution)/shard_map/ppermute | solution.py:634
  90.2 16.5 %collective-permute-done.5.refs_1_ = bf16[2,512,768]{2,1,0:T(8,128)(2,1)} collective-permute-done((bf16[2,512,768]{2,1,0:T(8,128)(2,1)}, bf16[2,512,768]{2,1,0:T(8,128)(2,1)}, u32[]{:S(2)}, u32[]{:S(2)}) %collective-permute-start.5) | collective-permute-done | bytes 1572896 | tf_op jit(solution)/shard_map/ppermute | solution.py:634
  106.7 1.2 collective-permute-start.14
  108.0 7.4 %receive.1 = (s32[64,8,128]{2,1,0:T(8,128)}, s32[64]{0:T(128)}) custom-call(s32[4]{0:T(128)} %pad_add_fusion.2.me, s32[72,128]{1,0:T(8,128)} %copy-done, s32[72,128]{1,0:T(8,128)} %copy-done.3, s32[72,128]{1,0:T(8,128)} %copy-done.2, s32[72,128]{1,0:T(8,128)} %copy-done.1), custom_call_target="tpu_custom_call" | custom-call | flops 1 | bytes 1 | tf_op jit(solution)/shard_map/receive/pallas_call | solution.py:139
  115.3 3.1 %collective-permute-start.10 = (bf16[2,512,768]{2,1,0:T(8,128)(2,1)}, bf16[2,512,768]{2,1,0:T(8,128)(2,1)}, u32[]{:S(2)}, u32[]{:S(2)}) collective-permute-start(bf16[2,512,768]{2,1,0:T(8,128)(2,1)} %get-tuple-element.86.refs_4_.refs_3_), channel_id=1, source_target_pairs={{0,2},{1,3},{2,6},{3,7},{4,0},{5,1},{6,4},{7,5},{8,10},{9,11},{10,... | collective-permute-start | bytes 4718600 | tf_op jit(solution)/shard_map/ppermute | solution.py:634
  118.5 5.0 %collective-permute-start.11 = (bf16[8,128,768]{2,1,0:T(8,128)(2,1)}, bf16[8,128,768]{2,1,0:T(8,128)(2,1)}, u32[]{:S(2)}, u32[]{:S(2)}) collective-permute-start(bf16[8,128,768]{2,1,0:T(8,128)(2,1)} %get-tuple-element.87), channel_id=1, source_target_pairs={{0,9},{1,8},{2,11},{3,10},{4,13},{5,12},{6,15},{7,14},{8,1},{9,0},... | collective-permute-start | bytes 4718600 | tf_op jit(solution)/shard_map/ppermute | solution.py:634
  123.5 12.6 %score.6 = (bf16[1040,512]{1,0:T(8,128)(2,1)}, bf16[1040,512]{1,0:T(8,128)(2,1)}, bf16[1040,512]{1,0:T(8,128)(2,1)}) custom-call(s32[4]{0:T(128)} %pad_add_fusion.2.me, s32[64]{0:T(128)} %get-tuple-element.74.ids, s32[64]{0:T(128)} %get-tuple-element.73.inv, s32[64,8,128]{2,1,0:T(8,128)} %get-tuple-element.75.meta, ...), custom_call_target="tpu_custom_call" | custom-call | flops 1 | bytes 1 | tf_op jit(solution)/shard_map/score/pallas_call | solution.py:411
  136.1 4.4 %collective-permute-done.12.refs_0_ = bf16[2,512,768]{2,1,0:T(8,128)(2,1)} collective-permute-done((bf16[2,512,768]{2,1,0:T(8,128)(2,1)}, bf16[2,512,768]{2,1,0:T(8,128)(2,1)}, u32[]{:S(2)}, u32[]{:S(2)}) %collective-permute-start.12) | collective-permute-done | bytes 1572896 | tf_op jit(solution)/shard_map/ppermute | solution.py:634
  140.4 1.2 collective-permute-start.15
  141.7 1.2 collective-permute-start.16
  142.9 2.3 cut.3
  145.2 3.2 %collective-permute-start.22 = (bf16[2,528,768]{2,1,0:T(8,128)(2,1)}, bf16[2,528,768]{2,1,0:T(8,128)(2,1)}, u32[]{:S(2)}, u32[]{:S(2)}) collective-permute-start(bf16[2,528,768]{2,1,0:T(8,128)(2,1)} %cut.3), channel_id=1, source_target_pairs={{0,2},{1,3},{2,6},{3,7},{4,0},{5,1},{6,4},{7,5},{8,10},{9,11},{10,... | collective-permute-start | bytes 4866056 | tf_op jit(solution)/shard_map/ppermute | solution.py:634
  148.4 10.7 %collective-permute-done.11.refs_1_ = bf16[8,128,768]{2,1,0:T(8,128)(2,1)} collective-permute-done((bf16[8,128,768]{2,1,0:T(8,128)(2,1)}, bf16[8,128,768]{2,1,0:T(8,128)(2,1)}, u32[]{:S(2)}, u32[]{:S(2)}) %collective-permute-start.11) | collective-permute-done | bytes 1572896 | tf_op jit(solution)/shard_map/ppermute | solution.py:634
  159.0 15.1 %collective-permute-done.10.refs_0_ = bf16[2,512,768]{2,1,0:T(8,128)(2,1)} collective-permute-done((bf16[2,512,768]{2,1,0:T(8,128)(2,1)}, bf16[2,512,768]{2,1,0:T(8,128)(2,1)}, u32[]{:S(2)}, u32[]{:S(2)}) %collective-permute-start.10) | collective-permute-done | bytes 1572896 | tf_op jit(solution)/shard_map/ppermute | solution.py:634
  174.2 7.7 %collective-permute-done.16.refs_3_ = bf16[1040,512]{1,0:T(8,128)(2,1)} collective-permute-done((bf16[1040,512]{1,0:T(8,128)(2,1)}, bf16[1040,512]{1,0:T(8,128)(2,1)}, u32[]{:S(2)}, u32[]{:S(2)}) %collective-permute-start.16) | collective-permute-done | bytes 1064992 | tf_op jit(solution)/shard_map/ppermute | solution.py:634
  183.1 11.9 %score.7 = (bf16[528,512]{1,0:T(8,128)(2,1)}, bf16[528,512]{1,0:T(8,128)(2,1)}, bf16[528,512]{1,0:T(8,128)(2,1)}) custom-call(s32[4]{0:T(128)} %pad_add_fusion.2.me, s32[64]{0:T(128)} %get-tuple-element.74.ids, s32[64]{0:T(128)} %get-tuple-element.73.inv, s32[64,8,128]{2,1,0:T(8,128)} %get-tuple-element.75.meta, ...), custom_call_target="tpu_custom_call" | custom-call | flops 1 | bytes 1 | tf_op jit(solution)/shard_map/score/pallas_call | solution.py:411
  195.0 1.2 collective-permute-start.19
  196.2 1.9 cut.5
  198.2 10.7 %collective-permute-done.22.source.refs_5_.refs_9_ = bf16[2,528,768]{2,1,0:T(8,128)(2,1)} collective-permute-done((bf16[2,528,768]{2,1,0:T(8,128)(2,1)}, bf16[2,528,768]{2,1,0:T(8,128)(2,1)}, u32[]{:S(2)}, u32[]{:S(2)}) %collective-permute-start.22) | collective-permute-done | bytes 1622048 | tf_op jit(solution)/shard_map/ppermute | solution.py:634
  208.9 3.1 %collective-permute-start.24 = (bf16[1,512,768]{2,1,0:T(8,128)(2,1)}, bf16[1,512,768]{2,1,0:T(8,128)(2,1)}, u32[]{:S(2)}, u32[]{:S(2)}) collective-permute-start(bf16[1,512,768]{2,1,0:T(8,128)(2,1)} %cut.5), channel_id=1, source_target_pairs={{0,2},{1,3},{2,6},{3,7},{4,0},{5,1},{6,4},{7,5},{8,10},{9,11},{10,... | collective-permute-start | bytes 2359304 | tf_op jit(solution)/shard_map/ppermute | solution.py:634
  212.0 2.0 cut.4
  214.0 1.3 collective-permute-start.23
  215.3 6.1 %score.8.refs_4_ = bf16[1040,512]{1,0:T(8,128)(2,1)} custom-call(s32[4]{0:T(128)} %pad_add_fusion.2.me, s32[64]{0:T(128)} %get-tuple-element.74.ids, s32[64]{0:T(128)} %get-tuple-element.73.inv, s32[64,8,128]{2,1,0:T(8,128)} %get-tuple-element.75.meta, bf16[8,128,768]{2,1,0:T(8,128)(2,1)} %collective-permute-done.20.refs_0_, bf16[8,512,768]{2,1,0:T(8,128)(2,1)} %bitcast.16, ...), custom_call_target="tpu_custom_call" | custom-call | flops 1 | bytes 1 | tf_op jit(solution)/shard_map/score/pallas_call | solution.py:411
  221.4 3.3 %collective-permute-start.21 = (bf16[528,512]{1,0:T(8,128)(2,1)}, bf16[528,512]{1,0:T(8,128)(2,1)}, u32[]{:S(2)}, u32[]{:S(2)}) collective-permute-start(bf16[528,512]{1,0:T(8,128)(2,1)} %get-tuple-element.110), channel_id=1, source_target_pairs={{0,9},{1,8},{2,11},{3,10},{4,13},{5,12},{6,15},{7,14},{8,1},{9,0},... | collective-permute-start | bytes 1622024 | tf_op jit(solution)/shard_map/ppermute | solution.py:634
  224.7 6.2 %score.9 = (bf16[544,512]{1,0:T(8,128)(2,1)}, bf16[544,512]{1,0:T(8,128)(2,1)}) custom-call(s32[4]{0:T(128)} %pad_add_fusion.2.me, s32[64]{0:T(128)} %get-tuple-element.74.ids, s32[64]{0:T(128)} %get-tuple-element.73.inv, s32[64,8,128]{2,1,0:T(8,128)} %get-tuple-element.75.meta, bf16[8,128,768]{2,1,0:T(8,128)(2,1)} %get-tuple-element.102.refs_0_, ...), custom_call_target="tpu_custom_call" | custom-call | flops 1 | bytes 1 | tf_op jit(solution)/shard_map/score/pallas_call | solution.py:411
  231.0 4.3 %collective-permute-done.23.refs_3_.refs_10_ = bf16[1,512,768]{2,1,0:T(8,128)(2,1)} collective-permute-done((bf16[1,512,768]{2,1,0:T(8,128)(2,1)}, bf16[1,512,768]{2,1,0:T(8,128)(2,1)}, u32[]{:S(2)}, u32[]{:S(2)}) %collective-permute-start.23) | collective-permute-done | bytes 786464 | tf_op jit(solution)/shard_map/ppermute | solution.py:634
  235.3 1.0 collective-permute-start.25
  236.3 6.2 %score.10 = (bf16[544,512]{1,0:T(8,128)(2,1)}, bf16[544,512]{1,0:T(8,128)(2,1)}) custom-call(s32[4]{0:T(128)} %pad_add_fusion.2.me, s32[64]{0:T(128)} %get-tuple-element.74.ids, s32[64]{0:T(128)} %get-tuple-element.73.inv, s32[64,8,128]{2,1,0:T(8,128)} %get-tuple-element.75.meta, ...), custom_call_target="tpu_custom_call", output_to_operand_aliasing={{0}: (9, {}), {1}: (10, {})} | custom-call | flops 1 | bytes 1 | tf_op jit(solution)/shard_map/score/pallas_call | solution.py:411
  242.6 1.8 collective-permute-start.27
  244.3 12.2 %score.11 = (bf16[528,512]{1,0:T(8,128)(2,1)}, bf16[528,512]{1,0:T(8,128)(2,1)}, bf16[528,512]{1,0:T(8,128)(2,1)}) custom-call(s32[4]{0:T(128)} %pad_add_fusion.2.me, s32[64]{0:T(128)} %get-tuple-element.74.ids, s32[64]{0:T(128)} %get-tuple-element.73.inv, s32[64,8,128]{2,1,0:T(8,128)} %get-tuple-element.75.meta, ...), custom_call_target="tpu_custom_call" | custom-call | flops 1 | bytes 1 | tf_op jit(solution)/shard_map/score/pallas_call | solution.py:411
  257.1 3.7 %assemble.3 = (bf16[32,128,512]{2,1,0:T(8,128)(2,1)}, f32[32,128]{1,0:T(8,128)}, f32[32,128]{1,0:T(8,128)}) custom-call(s32[64]{0:T(128)} %get-tuple-element.73.inv, bf16[1040,512]{1,0:T(8,128)(2,1)} %get-tuple-element.127.refs_0_, bf16[1040,512]{1,0:T(8,128)(2,1)} %get-tuple-element.128.refs_1_, bf16[1040,512]{1,0:T(8,128)(2,1)} %get-tuple-element.129.refs_2_, ...), custom_call_target="tpu_custom_call" | custom-call | flops 1 | bytes 1 | tf_op jit(solution)/shard_map/assemble/pallas_call | solution.py:512
  260.8 4.0 %assemble.4 = (bf16[32,128,512]{2,1,0:T(8,128)(2,1)}, f32[32,128]{1,0:T(8,128)}, f32[32,128]{1,0:T(8,128)}) custom-call(s32[64]{0:T(128)} %get-tuple-element.73.inv, bf16[528,512]{1,0:T(8,128)(2,1)} %get-tuple-element.122.refs_0_, bf16[528,512]{1,0:T(8,128)(2,1)} %get-tuple-element.123.refs_1_, ...), custom_call_target="tpu_custom_call", output_to_operand_aliasing={{0}: (6, {})} | custom-call | flops 1 | bytes 1 | tf_op jit(solution)/shard_map/assemble/pallas_call | solution.py:512
  264.8 4.7 %collective-permute-done.27.refs_2_ = bf16[544,512]{1,0:T(8,128)(2,1)} collective-permute-done((bf16[544,512]{1,0:T(8,128)(2,1)}, bf16[544,512]{1,0:T(8,128)(2,1)}, u32[]{:S(2)}, u32[]{:S(2)}) %collective-permute-start.27) | collective-permute-done | bytes 557088 | tf_op jit(solution)/shard_map/ppermute | solution.py:634
  269.5 4.4 %assemble.5 = (bf16[32,128,512]{2,1,0:T(8,128)(2,1)}, bf16[32,128]{1,0:T(8,128)(2,1)}, bf16[32,128]{1,0:T(8,128)(2,1)}) custom-call(s32[64]{0:T(128)} %get-tuple-element.73.inv, bf16[528,512]{1,0:T(8,128)(2,1)} %get-tuple-element.119.refs_8_.refs_0_, bf16[528,512]{1,0:T(8,128)(2,1)} %collective-permute-done.26.refs_1_, ...), custom_call_target="tpu_custom_call", output_to_operand_aliasing={{0}: (5, {})} | custom-call | flops 1 | bytes 1 | tf_op jit(solution)/shard_map/assemble/pallas_call | solution.py:512
  (56 shorter events, 3.8 us)
Async XLA Ops:
  0.6 5.3 %copy-start.6 = (s32[32]{0:T(128)S(1)}, s32[32]{0:T(128)}, u32[]{:S(2)}) copy-start(s32[32]{0:T(128)} %region.1) | copy-start | bytes 388
  0.6 5.3 %copy-start.7 = (s32[32]{0:T(128)S(1)}, s32[32]{0:T(128)}, u32[]{:S(2)}) copy-start(s32[32]{0:T(128)} %block.1) | copy-start | bytes 388
  0.7 5.3 %copy-start.4 = (s32[4096]{0:T(1024)S(1)}, s32[4096]{0:T(1024)}, u32[]{:S(2)}) copy-start(s32[4096]{0:T(1024)} %param.10) | copy-start | bytes 49156
  0.7 5.3 %copy-start.5 = (s32[4096]{0:T(1024)S(1)}, s32[4096]{0:T(1024)}, u32[]{:S(2)}) copy-start(s32[4096]{0:T(1024)} %param.9) | copy-start | bytes 49156
  3.6 35.7 %collective-permute-start.4 = (bf16[2,512,768]{2,1,0:T(8,128)(2,1)}, bf16[2,512,768]{2,1,0:T(8,128)(2,1)}, u32[]{:S(2)}, u32[]{:S(2)}) collective-permute-start(bf16[2,512,768]{2,1,0:T(8,128)(2,1)} %get-tuple-element.71.refs_0_), channel_id=1, source_target_pairs={{0,2},{1,3},{2,6},{3,7},{4,0},{5,1},{6,4},{7,5},{8,10},{9,11},{10,... | collective-permute-start | bytes 4718600 | tf_op jit(solution)/shard_map/ppermute | solution.py:634
  6.0 6.3 %copy-start = (s32[72,128]{1,0:T(8,128)}, s32[72,128]{1,0:T(8,128)S(1)}, u32[]{:S(2)}) copy-start(s32[72,128]{1,0:T(8,128)S(1)} %pad_add_fusion.refs_0_) | copy-start | bytes 110596
  6.0 6.3 %collective-permute-start.2 = (s32[72,128]{1,0:T(8,128)S(1)}, s32[72,128]{1,0:T(8,128)S(1)}, u32[]{:S(2)}, u32[]{:S(2)}) collective-permute-start(s32[72,128]{1,0:T(8,128)S(1)} %pad_add_fusion.refs_0_), channel_id=1, source_target_pairs={{0,9},{1,8},{2,11},{3,10},{4,13},{5,12},{6,15},{7,14},{8,1},{9,0},... | collective-permute-start | bytes 110600 | tf_op jit(solution)/shard_map/ppermute | solution.py:634
  8.2 4.2 %collective-permute-start.1 = (s32[72,128]{1,0:T(8,128)S(1)}, s32[72,128]{1,0:T(8,128)S(1)}, u32[]{:S(2)}, u32[]{:S(2)}) collective-permute-start(s32[72,128]{1,0:T(8,128)S(1)} %pad_add_fusion.refs_0_), channel_id=1, source_target_pairs={{0,1},{1,0},{2,3},{3,2},{4,5},{5,4},{6,7},{7,6},{8,9},{9,8},{10,11... | collective-permute-start | bytes 110600 | tf_op jit(solution)/shard_map/ppermute | solution.py:634
  8.4 4.0 %collective-permute-start = (s32[72,128]{1,0:T(8,128)S(1)}, s32[72,128]{1,0:T(8,128)S(1)}, u32[]{:S(2)}, u32[]{:S(2)}) collective-permute-start(s32[72,128]{1,0:T(8,128)S(1)} %pad_add_fusion.refs_0_), channel_id=1, source_target_pairs={{0,8},{1,9},{2,10},{3,11},{4,12},{5,13},{6,14},{7,15},{8,0},{9,1},... | collective-permute-start | bytes 110600 | tf_op jit(solution)/shard_map/ppermute | solution.py:634
  9.2 63.8 %collective-permute-start.6 = (bf16[2,512,768]{2,1,0:T(8,128)(2,1)}, bf16[2,512,768]{2,1,0:T(8,128)(2,1)}, u32[]{:S(2)}, u32[]{:S(2)}) collective-permute-start(bf16[2,512,768]{2,1,0:T(8,128)(2,1)} %get-tuple-element.72.refs_1_), channel_id=1, source_target_pairs={{0,2},{1,3},{2,6},{3,7},{4,0},{5,1},{6,4},{7,5},{8,10},{9,11},{10,... | collective-permute-start | bytes 4718600 | tf_op jit(solution)/shard_map/ppermute | solution.py:634
  12.4 0.6 copy-start.1
  12.4 0.6 copy-start.2
  12.4 0.6 copy-start.3
  18.0 55.1 %collective-permute-start.7 = (bf16[8,128,768]{2,1,0:T(8,128)(2,1)}, bf16[8,128,768]{2,1,0:T(8,128)(2,1)}, u32[]{:S(2)}, u32[]{:S(2)}) collective-permute-start(bf16[8,128,768]{2,1,0:T(8,128)(2,1)} %get-tuple-element.80), channel_id=1, source_target_pairs={{0,1},{1,0},{2,3},{3,2},{4,5},{5,4},{6,7},{7,6},{8,9},{9,8},{10,11... | collective-permute-start | bytes 4718600 | tf_op jit(solution)/shard_map/ppermute | solution.py:634
  39.3 33.7 %collective-permute-start.8 = (bf16[2,512,768]{2,1,0:T(8,128)(2,1)}, bf16[2,512,768]{2,1,0:T(8,128)(2,1)}, u32[]{:S(2)}, u32[]{:S(2)}) collective-permute-start(bf16[2,512,768]{2,1,0:T(8,128)(2,1)} %get-tuple-element.79.refs_4_.refs_2_), channel_id=1, source_target_pairs={{0,16},{1,17},{2,18},{3,19},{4,20},{5,21},{6,22},{7,23},{8,24},{9,... | collective-permute-start | bytes 4718600 | tf_op jit(solution)/shard_map/ppermute | solution.py:634
  40.5 49.7 %collective-permute-start.3 = (bf16[8,128,768]{2,1,0:T(8,128)(2,1)}, bf16[8,128,768]{2,1,0:T(8,128)(2,1)}, u32[]{:S(2)}, u32[]{:S(2)}) collective-permute-start(bf16[8,128,768]{2,1,0:T(8,128)(2,1)} %get-tuple-element.77), channel_id=1, source_target_pairs={{0,9},{1,8},{2,11},{3,10},{4,13},{5,12},{6,15},{7,14},{8,1},{9,0},... | collective-permute-start | bytes 4718600 | tf_op jit(solution)/shard_map/ppermute | solution.py:634
  44.6 62.1 %collective-permute-start.5 = (bf16[2,512,768]{2,1,0:T(8,128)(2,1)}, bf16[2,512,768]{2,1,0:T(8,128)(2,1)}, u32[]{:S(2)}, u32[]{:S(2)}) collective-permute-start(bf16[2,512,768]{2,1,0:T(8,128)(2,1)} %get-tuple-element.79.refs_4_.refs_2_), channel_id=1, source_target_pairs={{0,2},{1,3},{2,6},{3,7},{4,0},{5,1},{6,4},{7,5},{8,10},{9,11},{10,... | collective-permute-start | bytes 4718600 | tf_op jit(solution)/shard_map/ppermute | solution.py:634
  73.0 33.7 %collective-permute-start.9 = (bf16[2,512,768]{2,1,0:T(8,128)(2,1)}, bf16[2,512,768]{2,1,0:T(8,128)(2,1)}, u32[]{:S(2)}, u32[]{:S(2)}) collective-permute-start(bf16[2,512,768]{2,1,0:T(8,128)(2,1)} %get-tuple-element.83.refs_6_.refs_4_), channel_id=1, source_target_pairs={{0,16},{1,17},{2,18},{3,19},{4,20},{5,21},{6,22},{7,23},{8,24},{9,... | collective-permute-start | bytes 4718600 | tf_op jit(solution)/shard_map/ppermute | solution.py:634
  74.3 66.2 %collective-permute-start.12 = (bf16[2,512,768]{2,1,0:T(8,128)(2,1)}, bf16[2,512,768]{2,1,0:T(8,128)(2,1)}, u32[]{:S(2)}, u32[]{:S(2)}) collective-permute-start(bf16[2,512,768]{2,1,0:T(8,128)(2,1)} %get-tuple-element.83.refs_6_.refs_4_), channel_id=1, source_target_pairs={{0,2},{1,3},{2,6},{3,7},{4,0},{5,1},{6,4},{7,5},{8,10},{9,11},{10,... | collective-permute-start | bytes 4718600 | tf_op jit(solution)/shard_map/ppermute | solution.py:634
  77.4 58.7 %collective-permute-start.13 = (bf16[8,128,768]{2,1,0:T(8,128)(2,1)}, bf16[8,128,768]{2,1,0:T(8,128)(2,1)}, u32[]{:S(2)}, u32[]{:S(2)}) collective-permute-start(bf16[8,128,768]{2,1,0:T(8,128)(2,1)} %get-tuple-element.88), channel_id=1, source_target_pairs={{0,1},{1,0},{2,3},{3,2},{4,5},{5,4},{6,7},{7,6},{8,9},{9,8},{10,11... | collective-permute-start | bytes 4718600 | tf_op jit(solution)/shard_map/ppermute | solution.py:634
  106.7 33.7 %collective-permute-start.14 = (bf16[2,512,768]{2,1,0:T(8,128)(2,1)}, bf16[2,512,768]{2,1,0:T(8,128)(2,1)}, u32[]{:S(2)}, u32[]{:S(2)}) collective-permute-start(bf16[2,512,768]{2,1,0:T(8,128)(2,1)} %get-tuple-element.86.refs_4_.refs_3_), channel_id=1, source_target_pairs={{0,16},{1,17},{2,18},{3,19},{4,20},{5,21},{6,22},{7,23},{8,24},{9,... | collective-permute-start | bytes 4718600 | tf_op jit(solution)/shard_map/ppermute | solution.py:634
  115.3 58.8 %collective-permute-start.10 = (bf16[2,512,768]{2,1,0:T(8,128)(2,1)}, bf16[2,512,768]{2,1,0:T(8,128)(2,1)}, u32[]{:S(2)}, u32[]{:S(2)}) collective-permute-start(bf16[2,512,768]{2,1,0:T(8,128)(2,1)} %get-tuple-element.86.refs_4_.refs_3_), channel_id=1, source_target_pairs={{0,2},{1,3},{2,6},{3,7},{4,0},{5,1},{6,4},{7,5},{8,10},{9,11},{10,... | collective-permute-start | bytes 4718600 | tf_op jit(solution)/shard_map/ppermute | solution.py:634
  118.5 40.6 %collective-permute-start.11 = (bf16[8,128,768]{2,1,0:T(8,128)(2,1)}, bf16[8,128,768]{2,1,0:T(8,128)(2,1)}, u32[]{:S(2)}, u32[]{:S(2)}) collective-permute-start(bf16[8,128,768]{2,1,0:T(8,128)(2,1)} %get-tuple-element.87), channel_id=1, source_target_pairs={{0,9},{1,8},{2,11},{3,10},{4,13},{5,12},{6,15},{7,14},{8,1},{9,0},... | collective-permute-start | bytes 4718600 | tf_op jit(solution)/shard_map/ppermute | solution.py:634
  140.4 41.4 %collective-permute-start.15 = (bf16[2,512,768]{2,1,0:T(8,128)(2,1)}, bf16[2,512,768]{2,1,0:T(8,128)(2,1)}, u32[]{:S(2)}, u32[]{:S(2)}) collective-permute-start(bf16[2,512,768]{2,1,0:T(8,128)(2,1)} %get-tuple-element.95.refs_6_.source.refs_5_), channel_id=1, source_target_pairs={{0,16},{1,17},{2,18},{3,19},{4,20},{5,21},{6,22},{7,23},{8,24},{9,... | collective-permute-start | bytes 4718600 | tf_op jit(solution)/shard_map/ppermute | solution.py:634
  141.7 40.2 %collective-permute-start.16 = (bf16[1040,512]{1,0:T(8,128)(2,1)}, bf16[1040,512]{1,0:T(8,128)(2,1)}, u32[]{:S(2)}, u32[]{:S(2)}) collective-permute-start(bf16[1040,512]{1,0:T(8,128)(2,1)} %get-tuple-element.96), channel_id=1, source_target_pairs={{0,1},{1,0},{2,3},{3,2},{4,5},{5,4},{6,7},{7,6},{8,9},{9,8},{10,11... | collective-permute-start | bytes 3194888 | tf_op jit(solution)/shard_map/ppermute | solution.py:634
  145.2 63.7 %collective-permute-start.22 = (bf16[2,528,768]{2,1,0:T(8,128)(2,1)}, bf16[2,528,768]{2,1,0:T(8,128)(2,1)}, u32[]{:S(2)}, u32[]{:S(2)}) collective-permute-start(bf16[2,528,768]{2,1,0:T(8,128)(2,1)} %cut.3), channel_id=1, source_target_pairs={{0,2},{1,3},{2,6},{3,7},{4,0},{5,1},{6,4},{7,5},{8,10},{9,11},{10,... | collective-permute-start | bytes 4866056 | tf_op jit(solution)/shard_map/ppermute | solution.py:634
  181.9 32.1 %collective-permute-start.20 = (bf16[8,128,768]{2,1,0:T(8,128)(2,1)}, bf16[8,128,768]{2,1,0:T(8,128)(2,1)}, u32[]{:S(2)}, u32[]{:S(2)}) collective-permute-start(bf16[8,128,768]{2,1,0:T(8,128)(2,1)} %get-tuple-element.109), channel_id=1, source_target_pairs={{0,8},{1,9},{2,10},{3,11},{4,12},{5,13},{6,14},{7,15},{8,0},{9,1},... | collective-permute-start | bytes 4718600 | tf_op jit(solution)/shard_map/ppermute | solution.py:634
  182.3 39.1 %collective-permute-start.17 = (bf16[2,512,768]{2,1,0:T(8,128)(2,1)}, bf16[2,512,768]{2,1,0:T(8,128)(2,1)}, u32[]{:S(2)}, u32[]{:S(2)}) collective-permute-start(bf16[2,512,768]{2,1,0:T(8,128)(2,1)} %get-tuple-element.100.refs_3_.refs_7_), channel_id=1, source_target_pairs={{0,16},{1,17},{2,18},{3,19},{4,20},{5,21},{6,22},{7,23},{8,24},{9,... | collective-permute-start | bytes 4718600 | tf_op jit(solution)/shard_map/ppermute | solution.py:634
  182.5 38.9 %collective-permute-start.18 = (bf16[1040,512]{1,0:T(8,128)(2,1)}, bf16[1040,512]{1,0:T(8,128)(2,1)}, u32[]{:S(2)}, u32[]{:S(2)}) collective-permute-start(bf16[1040,512]{1,0:T(8,128)(2,1)} %get-tuple-element.101), channel_id=1, source_target_pairs={{0,9},{1,8},{2,11},{3,10},{4,13},{5,12},{6,15},{7,14},{8,1},{9,0},... | collective-permute-start | bytes 3194888 | tf_op jit(solution)/shard_map/ppermute | solution.py:634
  195.0 26.4 %collective-permute-start.19 = (bf16[528,512]{1,0:T(8,128)(2,1)}, bf16[528,512]{1,0:T(8,128)(2,1)}, u32[]{:S(2)}, u32[]{:S(2)}) collective-permute-start(bf16[528,512]{1,0:T(8,128)(2,1)} %get-tuple-element.107), channel_id=1, source_target_pairs={{0,1},{1,0},{2,3},{3,2},{4,5},{5,4},{6,7},{7,6},{8,9},{9,8},{10,11... | collective-permute-start | bytes 1622024 | tf_op jit(solution)/shard_map/ppermute | solution.py:634
  208.9 22.1 %collective-permute-start.24 = (bf16[1,512,768]{2,1,0:T(8,128)(2,1)}, bf16[1,512,768]{2,1,0:T(8,128)(2,1)}, u32[]{:S(2)}, u32[]{:S(2)}) collective-permute-start(bf16[1,512,768]{2,1,0:T(8,128)(2,1)} %cut.5), channel_id=1, source_target_pairs={{0,2},{1,3},{2,6},{3,7},{4,0},{5,1},{6,4},{7,5},{8,10},{9,11},{10,... | collective-permute-start | bytes 2359304 | tf_op jit(solution)/shard_map/ppermute | solution.py:634
  214.0 21.3 %collective-permute-start.23 = (bf16[1,512,768]{2,1,0:T(8,128)(2,1)}, bf16[1,512,768]{2,1,0:T(8,128)(2,1)}, u32[]{:S(2)}, u32[]{:S(2)}) collective-permute-start(bf16[1,512,768]{2,1,0:T(8,128)(2,1)} %cut.4), channel_id=1, source_target_pairs={{0,16},{1,17},{2,18},{3,19},{4,20},{5,21},{6,22},{7,23},{8,24},{9,... | collective-permute-start | bytes 2359304 | tf_op jit(solution)/shard_map/ppermute | solution.py:634
  221.4 13.8 %collective-permute-start.21 = (bf16[528,512]{1,0:T(8,128)(2,1)}, bf16[528,512]{1,0:T(8,128)(2,1)}, u32[]{:S(2)}, u32[]{:S(2)}) collective-permute-start(bf16[528,512]{1,0:T(8,128)(2,1)} %get-tuple-element.110), channel_id=1, source_target_pairs={{0,9},{1,8},{2,11},{3,10},{4,13},{5,12},{6,15},{7,14},{8,1},{9,0},... | collective-permute-start | bytes 1622024 | tf_op jit(solution)/shard_map/ppermute | solution.py:634
  235.3 9.1 %collective-permute-start.25 = (bf16[8,128,768]{2,1,0:T(8,128)(2,1)}, bf16[8,128,768]{2,1,0:T(8,128)(2,1)}, u32[]{:S(2)}, u32[]{:S(2)}) collective-permute-start(bf16[8,128,768]{2,1,0:T(8,128)(2,1)} %get-tuple-element.113), channel_id=1, source_target_pairs={{0,8},{1,9},{2,10},{3,11},{4,12},{5,13},{6,14},{7,15},{8,0},{9,1},... | collective-permute-start | bytes 4718600 | tf_op jit(solution)/shard_map/ppermute | solution.py:634
  236.2 24.5 %collective-permute-start.29 = (bf16[1040,512]{1,0:T(8,128)(2,1)}, bf16[1040,512]{1,0:T(8,128)(2,1)}, u32[]{:S(2)}, u32[]{:S(2)}) collective-permute-start(bf16[1040,512]{1,0:T(8,128)(2,1)} %get-tuple-element.125), channel_id=1, source_target_pairs={{0,8},{1,9},{2,10},{3,11},{4,12},{5,13},{6,14},{7,15},{8,0},{9,1},... | collective-permute-start | bytes 3194888 | tf_op jit(solution)/shard_map/ppermute | solution.py:634
  242.5 22.3 %collective-permute-start.28 = (bf16[544,512]{1,0:T(8,128)(2,1)}, bf16[544,512]{1,0:T(8,128)(2,1)}, u32[]{:S(2)}, u32[]{:S(2)}) collective-permute-start(bf16[544,512]{1,0:T(8,128)(2,1)} %get-tuple-element.121), channel_id=1, source_target_pairs={{0,9},{1,8},{2,11},{3,10},{4,13},{5,12},{6,15},{7,14},{8,1},{9,0},... | collective-permute-start | bytes 1671176 | tf_op jit(solution)/shard_map/ppermute | solution.py:634
  242.6 27.0 %collective-permute-start.27 = (bf16[544,512]{1,0:T(8,128)(2,1)}, bf16[544,512]{1,0:T(8,128)(2,1)}, u32[]{:S(2)}, u32[]{:S(2)}) collective-permute-start(bf16[544,512]{1,0:T(8,128)(2,1)} %get-tuple-element.118.refs_12_.refs_3_), channel_id=1, source_target_pairs={{0,1},{1,0},{2,3},{3,2},{4,5},{5,4},{6,7},{7,6},{8,9},{9,8},{10,11... | collective-permute-start | bytes 1671176 | tf_op jit(solution)/shard_map/ppermute | solution.py:634
  256.5 4.3 %collective-permute-start.30 = (bf16[528,512]{1,0:T(8,128)(2,1)}, bf16[528,512]{1,0:T(8,128)(2,1)}, u32[]{:S(2)}, u32[]{:S(2)}) collective-permute-start(bf16[528,512]{1,0:T(8,128)(2,1)} %get-tuple-element.126), channel_id=1, source_target_pairs={{0,8},{1,9},{2,10},{3,11},{4,12},{5,13},{6,14},{7,15},{8,0},{9,1},... | collective-permute-start | bytes 1622024 | tf_op jit(solution)/shard_map/ppermute | solution.py:634
  256.7 12.9 %collective-permute-start.26 = (bf16[528,512]{1,0:T(8,128)(2,1)}, bf16[528,512]{1,0:T(8,128)(2,1)}, u32[]{:S(2)}, u32[]{:S(2)}) collective-permute-start(bf16[528,512]{1,0:T(8,128)(2,1)} %get-tuple-element.120), channel_id=1, source_target_pairs={{0,8},{1,9},{2,10},{3,11},{4,12},{5,13},{6,14},{7,15},{8,0},{9,1},... | collective-permute-start | bytes 1622024 | tf_op jit(solution)/shard_map/ppermute | solution.py:634

commit v7 on v6

--- a/solution.py
+++ b/solution.py
@@ -413,7 +413,7 @@
             score_kernel, nz, cap, blk_dev, places, wide, runs, fetched, late, resident, len(before), len(extra)
         ),
         out_shape=[
-            jax.ShapeDtypeStruct((wide * TILE + (32 if late else 16), BLOCK), BF16) for d, _ in places
+            jax.ShapeDtypeStruct((wide * TILE + ((48 if d == 2 else 32) if late else 16), BLOCK), BF16) for d, _ in places
         ],
         in_specs=[SMEM, SMEM, SMEM, VMEM]
         + [ANY] * (len(runs) + 1)
@@ -459,7 +459,7 @@
                 at += 1
 
     def tail_rows(d):
-        return sources[d].shape[0] - spans[d][1] * TILE
+        return min(32, sources[d].shape[0] - spans[d][1] * TILE)
 
     def tail_copy(d):
         return pltpu.make_async_copy(
@@ -789,10 +789,10 @@
             waits.setdefault(done, []).append(("r", d, group))
         if k == last - 1:
             score([(d, three) for d in (2, 3)], (first_late, False), extra=[env["token"]])
-    score([(2, three), (3, three)], (first_late, True), True, [env["token"]])
     for d in (2, 3):
+        score([(d, three)], (first_late, True), True, [env["token"] if d == 2 else env["s", 2, three]])
         env["r", d, three] = exchange(env["s", d, three], d)
-    score([(1, two), (1, three), (0, three)], extra=[env["s", 2, three]])
+    score([(1, two), (1, three), (0, three)], extra=[env["s", 3, three]])
     for group in (one, two, three):
         env["r", 1, group] = exchange(env["s", 1, group], 1)
     outputs = place([(0, one), (2, one), (3, one)], [], [env["s", 2, three]])

time: 276 us -> 275 us (level)
  starting transfers between devices: 49.4 us -> 56.6 us
  Pallas kernels: 91.6 us -> 86.2 us
  waiting for transfers between devices: 131 us -> 128 us
    ppermute x31, starting transfers between devices: 49.4 us -> 56.6 us  [permute(): lax.ppermute(value, AXES, [(device(*a), device(*target(*a))) for a in eve...]
    pallas_call x6 -> x7, Pallas kernels: 55.1 us -> 49.8 us  [score_call(): pl.pallas_call(functools.partial(score_kernel, nz, cap, blk_dev, places,...]
  transfers between devices with their start and end apart: 31 -> 31, of which waited for: 11 -> 12; matrix products, arithmetic and copies ran while one was open for 0% -> 0% of each run, Pallas kernels for 31% -> 29%
where the time goes in v7:
time: 275 us; the launch traced here: 273 us
  waiting for transfers between devices  128 us (47%)
  Pallas kernels  86.2 us (31%)
  starting transfers between devices  56.6 us (21%)
    ppermute x31, waiting for transfers between devices, permute(): lax.ppermute(value, AXES, [(device(*a), device(*target(*a))) for a in eve...  128 us
    ppermute x31, starting transfers between devices, permute(): lax.ppermute(value, AXES, [(device(*a), device(*target(*a))) for a in eve...  56.6 us
    pallas_call x7, Pallas kernels, score_call(): pl.pallas_call(functools.partial(score_kernel, nz, cap, blk_dev, places,...  49.8 us
    pallas_call x3, Pallas kernels, assemble(): pl.pallas_call(functools.partial(assemble_kernel, spans, held_already, le...  12.1 us
    pallas_call x1, Pallas kernels, receive(): pl.pallas_call(functools.partial(receive_kernel, nz, cap, blk_dev, tile_d...  7.31 us
    pallas_call x3, Pallas kernels, cut(): pl.pallas_call(functools.partial(cut_kernel, first), out_shape=jax.ShapeD...  6.2 us
  transfers between devices with their start and end apart: 31, of which 12 were waited for; matrix products, arithmetic and copies ran while one was open for 0% of the time, Pallas kernels for 29%

profile of v7, /device:TPU:9, one launch (start us, length us, event | category | flops | bytes accessed | tf_op | source)
XLA Modules:
  0.0 273.3 jit_solution(12724742777391049069)
XLA Ops:
  0.7 2.9 %own_pieces.1 = (bf16[2,512,768]{2,1,0:T(8,128)(2,1)}, bf16[2,512,768]{2,1,0:T(8,128)(2,1)}) custom-call(bf16[8,512,768]{2,1,0:T(8,128)(2,1)} %bitcast.13), custom_call_target="tpu_custom_call" | custom-call | flops 1 | bytes 1 | tf_op jit(solution)/shard_map/own_pieces/pallas_call | solution.py:578
  3.6 2.4 collective-permute-start.4
  6.0 2.1 collective-permute-start.2
  9.5 2.9 %plan.1 = (s32[32]{0:T(128)}, s32[64]{0:T(128)}, f32[8,128]{1,0:T(8,128)}) custom-call(s32[4]{0:T(128)} %pad_add_fusion.2.me, s32[32]{0:T(128)} %region.1, s32[32]{0:T(128)} %block.1, bf16[2,512,768]{2,1,0:T(8,128)(2,1)} %get-tuple-element.69.refs_0_, bf16[2,512,768]{2,1,0:T(8,128)(2,1)} %get-tuple-element.70.refs_1_), custom_call_target="tpu_custom_call" | custom-call | flops 1 | bytes 1 | tf_op jit(solution)/shard_map/plan/pallas_call | solution.py:76
  13.0 5.0 %dispatch.1 = (bf16[8,128,768]{2,1,0:T(8,128)(2,1)}, bf16[8,128,768]{2,1,0:T(8,128)(2,1)}, bf16[8,128,768]{2,1,0:T(8,128)(2,1)}, bf16[8,128,768]{2,1,0:T(8,128)(...) custom-call(s32[32]{0:T(128)} %get-tuple-element.74.at_slot, bf16[32,128,768]{2,1,0:T(8,128)(2,1)} %bitcast.21, ...), custom_call_target="tpu_custom_call" | custom-call | flops 1 | bytes 1 | tf_op jit(solution)/shard_map/dispatch/pallas_call | solution.py:199
  18.0 1.7 collective-permute-start.7
  19.8 19.6 %collective-permute-done.4.refs_0_ = bf16[2,512,768]{2,1,0:T(8,128)(2,1)} collective-permute-done((bf16[2,512,768]{2,1,0:T(8,128)(2,1)}, bf16[2,512,768]{2,1,0:T(8,128)(2,1)}, u32[]{:S(2)}, u32[]{:S(2)}) %collective-permute-start.4) | collective-permute-done | bytes 1572896 | tf_op jit(solution)/shard_map/ppermute | solution.py:634
  39.3 1.2 collective-permute-start.8
  40.5 4.1 %collective-permute-start.3 = (bf16[8,128,768]{2,1,0:T(8,128)(2,1)}, bf16[8,128,768]{2,1,0:T(8,128)(2,1)}, u32[]{:S(2)}, u32[]{:S(2)}) collective-permute-start(bf16[8,128,768]{2,1,0:T(8,128)(2,1)} %get-tuple-element.75), channel_id=1, source_target_pairs={{0,9},{1,8},{2,11},{3,10},{4,13},{5,12},{6,15},{7,14},{8,1},{9,0},... | collective-permute-start | bytes 4718600 | tf_op jit(solution)/shard_map/ppermute | solution.py:634
  44.6 3.1 %collective-permute-start.5 = (bf16[2,512,768]{2,1,0:T(8,128)(2,1)}, bf16[2,512,768]{2,1,0:T(8,128)(2,1)}, u32[]{:S(2)}, u32[]{:S(2)}) collective-permute-start(bf16[2,512,768]{2,1,0:T(8,128)(2,1)} %get-tuple-element.77.refs_4_.refs_2_), channel_id=1, source_target_pairs={{0,2},{1,3},{2,6},{3,7},{4,0},{5,1},{6,4},{7,5},{8,10},{9,11},{10,... | collective-permute-start | bytes 4718600 | tf_op jit(solution)/shard_map/ppermute | solution.py:634
  47.7 25.3 %collective-permute-done.6.refs_0_ = bf16[2,512,768]{2,1,0:T(8,128)(2,1)} collective-permute-done((bf16[2,512,768]{2,1,0:T(8,128)(2,1)}, bf16[2,512,768]{2,1,0:T(8,128)(2,1)}, u32[]{:S(2)}, u32[]{:S(2)}) %collective-permute-start.6) | collective-permute-done | bytes 1572896 | tf_op jit(solution)/shard_map/ppermute | solution.py:634
  73.0 1.2 collective-permute-start.9
  74.3 3.2 %collective-permute-start.12 = (bf16[2,512,768]{2,1,0:T(8,128)(2,1)}, bf16[2,512,768]{2,1,0:T(8,128)(2,1)}, u32[]{:S(2)}, u32[]{:S(2)}) collective-permute-start(bf16[2,512,768]{2,1,0:T(8,128)(2,1)} %get-tuple-element.81.refs_6_.refs_4_), channel_id=1, source_target_pairs={{0,2},{1,3},{2,6},{3,7},{4,0},{5,1},{6,4},{7,5},{8,10},{9,11},{10,... | collective-permute-start | bytes 4718600 | tf_op jit(solution)/shard_map/ppermute | solution.py:634
  77.4 1.2 collective-permute-start.13
  78.7 11.6 %collective-permute-done.3.refs_0_ = bf16[8,128,768]{2,1,0:T(8,128)(2,1)} collective-permute-done((bf16[8,128,768]{2,1,0:T(8,128)(2,1)}, bf16[8,128,768]{2,1,0:T(8,128)(2,1)}, u32[]{:S(2)}, u32[]{:S(2)}) %collective-permute-start.3) | collective-permute-done | bytes 1572896 | tf_op jit(solution)/shard_map/ppermute | solution.py:634
  90.2 16.5 %collective-permute-done.5.refs_1_ = bf16[2,512,768]{2,1,0:T(8,128)(2,1)} collective-permute-done((bf16[2,512,768]{2,1,0:T(8,128)(2,1)}, bf16[2,512,768]{2,1,0:T(8,128)(2,1)}, u32[]{:S(2)}, u32[]{:S(2)}) %collective-permute-start.5) | collective-permute-done | bytes 1572896 | tf_op jit(solution)/shard_map/ppermute | solution.py:634
  106.7 1.2 collective-permute-start.14
  108.0 7.3 %receive.1 = (s32[64,8,128]{2,1,0:T(8,128)}, s32[64]{0:T(128)}) custom-call(s32[4]{0:T(128)} %pad_add_fusion.2.me, s32[72,128]{1,0:T(8,128)} %copy-done, s32[72,128]{1,0:T(8,128)} %copy-done.3, s32[72,128]{1,0:T(8,128)} %copy-done.2, s32[72,128]{1,0:T(8,128)} %copy-done.1), custom_call_target="tpu_custom_call" | custom-call | flops 1 | bytes 1 | tf_op jit(solution)/shard_map/receive/pallas_call | solution.py:139
  115.3 3.2 %collective-permute-start.10 = (bf16[2,512,768]{2,1,0:T(8,128)(2,1)}, bf16[2,512,768]{2,1,0:T(8,128)(2,1)}, u32[]{:S(2)}, u32[]{:S(2)}) collective-permute-start(bf16[2,512,768]{2,1,0:T(8,128)(2,1)} %get-tuple-element.84.refs_4_.refs_3_), channel_id=1, source_target_pairs={{0,2},{1,3},{2,6},{3,7},{4,0},{5,1},{6,4},{7,5},{8,10},{9,11},{10,... | collective-permute-start | bytes 4718600 | tf_op jit(solution)/shard_map/ppermute | solution.py:634
  118.5 5.1 %collective-permute-start.11 = (bf16[8,128,768]{2,1,0:T(8,128)(2,1)}, bf16[8,128,768]{2,1,0:T(8,128)(2,1)}, u32[]{:S(2)}, u32[]{:S(2)}) collective-permute-start(bf16[8,128,768]{2,1,0:T(8,128)(2,1)} %get-tuple-element.85), channel_id=1, source_target_pairs={{0,9},{1,8},{2,11},{3,10},{4,13},{5,12},{6,15},{7,14},{8,1},{9,0},... | collective-permute-start | bytes 4718600 | tf_op jit(solution)/shard_map/ppermute | solution.py:634
  123.6 15.3 %score.7 = (bf16[1040,512]{1,0:T(8,128)(2,1)}, bf16[1040,512]{1,0:T(8,128)(2,1)}, bf16[1040,512]{1,0:T(8,128)(2,1)}) custom-call(s32[4]{0:T(128)} %pad_add_fusion.2.me, s32[64]{0:T(128)} %get-tuple-element.72.ids, s32[64]{0:T(128)} %get-tuple-element.71.inv, s32[64,8,128]{2,1,0:T(8,128)} %get-tuple-element.73.meta, ...), custom_call_target="tpu_custom_call" | custom-call | flops 1 | bytes 1 | tf_op jit(solution)/shard_map/score/pallas_call | solution.py:411
  138.9 1.5 collective-permute-done.12.refs_0_
  140.5 1.2 collective-permute-start.15
  141.7 1.2 collective-permute-start.16
  142.9 2.3 cut.3
  145.2 3.2 %collective-permute-start.22 = (bf16[2,528,768]{2,1,0:T(8,128)(2,1)}, bf16[2,528,768]{2,1,0:T(8,128)(2,1)}, u32[]{:S(2)}, u32[]{:S(2)}) collective-permute-start(bf16[2,528,768]{2,1,0:T(8,128)(2,1)} %cut.3), channel_id=1, source_target_pairs={{0,2},{1,3},{2,6},{3,7},{4,0},{5,1},{6,4},{7,5},{8,10},{9,11},{10,... | collective-permute-start | bytes 4866056 | tf_op jit(solution)/shard_map/ppermute | solution.py:634
  148.4 10.8 %collective-permute-done.11.refs_1_ = bf16[8,128,768]{2,1,0:T(8,128)(2,1)} collective-permute-done((bf16[8,128,768]{2,1,0:T(8,128)(2,1)}, bf16[8,128,768]{2,1,0:T(8,128)(2,1)}, u32[]{:S(2)}, u32[]{:S(2)}) %collective-permute-start.11) | collective-permute-done | bytes 1572896 | tf_op jit(solution)/shard_map/ppermute | solution.py:634
  159.2 15.0 %collective-permute-done.10.refs_0_ = bf16[2,512,768]{2,1,0:T(8,128)(2,1)} collective-permute-done((bf16[2,512,768]{2,1,0:T(8,128)(2,1)}, bf16[2,512,768]{2,1,0:T(8,128)(2,1)}, u32[]{:S(2)}, u32[]{:S(2)}) %collective-permute-start.10) | collective-permute-done | bytes 1572896 | tf_op jit(solution)/shard_map/ppermute | solution.py:634
  174.2 7.6 %collective-permute-done.16.refs_3_ = bf16[1040,512]{1,0:T(8,128)(2,1)} collective-permute-done((bf16[1040,512]{1,0:T(8,128)(2,1)}, bf16[1040,512]{1,0:T(8,128)(2,1)}, u32[]{:S(2)}, u32[]{:S(2)}) %collective-permute-start.16) | collective-permute-done | bytes 1064992 | tf_op jit(solution)/shard_map/ppermute | solution.py:634
  183.2 2.0 score.8
  185.2 8.5 %collective-permute-start.19 = (bf16[528,512]{1,0:T(8,128)(2,1)}, bf16[528,512]{1,0:T(8,128)(2,1)}, u32[]{:S(2)}, u32[]{:S(2)}) collective-permute-start(bf16[528,512]{1,0:T(8,128)(2,1)} %get-tuple-element.105), channel_id=1, source_target_pairs={{0,1},{1,0},{2,3},{3,2},{4,5},{5,4},{6,7},{7,6},{8,9},{9,8},{10,11... | collective-permute-start | bytes 1622024 | tf_op jit(solution)/shard_map/ppermute | solution.py:634
  193.7 1.9 cut.5
  195.6 13.3 %collective-permute-done.22.source.refs_5_.refs_9_ = bf16[2,528,768]{2,1,0:T(8,128)(2,1)} collective-permute-done((bf16[2,528,768]{2,1,0:T(8,128)(2,1)}, bf16[2,528,768]{2,1,0:T(8,128)(2,1)}, u32[]{:S(2)}, u32[]{:S(2)}) %collective-permute-start.22) | collective-permute-done | bytes 1622048 | tf_op jit(solution)/shard_map/ppermute | solution.py:634
  208.9 3.1 %collective-permute-start.24 = (bf16[1,512,768]{2,1,0:T(8,128)(2,1)}, bf16[1,512,768]{2,1,0:T(8,128)(2,1)}, u32[]{:S(2)}, u32[]{:S(2)}) collective-permute-start(bf16[1,512,768]{2,1,0:T(8,128)(2,1)} %cut.5), channel_id=1, source_target_pairs={{0,2},{1,3},{2,6},{3,7},{4,0},{5,1},{6,4},{7,5},{8,10},{9,11},{10,... | collective-permute-start | bytes 2359304 | tf_op jit(solution)/shard_map/ppermute | solution.py:634
  212.0 2.0 cut.4
  214.0 1.3 collective-permute-start.23
  215.3 6.8 %score.9.refs_4_ = bf16[1040,512]{1,0:T(8,128)(2,1)} custom-call(s32[4]{0:T(128)} %pad_add_fusion.2.me, s32[64]{0:T(128)} %get-tuple-element.72.ids, s32[64]{0:T(128)} %get-tuple-element.71.inv, s32[64,8,128]{2,1,0:T(8,128)} %get-tuple-element.73.meta, bf16[8,128,768]{2,1,0:T(8,128)(2,1)} %collective-permute-done.20.refs_0_, bf16[8,512,768]{2,1,0:T(8,128)(2,1)} %bitcast.16, ...), custom_call_target="tpu_custom_call" | custom-call | flops 1 | bytes 1 | tf_op jit(solution)/shard_map/score/pallas_call | solution.py:411
  222.1 2.6 collective-permute-start.21
  224.8 7.6 %score.10 = (bf16[560,512]{1,0:T(8,128)(2,1)}, bf16[544,512]{1,0:T(8,128)(2,1)}) custom-call(s32[4]{0:T(128)} %pad_add_fusion.2.me, s32[64]{0:T(128)} %get-tuple-element.72.ids, s32[64]{0:T(128)} %get-tuple-element.71.inv, s32[64,8,128]{2,1,0:T(8,128)} %get-tuple-element.73.meta, bf16[8,128,768]{2,1,0:T(8,128)(2,1)} %get-tuple-element.100.refs_0_, ...), custom_call_target="tpu_custom_call" | custom-call | flops 1 | bytes 1 | tf_op jit(solution)/shard_map/score/pallas_call | solution.py:411
  232.4 3.0 %collective-permute-done.23.refs_3_.refs_2_.refs_10_ = bf16[1,512,768]{2,1,0:T(8,128)(2,1)} collective-permute-done((bf16[1,512,768]{2,1,0:T(8,128)(2,1)}, bf16[1,512,768]{2,1,0:T(8,128)(2,1)}, u32[]{:S(2)}, u32[]{:S(2)}) %collective-permute-start.23) | collective-permute-done | bytes 786464 | tf_op jit(solution)/shard_map/ppermute | solution.py:634
  236.3 4.5 %score.11.refs_5_.refs_3_ = bf16[560,512]{1,0:T(8,128)(2,1)} custom-call(s32[4]{0:T(128)} %pad_add_fusion.2.me, s32[64]{0:T(128)} %get-tuple-element.72.ids, s32[64]{0:T(128)} %get-tuple-element.71.inv, s32[64,8,128]{2,1,0:T(8,128)} %get-tuple-element.73.meta, bf16[8,128,768]{2,1,0:T(8,128)(2,1)} %get-tuple-element.100.refs_0_, ...), custom_call_target="tpu_custom_call", output_to_operand_aliasing={{}: (8, {})} | custom-call | flops 1 | bytes 1 | tf_op jit(solution)/shard_map/score/pallas_call | solution.py:411
  240.9 2.1 collective-permute-start.27
  243.0 4.5 %score.12.refs_12_ = bf16[544,512]{1,0:T(8,128)(2,1)} custom-call(s32[4]{0:T(128)} %pad_add_fusion.2.me, s32[64]{0:T(128)} %get-tuple-element.72.ids, s32[64]{0:T(128)} %get-tuple-element.71.inv, s32[64,8,128]{2,1,0:T(8,128)} %get-tuple-element.73.meta, bf16[8,128,768]{2,1,0:T(8,128)(2,1)} %get-tuple-element.101.refs_1_.refs_0_, ...), custom_call_target="tpu_custom_call", output_to_operand_aliasing={{}: (8, {})} | custom-call | flops 1 | bytes 1 | tf_op jit(solution)/shard_map/score/pallas_call | solution.py:411
  247.6 9.1 %score.13 = (bf16[528,512]{1,0:T(8,128)(2,1)}, bf16[528,512]{1,0:T(8,128)(2,1)}, bf16[528,512]{1,0:T(8,128)(2,1)}) custom-call(s32[4]{0:T(128)} %pad_add_fusion.2.me, s32[64]{0:T(128)} %get-tuple-element.72.ids, s32[64]{0:T(128)} %get-tuple-element.71.inv, s32[64,8,128]{2,1,0:T(8,128)} %get-tuple-element.73.meta, ...), custom_call_target="tpu_custom_call" | custom-call | flops 1 | bytes 1 | tf_op jit(solution)/shard_map/score/pallas_call | solution.py:411
  257.6 3.8 %assemble.3 = (bf16[32,128,512]{2,1,0:T(8,128)(2,1)}, f32[32,128]{1,0:T(8,128)}, f32[32,128]{1,0:T(8,128)}) custom-call(s32[64]{0:T(128)} %get-tuple-element.71.inv, bf16[1040,512]{1,0:T(8,128)(2,1)} %get-tuple-element.123.refs_0_, bf16[1040,512]{1,0:T(8,128)(2,1)} %get-tuple-element.124.refs_1_, bf16[1040,512]{1,0:T(8,128)(2,1)} %get-tuple-element.125.refs_2_, ...), custom_call_target="tpu_custom_call" | custom-call | flops 1 | bytes 1 | tf_op jit(solution)/shard_map/assemble/pallas_call | solution.py:512
  261.4 3.6 %assemble.4 = (bf16[32,128,512]{2,1,0:T(8,128)(2,1)}, f32[32,128]{1,0:T(8,128)}, f32[32,128]{1,0:T(8,128)}) custom-call(s32[64]{0:T(128)} %get-tuple-element.71.inv, bf16[528,512]{1,0:T(8,128)(2,1)} %get-tuple-element.118.refs_0_, bf16[528,512]{1,0:T(8,128)(2,1)} %get-tuple-element.119.refs_1_, ...), custom_call_target="tpu_custom_call", output_to_operand_aliasing={{0}: (6, {})} | custom-call | flops 1 | bytes 1 | tf_op jit(solution)/shard_map/assemble/pallas_call | solution.py:512
  265.1 3.4 %collective-permute-done.28.refs_3_ = bf16[544,512]{1,0:T(8,128)(2,1)} collective-permute-done((bf16[544,512]{1,0:T(8,128)(2,1)}, bf16[544,512]{1,0:T(8,128)(2,1)}, u32[]{:S(2)}, u32[]{:S(2)}) %collective-permute-start.28) | collective-permute-done | bytes 557088 | tf_op jit(solution)/shard_map/ppermute | solution.py:634
  268.5 4.6 %assemble.5 = (bf16[32,128,512]{2,1,0:T(8,128)(2,1)}, bf16[32,128]{1,0:T(8,128)(2,1)}, bf16[32,128]{1,0:T(8,128)(2,1)}) custom-call(s32[64]{0:T(128)} %get-tuple-element.71.inv, bf16[528,512]{1,0:T(8,128)(2,1)} %get-tuple-element.116.refs_8_.refs_0_, bf16[528,512]{1,0:T(8,128)(2,1)} %collective-permute-done.26.refs_1_, ...), custom_call_target="tpu_custom_call", output_to_operand_aliasing={{0}: (5, {})} | custom-call | flops 1 | bytes 1 | tf_op jit(solution)/shard_map/assemble/pallas_call | solution.py:512
  (57 shorter events, 5.4 us)
Async XLA Ops:
  0.6 5.3 %copy-start.6 = (s32[32]{0:T(128)S(1)}, s32[32]{0:T(128)}, u32[]{:S(2)}) copy-start(s32[32]{0:T(128)} %region.1) | copy-start | bytes 388
  0.6 5.3 %copy-start.7 = (s32[32]{0:T(128)S(1)}, s32[32]{0:T(128)}, u32[]{:S(2)}) copy-start(s32[32]{0:T(128)} %block.1) | copy-start | bytes 388
  0.7 5.3 %copy-start.4 = (s32[4096]{0:T(1024)S(1)}, s32[4096]{0:T(1024)}, u32[]{:S(2)}) copy-start(s32[4096]{0:T(1024)} %param.10) | copy-start | bytes 49156
  0.7 5.3 %copy-start.5 = (s32[4096]{0:T(1024)S(1)}, s32[4096]{0:T(1024)}, u32[]{:S(2)}) copy-start(s32[4096]{0:T(1024)} %param.9) | copy-start | bytes 49156
  3.6 35.7 %collective-permute-start.4 = (bf16[2,512,768]{2,1,0:T(8,128)(2,1)}, bf16[2,512,768]{2,1,0:T(8,128)(2,1)}, u32[]{:S(2)}, u32[]{:S(2)}) collective-permute-start(bf16[2,512,768]{2,1,0:T(8,128)(2,1)} %get-tuple-element.69.refs_0_), channel_id=1, source_target_pairs={{0,2},{1,3},{2,6},{3,7},{4,0},{5,1},{6,4},{7,5},{8,10},{9,11},{10,... | collective-permute-start | bytes 4718600 | tf_op jit(solution)/shard_map/ppermute | solution.py:634
  6.0 6.4 %copy-start = (s32[72,128]{1,0:T(8,128)}, s32[72,128]{1,0:T(8,128)S(1)}, u32[]{:S(2)}) copy-start(s32[72,128]{1,0:T(8,128)S(1)} %pad_add_fusion.refs_0_) | copy-start | bytes 110596
  6.0 6.4 %collective-permute-start.2 = (s32[72,128]{1,0:T(8,128)S(1)}, s32[72,128]{1,0:T(8,128)S(1)}, u32[]{:S(2)}, u32[]{:S(2)}) collective-permute-start(s32[72,128]{1,0:T(8,128)S(1)} %pad_add_fusion.refs_0_), channel_id=1, source_target_pairs={{0,9},{1,8},{2,11},{3,10},{4,13},{5,12},{6,15},{7,14},{8,1},{9,0},... | collective-permute-start | bytes 110600 | tf_op jit(solution)/shard_map/ppermute | solution.py:634
  8.2 4.2 %collective-permute-start.1 = (s32[72,128]{1,0:T(8,128)S(1)}, s32[72,128]{1,0:T(8,128)S(1)}, u32[]{:S(2)}, u32[]{:S(2)}) collective-permute-start(s32[72,128]{1,0:T(8,128)S(1)} %pad_add_fusion.refs_0_), channel_id=1, source_target_pairs={{0,1},{1,0},{2,3},{3,2},{4,5},{5,4},{6,7},{7,6},{8,9},{9,8},{10,11... | collective-permute-start | bytes 110600 | tf_op jit(solution)/shard_map/ppermute | solution.py:634
  8.4 4.0 %collective-permute-start = (s32[72,128]{1,0:T(8,128)S(1)}, s32[72,128]{1,0:T(8,128)S(1)}, u32[]{:S(2)}, u32[]{:S(2)}) collective-permute-start(s32[72,128]{1,0:T(8,128)S(1)} %pad_add_fusion.refs_0_), channel_id=1, source_target_pairs={{0,8},{1,9},{2,10},{3,11},{4,12},{5,13},{6,14},{7,15},{8,0},{9,1},... | collective-permute-start | bytes 110600 | tf_op jit(solution)/shard_map/ppermute | solution.py:634
  9.3 63.8 %collective-permute-start.6 = (bf16[2,512,768]{2,1,0:T(8,128)(2,1)}, bf16[2,512,768]{2,1,0:T(8,128)(2,1)}, u32[]{:S(2)}, u32[]{:S(2)}) collective-permute-start(bf16[2,512,768]{2,1,0:T(8,128)(2,1)} %get-tuple-element.70.refs_1_), channel_id=1, source_target_pairs={{0,2},{1,3},{2,6},{3,7},{4,0},{5,1},{6,4},{7,5},{8,10},{9,11},{10,... | collective-permute-start | bytes 4718600 | tf_op jit(solution)/shard_map/ppermute | solution.py:634
  12.4 0.6 copy-start.1
  12.4 0.6 copy-start.2
  12.4 0.6 copy-start.3
  18.0 55.0 %collective-permute-start.7 = (bf16[8,128,768]{2,1,0:T(8,128)(2,1)}, bf16[8,128,768]{2,1,0:T(8,128)(2,1)}, u32[]{:S(2)}, u32[]{:S(2)}) collective-permute-start(bf16[8,128,768]{2,1,0:T(8,128)(2,1)} %get-tuple-element.78), channel_id=1, source_target_pairs={{0,1},{1,0},{2,3},{3,2},{4,5},{5,4},{6,7},{7,6},{8,9},{9,8},{10,11... | collective-permute-start | bytes 4718600 | tf_op jit(solution)/shard_map/ppermute | solution.py:634
  39.3 33.7 %collective-permute-start.8 = (bf16[2,512,768]{2,1,0:T(8,128)(2,1)}, bf16[2,512,768]{2,1,0:T(8,128)(2,1)}, u32[]{:S(2)}, u32[]{:S(2)}) collective-permute-start(bf16[2,512,768]{2,1,0:T(8,128)(2,1)} %get-tuple-element.77.refs_4_.refs_2_), channel_id=1, source_target_pairs={{0,16},{1,17},{2,18},{3,19},{4,20},{5,21},{6,22},{7,23},{8,24},{9,... | collective-permute-start | bytes 4718600 | tf_op jit(solution)/shard_map/ppermute | solution.py:634
  40.5 49.7 %collective-permute-start.3 = (bf16[8,128,768]{2,1,0:T(8,128)(2,1)}, bf16[8,128,768]{2,1,0:T(8,128)(2,1)}, u32[]{:S(2)}, u32[]{:S(2)}) collective-permute-start(bf16[8,128,768]{2,1,0:T(8,128)(2,1)} %get-tuple-element.75), channel_id=1, source_target_pairs={{0,9},{1,8},{2,11},{3,10},{4,13},{5,12},{6,15},{7,14},{8,1},{9,0},... | collective-permute-start | bytes 4718600 | tf_op jit(solution)/shard_map/ppermute | solution.py:634
  44.6 62.1 %collective-permute-start.5 = (bf16[2,512,768]{2,1,0:T(8,128)(2,1)}, bf16[2,512,768]{2,1,0:T(8,128)(2,1)}, u32[]{:S(2)}, u32[]{:S(2)}) collective-permute-start(bf16[2,512,768]{2,1,0:T(8,128)(2,1)} %get-tuple-element.77.refs_4_.refs_2_), channel_id=1, source_target_pairs={{0,2},{1,3},{2,6},{3,7},{4,0},{5,1},{6,4},{7,5},{8,10},{9,11},{10,... | collective-permute-start | bytes 4718600 | tf_op jit(solution)/shard_map/ppermute | solution.py:634
  73.0 33.7 %collective-permute-start.9 = (bf16[2,512,768]{2,1,0:T(8,128)(2,1)}, bf16[2,512,768]{2,1,0:T(8,128)(2,1)}, u32[]{:S(2)}, u32[]{:S(2)}) collective-permute-start(bf16[2,512,768]{2,1,0:T(8,128)(2,1)} %get-tuple-element.81.refs_6_.refs_4_), channel_id=1, source_target_pairs={{0,16},{1,17},{2,18},{3,19},{4,20},{5,21},{6,22},{7,23},{8,24},{9,... | collective-permute-start | bytes 4718600 | tf_op jit(solution)/shard_map/ppermute | solution.py:634
  74.3 66.2 %collective-permute-start.12 = (bf16[2,512,768]{2,1,0:T(8,128)(2,1)}, bf16[2,512,768]{2,1,0:T(8,128)(2,1)}, u32[]{:S(2)}, u32[]{:S(2)}) collective-permute-start(bf16[2,512,768]{2,1,0:T(8,128)(2,1)} %get-tuple-element.81.refs_6_.refs_4_), channel_id=1, source_target_pairs={{0,2},{1,3},{2,6},{3,7},{4,0},{5,1},{6,4},{7,5},{8,10},{9,11},{10,... | collective-permute-start | bytes 4718600 | tf_op jit(solution)/shard_map/ppermute | solution.py:634
  77.4 61.5 %collective-permute-start.13 = (bf16[8,128,768]{2,1,0:T(8,128)(2,1)}, bf16[8,128,768]{2,1,0:T(8,128)(2,1)}, u32[]{:S(2)}, u32[]{:S(2)}) collective-permute-start(bf16[8,128,768]{2,1,0:T(8,128)(2,1)} %get-tuple-element.86), channel_id=1, source_target_pairs={{0,1},{1,0},{2,3},{3,2},{4,5},{5,4},{6,7},{7,6},{8,9},{9,8},{10,11... | collective-permute-start | bytes 4718600 | tf_op jit(solution)/shard_map/ppermute | solution.py:634
  106.7 33.7 %collective-permute-start.14 = (bf16[2,512,768]{2,1,0:T(8,128)(2,1)}, bf16[2,512,768]{2,1,0:T(8,128)(2,1)}, u32[]{:S(2)}, u32[]{:S(2)}) collective-permute-start(bf16[2,512,768]{2,1,0:T(8,128)(2,1)} %get-tuple-element.84.refs_4_.refs_3_), channel_id=1, source_target_pairs={{0,16},{1,17},{2,18},{3,19},{4,20},{5,21},{6,22},{7,23},{8,24},{9,... | collective-permute-start | bytes 4718600 | tf_op jit(solution)/shard_map/ppermute | solution.py:634
  115.3 58.9 %collective-permute-start.10 = (bf16[2,512,768]{2,1,0:T(8,128)(2,1)}, bf16[2,512,768]{2,1,0:T(8,128)(2,1)}, u32[]{:S(2)}, u32[]{:S(2)}) collective-permute-start(bf16[2,512,768]{2,1,0:T(8,128)(2,1)} %get-tuple-element.84.refs_4_.refs_3_), channel_id=1, source_target_pairs={{0,2},{1,3},{2,6},{3,7},{4,0},{5,1},{6,4},{7,5},{8,10},{9,11},{10,... | collective-permute-start | bytes 4718600 | tf_op jit(solution)/shard_map/ppermute | solution.py:634
  118.5 40.7 %collective-permute-start.11 = (bf16[8,128,768]{2,1,0:T(8,128)(2,1)}, bf16[8,128,768]{2,1,0:T(8,128)(2,1)}, u32[]{:S(2)}, u32[]{:S(2)}) collective-permute-start(bf16[8,128,768]{2,1,0:T(8,128)(2,1)} %get-tuple-element.85), channel_id=1, source_target_pairs={{0,9},{1,8},{2,11},{3,10},{4,13},{5,12},{6,15},{7,14},{8,1},{9,0},... | collective-permute-start | bytes 4718600 | tf_op jit(solution)/shard_map/ppermute | solution.py:634
  140.5 41.3 %collective-permute-start.15 = (bf16[2,512,768]{2,1,0:T(8,128)(2,1)}, bf16[2,512,768]{2,1,0:T(8,128)(2,1)}, u32[]{:S(2)}, u32[]{:S(2)}) collective-permute-start(bf16[2,512,768]{2,1,0:T(8,128)(2,1)} %get-tuple-element.93.refs_6_.source.refs_5_), channel_id=1, source_target_pairs={{0,16},{1,17},{2,18},{3,19},{4,20},{5,21},{6,22},{7,23},{8,24},{9,... | collective-permute-start | bytes 4718600 | tf_op jit(solution)/shard_map/ppermute | solution.py:634
  141.7 40.0 %collective-permute-start.16 = (bf16[1040,512]{1,0:T(8,128)(2,1)}, bf16[1040,512]{1,0:T(8,128)(2,1)}, u32[]{:S(2)}, u32[]{:S(2)}) collective-permute-start(bf16[1040,512]{1,0:T(8,128)(2,1)} %get-tuple-element.94), channel_id=1, source_target_pairs={{0,1},{1,0},{2,3},{3,2},{4,5},{5,4},{6,7},{7,6},{8,9},{9,8},{10,11... | collective-permute-start | bytes 3194888 | tf_op jit(solution)/shard_map/ppermute | solution.py:634
  145.2 63.7 %collective-permute-start.22 = (bf16[2,528,768]{2,1,0:T(8,128)(2,1)}, bf16[2,528,768]{2,1,0:T(8,128)(2,1)}, u32[]{:S(2)}, u32[]{:S(2)}) collective-permute-start(bf16[2,528,768]{2,1,0:T(8,128)(2,1)} %cut.3), channel_id=1, source_target_pairs={{0,2},{1,3},{2,6},{3,7},{4,0},{5,1},{6,4},{7,5},{8,10},{9,11},{10,... | collective-permute-start | bytes 4866056 | tf_op jit(solution)/shard_map/ppermute | solution.py:634
  181.7 32.3 %collective-permute-start.20 = (bf16[8,128,768]{2,1,0:T(8,128)(2,1)}, bf16[8,128,768]{2,1,0:T(8,128)(2,1)}, u32[]{:S(2)}, u32[]{:S(2)}) collective-permute-start(bf16[8,128,768]{2,1,0:T(8,128)(2,1)} %get-tuple-element.107), channel_id=1, source_target_pairs={{0,8},{1,9},{2,10},{3,11},{4,12},{5,13},{6,14},{7,15},{8,0},{9,1},... | collective-permute-start | bytes 4718600 | tf_op jit(solution)/shard_map/ppermute | solution.py:634
  182.2 39.9 %collective-permute-start.17 = (bf16[2,512,768]{2,1,0:T(8,128)(2,1)}, bf16[2,512,768]{2,1,0:T(8,128)(2,1)}, u32[]{:S(2)}, u32[]{:S(2)}) collective-permute-start(bf16[2,512,768]{2,1,0:T(8,128)(2,1)} %get-tuple-element.98.refs_3_.refs_7_), channel_id=1, source_target_pairs={{0,16},{1,17},{2,18},{3,19},{4,20},{5,21},{6,22},{7,23},{8,24},{9,... | collective-permute-start | bytes 4718600 | tf_op jit(solution)/shard_map/ppermute | solution.py:634
  182.5 39.6 %collective-permute-start.18 = (bf16[1040,512]{1,0:T(8,128)(2,1)}, bf16[1040,512]{1,0:T(8,128)(2,1)}, u32[]{:S(2)}, u32[]{:S(2)}) collective-permute-start(bf16[1040,512]{1,0:T(8,128)(2,1)} %get-tuple-element.99), channel_id=1, source_target_pairs={{0,9},{1,8},{2,11},{3,10},{4,13},{5,12},{6,15},{7,14},{8,1},{9,0},... | collective-permute-start | bytes 3194888 | tf_op jit(solution)/shard_map/ppermute | solution.py:634
  185.2 36.9 %collective-permute-start.19 = (bf16[528,512]{1,0:T(8,128)(2,1)}, bf16[528,512]{1,0:T(8,128)(2,1)}, u32[]{:S(2)}, u32[]{:S(2)}) collective-permute-start(bf16[528,512]{1,0:T(8,128)(2,1)} %get-tuple-element.105), channel_id=1, source_target_pairs={{0,1},{1,0},{2,3},{3,2},{4,5},{5,4},{6,7},{7,6},{8,9},{9,8},{10,11... | collective-permute-start | bytes 1622024 | tf_op jit(solution)/shard_map/ppermute | solution.py:634
  208.9 23.5 %collective-permute-start.24 = (bf16[1,512,768]{2,1,0:T(8,128)(2,1)}, bf16[1,512,768]{2,1,0:T(8,128)(2,1)}, u32[]{:S(2)}, u32[]{:S(2)}) collective-permute-start(bf16[1,512,768]{2,1,0:T(8,128)(2,1)} %cut.5), channel_id=1, source_target_pairs={{0,2},{1,3},{2,6},{3,7},{4,0},{5,1},{6,4},{7,5},{8,10},{9,11},{10,... | collective-permute-start | bytes 2359304 | tf_op jit(solution)/shard_map/ppermute | solution.py:634
  214.0 21.4 %collective-permute-start.23 = (bf16[1,512,768]{2,1,0:T(8,128)(2,1)}, bf16[1,512,768]{2,1,0:T(8,128)(2,1)}, u32[]{:S(2)}, u32[]{:S(2)}) collective-permute-start(bf16[1,512,768]{2,1,0:T(8,128)(2,1)} %cut.4), channel_id=1, source_target_pairs={{0,16},{1,17},{2,18},{3,19},{4,20},{5,21},{6,22},{7,23},{8,24},{9,... | collective-permute-start | bytes 2359304 | tf_op jit(solution)/shard_map/ppermute | solution.py:634
  222.1 13.7 %collective-permute-start.21 = (bf16[528,512]{1,0:T(8,128)(2,1)}, bf16[528,512]{1,0:T(8,128)(2,1)}, u32[]{:S(2)}, u32[]{:S(2)}) collective-permute-start(bf16[528,512]{1,0:T(8,128)(2,1)} %get-tuple-element.108), channel_id=1, source_target_pairs={{0,9},{1,8},{2,11},{3,10},{4,13},{5,12},{6,15},{7,14},{8,1},{9,0},... | collective-permute-start | bytes 1622024 | tf_op jit(solution)/shard_map/ppermute | solution.py:634
  235.8 11.8 %collective-permute-start.25 = (bf16[8,128,768]{2,1,0:T(8,128)(2,1)}, bf16[8,128,768]{2,1,0:T(8,128)(2,1)}, u32[]{:S(2)}, u32[]{:S(2)}) collective-permute-start(bf16[8,128,768]{2,1,0:T(8,128)(2,1)} %get-tuple-element.111), channel_id=1, source_target_pairs={{0,8},{1,9},{2,10},{3,11},{4,12},{5,13},{6,14},{7,15},{8,0},{9,1},... | collective-permute-start | bytes 4718600 | tf_op jit(solution)/shard_map/ppermute | solution.py:634
  236.2 25.2 %collective-permute-start.29 = (bf16[1040,512]{1,0:T(8,128)(2,1)}, bf16[1040,512]{1,0:T(8,128)(2,1)}, u32[]{:S(2)}, u32[]{:S(2)}) collective-permute-start(bf16[1040,512]{1,0:T(8,128)(2,1)} %get-tuple-element.121), channel_id=1, source_target_pairs={{0,8},{1,9},{2,10},{3,11},{4,12},{5,13},{6,14},{7,15},{8,0},{9,1},... | collective-permute-start | bytes 3194888 | tf_op jit(solution)/shard_map/ppermute | solution.py:634
  240.9 27.6 %collective-permute-start.27 = (bf16[560,512]{1,0:T(8,128)(2,1)}, bf16[560,512]{1,0:T(8,128)(2,1)}, u32[]{:S(2)}, u32[]{:S(2)}) collective-permute-start(bf16[560,512]{1,0:T(8,128)(2,1)} %score.11.refs_5_.refs_3_), channel_id=1, source_target_pairs={{0,1},{1,0},{2,3},{3,2},{4,5},{5,4},{6,7},{7,6},{8,9},{9,8},{10,11... | collective-permute-start | bytes 1720328 | tf_op jit(solution)/shard_map/ppermute | solution.py:634
  247.5 21.0 %collective-permute-start.28 = (bf16[544,512]{1,0:T(8,128)(2,1)}, bf16[544,512]{1,0:T(8,128)(2,1)}, u32[]{:S(2)}, u32[]{:S(2)}) collective-permute-start(bf16[544,512]{1,0:T(8,128)(2,1)} %score.12.refs_12_), channel_id=1, source_target_pairs={{0,9},{1,8},{2,11},{3,10},{4,13},{5,12},{6,15},{7,14},{8,1},{9,0},... | collective-permute-start | bytes 1671176 | tf_op jit(solution)/shard_map/ppermute | solution.py:634
  256.7 4.7 %collective-permute-start.30 = (bf16[528,512]{1,0:T(8,128)(2,1)}, bf16[528,512]{1,0:T(8,128)(2,1)}, u32[]{:S(2)}, u32[]{:S(2)}) collective-permute-start(bf16[528,512]{1,0:T(8,128)(2,1)} %get-tuple-element.122), channel_id=1, source_target_pairs={{0,8},{1,9},{2,10},{3,11},{4,12},{5,13},{6,14},{7,15},{8,0},{9,1},... | collective-permute-start | bytes 1622024 | tf_op jit(solution)/shard_map/ppermute | solution.py:634
  257.5 11.0 %collective-permute-start.26 = (bf16[528,512]{1,0:T(8,128)(2,1)}, bf16[528,512]{1,0:T(8,128)(2,1)}, u32[]{:S(2)}, u32[]{:S(2)}) collective-permute-start(bf16[528,512]{1,0:T(8,128)(2,1)} %get-tuple-element.117), channel_id=1, source_target_pairs={{0,8},{1,9},{2,10},{3,11},{4,12},{5,13},{6,14},{7,15},{8,0},{9,1},... | collective-permute-start | bytes 1622024 | tf_op jit(solution)/shard_map/ppermute | solution.py:634
